TPU v7x, 128 devices: a whole 4x4x4 slice. The times are simulated.
128 devices in a mesh: row: 16 (over x_lo, y, core), col: 8 (over z, x_hi).
Axes of the slice: x: 4 (x_hi: 2, x_lo: 2; x = x_hi * 2 + x_lo), y: 4, z: 4, core: 2. Of those that a mesh axis runs over, the one named last changes fastest.
Arguments:
- pair_map: bfloat16 [8, 48, 128, 1024], P(None, None, 'row', 'col'), may hold values from -6 to 6
- cotangent: bfloat16 [8, 48, 128, 1024], P(None, None, 'row', 'col'), may hold values from -6 to 6
- conv_weight: bfloat16 [24, 48, 3, 3], replicated, may hold values from -0.3125 to 0.3125
- conv_gain: float32 [24], replicated, may hold values from 0.1 to 1.9
- conv_bias: float32 [24], replicated, may hold values from -2 to 2
- mix_weight: bfloat16 [48, 24], replicated, may hold values from -1.25 to 1.25
- mix_gain: float32 [48], replicated, may hold values from 0.1 to 1.9
- mix_bias: float32 [48], replicated, may hold values from -2 to 2
Outputs:
- symmetric: bfloat16 [8, 48, 128, 1024], P(None, None, 'row', 'col')
- grad_input: bfloat16 [8, 48, 128, 1024], P(None, None, 'row', 'col')
- grad_conv: float32 [24, 48, 3, 3], replicated
- grad_mix: float32 [48, 24], replicated
All inputs are finite; a program needn't handle non-finite values.
Results may differ from a plain program's by a relative error of at most 0.0065.
Values may be sent and summed in bfloat16 or wider, within the bound.
No kernel may reach another device: no remote copies, remote signals or barrier semaphores. Data moves between devices by JAX's collectives and lax.ppermute only.
A program may use at most 64 MiB of HBM per device.

v0:
```python
import functools

import jax
import jax.numpy as jnp
from jax import lax
from jax.experimental import pallas as pl
from jax.experimental.pallas import tpu as pltpu
from jax.sharding import PartitionSpec as P

BF = jnp.bfloat16
F32 = jnp.float32
CH, MID, GROUPS, H, LANES, ROWS, COLS = 48, 24, 8, 8, 128, 16, 8
POS = GROUPS * LANES
CR, MR = CH * H, MID * H
TANH_SCALE = 0.7978845608028654
CUBIC = 0.044715
NN = (((1,), (0,)), ((), ()))
NT = (((1,), (1,)), ((), ()))
TN = (((0,), (0,)), ((), ()))


def smooth(v):
    t = jnp.tanh(TANH_SCALE * (v + CUBIC * (v * v * v)))
    return 0.5 * v * (1.0 + t)


def smooth_slope(v):
    s = v * v
    t = jnp.tanh(TANH_SCALE * (v + CUBIC * (v * s)))
    return 0.5 * (1.0 + t) + (0.5 * v) * (1.0 - t * t) * (TANH_SCALE * (1.0 + (3.0 * CUBIC) * s))


def dot(a, b, dims=NN):
    return lax.dot_general(a, b, dims, preferred_element_type=F32)


def iota(shape, dim):
    return lax.broadcasted_iota(jnp.int32, shape, dim)


def identity(n):
    return jnp.where(iota((n, n), 0) == iota((n, n), 1), 1.0, 0.0).astype(BF)


def lanes_of(rows):
    return iota((rows, LANES), 1)


def call(kernel, outs, args, name, smem=(), flops=4_000_000_000, scratch=()):
    specs = [
        pl.BlockSpec(memory_space=pltpu.SMEM if i in smem else pltpu.VMEM) for i in range(len(args))
    ]
    return pl.pallas_call(
        kernel,
        name=name,
        out_shape=[jax.ShapeDtypeStruct(s, t) for s, t in outs],
        in_specs=specs,
        out_specs=[pl.BlockSpec(memory_space=pltpu.VMEM) for _ in outs],
        scratch_shapes=list(scratch),
        compiler_params=pltpu.CompilerParams(vmem_limit_bytes=48 * 1024 * 1024),
        cost_estimate=pl.CostEstimate(flops=flops, bytes_accessed=1_000_000, transcendentals=0),
    )(*args)


def pack_rows(field, count):
    pairs = field.reshape(count // 2, 2, H, LANES)
    even, odd = pairs[:, 0], pairs[:, 1]
    low = iota(even.shape, 1) < 4
    last = jnp.where(low, pltpu.roll(even, 4, 1), odd)
    first = jnp.where(low, even, pltpu.roll(odd, 4, 1))
    return last, first


def send_rows(source, down, up, count):
    at_end = (lax.axis_index("row") == ROWS - 1).astype(jnp.int32)
    at_start = (lax.axis_index("row") == 0).astype(jnp.int32)
    for g in range(GROUPS):
        before = g - at_end
        last, _ = pack_rows(source[jnp.maximum(before, 0)].astype(F32), count)
        down[g] = jnp.where(before >= 0, last, 0.0).astype(BF)
        after = g + at_start
        _, first = pack_rows(source[jnp.minimum(after, GROUPS - 1)].astype(F32), count)
        up[g] = jnp.where(after < GROUPS, first, 0.0).astype(BF)


def rows_kernel(x, down, up):
    send_rows(x, down, up, CH)


def turn_out(value, eye, pieces, g, first_tile):
    turned = dot(eye, value, NT)
    for k in range(3):
        part = turned[:, k * LANES : (k + 1) * LANES].reshape(ROWS, H, LANES)
        pieces[:, g, first_tile + k] = part.astype(BF)


def turn_in(pieces, g, first_tile, buffer):
    parts = [
        pieces[r, g, first_tile : first_tile + 3].astype(F32).reshape(3 * H, LANES)
        for r in range(ROWS)
    ]
    lane = lanes_of(3 * H)
    for k in range(4):
        m = 1 << k
        high = (lane // (8 * m)) % 2 == 1
        for i in range(ROWS):
            if i & m:
                continue
            a, b = parts[i], parts[i | m]
            parts[i] = jnp.where(high, pltpu.roll(b, 8 * m, 1), a)
            parts[i | m] = jnp.where(high, b, pltpu.roll(a, LANES - 8 * m, 1))
    for i in range(ROWS):
        buffer[:, i] = parts[i].reshape(3, H, LANES)
    return buffer[...].reshape(CR, LANES)


def mirror_kernel(d, pieces):
    eye = identity(LANES)
    for g in range(GROUPS):
        turn_out(d[g].astype(F32).reshape(CR, LANES).astype(BF), eye, pieces, g, 0)


def weights_kernel(w, mix, cg, cb, mg, mb, a_out, b_out, mf_out, mb_out, cgf, cbf, mgf, mbf):
    for o in range(MID):
        cgf[o] = jnp.full((H, LANES), cg[o], F32)
        cbf[o] = jnp.full((H, LANES), cb[o], F32)
    for o in range(CH):
        mgf[o] = jnp.full((H, LANES), mg[o], F32)
        mbf[o] = jnp.full((H, LANES), mb[o], F32)

    def spread(n, own, width):
        col = iota((n, width), 1)
        half = (width - own) // 2
        rim = jnp.where(col < own + half, col - own, col - own - half) // 4
        return jnp.where(jnp.where(col < own, col // 8, rim) == iota((n, width), 0), 1.0, 0.0).astype(BF)

    def place(own, width):
        col, h = iota((H, width), 1), iota((H, width), 0)
        half = (width - own) // 2
        rim = jnp.where(col < own + half, (col - own) % 4 - 4, (col - own - half) % 4 + 8)
        return jnp.where(col < own, col % 8, rim) - h

    sf, st = spread(CH, CR, 2 * CR), spread(MID, MR, 2 * MR)
    pf, pt = place(CR, 2 * CR), place(MR, 2 * MR)
    for b in range(3):
        total_a = jnp.zeros((MID, H, 2 * CR), F32)
        total_b = jnp.zeros((CH, H, 2 * MR), F32)
        for a in range(3):
            tap = w[3 * a + b]
            mask = jnp.where(pf == 4 * (a - 1), 1.0, 0.0)
            total_a += dot(tap, sf)[:, None, :] * mask[None]
            mask = jnp.where(pt == -4 * (a - 1), 1.0, 0.0)
            total_b += dot(tap, st, TN)[:, None, :] * mask[None]
        a_out[b * MR : (b + 1) * MR] = total_a.reshape(MR, 2 * CR).astype(BF)
        b_out[b * CR : (b + 1) * CR] = total_b.reshape(CR, 2 * MR).astype(BF)
    mask = jnp.where(pf[:, :CR] == 0, 1.0, 0.0)
    mb_out[...] = (dot(mix[...], sf[:, :CR])[:, None, :] * mask[None]).reshape(MR, CR).astype(BF)
    mask = jnp.where(pt[:, :MR] == 0, 1.0, 0.0)
    mf_out[...] = (dot(mix[...], st[:, :MR], TN)[:, None, :] * mask[None]).reshape(CR, MR).astype(BF)


def act_kernel(x, above, below, act, edge):
    lane = lanes_of(CR)
    packed = jnp.zeros((CR, LANES), F32)
    for g in range(GROUPS):
        own = smooth(x[g].astype(F32).reshape(CR, LANES))
        high = smooth(above[g].astype(F32).reshape(CR // 2, LANES))
        low = smooth(below[g].astype(F32).reshape(CR // 2, LANES))
        rim = jnp.concatenate([high, low], axis=0)
        at = slice(g * LANES, (g + 1) * LANES)
        act[0:CR, at] = own.astype(BF)
        act[CR : 2 * CR, at] = rim.astype(BF)
        packed = jnp.where(lane // 8 == g, pltpu.roll(own, (8 * g - 124) % LANES, 1), packed)
        packed = jnp.where(lane // 8 == 8 + g, pltpu.roll(rim, (8 * g - 60) % LANES, 1), packed)
    edge[...] = packed.astype(BF)


def merge_edges(from_left, from_right):
    lane = lanes_of(from_left.shape[0])
    col = lax.axis_index("col")
    has_left = jnp.where(col > 0, 1.0, 0.0)
    has_right = jnp.where(col < COLS - 1, 1.0, 0.0)
    return jnp.where(
        lane % 8 < 4,
        pltpu.roll(from_right, LANES - 4, 1) * has_right,
        pltpu.roll(from_left, 4, 1) * has_left,
    )


def forward_kernel(
    x, act, from_left, from_right, weights, mixer, cg, cb, mg, mb,
    pre_out, hidden_out, rim_out, block_out, pieces,
):
    eye = identity(LANES)
    rim = merge_edges(from_left[...].astype(F32), from_right[...].astype(F32)).astype(BF)
    rim_out[...] = rim
    outer = dot(weights[:, 0:CR], rim) + pltpu.roll(dot(weights[:, CR : 2 * CR], rim), 64, 1)
    lane = lanes_of(MR)
    outer = jnp.where(lane % 8 < 4, outer[2 * MR : 3 * MR], outer[0:MR])
    gain, shift = cg[...].reshape(MR, LANES), cb[...].reshape(MR, LANES)
    for pair in range(GROUPS // 2):
        two = slice(pair * 2 * LANES, (pair + 1) * 2 * LANES)
        product = dot(weights[...], act[:, two])
        for half in range(2):
            g = 2 * pair + half
            p = product[:, half * LANES : (half + 1) * LANES]
            q = pltpu.roll(outer, (124 - 8 * g) % LANES, 1)
            inner = (
                p[MR : 2 * MR]
                + jnp.where(lane < 4, q, pltpu.roll(p[0:MR], 4, 1))
                + jnp.where(lane >= 124, q, pltpu.roll(p[2 * MR : 3 * MR], LANES - 4, 1))
            )
            pre = inner * gain + shift
            at = slice(g * LANES, (g + 1) * LANES)
            pre_out[:, at] = pre
            hidden_out[:, at] = smooth(pre).astype(BF)
        mixed = dot(mixer[...], hidden_out[:, two])
        for half in range(2):
            g = 2 * pair + half
            m = mixed[:, half * LANES : (half + 1) * LANES]
            value = x[g].astype(F32).reshape(CR, LANES) + m * mg[...].reshape(CR, LANES)
            value = (value + mb[...].reshape(CR, LANES)).astype(BF)
            block_out[g] = value.astype(F32).reshape(CH, H, LANES).astype(BF)
            turn_out(value, eye, pieces, g, 0)


def split(value):
    high = value.astype(BF)
    return high, (value - high.astype(F32)).astype(BF)


def exact_dot(value, onehot):
    high, low = split(value)
    return dot(high, onehot) + dot(low, onehot)


def backward_kernel(
    d, arrived, pre_in, hidden, act, rim, turned, mixer, cg, mg,
    grad_inner, down, up, half_sum, pieces,
    buffer, gmi, shifted, edge_rows, wide, mixwide,
):
    lane = lanes_of(MR)
    gain = cg[...].reshape(MR, LANES)
    packed = jnp.zeros((MR, LANES), F32)
    for pair in range(GROUPS // 2):
        two = slice(pair * 2 * LANES, (pair + 1) * 2 * LANES)
        for half in range(2):
            g = 2 * pair + half
            both = 0.5 * (d[g].astype(F32).reshape(CR, LANES) + turn_in(arrived, g, 0, buffer))
            half_sum[g] = both.reshape(CH, H, LANES)
            gmi[:, g * LANES : (g + 1) * LANES] = (both * mg[...].reshape(CR, LANES)).astype(BF)
        into = dot(mixer[...], gmi[:, two])
        for half in range(2):
            g = 2 * pair + half
            at = slice(g * LANES, (g + 1) * LANES)
            value = into[:, half * LANES : (half + 1) * LANES] * smooth_slope(pre_in[:, at]) * gain
            grad_inner[g] = value.reshape(MID, H, LANES).astype(BF)
            shifted[0:MR, at] = jnp.where(lane < 124, pltpu.roll(value, LANES - 4, 1), 0.0).astype(BF)
            shifted[MR : 2 * MR, at] = value.astype(BF)
            shifted[2 * MR : 3 * MR, at] = jnp.where(lane >= 4, pltpu.roll(value, 4, 1), 0.0).astype(BF)
            packed = jnp.where(lane // 8 == g, pltpu.roll(value, (8 * g - 124) % LANES, 1), packed)
    send_rows(grad_inner, down, up, MID)

    packed = packed + pltpu.roll(packed, 64, 1)
    edge_rows[0:MR] = jnp.where(lane % 8 >= 4, packed, 0.0).astype(BF)
    edge_rows[MR : 2 * MR] = jnp.zeros((MR, LANES), BF)
    edge_rows[2 * MR : 3 * MR] = jnp.where(lane % 8 < 4, packed, 0.0).astype(BF)
    lane_c = lanes_of(CR)
    rim_value = rim[...].astype(F32)
    rim_own = jnp.where(lane_c < 64, rim_value, 0.0).astype(BF)
    rim_far = jnp.where(lane_c >= 64, rim_value, 0.0).astype(BF)
    for k in range(2):
        rows = slice(k * CR, (k + 1) * CR)
        wide[:, rows] = dot(shifted[...], act[rows], NT) + dot(edge_rows[...], (rim_own, rim_far)[k], NT)
    mixwide[...] = dot(hidden[...], gmi[...], NT)

    h, col = iota((H, CR), 0), iota((H, CR), 1)
    same = jnp.where(col % 8 == h, 1.0, 0.0)[None]
    other = jnp.where(col % 8 == (h + 4) % 8, 1.0, 0.0)[None]
    far = jnp.where((col - jnp.where(col < CR // 2, 0, CR // 2)) % 4 == jnp.where(col < CR // 2, h, h - 4), 1.0, 0.0)[None]
    col, lane_s = iota((CR, LANES), 0), iota((CR, LANES), 1)

    def gather(keep, channel, side):
        return jnp.where(jnp.logical_and(keep, channel + 64 * side == lane_s), 1.0, 0.0).astype(BF)

    blocks = []
    sums = []
    for b in range(3):
        block = wide[b * MR : (b + 1) * MR]
        own = block[:, 0:CR].reshape(MID, H, CR)
        rest = block[:, CR : 2 * CR].reshape(MID, H, CR)
        sums.append([jnp.sum(own * same, axis=1), jnp.sum(own * other, axis=1), jnp.sum(rest * far, axis=1)])
    mixed = jnp.sum(mixwide[...].reshape(MID, H, CR) * same, axis=1)
    always = col >= 0
    own_low = col % 8 < 4
    rest_low = col < CR // 2
    rest_channel = jnp.where(rest_low, col, col - CR // 2) // 4
    for index in range(10):
        side = index % 2
        if index == 9:
            value = exact_dot(mixed, gather(always, col // 8, side))
        else:
            a, b = index // 3, index % 3
            if a == 1:
                value = exact_dot(sums[b][0], gather(always, col // 8, side))
            else:
                low = a == 0
                keep_own = own_low if low else jnp.logical_not(own_low)
                keep_rest = rest_low if low else jnp.logical_not(rest_low)
                value = exact_dot(sums[b][1], gather(keep_own, col // 8, side))
                value += exact_dot(sums[b][2], gather(keep_rest, rest_channel, side))
        blocks.append(value)
    for p in range(5):
        value = blocks[2 * p] + blocks[2 * p + 1]
        high = value.astype(BF).astype(F32)
        low = value - high
        for k in range(3):
            r = 3 * p + k
            rows = slice(k * H, (k + 1) * H)
            pieces[r, :, 0] = jnp.broadcast_to(high[rows][None], (COLS, H, LANES)).astype(BF)
            pieces[r, :, 1] = jnp.broadcast_to(low[rows][None], (COLS, H, LANES)).astype(BF)
    pieces[ROWS - 1, :, 0:2] = jnp.zeros((COLS, 2, H, LANES), BF)
    for r in range(ROWS):
        pieces[r, :, 2:5] = turned[r]


def spread_kernel(grad_inner, above, below, weights, main, edge, rhs):
    lane = lanes_of(CR)
    packed = jnp.zeros((CR, LANES), F32)
    for pair in range(GROUPS // 2):
        for half in range(2):
            g = 2 * pair + half
            at = slice(half * LANES, (half + 1) * LANES)
            rhs[0:MR, at] = grad_inner[g].astype(F32).reshape(MR, LANES).astype(BF)
            rhs[MR : MR + MR // 2, at] = above[g].astype(F32).reshape(MR // 2, LANES).astype(BF)
            rhs[MR + MR // 2 : 2 * MR, at] = below[g].astype(F32).reshape(MR // 2, LANES).astype(BF)
        product = dot(weights[...], rhs[...])
        for half in range(2):
            g = 2 * pair + half
            p = product[:, half * LANES : (half + 1) * LANES]
            left, mid, right = p[0:CR], p[CR : 2 * CR], p[2 * CR : 3 * CR]
            main[:, g * LANES : (g + 1) * LANES] = (
                mid
                + jnp.where(lane < 124, pltpu.roll(left, LANES - 4, 1), 0.0)
                + jnp.where(lane >= 4, pltpu.roll(right, 4, 1), 0.0)
            )
            out = jnp.where(lane >= 124, right, left)
            packed = jnp.where(lane // 8 == g, pltpu.roll(out, (8 * g - 124) % LANES, 1), packed)
    edge[...] = packed[0 : CR // 2] + pltpu.roll(packed[CR // 2 : CR], 64, 1)


def input_kernel(x, half_sum, main, from_left, from_right, grad_input):
    lane = lanes_of(CR)
    rim = merge_edges(from_left[...], from_right[...])
    rim = jnp.concatenate([rim, pltpu.roll(rim, 64, 1)], axis=0)
    for g in range(GROUPS):
        q = pltpu.roll(rim, (124 - 8 * g) % LANES, 1)
        total = main[:, g * LANES : (g + 1) * LANES]
        total = total + jnp.where(jnp.logical_or(lane < 4, lane >= 124), q, 0.0)
        slope = smooth_slope(x[g].astype(F32).reshape(CR, LANES))
        value = half_sum[g].reshape(CR, LANES) + total * slope
        grad_input[g] = value.reshape(CH, H, LANES).astype(BF)


def total_kernel(arrived, out):
    total = jnp.zeros((H, LANES), F32)
    for g in range(GROUPS):
        part = arrived[:, g].astype(F32)
        total += jnp.sum(part[:, 0] + part[:, 1], axis=0)
    out[...] = jnp.broadcast_to((total * (1.0 / (ROWS * H * COLS)))[None], (ROWS, H, LANES))


def symmetric_kernel(block, arrived, out, buffer):
    for g in range(GROUPS):
        value = 0.5 * (block[g].astype(F32).reshape(CR, LANES) + turn_in(arrived, g, 2, buffer))
        out[g] = value.reshape(CH, H, LANES).astype(BF)


def unpack_kernel(tiles, conv, mix):
    for p in range(5):
        value = tiles[3 * p : 3 * p + 3].reshape(3 * H, LANES)
        conv[2 * p] = value[:, 0:CH]
        if p < 4:
            conv[2 * p + 1] = value[:, 64 : 64 + CH]
        else:
            mix[...] = value[:, 64 : 64 + CH]


def both_ways(first, second, axis):
    count = lax.axis_size(axis)
    onward = [(i, (i + 1) % count) for i in range(count)]
    back = [(t, s) for s, t in onward]
    return lax.ppermute(first, axis, onward), lax.ppermute(second, axis, back)


def local(pair_map, cotangent, conv_weight, conv_gain, conv_bias, mix_weight, mix_gain, mix_bias):
    tile = (GROUPS, CH, H, LANES)
    everyone = ("row", "col")
    down, up = call(rows_kernel, [((GROUPS, CH // 2, H, LANES), BF)] * 2, (pair_map,), "rows")
    above, below = both_ways(down, up, "row")
    (d_pieces,) = call(mirror_kernel, [((ROWS, COLS, 3, H, LANES), BF)], (cotangent,), "turn_d")
    d_pieces = d_pieces.reshape(ROWS * COLS, 3, H, LANES)
    d_arrived = lax.all_to_all(d_pieces, everyone, 0, 0, tiled=True)
    d_arrived = d_arrived.reshape(ROWS, COLS, 3, H, LANES)

    taps = jnp.transpose(conv_weight, (2, 3, 0, 1)).reshape(9, MID, CH)
    wf, wb, mf, mbk, cg, cb, mg, mb = call(
        weights_kernel,
        [((3 * MR, 2 * CR), BF), ((3 * CR, 2 * MR), BF), ((CR, MR), BF), ((MR, CR), BF)]
        + [((MID, H, LANES), F32)] * 2
        + [((CH, H, LANES), F32)] * 2,
        (taps, mix_weight.T, conv_gain, conv_bias, mix_gain, mix_bias),
        "weights",
        smem=(2, 3, 4, 5),
    )
    act, edge = call(
        act_kernel, [((2 * CR, POS), BF), ((CR, LANES), BF)], (pair_map, above, below), "act"
    )
    from_left, from_right = both_ways(edge, edge, "col")
    pre, hidden, rim, block, b_turned = call(
        forward_kernel,
        [((MR, POS), F32), ((MR, POS), BF), ((CR, LANES), BF), (tile, BF), ((ROWS, COLS, 3, H, LANES), BF)],
        (pair_map, act, from_left, from_right, wf, mf, cg, cb, mg, mb),
        "forward",
    )
    grad_inner, g_down, g_up, half_sum, pieces = call(
        backward_kernel,
        [
            ((GROUPS, MID, H, LANES), BF),
            ((GROUPS, MID // 2, H, LANES), BF),
            ((GROUPS, MID // 2, H, LANES), BF),
            (tile, F32),
            ((ROWS, COLS, 5, H, LANES), BF),
        ],
        (cotangent, d_arrived, pre, hidden, act, rim, b_turned, mbk, cg, mg),
        "backward",
        scratch=[
            pltpu.VMEM((3, ROWS, H, LANES), F32),
            pltpu.VMEM((CR, POS), BF),
            pltpu.VMEM((3 * MR, POS), BF),
            pltpu.VMEM((3 * MR, LANES), BF),
            pltpu.VMEM((3 * MR, 2 * CR), F32),
            pltpu.VMEM((MR, CR), F32),
        ],
    )
    arrived = lax.all_to_all(pieces.reshape(ROWS * COLS, 5, H, LANES), everyone, 0, 0, tiled=True)
    arrived = arrived.reshape(ROWS, COLS, 5, H, LANES)
    g_above, g_below = both_ways(g_down, g_up, "row")
    main, g_edge = call(
        spread_kernel,
        [((CR, POS), F32), ((CR // 2, LANES), F32)],
        (grad_inner, g_above, g_below, wb),
        "spread",
        scratch=[pltpu.VMEM((2 * MR, 2 * LANES), BF)],
    )
    g_left, g_right = both_ways(g_edge, g_edge, "col")
    (grad_input,) = call(input_kernel, [(tile, BF)], (pair_map, half_sum, main, g_left, g_right), "grad_input")
    (sums,) = pl.pallas_call(
        total_kernel,
        name="total",
        grid=(1,),
        out_shape=[jax.ShapeDtypeStruct((ROWS, H, LANES), F32)],
        in_specs=[pl.BlockSpec((ROWS, COLS, 2, H, LANES), lambda i: (0, 0, 0, 0, 0))],
        out_specs=[pl.BlockSpec((ROWS, H, LANES), lambda i: (0, 0, 0))],
        cost_estimate=pl.CostEstimate(flops=500_000_000, bytes_accessed=600_000, transcendentals=0),
    )(arrived)
    sums = lax.all_to_all(sums, "row", 0, 0, tiled=True)
    (symmetric,) = call(
        symmetric_kernel, [(tile, BF)], (block, arrived), "symmetric",
        scratch=[pltpu.VMEM((3, ROWS, H, LANES), F32)],
    )
    conv, mix = call(
        unpack_kernel, [((9, MID, CH), F32), ((MID, CH), F32)], (sums,), "unpack", flops=100_000_000
    )
    grad_conv = jnp.transpose(conv.reshape(3, 3, MID, CH), (2, 3, 0, 1))
    return symmetric, grad_input, grad_conv, mix.T


def solution(mesh):
    field = P(None, None, "row", "col")
    return jax.shard_map(
        local,
        mesh=mesh,
        in_specs=(field, field, P(), P(), P(), P(), P(), P()),
        out_specs=(field, field, P(), P()),
        check_vma=False,
    )
```

profile of v0, /device:TPU:1, one launch (start us, length us, event | category | flops | bytes accessed | tf_op | source)
XLA Modules:
  0.0 118.0 jit_solution(1525084806292889701)
XLA Ops:
  2.7 2.7 %collective-permute-start = (bf16[8,24,8,128]{3,2,1,0:T(8,128)(2,1)}, bf16[8,24,8,128]{3,2,1,0:T(8,128)(2,1)S(1)}, u32[]{:S(2)}, u32[]{:S(2)}) collective-permute-start(bf16[8,24,8,128]{3,2,1,0:T(8,128)(2,1)} %get-tuple-element.30), channel_id=1, source_target_pairs={{0,8},{8,16},{16,24},{24,32},{32,40},{40,48},{48,56},{56,64},{64,7... | collective-permute-start | bytes 1179656 | tf_op jit(solution)/shard_map/ppermute | solution.py:393
  5.4 1.3 %turn_d.1 = bf16[16,8,3,8,128]{4,3,2,1,0:T(8,128)(2,1)} custom-call(bf16[8,48,8,128]{3,2,1,0:T(8,128)(2,1)S(1)} %copy-done.2), custom_call_target="tpu_custom_call" | custom-call | flops 4000000000 | bytes 1000000 | tf_op jit(solution)/shard_map/turn_d/pallas_call | solution.py:53
  6.8 10.6 %all-to-all-start = ((bf16[128,3,8,128]{3,2,1,0:T(8,128)(2,1)}), bf16[128,3,8,128]{3,2,1,0:T(8,128)(2,1)S(1)}, u32[]{:S(2)}, u32[]{:S(2)}) async-start(bf16[128,3,8,128]{3,2,1,0:T(8,128)(2,1)} %bitcast.3), calls=%async_computation | async-start | bytes 1572864 | tf_op jit(solution)/shard_map/all_to_all | solution.py:403
  17.4 1.4 %act.1 = (bf16[768,1024]{1,0:T(8,128)(2,1)S(1)}, bf16[384,128]{1,0:T(8,128)(2,1)S(1)}) custom-call(bf16[8,48,8,128]{3,2,1,0:T(8,128)(2,1)S(1)} %copy-done.4, bf16[8,24,8,128]{3,2,1,0:T(8,128)(2,1)S(1)} %collective-permute-done.above, bf16[8,24,8,128]{3,2,1,0:T(8,128)(2,1)S(1)} %collective-permute-done.1.below), custom_call_target="tpu_custom_call" | custom-call | flops 4000000000 | bytes 1000000 | tf_op jit(solution)/shard_map/act/pallas_call | solution.py:53
  20.0 5.7 %collective-permute-start.3 = (bf16[384,128]{1,0:T(8,128)(2,1)S(1)}, bf16[384,128]{1,0:T(8,128)(2,1)S(1)}, u32[]{:S(2)}, u32[]{:S(2)}) collective-permute-start(bf16[384,128]{1,0:T(8,128)(2,1)S(1)} %get-tuple-element.33), channel_id=1, source_target_pairs={{1,0},{2,1},{3,2},{4,3},{5,4},{6,5},{7,6},{0,7},{9,8},{10,9},{11,1... | collective-permute-start | bytes 294920 | tf_op jit(solution)/shard_map/ppermute | solution.py:393
  25.7 2.3 %weights.1 = (bf16[576,768]{1,0:T(8,128)(2,1)S(1)}, bf16[1152,384]{1,0:T(8,128)(2,1)S(1)}, bf16[384,192]{1,0:T(8,128)(2,1)S(1)}, bf16[192,384]{1,0:T(8,128)(2,1)...) custom-call(bf16[9,24,48]{2,1,0:T(8,128)(2,1)S(1)} %bitcast.15, ...), custom_call_target="tpu_custom_call" | custom-call | flops 4000000000 | bytes 1000000 | tf_op jit(solution)/shard_map/weights/pallas_call | solution.py:53
  29.6 1.2 %collective-permute-done.3.from_right = bf16[384,128]{1,0:T(8,128)(2,1)S(1)} collective-permute-done((bf16[384,128]{1,0:T(8,128)(2,1)S(1)}, bf16[384,128]{1,0:T(8,128)(2,1)S(1)}, u32[]{:S(2)}, u32[]{:S(2)}) %collective-permute-start.3) | collective-permute-done | bytes 98336 | tf_op jit(solution)/shard_map/ppermute | solution.py:393
  30.8 4.9 %collective-permute-done.2.from_left = bf16[384,128]{1,0:T(8,128)(2,1)S(1)} collective-permute-done((bf16[384,128]{1,0:T(8,128)(2,1)S(1)}, bf16[384,128]{1,0:T(8,128)(2,1)S(1)}, u32[]{:S(2)}, u32[]{:S(2)}) %collective-permute-start.2) | collective-permute-done | bytes 98336 | tf_op jit(solution)/shard_map/ppermute | solution.py:393
  35.8 5.9 %forward.1 = (f32[192,1024]{1,0:T(8,128)S(1)}, bf16[192,1024]{1,0:T(8,128)(2,1)S(1)}, bf16[384,128]{1,0:T(8,128)(2,1)S(1)}, bf16[8,48,8,128]{3,2,1,0:T(8,128)(2,1)S(1)}, bf16[16,8,3,8,128]{4,3,2,1,0:T(8,128)(2,1)S(1)}) custom-call(bf16[8,48,8,128]{3,2,1,0:T(8,128)(2,1)S(1)} %copy-done.4, bf16[768,1024]{1,0:T(8,128)(2,1)} %copy-done.12, ...), custom_call_target="tpu_custom_call" | custom-call | flops 4000000000 | bytes 1000000 | tf_op jit(solution)/shard_map/forward/pallas_call | solution.py:53
  51.3 7.9 %backward.1 = (bf16[8,24,8,128]{3,2,1,0:T(8,128)(2,1)S(1)}, bf16[8,12,8,128]{3,2,1,0:T(8,128)(2,1)S(1)}, bf16[8,12,8,128]{3,2,1,0:T(8,128)(2,1)S(1)}, f32[8,48,8...) custom-call(bf16[8,48,8,128]{3,2,1,0:T(8,128)(2,1)S(1)} %copy-done.2, bf16[16,8,3,8,128]{4,3,2,1,0:T(8,128)(2,1)S(1)} %bitcast.14, ...), custom_call_target="tpu_custom_call" | custom-call | flops 4000000000 | bytes 1000000 | tf_op jit(solution)/shard_map/backward/pallas_call | solution.py:53
  59.9 5.4 %all-to-all-start.1 = ((bf16[128,5,8,128]{3,2,1,0:T(8,128)(2,1)}), bf16[128,5,8,128]{3,2,1,0:T(8,128)(2,1)S(1)}, u32[]{:S(2)}, u32[]{:S(2)}) async-start(bf16[128,5,8,128]{3,2,1,0:T(8,128)(2,1)} %bitcast.5), calls=%async_computation.1 | async-start | bytes 2621440 | tf_op jit(solution)/shard_map/all_to_all | solution.py:446
  65.4 1.7 %collective-permute-start.4 = (bf16[8,12,8,128]{3,2,1,0:T(8,128)(2,1)S(1)}, bf16[8,12,8,128]{3,2,1,0:T(8,128)(2,1)S(1)}, u32[]{:S(2)}, u32[]{:S(2)}) collective-permute-start(bf16[8,12,8,128]{3,2,1,0:T(8,128)(2,1)S(1)} %get-tuple-element.49), channel_id=1, source_target_pairs={{0,8},{8,16},{16,24},{24,32},{32,40},{40,48},{48,56},{56,64},{64,7... | collective-permute-start | bytes 589832 | tf_op jit(solution)/shard_map/ppermute | solution.py:393
  67.1 13.8 %collective-permute-done.4.above = bf16[8,12,8,128]{3,2,1,0:T(8,128)(2,1)S(1)} collective-permute-done((bf16[8,12,8,128]{3,2,1,0:T(8,128)(2,1)S(1)}, bf16[8,12,8,128]{3,2,1,0:T(8,128)(2,1)S(1)}, u32[]{:S(2)}, u32[]{:S(2)}) %collective-permute-start.4) | collective-permute-done | bytes 196640 | tf_op jit(solution)/shard_map/ppermute | solution.py:393
  80.8 2.6 %collective-permute-done.5.below = bf16[8,12,8,128]{3,2,1,0:T(8,128)(2,1)S(1)} collective-permute-done((bf16[8,12,8,128]{3,2,1,0:T(8,128)(2,1)S(1)}, bf16[8,12,8,128]{3,2,1,0:T(8,128)(2,1)S(1)}, u32[]{:S(2)}, u32[]{:S(2)}) %collective-permute-start.5) | collective-permute-done | bytes 196640 | tf_op jit(solution)/shard_map/ppermute | solution.py:393
  84.6 2.0 %spread.1 = (f32[384,1024]{1,0:T(8,128)S(1)}, f32[192,128]{1,0:T(8,128)S(1)}) custom-call(bf16[8,24,8,128]{3,2,1,0:T(8,128)(2,1)S(1)} %copy-done.20, bf16[8,12,8,128]{3,2,1,0:T(8,128)(2,1)S(1)} %collective-permute-done.4.above, bf16[8,12,8,128]{3,2,1,0:T(8,128)(2,1)S(1)} %collective-permute-done.5.below, bf16[1152,384]{1,0:T(8,128)(2,1)S(1)} %copy-done.18), custom_call_target="tpu_custom_call" | custom-call | flops 4000000000 | bytes 1000000 | tf_op jit(solution)/shard_map/spread/pallas_call | solution.py:53
  86.6 5.6 %collective-permute-start.7 = (f32[192,128]{1,0:T(8,128)S(1)}, f32[192,128]{1,0:T(8,128)S(1)}, u32[]{:S(2)}, u32[]{:S(2)}) collective-permute-start(f32[192,128]{1,0:T(8,128)S(1)} %get-tuple-element.53), channel_id=1, source_target_pairs={{1,0},{2,1},{3,2},{4,3},{5,4},{6,5},{7,6},{0,7},{9,8},{10,9},{11,1... | collective-permute-start | bytes 294920 | tf_op jit(solution)/shard_map/ppermute | solution.py:393
  92.2 1.6 %collective-permute-done.7.from_right = f32[192,128]{1,0:T(8,128)S(1)} collective-permute-done((f32[192,128]{1,0:T(8,128)S(1)}, f32[192,128]{1,0:T(8,128)S(1)}, u32[]{:S(2)}, u32[]{:S(2)}) %collective-permute-start.7) | collective-permute-done | bytes 98336 | tf_op jit(solution)/shard_map/ppermute | solution.py:393
  93.9 5.5 %collective-permute-done.6.from_left = f32[192,128]{1,0:T(8,128)S(1)} collective-permute-done((f32[192,128]{1,0:T(8,128)S(1)}, f32[192,128]{1,0:T(8,128)S(1)}, u32[]{:S(2)}, u32[]{:S(2)}) %collective-permute-start.6) | collective-permute-done | bytes 98336 | tf_op jit(solution)/shard_map/ppermute | solution.py:393
  99.4 2.1 %grad_input.1 = bf16[8,48,8,128]{3,2,1,0:T(8,128)(2,1)} custom-call(bf16[8,48,8,128]{3,2,1,0:T(8,128)(2,1)S(1)} %copy-done.4, f32[8,48,8,128]{3,2,1,0:T(8,128)S(1)} %copy-done.11, f32[384,1024]{1,0:T(8,128)S(1)} %get-tuple-element.52.main, f32[192,128]{1,0:T(8,128)S(1)} %collective-permute-done.6.from_left, f32[192,128]{1,0:T(8,128)S(1)} %collective-permute-done.7.from_right), custom_call_target="tpu_custom_call" | custom-call | flops 4000000000 | bytes 1000000 | tf_op jit(solution)/shard_map/grad_input/pallas_call | solution.py:53
  102.6 1.8 %total.1 = f32[16,8,128]{2,1,0:T(8,128)} custom-call(bf16[16,8,5,8,128]{4,3,2,1,0:T(8,128)(2,1)} %bitcast.12), custom_call_target="tpu_custom_call" | custom-call | flops 500000000 | bytes 600000 | tf_op jit(solution)/shard_map/total/pallas_call | solution.py:458
  104.4 7.0 %all-to-all-start.2 = ((f32[16,8,128]{2,1,0:T(8,128)}), f32[16,8,128]{2,1,0:T(8,128)S(1)}, u32[]{:S(2)}, u32[]{:S(2)}) async-start(f32[16,8,128]{2,1,0:T(8,128)} %total.1), calls=%async_computation.2 | async-start | bytes 131072 | tf_op jit(solution)/shard_map/all_to_all | solution.py:467
  111.4 1.3 %copy-done.1 = bf16[128,5,8,128]{3,2,1,0:T(8,128)(2,1)S(1)} copy-done((bf16[128,5,8,128]{3,2,1,0:T(8,128)(2,1)S(1)}, bf16[128,5,8,128]{3,2,1,0:T(8,128)(2,1)}, u32[]{:S(2)}) %copy-start.1) | copy-done | bytes 1310744
  112.7 2.9 %symmetric.1 = bf16[8,48,8,128]{3,2,1,0:T(8,128)(2,1)} custom-call(bf16[8,48,8,128]{3,2,1,0:T(8,128)(2,1)S(1)} %copy-done.16, bf16[16,8,5,8,128]{4,3,2,1,0:T(8,128)(2,1)S(1)} %bitcast.13), custom_call_target="tpu_custom_call" | custom-call | flops 4000000000 | bytes 1000000 | tf_op jit(solution)/shard_map/symmetric/pallas_call | solution.py:53
  115.6 1.7 %all-to-all-done.2.tiles = f32[16,8,128]{2,1,0:T(8,128)S(1)} async-done(((f32[16,8,128]{2,1,0:T(8,128)}), f32[16,8,128]{2,1,0:T(8,128)S(1)}, u32[]{:S(2)}, u32[]{:S(2)}) %all-to-all-start.2) | async-done | bytes 65568 | tf_op jit(solution)/shard_map/all_to_all | solution.py:467
  (71 shorter events, 18.2 us)
Async XLA Ops:
  0.6 4.8 %copy-start.2 = (bf16[8,48,8,128]{3,2,1,0:T(8,128)(2,1)S(1)}, bf16[8,48,8,128]{3,2,1,0:T(8,128)(2,1)}, u32[]{:S(2)}) copy-start(bf16[8,48,8,128]{3,2,1,0:T(8,128)(2,1)} %d.3) | copy-start | bytes 2359300
  2.7 14.7 %collective-permute-start = (bf16[8,24,8,128]{3,2,1,0:T(8,128)(2,1)}, bf16[8,24,8,128]{3,2,1,0:T(8,128)(2,1)S(1)}, u32[]{:S(2)}, u32[]{:S(2)}) collective-permute-start(bf16[8,24,8,128]{3,2,1,0:T(8,128)(2,1)} %get-tuple-element.30), channel_id=1, source_target_pairs={{0,8},{8,16},{16,24},{24,32},{32,40},{40,48},{48,56},{56,64},{64,7... | collective-permute-start | bytes 1179656 | tf_op jit(solution)/shard_map/ppermute | solution.py:393
  5.4 12.0 %collective-permute-start.1 = (bf16[8,24,8,128]{3,2,1,0:T(8,128)(2,1)S(1)}, bf16[8,24,8,128]{3,2,1,0:T(8,128)(2,1)S(1)}, u32[]{:S(2)}, u32[]{:S(2)}) collective-permute-start(bf16[8,24,8,128]{3,2,1,0:T(8,128)(2,1)S(1)} %get-tuple-element.31), channel_id=1, source_target_pairs={{8,0},{16,8},{24,16},{32,24},{40,32},{48,40},{56,48},{64,56},{72,6... | collective-permute-start | bytes 1179656 | tf_op jit(solution)/shard_map/ppermute | solution.py:393
  6.8 10.7 %copy-start.4 = (bf16[8,48,8,128]{3,2,1,0:T(8,128)(2,1)S(1)}, bf16[8,48,8,128]{3,2,1,0:T(8,128)(2,1)}, u32[]{:S(2)}) copy-start(bf16[8,48,8,128]{3,2,1,0:T(8,128)(2,1)} %x.7) | copy-start | bytes 2359300
  6.8 38.7 %all-to-all-start = ((bf16[128,3,8,128]{3,2,1,0:T(8,128)(2,1)}), bf16[128,3,8,128]{3,2,1,0:T(8,128)(2,1)S(1)}, u32[]{:S(2)}, u32[]{:S(2)}) async-start(bf16[128,3,8,128]{3,2,1,0:T(8,128)(2,1)} %bitcast.3), calls=%async_computation | async-start | bytes 1572864 | tf_op jit(solution)/shard_map/all_to_all | solution.py:403
  17.3 8.4 %copy-start.5 = (bf16[24,48,3,3]{1,0,3,2:T(8,128)(2,1)S(1)}, bf16[24,48,3,3]{1,0,3,2:T(8,128)(2,1)}, u32[]{:S(2)}) copy-start(bf16[24,48,3,3]{1,0,3,2:T(8,128)(2,1)} %param.10) | copy-start | bytes 62212
  17.3 8.4 %copy-start.6 = (bf16[48,24]{0,1:T(8,128)(2,1)S(1)}, bf16[48,24]{0,1:T(8,128)(2,1)}, u32[]{:S(2)}) copy-start(bf16[48,24]{0,1:T(8,128)(2,1)} %param.13) | copy-start | bytes 6916
  17.3 8.4 %copy-start.7 = (f32[24]{0:T(128)S(1)}, f32[24]{0:T(128)}, u32[]{:S(2)}) copy-start(f32[24]{0:T(128)} %cg.1) | copy-start | bytes 292
  17.4 8.4 %copy-start.8 = (f32[24]{0:T(128)S(1)}, f32[24]{0:T(128)}, u32[]{:S(2)}) copy-start(f32[24]{0:T(128)} %cb.1) | copy-start | bytes 292
  17.4 8.4 %copy-start.9 = (f32[48]{0:T(128)S(1)}, f32[48]{0:T(128)}, u32[]{:S(2)}) copy-start(f32[48]{0:T(128)} %mg.1) | copy-start | bytes 580
  17.4 8.4 %copy-start.10 = (f32[48]{0:T(128)S(1)}, f32[48]{0:T(128)}, u32[]{:S(2)}) copy-start(f32[48]{0:T(128)} %mb.1) | copy-start | bytes 580
  20.0 10.8 %collective-permute-start.3 = (bf16[384,128]{1,0:T(8,128)(2,1)S(1)}, bf16[384,128]{1,0:T(8,128)(2,1)S(1)}, u32[]{:S(2)}, u32[]{:S(2)}) collective-permute-start(bf16[384,128]{1,0:T(8,128)(2,1)S(1)} %get-tuple-element.33), channel_id=1, source_target_pairs={{1,0},{2,1},{3,2},{4,3},{5,4},{6,5},{7,6},{0,7},{9,8},{10,9},{11,1... | collective-permute-start | bytes 294920 | tf_op jit(solution)/shard_map/ppermute | solution.py:393
  25.7 10.1 %collective-permute-start.2 = (bf16[384,128]{1,0:T(8,128)(2,1)S(1)}, bf16[384,128]{1,0:T(8,128)(2,1)S(1)}, u32[]{:S(2)}, u32[]{:S(2)}) collective-permute-start(bf16[384,128]{1,0:T(8,128)(2,1)S(1)} %get-tuple-element.33), channel_id=1, source_target_pairs={{0,1},{1,2},{2,3},{3,4},{4,5},{5,6},{6,7},{7,0},{8,9},{9,10},{10,1... | collective-permute-start | bytes 294920 | tf_op jit(solution)/shard_map/ppermute | solution.py:393
  29.6 12.1 %copy-start.23 = (f32[48,8,128]{2,1,0:T(8,128)}, f32[48,8,128]{2,1,0:T(8,128)S(1)}, u32[]{:S(2)}) copy-start(f32[48,8,128]{2,1,0:T(8,128)S(1)} %get-tuple-element.38.mg) | copy-start | bytes 589828
  59.9 23.6 %copy-start.20 = (bf16[8,24,8,128]{3,2,1,0:T(8,128)(2,1)S(1)}, bf16[8,24,8,128]{3,2,1,0:T(8,128)(2,1)}, u32[]{:S(2)}) copy-start(bf16[8,24,8,128]{3,2,1,0:T(8,128)(2,1)} %copy-done.19) | copy-start | bytes 1179652
  59.9 41.6 %all-to-all-start.1 = ((bf16[128,5,8,128]{3,2,1,0:T(8,128)(2,1)}), bf16[128,5,8,128]{3,2,1,0:T(8,128)(2,1)S(1)}, u32[]{:S(2)}, u32[]{:S(2)}) async-start(bf16[128,5,8,128]{3,2,1,0:T(8,128)(2,1)} %bitcast.5), calls=%async_computation.1 | async-start | bytes 2621440 | tf_op jit(solution)/shard_map/all_to_all | solution.py:446
  65.4 15.5 %collective-permute-start.4 = (bf16[8,12,8,128]{3,2,1,0:T(8,128)(2,1)S(1)}, bf16[8,12,8,128]{3,2,1,0:T(8,128)(2,1)S(1)}, u32[]{:S(2)}, u32[]{:S(2)}) collective-permute-start(bf16[8,12,8,128]{3,2,1,0:T(8,128)(2,1)S(1)} %get-tuple-element.49), channel_id=1, source_target_pairs={{0,8},{8,16},{16,24},{24,32},{32,40},{40,48},{48,56},{56,64},{64,7... | collective-permute-start | bytes 589832 | tf_op jit(solution)/shard_map/ppermute | solution.py:393
  67.1 16.4 %collective-permute-start.5 = (bf16[8,12,8,128]{3,2,1,0:T(8,128)(2,1)S(1)}, bf16[8,12,8,128]{3,2,1,0:T(8,128)(2,1)S(1)}, u32[]{:S(2)}, u32[]{:S(2)}) collective-permute-start(bf16[8,12,8,128]{3,2,1,0:T(8,128)(2,1)S(1)} %get-tuple-element.50), channel_id=1, source_target_pairs={{8,0},{16,8},{24,16},{32,24},{40,32},{48,40},{56,48},{64,56},{72,6... | collective-permute-start | bytes 589832 | tf_op jit(solution)/shard_map/ppermute | solution.py:393
  84.6 14.7 %copy-start.11 = (f32[8,48,8,128]{3,2,1,0:T(8,128)S(1)}, f32[8,48,8,128]{3,2,1,0:T(8,128)}, u32[]{:S(2)}) copy-start(f32[8,48,8,128]{3,2,1,0:T(8,128)} %get-tuple-element.47.half_sum) | copy-start | bytes 4718596
  86.6 7.3 %collective-permute-start.7 = (f32[192,128]{1,0:T(8,128)S(1)}, f32[192,128]{1,0:T(8,128)S(1)}, u32[]{:S(2)}, u32[]{:S(2)}) collective-permute-start(f32[192,128]{1,0:T(8,128)S(1)} %get-tuple-element.53), channel_id=1, source_target_pairs={{1,0},{2,1},{3,2},{4,3},{5,4},{6,5},{7,6},{0,7},{9,8},{10,9},{11,1... | collective-permute-start | bytes 294920 | tf_op jit(solution)/shard_map/ppermute | solution.py:393
  92.2 7.2 %collective-permute-start.6 = (f32[192,128]{1,0:T(8,128)S(1)}, f32[192,128]{1,0:T(8,128)S(1)}, u32[]{:S(2)}, u32[]{:S(2)}) collective-permute-start(f32[192,128]{1,0:T(8,128)S(1)} %get-tuple-element.53), channel_id=1, source_target_pairs={{0,1},{1,2},{2,3},{3,4},{4,5},{5,6},{6,7},{7,0},{8,9},{9,10},{10,1... | collective-permute-start | bytes 294920 | tf_op jit(solution)/shard_map/ppermute | solution.py:393
  101.5 9.9 %copy-start.16 = (bf16[8,48,8,128]{3,2,1,0:T(8,128)(2,1)S(1)}, bf16[8,48,8,128]{3,2,1,0:T(8,128)(2,1)}, u32[]{:S(2)}) copy-start(bf16[8,48,8,128]{3,2,1,0:T(8,128)(2,1)} %copy-done.15) | copy-start | bytes 2359300
  104.4 12.9 %all-to-all-start.2 = ((f32[16,8,128]{2,1,0:T(8,128)}), f32[16,8,128]{2,1,0:T(8,128)S(1)}, u32[]{:S(2)}, u32[]{:S(2)}) async-start(f32[16,8,128]{2,1,0:T(8,128)} %total.1), calls=%async_computation.2 | async-start | bytes 131072 | tf_op jit(solution)/shard_map/all_to_all | solution.py:467
  111.4 1.3 %copy-start.1 = (bf16[128,5,8,128]{3,2,1,0:T(8,128)(2,1)S(1)}, bf16[128,5,8,128]{3,2,1,0:T(8,128)(2,1)}, u32[]{:S(2)}) copy-start(bf16[128,5,8,128]{3,2,1,0:T(8,128)(2,1)} %copy-done) | copy-start | bytes 3932164
  (18 other events, 16.5 us)
where the time goes:
time: 119 us; the launch traced here: 118 us
  starting transfers between devices  38.7 us (33%)
  waiting for transfers between devices  31.4 us (26%)
  Pallas kernels  29.2 us (25%)
  local copies, waits for them, and re-layouts  17.9 us (15%)
    ppermute x8, waiting for transfers between devices, both_ways(): return (lax.ppermute(first, axis, onward), lax.ppermute(second, axis, back))  29.7 us
    pallas_call x10, Pallas kernels, call(): pl.pallas_call(kernel, name=name, out_shape=[jax.ShapeDtypeStruct(s, t) f...  27.4 us
    unnamed x62, local copies, waits for them, and re-layouts  17.9 us
    ppermute x8, starting transfers between devices, both_ways(): return (lax.ppermute(first, axis, onward), lax.ppermute(second, axis, back))  15.7 us
    all_to_all x1, starting transfers between devices, local(): d_arrived = lax.all_to_all(d_pieces, everyone, 0, 0, tiled=True)  10.6 us
    all_to_all x1, starting transfers between devices, local(): sums = lax.all_to_all(sums, 'row', 0, 0, tiled=True)  7.01 us
    all_to_all x1, starting transfers between devices, local(): lax.all_to_all(pieces.reshape(ROWS * COLS, 5, H, LANES), everyone, 0, 0,...  5.44 us
  transfers between devices with their start and end apart: 11, of which 7 were waited for; matrix products, arithmetic and copies ran while one was open for 0% of the time, Pallas kernels for 15%

commit v1 on v0

--- a/solution.py
+++ b/solution.py
@@ -46,20 +46,57 @@
     return iota((rows, LANES), 1)
 
 
-def call(kernel, outs, args, name, smem=(), flops=4_000_000_000, scratch=()):
+class Far:
+    def __init__(self, sems):
+        self.sems, self.used, self.open = sems, 0, []
+
+    def start(self, source, target):
+        copy = pltpu.make_async_copy(source, target, self.sems.at[self.used])
+        self.used += 1
+        copy.start()
+        return copy
+
+    def send(self, source, target):
+        self.open.append(self.start(source, target))
+
+    def finish(self):
+        for copy in self.open:
+            copy.wait()
+
+
+def call(kernel, outs, args, name, smem=(), far=(), far_out=(), flops=4_000_000_000, scratch=(), copies=0, limit=16):
     specs = [
-        pl.BlockSpec(memory_space=pltpu.SMEM if i in smem else pltpu.VMEM) for i in range(len(args))
+        pl.BlockSpec(memory_space=pltpu.SMEM if i in smem else pltpu.HBM if i in far else pltpu.VMEM)
+        for i in range(len(args))
     ]
+    scratch = list(scratch)
+    if copies:
+        scratch.append(pltpu.SemaphoreType.DMA((copies,)))
     return pl.pallas_call(
         kernel,
         name=name,
-        out_shape=[jax.ShapeDtypeStruct(s, t) for s, t in outs],
+        out_shape=[
+            pltpu.HBM(s, t) if i in far_out else jax.ShapeDtypeStruct(s, t)
+            for i, (s, t) in enumerate(outs)
+        ],
         in_specs=specs,
-        out_specs=[pl.BlockSpec(memory_space=pltpu.VMEM) for _ in outs],
-        scratch_shapes=list(scratch),
-        compiler_params=pltpu.CompilerParams(vmem_limit_bytes=48 * 1024 * 1024),
+        out_specs=[
+            pl.BlockSpec(memory_space=pltpu.HBM if i in far_out else pltpu.VMEM)
+            for i in range(len(outs))
+        ],
+        scratch_shapes=scratch,
+        compiler_params=pltpu.CompilerParams(vmem_limit_bytes=limit * 1024 * 1024),
         cost_estimate=pl.CostEstimate(flops=flops, bytes_accessed=1_000_000, transcendentals=0),
-    )(*args)
+    )(
+        *(
+            pltpu.with_memory_space_constraint(v, pltpu.HBM) if i in far else v
+            for i, v in enumerate(args)
+        )
+    )
+
+
+def splat(values, count):
+    return jnp.concatenate([jnp.full((H, LANES), values[o], F32) for o in range(count)], axis=0)
 
 
 def pack_rows(field, count):
@@ -83,8 +120,12 @@
         up[g] = jnp.where(after < GROUPS, first, 0.0).astype(BF)
 
 
-def rows_kernel(x, down, up):
-    send_rows(x, down, up, CH)
+def rows_kernel(x, down, up, held, sems):
+    far = Far(sems)
+    loads = [far.start(x.at[g], held.at[g]) for g in range(GROUPS)]
+    for load in loads:
+        load.wait()
+    send_rows(held, down, up, CH)
 
 
 def turn_out(value, eye, pieces, g, first_tile):
@@ -114,19 +155,19 @@
     return buffer[...].reshape(CR, LANES)
 
 
-def mirror_kernel(d, pieces):
+def mirror_kernel(d, pieces, held, turned, sems):
+    far = Far(sems)
+    loads = [far.start(d.at[g], held.at[g]) for g in range(GROUPS)]
     eye = identity(LANES)
     for g in range(GROUPS):
-        turn_out(d[g].astype(F32).reshape(CR, LANES).astype(BF), eye, pieces, g, 0)
-
-
-def weights_kernel(w, mix, cg, cb, mg, mb, a_out, b_out, mf_out, mb_out, cgf, cbf, mgf, mbf):
-    for o in range(MID):
-        cgf[o] = jnp.full((H, LANES), cg[o], F32)
-        cbf[o] = jnp.full((H, LANES), cb[o], F32)
-    for o in range(CH):
-        mgf[o] = jnp.full((H, LANES), mg[o], F32)
-        mbf[o] = jnp.full((H, LANES), mb[o], F32)
+        loads[g].wait()
+        turn_out(held[g].astype(F32).reshape(CR, LANES).astype(BF), eye, turned, g, 0)
+        far.send(turned.at[:, g], pieces.at[:, g])
+    far.finish()
+
+
+def weights_kernel(w, mix, a_out, b_far, mf_out, mb_far, b_out, mb_out, sems):
+    far = Far(sems)
 
     def spread(n, own, width):
         col = iota((n, width), 1)
@@ -157,13 +198,19 @@
     mb_out[...] = (dot(mix[...], sf[:, :CR])[:, None, :] * mask[None]).reshape(MR, CR).astype(BF)
     mask = jnp.where(pt[:, :MR] == 0, 1.0, 0.0)
     mf_out[...] = (dot(mix[...], st[:, :MR], TN)[:, None, :] * mask[None]).reshape(CR, MR).astype(BF)
-
-
-def act_kernel(x, above, below, act, edge):
+    far.send(b_out, b_far)
+    far.send(mb_out, mb_far)
+    far.finish()
+
+
+def act_kernel(x, above, below, act, edge, act_far, held, sems):
+    far = Far(sems)
+    loads = [far.start(x.at[g], held.at[g]) for g in range(GROUPS)]
     lane = lanes_of(CR)
     packed = jnp.zeros((CR, LANES), F32)
     for g in range(GROUPS):
-        own = smooth(x[g].astype(F32).reshape(CR, LANES))
+        loads[g].wait()
+        own = smooth(held[g].astype(F32).reshape(CR, LANES))
         high = smooth(above[g].astype(F32).reshape(CR // 2, LANES))
         low = smooth(below[g].astype(F32).reshape(CR // 2, LANES))
         rim = jnp.concatenate([high, low], axis=0)
@@ -173,6 +220,8 @@
         packed = jnp.where(lane // 8 == g, pltpu.roll(own, (8 * g - 124) % LANES, 1), packed)
         packed = jnp.where(lane // 8 == 8 + g, pltpu.roll(rim, (8 * g - 60) % LANES, 1), packed)
     edge[...] = packed.astype(BF)
+    far.send(act, act_far)
+    far.finish()
 
 
 def merge_edges(from_left, from_right):
@@ -188,16 +237,22 @@
 
 
 def forward_kernel(
-    x, act, from_left, from_right, weights, mixer, cg, cb, mg, mb,
-    pre_out, hidden_out, rim_out, block_out, pieces,
+    x_far, act, from_left, from_right, weights, mixer, cg, cb, mg, mb,
+    pre_far, hidden_far, rim_far, block_far, pieces_far,
+    x, pre_out, hidden_out, rim_out, block_out, pieces, sems,
 ):
+    far = Far(sems)
+    load = far.start(x_far, x)
     eye = identity(LANES)
     rim = merge_edges(from_left[...].astype(F32), from_right[...].astype(F32)).astype(BF)
     rim_out[...] = rim
+    far.send(rim_out, rim_far)
     outer = dot(weights[:, 0:CR], rim) + pltpu.roll(dot(weights[:, CR : 2 * CR], rim), 64, 1)
     lane = lanes_of(MR)
     outer = jnp.where(lane % 8 < 4, outer[2 * MR : 3 * MR], outer[0:MR])
-    gain, shift = cg[...].reshape(MR, LANES), cb[...].reshape(MR, LANES)
+    gain, shift = splat(cg, MID), splat(cb, MID)
+    gain_out, shift_out = splat(mg, CH), splat(mb, CH)
+    load.wait()
     for pair in range(GROUPS // 2):
         two = slice(pair * 2 * LANES, (pair + 1) * 2 * LANES)
         product = dot(weights[...], act[:, two])
@@ -218,10 +273,15 @@
         for half in range(2):
             g = 2 * pair + half
             m = mixed[:, half * LANES : (half + 1) * LANES]
-            value = x[g].astype(F32).reshape(CR, LANES) + m * mg[...].reshape(CR, LANES)
-            value = (value + mb[...].reshape(CR, LANES)).astype(BF)
+            value = x[g].astype(F32).reshape(CR, LANES) + m * gain_out
+            value = (value + shift_out).astype(BF)
             block_out[g] = value.astype(F32).reshape(CH, H, LANES).astype(BF)
             turn_out(value, eye, pieces, g, 0)
+            far.send(block_out.at[g], block_far.at[g])
+            far.send(pieces.at[:, g], pieces_far.at[:, g])
+    far.send(pre_out, pre_far)
+    far.send(hidden_out, hidden_far)
+    far.finish()
 
 
 def split(value):
@@ -235,12 +295,18 @@
 
 
 def backward_kernel(
-    d, arrived, pre_in, hidden, act, rim, turned, mixer, cg, mg,
-    grad_inner, down, up, half_sum, pieces,
-    buffer, gmi, shifted, edge_rows, wide, mixwide,
+    d_far, arrived, pre_far, hidden_far, act_far, rim_far, turned_far, mixer_far, cg, mg,
+    grad_inner_far, down_far, up_far, half_sum_far, pieces_far,
+    d, pre_in, hidden, act, rim, turned, mixer, grad_inner, down, up, half_sum, pieces,
+    buffer, gmi, shifted, edge_rows, wide, mixwide, sems,
 ):
+    far = Far(sems)
+    loads = [far.start(d_far, d), far.start(mixer_far, mixer), far.start(pre_far, pre_in)]
+    late = [far.start(act_far, act), far.start(rim_far, rim), far.start(hidden_far, hidden), far.start(turned_far, turned)]
     lane = lanes_of(MR)
-    gain = cg[...].reshape(MR, LANES)
+    gain, gain_out = splat(cg, MID), splat(mg, CH)
+    for load in loads:
+        load.wait()
     packed = jnp.zeros((MR, LANES), F32)
     for pair in range(GROUPS // 2):
         two = slice(pair * 2 * LANES, (pair + 1) * 2 * LANES)
@@ -248,7 +314,7 @@
             g = 2 * pair + half
             both = 0.5 * (d[g].astype(F32).reshape(CR, LANES) + turn_in(arrived, g, 0, buffer))
             half_sum[g] = both.reshape(CH, H, LANES)
-            gmi[:, g * LANES : (g + 1) * LANES] = (both * mg[...].reshape(CR, LANES)).astype(BF)
+            gmi[:, g * LANES : (g + 1) * LANES] = (both * gain_out).astype(BF)
         into = dot(mixer[...], gmi[:, two])
         for half in range(2):
             g = 2 * pair + half
@@ -260,6 +326,12 @@
             shifted[2 * MR : 3 * MR, at] = jnp.where(lane >= 4, pltpu.roll(value, 4, 1), 0.0).astype(BF)
             packed = jnp.where(lane // 8 == g, pltpu.roll(value, (8 * g - 124) % LANES, 1), packed)
     send_rows(grad_inner, down, up, MID)
+    far.send(down, down_far)
+    far.send(up, up_far)
+    far.send(grad_inner, grad_inner_far)
+    far.send(half_sum, half_sum_far)
+    for load in late:
+        load.wait()
 
     packed = packed + pltpu.roll(packed, 64, 1)
     edge_rows[0:MR] = jnp.where(lane % 8 >= 4, packed, 0.0).astype(BF)
@@ -268,16 +340,16 @@
     lane_c = lanes_of(CR)
     rim_value = rim[...].astype(F32)
     rim_own = jnp.where(lane_c < 64, rim_value, 0.0).astype(BF)
-    rim_far = jnp.where(lane_c >= 64, rim_value, 0.0).astype(BF)
+    rim_rest = jnp.where(lane_c >= 64, rim_value, 0.0).astype(BF)
     for k in range(2):
         rows = slice(k * CR, (k + 1) * CR)
-        wide[:, rows] = dot(shifted[...], act[rows], NT) + dot(edge_rows[...], (rim_own, rim_far)[k], NT)
+        wide[:, rows] = dot(shifted[...], act[rows], NT) + dot(edge_rows[...], (rim_own, rim_rest)[k], NT)
     mixwide[...] = dot(hidden[...], gmi[...], NT)
 
     h, col = iota((H, CR), 0), iota((H, CR), 1)
     same = jnp.where(col % 8 == h, 1.0, 0.0)[None]
     other = jnp.where(col % 8 == (h + 4) % 8, 1.0, 0.0)[None]
-    far = jnp.where((col - jnp.where(col < CR // 2, 0, CR // 2)) % 4 == jnp.where(col < CR // 2, h, h - 4), 1.0, 0.0)[None]
+    across = jnp.where((col - jnp.where(col < CR // 2, 0, CR // 2)) % 4 == jnp.where(col < CR // 2, h, h - 4), 1.0, 0.0)[None]
     col, lane_s = iota((CR, LANES), 0), iota((CR, LANES), 1)
 
     def gather(keep, channel, side):
@@ -289,7 +361,7 @@
         block = wide[b * MR : (b + 1) * MR]
         own = block[:, 0:CR].reshape(MID, H, CR)
         rest = block[:, CR : 2 * CR].reshape(MID, H, CR)
-        sums.append([jnp.sum(own * same, axis=1), jnp.sum(own * other, axis=1), jnp.sum(rest * far, axis=1)])
+        sums.append([jnp.sum(own * same, axis=1), jnp.sum(own * other, axis=1), jnp.sum(rest * across, axis=1)])
     mixed = jnp.sum(mixwide[...].reshape(MID, H, CR) * same, axis=1)
     always = col >= 0
     own_low = col % 8 < 4
@@ -322,9 +394,15 @@
     pieces[ROWS - 1, :, 0:2] = jnp.zeros((COLS, 2, H, LANES), BF)
     for r in range(ROWS):
         pieces[r, :, 2:5] = turned[r]
-
-
-def spread_kernel(grad_inner, above, below, weights, main, edge, rhs):
+    far.send(pieces, pieces_far)
+    far.finish()
+
+
+def spread_kernel(grad_inner_far, above, below, weights_far, after, main, edge, rhs, grad_inner, weights, sems):
+    far = Far(sems)
+    loads = [far.start(grad_inner_far, grad_inner), far.start(weights_far, weights)]
+    for load in loads:
+        load.wait()
     lane = lanes_of(CR)
     packed = jnp.zeros((CR, LANES), F32)
     for pair in range(GROUPS // 2):
@@ -349,31 +427,46 @@
     edge[...] = packed[0 : CR // 2] + pltpu.roll(packed[CR // 2 : CR], 64, 1)
 
 
-def input_kernel(x, half_sum, main, from_left, from_right, grad_input):
+def input_kernel(x_far, half_far, main, from_left, from_right, out_far, x, half_sum, grad_input, sems):
+    far = Far(sems)
+    loads = [(far.start(x_far.at[g], x.at[g]), far.start(half_far.at[g], half_sum.at[g])) for g in range(GROUPS)]
     lane = lanes_of(CR)
     rim = merge_edges(from_left[...], from_right[...])
     rim = jnp.concatenate([rim, pltpu.roll(rim, 64, 1)], axis=0)
     for g in range(GROUPS):
+        for load in loads[g]:
+            load.wait()
         q = pltpu.roll(rim, (124 - 8 * g) % LANES, 1)
         total = main[:, g * LANES : (g + 1) * LANES]
         total = total + jnp.where(jnp.logical_or(lane < 4, lane >= 124), q, 0.0)
         slope = smooth_slope(x[g].astype(F32).reshape(CR, LANES))
         value = half_sum[g].reshape(CR, LANES) + total * slope
         grad_input[g] = value.reshape(CH, H, LANES).astype(BF)
+        far.send(grad_input.at[g], out_far.at[g])
+    far.finish()
 
 
 def total_kernel(arrived, out):
     total = jnp.zeros((H, LANES), F32)
-    for g in range(GROUPS):
-        part = arrived[:, g].astype(F32)
+    for g in range(COLS):
+        part = arrived[:, g, 0:2].astype(F32)
         total += jnp.sum(part[:, 0] + part[:, 1], axis=0)
     out[...] = jnp.broadcast_to((total * (1.0 / (ROWS * H * COLS)))[None], (ROWS, H, LANES))
 
 
-def symmetric_kernel(block, arrived, out, buffer):
+def symmetric_kernel(block_far, arrived_far, out_far, block, arrived, out, buffer, sems):
+    far = Far(sems)
+    loads = [
+        (far.start(block_far.at[g], block.at[g]), far.start(arrived_far.at[:, g, 2:5], arrived.at[:, g]))
+        for g in range(GROUPS)
+    ]
     for g in range(GROUPS):
-        value = 0.5 * (block[g].astype(F32).reshape(CR, LANES) + turn_in(arrived, g, 2, buffer))
+        for load in loads[g]:
+            load.wait()
+        value = 0.5 * (block[g].astype(F32).reshape(CR, LANES) + turn_in(arrived, g, 0, buffer))
         out[g] = value.reshape(CH, H, LANES).astype(BF)
+        far.send(out.at[g], out_far.at[g])
+    far.finish()
 
 
 def unpack_kernel(tiles, conv, mix):
@@ -395,82 +488,95 @@
 
 def local(pair_map, cotangent, conv_weight, conv_gain, conv_bias, mix_weight, mix_gain, mix_bias):
     tile = (GROUPS, CH, H, LANES)
+    cut = (ROWS, COLS, 3, H, LANES)
     everyone = ("row", "col")
-    down, up = call(rows_kernel, [((GROUPS, CH // 2, H, LANES), BF)] * 2, (pair_map,), "rows")
+    vmem = pltpu.VMEM
+    down, up = call(
+        rows_kernel, [((GROUPS, CH // 2, H, LANES), BF)] * 2, (pair_map,), "rows",
+        far=(0,), scratch=[vmem(tile, BF)], copies=GROUPS,
+    )
     above, below = both_ways(down, up, "row")
-    (d_pieces,) = call(mirror_kernel, [((ROWS, COLS, 3, H, LANES), BF)], (cotangent,), "turn_d")
-    d_pieces = d_pieces.reshape(ROWS * COLS, 3, H, LANES)
-    d_arrived = lax.all_to_all(d_pieces, everyone, 0, 0, tiled=True)
-    d_arrived = d_arrived.reshape(ROWS, COLS, 3, H, LANES)
+    (d_pieces,) = call(
+        mirror_kernel, [(cut, BF)], (cotangent,), "turn_d",
+        far=(0,), far_out=(0,), scratch=[vmem(tile, BF), vmem(cut, BF)], copies=2 * GROUPS,
+    )
+    d_arrived = lax.all_to_all(d_pieces.reshape(ROWS * COLS, 3, H, LANES), everyone, 0, 0, tiled=True)
+    d_arrived = d_arrived.reshape(cut)
 
     taps = jnp.transpose(conv_weight, (2, 3, 0, 1)).reshape(9, MID, CH)
-    wf, wb, mf, mbk, cg, cb, mg, mb = call(
+    wf, wb, mf, mbk = call(
         weights_kernel,
-        [((3 * MR, 2 * CR), BF), ((3 * CR, 2 * MR), BF), ((CR, MR), BF), ((MR, CR), BF)]
-        + [((MID, H, LANES), F32)] * 2
-        + [((CH, H, LANES), F32)] * 2,
-        (taps, mix_weight.T, conv_gain, conv_bias, mix_gain, mix_bias),
-        "weights",
-        smem=(2, 3, 4, 5),
-    )
-    act, edge = call(
-        act_kernel, [((2 * CR, POS), BF), ((CR, LANES), BF)], (pair_map, above, below), "act"
+        [((3 * MR, 2 * CR), BF), ((3 * CR, 2 * MR), BF), ((CR, MR), BF), ((MR, CR), BF)],
+        (taps, mix_weight.T), "weights", far_out=(1, 3),
+        scratch=[vmem((3 * CR, 2 * MR), BF), vmem((MR, CR), BF)], copies=2,
+    )
+    act, edge, act_far = call(
+        act_kernel,
+        [((2 * CR, POS), BF), ((CR, LANES), BF), ((2 * CR, POS), BF)],
+        (pair_map, above, below), "act", far=(0,), far_out=(2,),
+        scratch=[vmem(tile, BF)], copies=GROUPS + 1,
     )
     from_left, from_right = both_ways(edge, edge, "col")
+    forward_outs = [((MR, POS), F32), ((MR, POS), BF), ((CR, LANES), BF), (tile, BF), (cut, BF)]
     pre, hidden, rim, block, b_turned = call(
         forward_kernel,
-        [((MR, POS), F32), ((MR, POS), BF), ((CR, LANES), BF), (tile, BF), ((ROWS, COLS, 3, H, LANES), BF)],
-        (pair_map, act, from_left, from_right, wf, mf, cg, cb, mg, mb),
-        "forward",
-    )
+        forward_outs,
+        (pair_map, act, from_left, from_right, wf, mf, conv_gain, conv_bias, mix_gain, mix_bias),
+        "forward", smem=(6, 7, 8, 9), far=(0,), far_out=(0, 1, 2, 3, 4),
+        scratch=[vmem(tile, BF)] + [vmem(s, t) for s, t in forward_outs], copies=2 * GROUPS + 4,
+    )
+    backward_outs = [
+        ((GROUPS, MID, H, LANES), BF),
+        ((GROUPS, MID // 2, H, LANES), BF),
+        ((GROUPS, MID // 2, H, LANES), BF),
+        (tile, F32),
+        ((ROWS, COLS, 5, H, LANES), BF),
+    ]
     grad_inner, g_down, g_up, half_sum, pieces = call(
         backward_kernel,
-        [
-            ((GROUPS, MID, H, LANES), BF),
-            ((GROUPS, MID // 2, H, LANES), BF),
-            ((GROUPS, MID // 2, H, LANES), BF),
-            (tile, F32),
-            ((ROWS, COLS, 5, H, LANES), BF),
+        backward_outs,
+        (cotangent, d_arrived, pre, hidden, act_far, rim, b_turned, mbk, conv_gain, mix_gain),
+        "backward", smem=(8, 9), far=(0, 2, 3, 4, 5, 6, 7), far_out=(0, 1, 2, 3, 4),
+        scratch=[
+            vmem(tile, BF), vmem((MR, POS), F32), vmem((MR, POS), BF), vmem((2 * CR, POS), BF),
+            vmem((CR, LANES), BF), vmem(cut, BF), vmem((MR, CR), BF),
+        ]
+        + [vmem(s, t) for s, t in backward_outs]
+        + [
+            vmem((3, ROWS, H, LANES), F32),
+            vmem((CR, POS), BF),
+            vmem((3 * MR, POS), BF),
+            vmem((3 * MR, LANES), BF),
+            vmem((3 * MR, 2 * CR), F32),
+            vmem((MR, CR), F32),
         ],
-        (cotangent, d_arrived, pre, hidden, act, rim, b_turned, mbk, cg, mg),
-        "backward",
-        scratch=[
-            pltpu.VMEM((3, ROWS, H, LANES), F32),
-            pltpu.VMEM((CR, POS), BF),
-            pltpu.VMEM((3 * MR, POS), BF),
-            pltpu.VMEM((3 * MR, LANES), BF),
-            pltpu.VMEM((3 * MR, 2 * CR), F32),
-            pltpu.VMEM((MR, CR), F32),
-        ],
+        copies=12, limit=32,
     )
     arrived = lax.all_to_all(pieces.reshape(ROWS * COLS, 5, H, LANES), everyone, 0, 0, tiled=True)
     arrived = arrived.reshape(ROWS, COLS, 5, H, LANES)
     g_above, g_below = both_ways(g_down, g_up, "row")
+    (sums,) = call(
+        total_kernel, [((ROWS, H, LANES), F32)], (arrived,), "total", flops=500_000_000
+    )
+    spread_sums = lax.all_to_all(sums, "row", 0, 0, tiled=True)
     main, g_edge = call(
         spread_kernel,
         [((CR, POS), F32), ((CR // 2, LANES), F32)],
-        (grad_inner, g_above, g_below, wb),
-        "spread",
-        scratch=[pltpu.VMEM((2 * MR, 2 * LANES), BF)],
+        (grad_inner, g_above, g_below, wb, sums),
+        "spread", far=(0, 3), copies=2,
+        scratch=[vmem((2 * MR, 2 * LANES), BF), vmem((GROUPS, MID, H, LANES), BF), vmem((3 * CR, 2 * MR), BF)],
     )
     g_left, g_right = both_ways(g_edge, g_edge, "col")
-    (grad_input,) = call(input_kernel, [(tile, BF)], (pair_map, half_sum, main, g_left, g_right), "grad_input")
-    (sums,) = pl.pallas_call(
-        total_kernel,
-        name="total",
-        grid=(1,),
-        out_shape=[jax.ShapeDtypeStruct((ROWS, H, LANES), F32)],
-        in_specs=[pl.BlockSpec((ROWS, COLS, 2, H, LANES), lambda i: (0, 0, 0, 0, 0))],
-        out_specs=[pl.BlockSpec((ROWS, H, LANES), lambda i: (0, 0, 0))],
-        cost_estimate=pl.CostEstimate(flops=500_000_000, bytes_accessed=600_000, transcendentals=0),
-    )(arrived)
-    sums = lax.all_to_all(sums, "row", 0, 0, tiled=True)
+    (grad_input,) = call(
+        input_kernel, [(tile, BF)], (pair_map, half_sum, main, g_left, g_right), "grad_input",
+        far=(0, 1), far_out=(0,), scratch=[vmem(tile, BF), vmem(tile, F32), vmem(tile, BF)], copies=3 * GROUPS,
+    )
     (symmetric,) = call(
-        symmetric_kernel, [(tile, BF)], (block, arrived), "symmetric",
-        scratch=[pltpu.VMEM((3, ROWS, H, LANES), F32)],
+        symmetric_kernel, [(tile, BF)], (block, arrived), "symmetric", far=(0, 1), far_out=(0,),
+        scratch=[vmem(tile, BF), vmem(cut, BF), vmem(tile, BF), vmem((3, ROWS, H, LANES), F32)], copies=3 * GROUPS,
     )
     conv, mix = call(
-        unpack_kernel, [((9, MID, CH), F32), ((MID, CH), F32)], (sums,), "unpack", flops=100_000_000
+        unpack_kernel, [((9, MID, CH), F32), ((MID, CH), F32)], (spread_sums,), "unpack", flops=100_000_000
     )
     grad_conv = jnp.transpose(conv.reshape(3, 3, MID, CH), (2, 3, 0, 1))
     return symmetric, grad_input, grad_conv, mix.T

time: 119 us -> 104 us (0.87)
  local copies, waits for them, and re-layouts: 17.9 us -> 0.05 us
  Pallas kernels: 29.2 us -> 41.8 us
  waiting for transfers between devices: 31.4 us -> 25.3 us
  starting transfers between devices: 38.7 us -> 34.9 us
    ppermute x8, waiting for transfers between devices: 29.7 us -> 6.58 us  [both_ways(): return (lax.ppermute(first, axis, onward), lax.ppermute(second, axis, back))]
    all_to_all x1, waiting for transfers between devices: 0.01 us -> 18.7 us  [local(): lax.all_to_all(pieces.reshape(ROWS * COLS, 5, H, LANES), everyone, 0, 0,...]
    unnamed x62 -> x18, local copies, waits for them, and re-layouts: 17.9 us -> 0.05 us
    pallas_call x11, Pallas kernels: 29.2 us -> 41.8 us  [call(): pl.pallas_call(kernel, name=name, out_shape=[pltpu.HBM(s, t) if i in far_...]
    ppermute x8, starting transfers between devices: 15.7 us -> 13.3 us  [both_ways(): return (lax.ppermute(first, axis, onward), lax.ppermute(second, axis, back))]
    all_to_all x2, waiting for transfers between devices: 1.68 us -> 0.01 us  [the longest x1 0.01 us: local(): lax.all_to_all(d_pieces.reshape(ROWS * COLS, 3, H, LANES), everyone, 0, 0...]
    all_to_all x2, starting transfers between devices: 17.6 us -> 16.1 us  [the longest x1 10.6 us: local(): lax.all_to_all(d_pieces.reshape(ROWS * COLS, 3, H, LANES), everyone, 0, 0...]
  transfers between devices with their start and end apart: 11 -> 11, of which waited for: 7 -> 4; matrix products, arithmetic and copies ran while one was open for 0% -> 0% of each run, Pallas kernels for 15% -> 26%
where the time goes in v1:
time: 104 us; the launch traced here: 103 us
  Pallas kernels  41.8 us (40%)
  starting transfers between devices  34.9 us (34%)
  waiting for transfers between devices  25.3 us (24%)
  between operations  1.04 us (1%)
    pallas_call x11, Pallas kernels, call(): pl.pallas_call(kernel, name=name, out_shape=[pltpu.HBM(s, t) if i in far_...  41.8 us
    all_to_all x1, waiting for transfers between devices, local(): lax.all_to_all(pieces.reshape(ROWS * COLS, 5, H, LANES), everyone, 0, 0,...  18.7 us
    ppermute x8, starting transfers between devices, both_ways(): return (lax.ppermute(first, axis, onward), lax.ppermute(second, axis, back))  13.3 us
    all_to_all x1, starting transfers between devices, local(): lax.all_to_all(d_pieces.reshape(ROWS * COLS, 3, H, LANES), everyone, 0, 0...  10.6 us
    ppermute x8, waiting for transfers between devices, both_ways(): return (lax.ppermute(first, axis, onward), lax.ppermute(second, axis, back))  6.58 us
    all_to_all x1, starting transfers between devices, local(): spread_sums = lax.all_to_all(sums, 'row', 0, 0, tiled=True)  5.59 us
    all_to_all x1, starting transfers between devices, local(): lax.all_to_all(pieces.reshape(ROWS * COLS, 5, H, LANES), everyone, 0, 0,...  5.45 us
  transfers between devices with their start and end apart: 11, of which 4 were waited for; matrix products, arithmetic and copies ran while one was open for 0% of the time, Pallas kernels for 26%

profile of v1, /device:TPU:1, one launch (start us, length us, event | category | flops | bytes accessed | tf_op | source)
XLA Modules:
  0.0 103.0 jit_solution(8567732919298768304)
XLA Ops:
  0.6 1.5 %rows.1 = (bf16[8,24,8,128]{3,2,1,0:T(8,128)(2,1)S(1)}, bf16[8,24,8,128]{3,2,1,0:T(8,128)(2,1)S(1)}) custom-call(bf16[8,48,8,128]{3,2,1,0:T(8,128)(2,1)} %x_far.3), custom_call_target="tpu_custom_call" | custom-call | flops 4000000000 | bytes 1000000 | tf_op jit(solution)/shard_map/rows/pallas_call | solution.py:75
  2.2 2.8 %collective-permute-start = (bf16[8,24,8,128]{3,2,1,0:T(8,128)(2,1)S(1)}, bf16[8,24,8,128]{3,2,1,0:T(8,128)(2,1)S(1)}, u32[]{:S(2)}, u32[]{:S(2)}) collective-permute-start(bf16[8,24,8,128]{3,2,1,0:T(8,128)(2,1)S(1)} %get-tuple-element.27), channel_id=1, source_target_pairs={{0,8},{8,16},{16,24},{24,32},{32,40},{40,48},{48,56},{56,64},{64,7... | collective-permute-start | bytes 1179656 | tf_op jit(solution)/shard_map/ppermute | solution.py:486
  4.9 3.2 %turn_d.1 = bf16[16,8,3,8,128]{4,3,2,1,0:T(8,128)(2,1)} custom-call(bf16[8,48,8,128]{3,2,1,0:T(8,128)(2,1)} %d_far.1), custom_call_target="tpu_custom_call" | custom-call | flops 4000000000 | bytes 1000000 | tf_op jit(solution)/shard_map/turn_d/pallas_call | solution.py:75
  8.1 10.6 %all-to-all-start = ((bf16[128,3,8,128]{3,2,1,0:T(8,128)(2,1)}), bf16[128,3,8,128]{3,2,1,0:T(8,128)(2,1)S(1)}, u32[]{:S(2)}, u32[]{:S(2)}) async-start(bf16[128,3,8,128]{3,2,1,0:T(8,128)(2,1)} %bitcast.18), calls=%async_computation | async-start | bytes 1572864 | tf_op jit(solution)/shard_map/all_to_all | solution.py:503
  18.7 0.0 copy-start.2
  18.8 3.8 %act.1 = (bf16[768,1024]{1,0:T(8,128)(2,1)S(1)}, bf16[384,128]{1,0:T(8,128)(2,1)S(1)}, bf16[768,1024]{1,0:T(8,128)(2,1)}) custom-call(bf16[8,48,8,128]{3,2,1,0:T(8,128)(2,1)} %x_far.3, bf16[8,24,8,128]{3,2,1,0:T(8,128)(2,1)S(1)} %collective-permute-done.above, bf16[8,24,8,128]{3,2,1,0:T(8,128)(2,1)S(1)} %collective-permute-done.1.below), custom_call_target="tpu_custom_call" | custom-call | flops 4000000000 | bytes 1000000 | tf_op jit(solution)/shard_map/act/pallas_call | solution.py:75
  22.6 5.8 %collective-permute-start.3 = (bf16[384,128]{1,0:T(8,128)(2,1)S(1)}, bf16[384,128]{1,0:T(8,128)(2,1)S(1)}, u32[]{:S(2)}, u32[]{:S(2)}) collective-permute-start(bf16[384,128]{1,0:T(8,128)(2,1)S(1)} %get-tuple-element.30), channel_id=1, source_target_pairs={{1,0},{2,1},{3,2},{4,3},{5,4},{6,5},{7,6},{0,7},{9,8},{10,9},{11,1... | collective-permute-start | bytes 294920 | tf_op jit(solution)/shard_map/ppermute | solution.py:486
  28.4 2.6 %weights.1 = (bf16[576,768]{1,0:T(8,128)(2,1)S(1)}, bf16[1152,384]{1,0:T(8,128)(2,1)}, bf16[384,192]{1,0:T(8,128)(2,1)S(1)}, bf16[192,384]{1,0:T(8,128)(2,1)}) custom-call(bf16[9,24,48]{2,1,0:T(8,128)(2,1)S(1)} %bitcast.15, bf16[24,48]{1,0:T(8,128)(2,1)S(1)} %bitcast.16), custom_call_target="tpu_custom_call" | custom-call | flops 4000000000 | bytes 1000000 | tf_op jit(solution)/shard_map/weights/pallas_call | solution.py:75
  31.0 1.2 %collective-permute-done.3.from_right = bf16[384,128]{1,0:T(8,128)(2,1)S(1)} collective-permute-done((bf16[384,128]{1,0:T(8,128)(2,1)S(1)}, bf16[384,128]{1,0:T(8,128)(2,1)S(1)}, u32[]{:S(2)}, u32[]{:S(2)}) %collective-permute-start.3) | collective-permute-done | bytes 98336 | tf_op jit(solution)/shard_map/ppermute | solution.py:486
  32.2 4.9 %collective-permute-done.2.from_left = bf16[384,128]{1,0:T(8,128)(2,1)S(1)} collective-permute-done((bf16[384,128]{1,0:T(8,128)(2,1)S(1)}, bf16[384,128]{1,0:T(8,128)(2,1)S(1)}, u32[]{:S(2)}, u32[]{:S(2)}) %collective-permute-start.2) | collective-permute-done | bytes 98336 | tf_op jit(solution)/shard_map/ppermute | solution.py:486
  37.2 7.2 %forward.1 = (f32[192,1024]{1,0:T(8,128)}, bf16[192,1024]{1,0:T(8,128)(2,1)}, bf16[384,128]{1,0:T(8,128)(2,1)}, bf16[8,48,8,128]{3,2,1,0:T(8,128)(2,1)}, bf16[16,8,3,8,128]{4,3,2,1,0:T(8,128)(2,1)}) custom-call(bf16[8,48,8,128]{3,2,1,0:T(8,128)(2,1)} %x_far.3, bf16[768,1024]{1,0:T(8,128)(2,1)S(1)} %get-tuple-element.29.act, ...), custom_call_target="tpu_custom_call" | custom-call | flops 4000000000 | bytes 1000000 | tf_op jit(solution)/shard_map/forward/pallas_call | solution.py:75
  44.4 10.1 %backward.1 = (bf16[8,24,8,128]{3,2,1,0:T(8,128)(2,1)}, bf16[8,12,8,128]{3,2,1,0:T(8,128)(2,1)}, bf16[8,12,8,128]{3,2,1,0:T(8,128)(2,1)}, f32[8,48,8,128]{3,2,1,0:T(8,128)}, bf16[16,8,5,8,128]{4,3,2,1,0:T(8,128)(2,1)}) custom-call(bf16[8,48,8,128]{3,2,1,0:T(8,128)(2,1)} %d_far.1, bf16[16,8,3,8,128]{4,3,2,1,0:T(8,128)(2,1)S(1)} %bitcast.14, ...), custom_call_target="tpu_custom_call" | custom-call | flops 4000000000 | bytes 1000000 | tf_op jit(solution)/shard_map/backward/pallas_call | solution.py:75
  54.6 5.4 %all-to-all-start.1 = ((bf16[128,5,8,128]{3,2,1,0:T(8,128)(2,1)}), bf16[128,5,8,128]{3,2,1,0:T(8,128)(2,1)S(1)}, u32[]{:S(2)}, u32[]{:S(2)}) async-start(bf16[128,5,8,128]{3,2,1,0:T(8,128)(2,1)} %bitcast.17), calls=%async_computation.1 | async-start | bytes 2621440 | tf_op jit(solution)/shard_map/all_to_all | solution.py:555
  60.0 1.7 %collective-permute-start.4 = (bf16[8,12,8,128]{3,2,1,0:T(8,128)(2,1)S(1)}, bf16[8,12,8,128]{3,2,1,0:T(8,128)(2,1)S(1)}, u32[]{:S(2)}, u32[]{:S(2)}) collective-permute-start(bf16[8,12,8,128]{3,2,1,0:T(8,128)(2,1)S(1)} %copy-done.8), channel_id=1, source_target_pairs={{0,8},{8,16},{16,24},{24,32},{32,40},{40,48},{48,56},{56,64},{64,7... | collective-permute-start | bytes 589832 | tf_op jit(solution)/shard_map/ppermute | solution.py:486
  61.7 18.7 %all-to-all-done.1 = bf16[128,5,8,128]{3,2,1,0:T(8,128)(2,1)S(1)} async-done(((bf16[128,5,8,128]{3,2,1,0:T(8,128)(2,1)}), bf16[128,5,8,128]{3,2,1,0:T(8,128)(2,1)S(1)}, u32[]{:S(2)}, u32[]{:S(2)}) %all-to-all-start.1) | async-done | bytes 1310752 | tf_op jit(solution)/shard_map/all_to_all | solution.py:555
  80.5 0.8 total.1.after
  81.3 5.6 %all-to-all-start.2 = ((f32[16,8,128]{2,1,0:T(8,128)}), f32[16,8,128]{2,1,0:T(8,128)S(1)}, u32[]{:S(2)}, u32[]{:S(2)}) async-start(f32[16,8,128]{2,1,0:T(8,128)} %total.1.after), calls=%async_computation.2 | async-start | bytes 131072 | tf_op jit(solution)/shard_map/all_to_all | solution.py:561
  86.9 4.1 %spread.1 = (f32[384,1024]{1,0:T(8,128)S(1)}, f32[192,128]{1,0:T(8,128)S(1)}) custom-call(bf16[8,24,8,128]{3,2,1,0:T(8,128)(2,1)} %get-tuple-element.42.grad_inner_far, bf16[8,12,8,128]{3,2,1,0:T(8,128)(2,1)S(1)} %collective-permute-done.4.above, bf16[8,12,8,128]{3,2,1,0:T(8,128)(2,1)S(1)} %collective-permute-done.5.below, ...), custom_call_target="tpu_custom_call" | custom-call | flops 4000000000 | bytes 1000000 | tf_op jit(solution)/shard_map/spread/pallas_call | solution.py:75
  91.0 1.3 %collective-permute-start.7 = (f32[192,128]{1,0:T(8,128)S(1)}, f32[192,128]{1,0:T(8,128)S(1)}, u32[]{:S(2)}, u32[]{:S(2)}) collective-permute-start(f32[192,128]{1,0:T(8,128)S(1)} %get-tuple-element.47), channel_id=1, source_target_pairs={{1,0},{2,1},{3,2},{4,3},{5,4},{6,5},{7,6},{0,7},{9,8},{10,9},{11,1... | collective-permute-start | bytes 294920 | tf_op jit(solution)/shard_map/ppermute | solution.py:486
  92.3 1.7 %collective-permute-start.6 = (f32[192,128]{1,0:T(8,128)S(1)}, f32[192,128]{1,0:T(8,128)S(1)}, u32[]{:S(2)}, u32[]{:S(2)}) collective-permute-start(f32[192,128]{1,0:T(8,128)S(1)} %get-tuple-element.47), channel_id=1, source_target_pairs={{0,1},{1,2},{2,3},{3,4},{4,5},{5,6},{6,7},{7,0},{8,9},{9,10},{10,1... | collective-permute-start | bytes 294920 | tf_op jit(solution)/shard_map/ppermute | solution.py:486
  94.1 4.5 %symmetric.1 = bf16[8,48,8,128]{3,2,1,0:T(8,128)(2,1)} custom-call(bf16[8,48,8,128]{3,2,1,0:T(8,128)(2,1)} %get-tuple-element.33.block_far, bf16[16,8,5,8,128]{4,3,2,1,0:T(8,128)(2,1)} %bitcast.13), custom_call_target="tpu_custom_call" | custom-call | flops 4000000000 | bytes 1000000 | tf_op jit(solution)/shard_map/symmetric/pallas_call | solution.py:75
  98.6 0.7 unpack.1
  99.3 0.5 collective-permute-done.6.from_left
  99.8 3.1 %grad_input.1 = bf16[8,48,8,128]{3,2,1,0:T(8,128)(2,1)} custom-call(bf16[8,48,8,128]{3,2,1,0:T(8,128)(2,1)} %x_far.3, f32[8,48,8,128]{3,2,1,0:T(8,128)} %get-tuple-element.41.half_far, f32[384,1024]{1,0:T(8,128)S(1)} %get-tuple-element.46.main, f32[192,128]{1,0:T(8,128)S(1)} %collective-permute-done.6.from_left, f32[192,128]{1,0:T(8,128)S(1)} %collective-permute-done.7.from_right), custom_call_target="tpu_custom_call" | custom-call | flops 4000000000 | bytes 1000000 | tf_op jit(solution)/shard_map/grad_input/pallas_call | solution.py:75
  (27 shorter events, 0.1 us)
Async XLA Ops:
  2.2 16.6 %collective-permute-start = (bf16[8,24,8,128]{3,2,1,0:T(8,128)(2,1)S(1)}, bf16[8,24,8,128]{3,2,1,0:T(8,128)(2,1)S(1)}, u32[]{:S(2)}, u32[]{:S(2)}) collective-permute-start(bf16[8,24,8,128]{3,2,1,0:T(8,128)(2,1)S(1)} %get-tuple-element.27), channel_id=1, source_target_pairs={{0,8},{8,16},{16,24},{24,32},{32,40},{40,48},{48,56},{56,64},{64,7... | collective-permute-start | bytes 1179656 | tf_op jit(solution)/shard_map/ppermute | solution.py:486
  4.9 13.8 %collective-permute-start.1 = (bf16[8,24,8,128]{3,2,1,0:T(8,128)(2,1)S(1)}, bf16[8,24,8,128]{3,2,1,0:T(8,128)(2,1)S(1)}, u32[]{:S(2)}, u32[]{:S(2)}) collective-permute-start(bf16[8,24,8,128]{3,2,1,0:T(8,128)(2,1)S(1)} %get-tuple-element.28), channel_id=1, source_target_pairs={{8,0},{16,8},{24,16},{32,24},{40,32},{48,40},{56,48},{64,56},{72,6... | collective-permute-start | bytes 1179656 | tf_op jit(solution)/shard_map/ppermute | solution.py:486
  8.1 36.2 %all-to-all-start = ((bf16[128,3,8,128]{3,2,1,0:T(8,128)(2,1)}), bf16[128,3,8,128]{3,2,1,0:T(8,128)(2,1)S(1)}, u32[]{:S(2)}, u32[]{:S(2)}) async-start(bf16[128,3,8,128]{3,2,1,0:T(8,128)(2,1)} %bitcast.18), calls=%async_computation | async-start | bytes 1572864 | tf_op jit(solution)/shard_map/all_to_all | solution.py:503
  18.7 9.6 %copy-start.1 = (bf16[24,48,3,3]{1,0,3,2:T(8,128)(2,1)S(1)}, bf16[24,48,3,3]{1,0,3,2:T(8,128)(2,1)}, u32[]{:S(2)}) copy-start(bf16[24,48,3,3]{1,0,3,2:T(8,128)(2,1)} %param.10) | copy-start | bytes 62212
  18.7 9.6 %copy-start.2 = (bf16[48,24]{0,1:T(8,128)(2,1)S(1)}, bf16[48,24]{0,1:T(8,128)(2,1)}, u32[]{:S(2)}) copy-start(bf16[48,24]{0,1:T(8,128)(2,1)} %param.13) | copy-start | bytes 6916
  22.6 9.7 %collective-permute-start.3 = (bf16[384,128]{1,0:T(8,128)(2,1)S(1)}, bf16[384,128]{1,0:T(8,128)(2,1)S(1)}, u32[]{:S(2)}, u32[]{:S(2)}) collective-permute-start(bf16[384,128]{1,0:T(8,128)(2,1)S(1)} %get-tuple-element.30), channel_id=1, source_target_pairs={{1,0},{2,1},{3,2},{4,3},{5,4},{6,5},{7,6},{0,7},{9,8},{10,9},{11,1... | collective-permute-start | bytes 294920 | tf_op jit(solution)/shard_map/ppermute | solution.py:486
  28.3 8.8 %collective-permute-start.2 = (bf16[384,128]{1,0:T(8,128)(2,1)S(1)}, bf16[384,128]{1,0:T(8,128)(2,1)S(1)}, u32[]{:S(2)}, u32[]{:S(2)}) collective-permute-start(bf16[384,128]{1,0:T(8,128)(2,1)S(1)} %get-tuple-element.30), channel_id=1, source_target_pairs={{0,1},{1,2},{2,3},{3,4},{4,5},{5,6},{6,7},{7,0},{8,9},{9,10},{10,1... | collective-permute-start | bytes 294920 | tf_op jit(solution)/shard_map/ppermute | solution.py:486
  28.3 8.8 %copy-start.3 = (f32[24]{0:T(128)S(1)}, f32[24]{0:T(128)}, u32[]{:S(2)}) copy-start(f32[24]{0:T(128)} %cb.1) | copy-start | bytes 292
  28.4 8.8 %copy-start.4 = (f32[48]{0:T(128)S(1)}, f32[48]{0:T(128)}, u32[]{:S(2)}) copy-start(f32[48]{0:T(128)} %mb.1) | copy-start | bytes 580
  28.4 8.8 %copy-start.5 = (f32[24]{0:T(128)S(1)}, f32[24]{0:T(128)}, u32[]{:S(2)}) copy-start(f32[24]{0:T(128)} %cg.3) | copy-start | bytes 292
  28.4 8.8 %copy-start.6 = (f32[48]{0:T(128)S(1)}, f32[48]{0:T(128)}, u32[]{:S(2)}) copy-start(f32[48]{0:T(128)} %mg.3) | copy-start | bytes 580
  54.5 5.5 %copy-start.8 = (bf16[8,12,8,128]{3,2,1,0:T(8,128)(2,1)S(1)}, bf16[8,12,8,128]{3,2,1,0:T(8,128)(2,1)}, u32[]{:S(2)}) copy-start(bf16[8,12,8,128]{3,2,1,0:T(8,128)(2,1)} %get-tuple-element.43) | copy-start | bytes 589828
  54.5 7.2 %copy-start.7 = (bf16[8,12,8,128]{3,2,1,0:T(8,128)(2,1)S(1)}, bf16[8,12,8,128]{3,2,1,0:T(8,128)(2,1)}, u32[]{:S(2)}) copy-start(bf16[8,12,8,128]{3,2,1,0:T(8,128)(2,1)} %get-tuple-element.44) | copy-start | bytes 589828
  54.6 25.9 %all-to-all-start.1 = ((bf16[128,5,8,128]{3,2,1,0:T(8,128)(2,1)}), bf16[128,5,8,128]{3,2,1,0:T(8,128)(2,1)S(1)}, u32[]{:S(2)}, u32[]{:S(2)}) async-start(bf16[128,5,8,128]{3,2,1,0:T(8,128)(2,1)} %bitcast.17), calls=%async_computation.1 | async-start | bytes 2621440 | tf_op jit(solution)/shard_map/all_to_all | solution.py:555
  60.0 26.9 %collective-permute-start.4 = (bf16[8,12,8,128]{3,2,1,0:T(8,128)(2,1)S(1)}, bf16[8,12,8,128]{3,2,1,0:T(8,128)(2,1)S(1)}, u32[]{:S(2)}, u32[]{:S(2)}) collective-permute-start(bf16[8,12,8,128]{3,2,1,0:T(8,128)(2,1)S(1)} %copy-done.8), channel_id=1, source_target_pairs={{0,8},{8,16},{16,24},{24,32},{32,40},{40,48},{48,56},{56,64},{64,7... | collective-permute-start | bytes 589832 | tf_op jit(solution)/shard_map/ppermute | solution.py:486
  61.7 25.2 %collective-permute-start.5 = (bf16[8,12,8,128]{3,2,1,0:T(8,128)(2,1)S(1)}, bf16[8,12,8,128]{3,2,1,0:T(8,128)(2,1)S(1)}, u32[]{:S(2)}, u32[]{:S(2)}) collective-permute-start(bf16[8,12,8,128]{3,2,1,0:T(8,128)(2,1)S(1)} %copy-done.7), channel_id=1, source_target_pairs={{8,0},{16,8},{24,16},{32,24},{40,32},{48,40},{56,48},{64,56},{72,6... | collective-permute-start | bytes 589832 | tf_op jit(solution)/shard_map/ppermute | solution.py:486
  80.5 10.5 %copy-start = (bf16[128,5,8,128]{3,2,1,0:T(8,128)(2,1)}, bf16[128,5,8,128]{3,2,1,0:T(8,128)(2,1)S(1)}, u32[]{:S(2)}) copy-start(bf16[128,5,8,128]{3,2,1,0:T(8,128)(2,1)S(1)} %all-to-all-done.1) | copy-start | bytes 3932164
  81.3 17.3 %all-to-all-start.2 = ((f32[16,8,128]{2,1,0:T(8,128)}), f32[16,8,128]{2,1,0:T(8,128)S(1)}, u32[]{:S(2)}, u32[]{:S(2)}) async-start(f32[16,8,128]{2,1,0:T(8,128)} %total.1.after), calls=%async_computation.2 | async-start | bytes 131072 | tf_op jit(solution)/shard_map/all_to_all | solution.py:561
  91.0 8.3 %collective-permute-start.7 = (f32[192,128]{1,0:T(8,128)S(1)}, f32[192,128]{1,0:T(8,128)S(1)}, u32[]{:S(2)}, u32[]{:S(2)}) collective-permute-start(f32[192,128]{1,0:T(8,128)S(1)} %get-tuple-element.47), channel_id=1, source_target_pairs={{1,0},{2,1},{3,2},{4,3},{5,4},{6,5},{7,6},{0,7},{9,8},{10,9},{11,1... | collective-permute-start | bytes 294920 | tf_op jit(solution)/shard_map/ppermute | solution.py:486
  92.3 7.4 %collective-permute-start.6 = (f32[192,128]{1,0:T(8,128)S(1)}, f32[192,128]{1,0:T(8,128)S(1)}, u32[]{:S(2)}, u32[]{:S(2)}) collective-permute-start(f32[192,128]{1,0:T(8,128)S(1)} %get-tuple-element.47), channel_id=1, source_target_pairs={{0,1},{1,2},{2,3},{3,4},{4,5},{5,6},{6,7},{7,0},{8,9},{9,10},{10,1... | collective-permute-start | bytes 294920 | tf_op jit(solution)/shard_map/ppermute | solution.py:486

commit v2 on v1

--- a/solution.py
+++ b/solution.py
@@ -64,7 +64,7 @@
             copy.wait()
 
 
-def call(kernel, outs, args, name, smem=(), far=(), far_out=(), flops=4_000_000_000, scratch=(), copies=0, limit=16):
+def call(kernel, outs, args, name, smem=(), far=(), far_out=(), flops=4_000_000_000, scratch=(), copies=0, limit=16, alias=None):
     specs = [
         pl.BlockSpec(memory_space=pltpu.SMEM if i in smem else pltpu.HBM if i in far else pltpu.VMEM)
         for i in range(len(args))
@@ -85,6 +85,7 @@
             for i in range(len(outs))
         ],
         scratch_shapes=scratch,
+        input_output_aliases=alias or {},
         compiler_params=pltpu.CompilerParams(vmem_limit_bytes=limit * 1024 * 1024),
         cost_estimate=pl.CostEstimate(flops=flops, bytes_accessed=1_000_000, transcendentals=0),
     )(
@@ -155,18 +156,16 @@
     return buffer[...].reshape(CR, LANES)
 
 
-def mirror_kernel(d, pieces, held, turned, sems):
-    far = Far(sems)
-    loads = [far.start(d.at[g], held.at[g]) for g in range(GROUPS)]
+def mirror_kernel(d, pieces, turned, sems):
+    far = Far(sems)
     eye = identity(LANES)
     for g in range(GROUPS):
-        loads[g].wait()
-        turn_out(held[g].astype(F32).reshape(CR, LANES).astype(BF), eye, turned, g, 0)
+        turn_out(d[g].astype(F32).reshape(CR, LANES).astype(BF), eye, turned, g, 0)
         far.send(turned.at[:, g], pieces.at[:, g])
     far.finish()
 
 
-def weights_kernel(w, mix, a_out, b_far, mf_out, mb_far, b_out, mb_out, sems):
+def weights_kernel(w, mix, a_out, b_far, mf_out, mb_far, a_far, mf_far, b_out, mb_out, sems):
     far = Far(sems)
 
     def spread(n, own, width):
@@ -200,6 +199,8 @@
     mf_out[...] = (dot(mix[...], st[:, :MR], TN)[:, None, :] * mask[None]).reshape(CR, MR).astype(BF)
     far.send(b_out, b_far)
     far.send(mb_out, mb_far)
+    far.send(a_out, a_far)
+    far.send(mf_out, mf_far)
     far.finish()
 
 
@@ -236,22 +237,22 @@
     )
 
 
-def forward_kernel(
-    x_far, act, from_left, from_right, weights, mixer, cg, cb, mg, mb,
-    pre_far, hidden_far, rim_far, block_far, pieces_far,
-    x, pre_out, hidden_out, rim_out, block_out, pieces, sems,
+def at_edge(lane):
+    return jnp.logical_or(lane < 4, lane >= 124)
+
+
+def inside_kernel(
+    x_far, act, weights, mixer, cg, cb, mg, mb,
+    slope_far, hidden_far, block_far, pieces_far, edge_inner_far, edge_x_far,
+    x, slope, hidden, block, pieces, edge_inner, edge_x, sems,
 ):
     far = Far(sems)
     load = far.start(x_far, x)
     eye = identity(LANES)
-    rim = merge_edges(from_left[...].astype(F32), from_right[...].astype(F32)).astype(BF)
-    rim_out[...] = rim
-    far.send(rim_out, rim_far)
-    outer = dot(weights[:, 0:CR], rim) + pltpu.roll(dot(weights[:, CR : 2 * CR], rim), 64, 1)
-    lane = lanes_of(MR)
-    outer = jnp.where(lane % 8 < 4, outer[2 * MR : 3 * MR], outer[0:MR])
+    lane, lane_c = lanes_of(MR), lanes_of(CR)
     gain, shift = splat(cg, MID), splat(cb, MID)
     gain_out, shift_out = splat(mg, CH), splat(mb, CH)
+    packed, packed_x = jnp.zeros((MR, LANES), F32), jnp.zeros((CR, LANES), F32)
     load.wait()
     for pair in range(GROUPS // 2):
         two = slice(pair * 2 * LANES, (pair + 1) * 2 * LANES)
@@ -259,28 +260,33 @@
         for half in range(2):
             g = 2 * pair + half
             p = product[:, half * LANES : (half + 1) * LANES]
-            q = pltpu.roll(outer, (124 - 8 * g) % LANES, 1)
             inner = (
                 p[MR : 2 * MR]
-                + jnp.where(lane < 4, q, pltpu.roll(p[0:MR], 4, 1))
-                + jnp.where(lane >= 124, q, pltpu.roll(p[2 * MR : 3 * MR], LANES - 4, 1))
+                + jnp.where(lane < 4, 0.0, pltpu.roll(p[0:MR], 4, 1))
+                + jnp.where(lane >= 124, 0.0, pltpu.roll(p[2 * MR : 3 * MR], LANES - 4, 1))
             )
+            packed = jnp.where(lane // 8 == g, pltpu.roll(inner, (8 * g - 124) % LANES, 1), packed)
             pre = inner * gain + shift
             at = slice(g * LANES, (g + 1) * LANES)
-            pre_out[:, at] = pre
-            hidden_out[:, at] = smooth(pre).astype(BF)
-        mixed = dot(mixer[...], hidden_out[:, two])
+            slope[:, at] = smooth_slope(pre) * gain
+            hidden[:, at] = smooth(pre).astype(BF)
+        mixed = dot(mixer[...], hidden[:, two])
         for half in range(2):
             g = 2 * pair + half
             m = mixed[:, half * LANES : (half + 1) * LANES]
-            value = x[g].astype(F32).reshape(CR, LANES) + m * gain_out
-            value = (value + shift_out).astype(BF)
-            block_out[g] = value.astype(F32).reshape(CH, H, LANES).astype(BF)
+            own = x[g].astype(F32).reshape(CR, LANES)
+            packed_x = jnp.where(lane_c // 8 == g, pltpu.roll(own, (8 * g - 124) % LANES, 1), packed_x)
+            value = (own + m * gain_out + shift_out).astype(BF)
+            block[g] = value.astype(F32).reshape(CH, H, LANES).astype(BF)
             turn_out(value, eye, pieces, g, 0)
-            far.send(block_out.at[g], block_far.at[g])
-            far.send(pieces.at[:, g], pieces_far.at[:, g])
-    far.send(pre_out, pre_far)
-    far.send(hidden_out, hidden_far)
+            far.send(block.at[g], block_far.at[g])
+            far.send(pieces.at[:, g], pieces_far.at[:, g, 2:5])
+    edge_inner[...] = packed
+    edge_x[...] = packed_x
+    far.send(slope, slope_far)
+    far.send(hidden, hidden_far)
+    far.send(edge_inner, edge_inner_far)
+    far.send(edge_x, edge_x_far)
     far.finish()
 
 
@@ -294,18 +300,49 @@
     return dot(high, onehot) + dot(low, onehot)
 
 
-def backward_kernel(
-    d_far, arrived, pre_far, hidden_far, act_far, rim_far, turned_far, mixer_far, cg, mg,
-    grad_inner_far, down_far, up_far, half_sum_far, pieces_far,
-    d, pre_in, hidden, act, rim, turned, mixer, grad_inner, down, up, half_sum, pieces,
-    buffer, gmi, shifted, edge_rows, wide, mixwide, sems,
+def inner_kernel(
+    d_far, arrived, slope_far, hidden_far, edge_inner_far, edge_x_far, from_left, from_right,
+    weights_far, mixer_far, back_far, pieces_in, cg, cb, mg, mb,
+    grad_inner_far, down, up, half_sum_far, pieces_far, edge_block_far, gmi, shifted, edge_rows, hidden_out, rim_out,
+    d, slope, hidden, edge_inner, edge_x, weights, mixer, back, grad_inner, half_sum, ends, edge_block, buffer, sems,
 ):
     far = Far(sems)
-    loads = [far.start(d_far, d), far.start(mixer_far, mixer), far.start(pre_far, pre_in)]
-    late = [far.start(act_far, act), far.start(rim_far, rim), far.start(hidden_far, hidden), far.start(turned_far, turned)]
-    lane = lanes_of(MR)
-    gain, gain_out = splat(cg, MID), splat(mg, CH)
-    for load in loads:
+    first = [far.start(weights_far.at[0:MR], weights.at[0:MR])]
+    first.append(far.start(weights_far.at[2 * MR : 3 * MR], weights.at[MR : 2 * MR]))
+    first += [far.start(edge_inner_far, edge_inner), far.start(edge_x_far, edge_x), far.start(mixer_far, mixer)]
+    later = [far.start(d_far, d), far.start(slope_far, slope), far.start(back_far, back), far.start(hidden_far, hidden)]
+    tails = [
+        far.start(pieces_in.at[r, :, 2:5], ends.at[i]) for i, r in enumerate((0, ROWS - 1))
+    ]
+    lane, lane_c = lanes_of(MR), lanes_of(CR)
+    gain, shift = splat(cg, MID), splat(cb, MID)
+    gain_out, shift_out = splat(mg, CH), splat(mb, CH)
+    rim = merge_edges(from_left[...].astype(F32), from_right[...].astype(F32)).astype(BF)
+    rim_out[...] = rim
+    for load in first:
+        load.wait()
+    outer = dot(weights[:, 0:CR], rim) + pltpu.roll(dot(weights[:, CR : 2 * CR], rim), 64, 1)
+    outer = jnp.where(lane % 8 < 4, outer[MR : 2 * MR], outer[0:MR])
+    pre = (edge_inner[...] + outer) * gain + shift
+    slope_edge = smooth_slope(pre) * gain
+    hidden_edge = smooth(pre).astype(BF)
+    mixed = dot(mixer[...], hidden_edge)
+    value = (edge_x[...] + mixed * gain_out + shift_out).astype(BF)
+    edge_block[...] = value.astype(F32)
+    far.send(edge_block, edge_block_far)
+    hidden_edge = hidden_edge.astype(F32)
+    turned = dot(identity(LANES), value, NT)
+    for load in tails:
+        load.wait()
+    low = iota((COLS, H, LANES), 1) < 4
+    for k in range(3):
+        part = pltpu.roll(turned[0 : COLS * H, k * LANES : (k + 1) * LANES].reshape(COLS, H, LANES), 4, 1)
+        ends[0, :, k] = jnp.where(low, part, ends[0, :, k].astype(F32)).astype(BF)
+        ends[1, :, k] = jnp.where(low, ends[1, :, k].astype(F32), part).astype(BF)
+    for i, r in enumerate((0, ROWS - 1)):
+        far.send(ends.at[i], pieces_far.at[r, :, 2:5])
+
+    for load in later:
         load.wait()
     packed = jnp.zeros((MR, LANES), F32)
     for pair in range(GROUPS // 2):
@@ -315,41 +352,50 @@
             both = 0.5 * (d[g].astype(F32).reshape(CR, LANES) + turn_in(arrived, g, 0, buffer))
             half_sum[g] = both.reshape(CH, H, LANES)
             gmi[:, g * LANES : (g + 1) * LANES] = (both * gain_out).astype(BF)
-        into = dot(mixer[...], gmi[:, two])
+        into = dot(back[...], gmi[:, two])
         for half in range(2):
             g = 2 * pair + half
             at = slice(g * LANES, (g + 1) * LANES)
-            value = into[:, half * LANES : (half + 1) * LANES] * smooth_slope(pre_in[:, at]) * gain
+            turn = (124 - 8 * g) % LANES
+            here = jnp.where(at_edge(lane), pltpu.roll(slope_edge, turn, 1), slope[:, at])
+            value = into[:, half * LANES : (half + 1) * LANES] * here
             grad_inner[g] = value.reshape(MID, H, LANES).astype(BF)
             shifted[0:MR, at] = jnp.where(lane < 124, pltpu.roll(value, LANES - 4, 1), 0.0).astype(BF)
             shifted[MR : 2 * MR, at] = value.astype(BF)
             shifted[2 * MR : 3 * MR, at] = jnp.where(lane >= 4, pltpu.roll(value, 4, 1), 0.0).astype(BF)
             packed = jnp.where(lane // 8 == g, pltpu.roll(value, (8 * g - 124) % LANES, 1), packed)
-    send_rows(grad_inner, down, up, MID)
-    far.send(down, down_far)
-    far.send(up, up_far)
+            here = jnp.where(at_edge(lane), pltpu.roll(hidden_edge, turn, 1), hidden[:, at].astype(F32))
+            hidden_out[:, at] = here.astype(BF)
     far.send(grad_inner, grad_inner_far)
     far.send(half_sum, half_sum_far)
-    for load in late:
-        load.wait()
-
+    send_rows(grad_inner, down, up, MID)
     packed = packed + pltpu.roll(packed, 64, 1)
     edge_rows[0:MR] = jnp.where(lane % 8 >= 4, packed, 0.0).astype(BF)
     edge_rows[MR : 2 * MR] = jnp.zeros((MR, LANES), BF)
     edge_rows[2 * MR : 3 * MR] = jnp.where(lane % 8 < 4, packed, 0.0).astype(BF)
+    far.finish()
+
+
+def sums_kernel(
+    act_far, gmi, shifted, edge_rows, hidden, rim, pieces_in, pieces_far, act, sums_out, wide, mixwide, sems
+):
+    far = Far(sems)
+    loads = [far.start(act_far.at[k * CR : (k + 1) * CR], act.at[k * CR : (k + 1) * CR]) for k in range(2)]
     lane_c = lanes_of(CR)
     rim_value = rim[...].astype(F32)
     rim_own = jnp.where(lane_c < 64, rim_value, 0.0).astype(BF)
     rim_rest = jnp.where(lane_c >= 64, rim_value, 0.0).astype(BF)
+    mixwide[...] = dot(hidden[...], gmi[...], NT)
     for k in range(2):
         rows = slice(k * CR, (k + 1) * CR)
+        loads[k].wait()
         wide[:, rows] = dot(shifted[...], act[rows], NT) + dot(edge_rows[...], (rim_own, rim_rest)[k], NT)
-    mixwide[...] = dot(hidden[...], gmi[...], NT)
 
     h, col = iota((H, CR), 0), iota((H, CR), 1)
     same = jnp.where(col % 8 == h, 1.0, 0.0)[None]
     other = jnp.where(col % 8 == (h + 4) % 8, 1.0, 0.0)[None]
-    across = jnp.where((col - jnp.where(col < CR // 2, 0, CR // 2)) % 4 == jnp.where(col < CR // 2, h, h - 4), 1.0, 0.0)[None]
+    low_half = col < CR // 2
+    across = jnp.where(jnp.where(low_half, col, col - CR // 2) % 4 == jnp.where(low_half, h, h - 4), 1.0, 0.0)[None]
     col, lane_s = iota((CR, LANES), 0), iota((CR, LANES), 1)
 
     def gather(keep, channel, side):
@@ -389,16 +435,14 @@
         for k in range(3):
             r = 3 * p + k
             rows = slice(k * H, (k + 1) * H)
-            pieces[r, :, 0] = jnp.broadcast_to(high[rows][None], (COLS, H, LANES)).astype(BF)
-            pieces[r, :, 1] = jnp.broadcast_to(low[rows][None], (COLS, H, LANES)).astype(BF)
-    pieces[ROWS - 1, :, 0:2] = jnp.zeros((COLS, 2, H, LANES), BF)
-    for r in range(ROWS):
-        pieces[r, :, 2:5] = turned[r]
-    far.send(pieces, pieces_far)
-    far.finish()
-
-
-def spread_kernel(grad_inner_far, above, below, weights_far, after, main, edge, rhs, grad_inner, weights, sems):
+            sums_out[r, :, 0] = jnp.broadcast_to(high[rows][None], (COLS, H, LANES)).astype(BF)
+            sums_out[r, :, 1] = jnp.broadcast_to(low[rows][None], (COLS, H, LANES)).astype(BF)
+    sums_out[ROWS - 1] = jnp.zeros((COLS, 2, H, LANES), BF)
+    far.send(sums_out, pieces_far.at[:, :, 0:2])
+    far.finish()
+
+
+def spread_kernel(grad_inner_far, above, below, weights_far, main, edge, rhs, grad_inner, weights, sems):
     far = Far(sems)
     loads = [far.start(grad_inner_far, grad_inner), far.start(weights_far, weights)]
     for load in loads:
@@ -454,16 +498,21 @@
     out[...] = jnp.broadcast_to((total * (1.0 / (ROWS * H * COLS)))[None], (ROWS, H, LANES))
 
 
-def symmetric_kernel(block_far, arrived_far, out_far, block, arrived, out, buffer, sems):
+def symmetric_kernel(block_far, edge_far, arrived_far, out_far, edge, block, arrived, out, buffer, sems):
     far = Far(sems)
     loads = [
         (far.start(block_far.at[g], block.at[g]), far.start(arrived_far.at[:, g, 2:5], arrived.at[:, g]))
         for g in range(GROUPS)
     ]
+    far.start(edge_far, edge).wait()
+    lane = lanes_of(CR)
     for g in range(GROUPS):
         for load in loads[g]:
             load.wait()
-        value = 0.5 * (block[g].astype(F32).reshape(CR, LANES) + turn_in(arrived, g, 0, buffer))
+        own = jnp.where(
+            at_edge(lane), pltpu.roll(edge[...], (124 - 8 * g) % LANES, 1), block[g].astype(F32).reshape(CR, LANES)
+        )
+        value = 0.5 * (own + turn_in(arrived, g, 0, buffer))
         out[g] = value.reshape(CH, H, LANES).astype(BF)
         far.send(out.at[g], out_far.at[g])
     far.finish()
@@ -498,17 +547,18 @@
     above, below = both_ways(down, up, "row")
     (d_pieces,) = call(
         mirror_kernel, [(cut, BF)], (cotangent,), "turn_d",
-        far=(0,), far_out=(0,), scratch=[vmem(tile, BF), vmem(cut, BF)], copies=2 * GROUPS,
+        far_out=(0,), scratch=[vmem(cut, BF)], copies=GROUPS,
     )
     d_arrived = lax.all_to_all(d_pieces.reshape(ROWS * COLS, 3, H, LANES), everyone, 0, 0, tiled=True)
     d_arrived = d_arrived.reshape(cut)
 
     taps = jnp.transpose(conv_weight, (2, 3, 0, 1)).reshape(9, MID, CH)
-    wf, wb, mf, mbk = call(
+    wf, wb, mf, mbk, wf_far, mf_far = call(
         weights_kernel,
-        [((3 * MR, 2 * CR), BF), ((3 * CR, 2 * MR), BF), ((CR, MR), BF), ((MR, CR), BF)],
-        (taps, mix_weight.T), "weights", far_out=(1, 3),
-        scratch=[vmem((3 * CR, 2 * MR), BF), vmem((MR, CR), BF)], copies=2,
+        [((3 * MR, 2 * CR), BF), ((3 * CR, 2 * MR), BF), ((CR, MR), BF), ((MR, CR), BF)]
+        + [((3 * MR, 2 * CR), BF), ((CR, MR), BF)],
+        (taps, mix_weight.T), "weights", far_out=(1, 3, 4, 5),
+        scratch=[vmem((3 * CR, 2 * MR), BF), vmem((MR, CR), BF)], copies=4,
     )
     act, edge, act_far = call(
         act_kernel,
@@ -517,44 +567,59 @@
         scratch=[vmem(tile, BF)], copies=GROUPS + 1,
     )
     from_left, from_right = both_ways(edge, edge, "col")
-    forward_outs = [((MR, POS), F32), ((MR, POS), BF), ((CR, LANES), BF), (tile, BF), (cut, BF)]
-    pre, hidden, rim, block, b_turned = call(
-        forward_kernel,
-        forward_outs,
-        (pair_map, act, from_left, from_right, wf, mf, conv_gain, conv_bias, mix_gain, mix_bias),
-        "forward", smem=(6, 7, 8, 9), far=(0,), far_out=(0, 1, 2, 3, 4),
-        scratch=[vmem(tile, BF)] + [vmem(s, t) for s, t in forward_outs], copies=2 * GROUPS + 4,
-    )
-    backward_outs = [
-        ((GROUPS, MID, H, LANES), BF),
-        ((GROUPS, MID // 2, H, LANES), BF),
-        ((GROUPS, MID // 2, H, LANES), BF),
-        (tile, F32),
-        ((ROWS, COLS, 5, H, LANES), BF),
-    ]
-    grad_inner, g_down, g_up, half_sum, pieces = call(
-        backward_kernel,
-        backward_outs,
-        (cotangent, d_arrived, pre, hidden, act_far, rim, b_turned, mbk, conv_gain, mix_gain),
-        "backward", smem=(8, 9), far=(0, 2, 3, 4, 5, 6, 7), far_out=(0, 1, 2, 3, 4),
+    five = (ROWS, COLS, 5, H, LANES)
+    slope, hidden, block, pieces, edge_inner, edge_x = call(
+        inside_kernel,
+        [((MR, POS), F32), ((MR, POS), BF), (tile, BF), (five, BF), ((MR, LANES), F32), ((CR, LANES), F32)],
+        (pair_map, act, wf, mf, conv_gain, conv_bias, mix_gain, mix_bias),
+        "inside", smem=(4, 5, 6, 7), far=(0,), far_out=(0, 1, 2, 3, 4, 5),
         scratch=[
-            vmem(tile, BF), vmem((MR, POS), F32), vmem((MR, POS), BF), vmem((2 * CR, POS), BF),
-            vmem((CR, LANES), BF), vmem(cut, BF), vmem((MR, CR), BF),
-        ]
-        + [vmem(s, t) for s, t in backward_outs]
-        + [
-            vmem((3, ROWS, H, LANES), F32),
-            vmem((CR, POS), BF),
-            vmem((3 * MR, POS), BF),
-            vmem((3 * MR, LANES), BF),
-            vmem((3 * MR, 2 * CR), F32),
-            vmem((MR, CR), F32),
+            vmem(tile, BF), vmem((MR, POS), F32), vmem((MR, POS), BF), vmem(tile, BF), vmem(cut, BF),
+            vmem((MR, LANES), F32), vmem((CR, LANES), F32),
         ],
-        copies=12, limit=32,
-    )
+        copies=2 * GROUPS + 5,
+    )
+    grad_inner, g_down, g_up, half_sum, pieces, edge_block, gmi, shifted, edge_rows, hidden, rim = call(
+        inner_kernel,
+        [
+            ((GROUPS, MID, H, LANES), BF),
+            ((GROUPS, MID // 2, H, LANES), BF),
+            ((GROUPS, MID // 2, H, LANES), BF),
+            (tile, F32),
+            (five, BF),
+            ((CR, LANES), F32),
+            ((CR, POS), BF),
+            ((3 * MR, POS), BF),
+            ((3 * MR, LANES), BF),
+            ((MR, POS), BF),
+            ((CR, LANES), BF),
+        ],
+        (
+            cotangent, d_arrived, slope, hidden, edge_inner, edge_x, from_left, from_right,
+            wf_far, mf_far, mbk, pieces, conv_gain, conv_bias, mix_gain, mix_bias,
+        ),
+        "inner", smem=(12, 13, 14, 15), far=(0, 2, 3, 4, 5, 8, 9, 10, 11), far_out=(0, 3, 4, 5), alias={11: 4},
+        scratch=[
+            vmem(tile, BF), vmem((MR, POS), F32), vmem((MR, POS), BF), vmem((MR, LANES), F32), vmem((CR, LANES), F32),
+            vmem((2 * MR, 2 * CR), BF), vmem((CR, MR), BF), vmem((MR, CR), BF),
+            vmem((GROUPS, MID, H, LANES), BF), vmem(tile, F32), vmem((2, COLS, 3, H, LANES), BF),
+            vmem((CR, LANES), F32), vmem((3, ROWS, H, LANES), F32),
+        ],
+        copies=16,
+    )
+    g_above, g_below = both_ways(g_down, g_up, "row")
+    (pieces,) = call(
+        sums_kernel, [(five, BF)], (act_far, gmi, shifted, edge_rows, hidden, rim, pieces), "sums",
+        far=(0, 6), far_out=(0,), alias={6: 0},
+        scratch=[
+            vmem((2 * CR, POS), BF), vmem((ROWS, COLS, 2, H, LANES), BF),
+            vmem((3 * MR, 2 * CR), F32), vmem((MR, CR), F32),
+        ],
+        copies=3,
+    )
+    pieces, g_above, g_below = lax.optimization_barrier((pieces, g_above, g_below))
     arrived = lax.all_to_all(pieces.reshape(ROWS * COLS, 5, H, LANES), everyone, 0, 0, tiled=True)
-    arrived = arrived.reshape(ROWS, COLS, 5, H, LANES)
-    g_above, g_below = both_ways(g_down, g_up, "row")
+    arrived = arrived.reshape(five)
     (sums,) = call(
         total_kernel, [((ROWS, H, LANES), F32)], (arrived,), "total", flops=500_000_000
     )
@@ -562,18 +627,22 @@
     main, g_edge = call(
         spread_kernel,
         [((CR, POS), F32), ((CR // 2, LANES), F32)],
-        (grad_inner, g_above, g_below, wb, sums),
+        (grad_inner, g_above, g_below, wb),
         "spread", far=(0, 3), copies=2,
         scratch=[vmem((2 * MR, 2 * LANES), BF), vmem((GROUPS, MID, H, LANES), BF), vmem((3 * CR, 2 * MR), BF)],
     )
     g_left, g_right = both_ways(g_edge, g_edge, "col")
+    g_left, g_right, _ = lax.optimization_barrier((g_left, g_right, sums))
     (grad_input,) = call(
         input_kernel, [(tile, BF)], (pair_map, half_sum, main, g_left, g_right), "grad_input",
         far=(0, 1), far_out=(0,), scratch=[vmem(tile, BF), vmem(tile, F32), vmem(tile, BF)], copies=3 * GROUPS,
     )
     (symmetric,) = call(
-        symmetric_kernel, [(tile, BF)], (block, arrived), "symmetric", far=(0, 1), far_out=(0,),
-        scratch=[vmem(tile, BF), vmem(cut, BF), vmem(tile, BF), vmem((3, ROWS, H, LANES), F32)], copies=3 * GROUPS,
+        symmetric_kernel, [(tile, BF)], (block, edge_block, arrived), "symmetric", far=(0, 1, 2), far_out=(0,),
+        scratch=[
+            vmem((CR, LANES), F32), vmem(tile, BF), vmem(cut, BF), vmem(tile, BF), vmem((3, ROWS, H, LANES), F32),
+        ],
+        copies=3 * GROUPS + 1,
     )
     conv, mix = call(
         unpack_kernel, [((9, MID, CH), F32), ((MID, CH), F32)], (spread_sums,), "unpack", flops=100_000_000

time: 104 us -> 98.7 us (0.949)
  waiting for transfers between devices: 25.3 us -> 11.4 us
  starting transfers between devices: 34.9 us -> 42.1 us
  Pallas kernels: 41.8 us -> 43.7 us
    all_to_all x1, waiting for transfers between devices: 18.7 us -> 11.3 us  [local(): lax.all_to_all(pieces.reshape(ROWS * COLS, 5, H, LANES), everyone, 0, 0,...]
    ppermute x8, waiting for transfers between devices: 6.58 us -> 0.06 us  [both_ways(): return (lax.ppermute(first, axis, onward), lax.ppermute(second, axis, back))]
    ppermute x8, starting transfers between devices: 13.3 us -> 17.3 us  [both_ways(): return (lax.ppermute(first, axis, onward), lax.ppermute(second, axis, back))]
    all_to_all x1, starting transfers between devices: 5.45 us -> 8.58 us  [local(): lax.all_to_all(pieces.reshape(ROWS * COLS, 5, H, LANES), everyone, 0, 0,...]
    pallas_call x11 -> x12, Pallas kernels: 41.8 us -> 43.7 us  [call(): pl.pallas_call(kernel, name=name, out_shape=[pltpu.HBM(s, t) if i in far_...]
  transfers between devices with their start and end apart: 11 -> 11, of which waited for: 4 -> 1; matrix products, arithmetic and copies ran while one was open for 0% -> 0% of each run, Pallas kernels for 26% -> 34%
where the time goes in v2:
time: 98.7 us; the launch traced here: 98.2 us
  Pallas kernels  43.7 us (44%)
  starting transfers between devices  42.1 us (43%)
  waiting for transfers between devices  11.4 us (12%)
    pallas_call x12, Pallas kernels, call(): pl.pallas_call(kernel, name=name, out_shape=[pltpu.HBM(s, t) if i in far_...  43.7 us
    ppermute x8, starting transfers between devices, both_ways(): return (lax.ppermute(first, axis, onward), lax.ppermute(second, axis, back))  17.3 us
    all_to_all x1, waiting for transfers between devices, local(): lax.all_to_all(pieces.reshape(ROWS * COLS, 5, H, LANES), everyone, 0, 0,...  11.3 us
    all_to_all x1, starting transfers between devices, local(): lax.all_to_all(d_pieces.reshape(ROWS * COLS, 3, H, LANES), everyone, 0, 0...  10.6 us
    all_to_all x1, starting transfers between devices, local(): lax.all_to_all(pieces.reshape(ROWS * COLS, 5, H, LANES), everyone, 0, 0,...  8.58 us
    all_to_all x1, starting transfers between devices, local(): spread_sums = lax.all_to_all(sums, 'row', 0, 0, tiled=True)  5.72 us
  transfers between devices with their start and end apart: 11, of which 1 were waited for; matrix products, arithmetic and copies ran while one was open for 0% of the time, Pallas kernels for 34%

profile of v2, /device:TPU:1, one launch (start us, length us, event | category | flops | bytes accessed | tf_op | source)
XLA Modules:
  0.0 98.2 jit_solution(1141053954936369673)
XLA Ops:
  0.6 0.0 copy-start.1
  0.6 1.6 %rows.1 = (bf16[8,24,8,128]{3,2,1,0:T(8,128)(2,1)S(1)}, bf16[8,24,8,128]{3,2,1,0:T(8,128)(2,1)S(1)}) custom-call(bf16[8,48,8,128]{3,2,1,0:T(8,128)(2,1)} %x_far.3), custom_call_target="tpu_custom_call" | custom-call | flops 4000000000 | bytes 1000000 | tf_op jit(solution)/shard_map/rows/pallas_call | solution.py:75
  2.2 2.8 %collective-permute-start = (bf16[8,24,8,128]{3,2,1,0:T(8,128)(2,1)S(1)}, bf16[8,24,8,128]{3,2,1,0:T(8,128)(2,1)S(1)}, u32[]{:S(2)}, u32[]{:S(2)}) collective-permute-start(bf16[8,24,8,128]{3,2,1,0:T(8,128)(2,1)S(1)} %get-tuple-element.41), channel_id=1, source_target_pairs={{0,8},{8,16},{16,24},{24,32},{32,40},{40,48},{48,56},{56,64},{64,7... | collective-permute-start | bytes 1179656 | tf_op jit(solution)/shard_map/ppermute | solution.py:535
  5.0 1.2 %turn_d.1 = bf16[16,8,3,8,128]{4,3,2,1,0:T(8,128)(2,1)} custom-call(bf16[8,48,8,128]{3,2,1,0:T(8,128)(2,1)S(1)} %copy-done.1), custom_call_target="tpu_custom_call" | custom-call | flops 4000000000 | bytes 1000000 | tf_op jit(solution)/shard_map/turn_d/pallas_call | solution.py:75
  6.2 0.0 copy-start.3
  6.2 10.6 %all-to-all-start = ((bf16[128,3,8,128]{3,2,1,0:T(8,128)(2,1)}), bf16[128,3,8,128]{3,2,1,0:T(8,128)(2,1)S(1)}, u32[]{:S(2)}, u32[]{:S(2)}) async-start(bf16[128,3,8,128]{3,2,1,0:T(8,128)(2,1)} %bitcast.18), calls=%async_computation | async-start | bytes 1572864 | tf_op jit(solution)/shard_map/all_to_all | solution.py:552
  16.8 3.0 %weights.1 = (bf16[576,768]{1,0:T(8,128)(2,1)S(1)}, bf16[1152,384]{1,0:T(8,128)(2,1)}, bf16[384,192]{1,0:T(8,128)(2,1)S(1)}, bf16[192,384]{1,0:T(8,128)(2,1)}, b...) custom-call(bf16[9,24,48]{2,1,0:T(8,128)(2,1)S(1)} %bitcast.15, bf16[24,48]{1,0:T(8,128)(2,1)S(1)} %bitcast.16), custom_call_target="tpu_custom_call" | custom-call | flops 4000000000 | bytes 1000000 | tf_op jit(solution)/shard_map/weights/pallas_call | solution.py:75
  19.8 0.0 copy-start.5
  19.9 3.8 %act.1 = (bf16[768,1024]{1,0:T(8,128)(2,1)S(1)}, bf16[384,128]{1,0:T(8,128)(2,1)S(1)}, bf16[768,1024]{1,0:T(8,128)(2,1)}) custom-call(bf16[8,48,8,128]{3,2,1,0:T(8,128)(2,1)} %x_far.3, bf16[8,24,8,128]{3,2,1,0:T(8,128)(2,1)S(1)} %collective-permute-done.above, bf16[8,24,8,128]{3,2,1,0:T(8,128)(2,1)S(1)} %collective-permute-done.1.below), custom_call_target="tpu_custom_call" | custom-call | flops 4000000000 | bytes 1000000 | tf_op jit(solution)/shard_map/act/pallas_call | solution.py:75
  23.7 5.8 %collective-permute-start.3 = (bf16[384,128]{1,0:T(8,128)(2,1)S(1)}, bf16[384,128]{1,0:T(8,128)(2,1)S(1)}, u32[]{:S(2)}, u32[]{:S(2)}) collective-permute-start(bf16[384,128]{1,0:T(8,128)(2,1)S(1)} %get-tuple-element.51), channel_id=1, source_target_pairs={{1,0},{2,1},{3,2},{4,3},{5,4},{6,5},{7,6},{0,7},{9,8},{10,9},{11,1... | collective-permute-start | bytes 294920 | tf_op jit(solution)/shard_map/ppermute | solution.py:535
  29.5 7.0 %inside.1 = (f32[192,1024]{1,0:T(8,128)}, bf16[192,1024]{1,0:T(8,128)(2,1)}, bf16[8,48,8,128]{3,2,1,0:T(8,128)(2,1)}, bf16[16,8,5,8,128]{4,3,2,1,0:T(8,128)(2,1)...) custom-call(bf16[8,48,8,128]{3,2,1,0:T(8,128)(2,1)} %x_far.3, bf16[768,1024]{1,0:T(8,128)(2,1)S(1)} %get-tuple-element.43.act, ...), custom_call_target="tpu_custom_call" | custom-call | flops 4000000000 | bytes 1000000 | tf_op jit(solution)/shard_map/inside/pallas_call | solution.py:75
  36.5 0.0 collective-permute-done.2.from_left
  36.6 7.9 %inner.1 = (bf16[8,24,8,128]{3,2,1,0:T(8,128)(2,1)}, bf16[8,12,8,128]{3,2,1,0:T(8,128)(2,1)S(1)}, bf16[8,12,8,128]{3,2,1,0:T(8,128)(2,1)S(1)}, f32[8,48,8,128]{3...) custom-call(bf16[8,48,8,128]{3,2,1,0:T(8,128)(2,1)} %d_far.1, ...), custom_call_target="tpu_custom_call", output_to_operand_aliasing={{4}: (11, {})} | custom-call | flops 4000000000 | bytes 1000000 | tf_op jit(solution)/shard_map/inner/pallas_call | solution.py:75
  44.5 3.0 %collective-permute-start.4 = (bf16[8,12,8,128]{3,2,1,0:T(8,128)(2,1)S(1)}, bf16[8,12,8,128]{3,2,1,0:T(8,128)(2,1)S(1)}, u32[]{:S(2)}, u32[]{:S(2)}) collective-permute-start(bf16[8,12,8,128]{3,2,1,0:T(8,128)(2,1)S(1)} %get-tuple-element.64), channel_id=1, source_target_pairs={{0,8},{8,16},{16,24},{24,32},{32,40},{40,48},{48,56},{56,64},{64,7... | collective-permute-start | bytes 589832 | tf_op jit(solution)/shard_map/ppermute | solution.py:535
  47.5 5.8 %sums.1 = bf16[16,8,5,8,128]{4,3,2,1,0:T(8,128)(2,1)} custom-call(bf16[768,1024]{1,0:T(8,128)(2,1)} %get-tuple-element.57.act_far, bf16[384,1024]{1,0:T(8,128)(2,1)S(1)} %get-tuple-element.58.gmi, bf16[576,1024]{1,0:T(8,128)(2,1)S(1)} %get-tuple-element.59.shifted, bf16[576,128]{1,0:T(8,128)(2,1)S(1)} %get-tuple-element.60.edge_rows, ...), custom_call_target="tpu_custom_call", output_to_operand_aliasing={{}: (6, {})} | custom-call | flops 4000000000 | bytes 1000000 | tf_op jit(solution)/shard_map/sums/pallas_call | solution.py:75
  53.3 8.6 %all-to-all-start.1 = ((bf16[128,5,8,128]{3,2,1,0:T(8,128)(2,1)}), bf16[128,5,8,128]{3,2,1,0:T(8,128)(2,1)S(1)}, u32[]{:S(2)}, u32[]{:S(2)}) async-start(bf16[128,5,8,128]{3,2,1,0:T(8,128)(2,1)} %bitcast.17), calls=%async_computation.1 | async-start | bytes 2621440 | tf_op jit(solution)/shard_map/all_to_all | solution.py:621
  61.9 3.2 %spread.1 = (f32[384,1024]{1,0:T(8,128)S(1)}, f32[192,128]{1,0:T(8,128)S(1)}) custom-call(bf16[8,24,8,128]{3,2,1,0:T(8,128)(2,1)} %get-tuple-element.68.grad_inner_far, bf16[8,12,8,128]{3,2,1,0:T(8,128)(2,1)S(1)} %collective-permute-done.4.above, bf16[8,12,8,128]{3,2,1,0:T(8,128)(2,1)S(1)} %collective-permute-done.5.below, ...), custom_call_target="tpu_custom_call" | custom-call | flops 4000000000 | bytes 1000000 | tf_op jit(solution)/shard_map/spread/pallas_call | solution.py:75
  65.2 5.8 %collective-permute-start.7 = (f32[192,128]{1,0:T(8,128)S(1)}, f32[192,128]{1,0:T(8,128)S(1)}, u32[]{:S(2)}, u32[]{:S(2)}) collective-permute-start(f32[192,128]{1,0:T(8,128)S(1)} %get-tuple-element.73), channel_id=1, source_target_pairs={{1,0},{2,1},{3,2},{4,3},{5,4},{6,5},{7,6},{0,7},{9,8},{10,9},{11,1... | collective-permute-start | bytes 294920 | tf_op jit(solution)/shard_map/ppermute | solution.py:535
  70.9 11.3 %all-to-all-done.1 = bf16[128,5,8,128]{3,2,1,0:T(8,128)(2,1)S(1)} async-done(((bf16[128,5,8,128]{3,2,1,0:T(8,128)(2,1)}), bf16[128,5,8,128]{3,2,1,0:T(8,128)(2,1)S(1)}, u32[]{:S(2)}, u32[]{:S(2)}) %all-to-all-start.1) | async-done | bytes 1310752 | tf_op jit(solution)/shard_map/all_to_all | solution.py:621
  82.2 0.8 total.1
  83.0 5.7 %all-to-all-start.2 = ((f32[16,8,128]{2,1,0:T(8,128)}), f32[16,8,128]{2,1,0:T(8,128)S(1)}, u32[]{:S(2)}, u32[]{:S(2)}) async-start(f32[16,8,128]{2,1,0:T(8,128)} %total.1), calls=%async_computation.2 | async-start | bytes 131072 | tf_op jit(solution)/shard_map/all_to_all | solution.py:626
  88.8 5.5 %symmetric.1 = bf16[8,48,8,128]{3,2,1,0:T(8,128)(2,1)} custom-call(bf16[8,48,8,128]{3,2,1,0:T(8,128)(2,1)} %get-tuple-element.46.block_far, f32[384,128]{1,0:T(8,128)} %get-tuple-element.56.edge_far, bf16[16,8,5,8,128]{4,3,2,1,0:T(8,128)(2,1)} %bitcast.13), custom_call_target="tpu_custom_call" | custom-call | flops 4000000000 | bytes 1000000 | tf_op jit(solution)/shard_map/symmetric/pallas_call | solution.py:75
  94.3 3.1 %grad_input.1 = bf16[8,48,8,128]{3,2,1,0:T(8,128)(2,1)} custom-call(bf16[8,48,8,128]{3,2,1,0:T(8,128)(2,1)} %x_far.3, f32[8,48,8,128]{3,2,1,0:T(8,128)} %get-tuple-element.67.half_far, f32[384,1024]{1,0:T(8,128)S(1)} %get-tuple-element.72.main, f32[192,128]{1,0:T(8,128)S(1)} %collective-permute-done.6.from_left, f32[192,128]{1,0:T(8,128)S(1)} %collective-permute-done.7.from_right), custom_call_target="tpu_custom_call" | custom-call | flops 4000000000 | bytes 1000000 | tf_op jit(solution)/shard_map/grad_input/pallas_call | solution.py:75
  97.4 0.7 unpack.1
  (26 shorter events, 0.1 us)
Async XLA Ops:
  0.6 4.4 %copy-start.1 = (bf16[8,48,8,128]{3,2,1,0:T(8,128)(2,1)S(1)}, bf16[8,48,8,128]{3,2,1,0:T(8,128)(2,1)}, u32[]{:S(2)}) copy-start(bf16[8,48,8,128]{3,2,1,0:T(8,128)(2,1)} %d_far.1) | copy-start | bytes 2359300
  2.2 17.6 %collective-permute-start = (bf16[8,24,8,128]{3,2,1,0:T(8,128)(2,1)S(1)}, bf16[8,24,8,128]{3,2,1,0:T(8,128)(2,1)S(1)}, u32[]{:S(2)}, u32[]{:S(2)}) collective-permute-start(bf16[8,24,8,128]{3,2,1,0:T(8,128)(2,1)S(1)} %get-tuple-element.41), channel_id=1, source_target_pairs={{0,8},{8,16},{16,24},{24,32},{32,40},{40,48},{48,56},{56,64},{64,7... | collective-permute-start | bytes 1179656 | tf_op jit(solution)/shard_map/ppermute | solution.py:535
  5.0 14.9 %collective-permute-start.1 = (bf16[8,24,8,128]{3,2,1,0:T(8,128)(2,1)S(1)}, bf16[8,24,8,128]{3,2,1,0:T(8,128)(2,1)S(1)}, u32[]{:S(2)}, u32[]{:S(2)}) collective-permute-start(bf16[8,24,8,128]{3,2,1,0:T(8,128)(2,1)S(1)} %get-tuple-element.42), channel_id=1, source_target_pairs={{8,0},{16,8},{24,16},{32,24},{40,32},{48,40},{56,48},{64,56},{72,6... | collective-permute-start | bytes 1179656 | tf_op jit(solution)/shard_map/ppermute | solution.py:535
  6.2 10.6 %copy-start.2 = (bf16[24,48,3,3]{1,0,3,2:T(8,128)(2,1)S(1)}, bf16[24,48,3,3]{1,0,3,2:T(8,128)(2,1)}, u32[]{:S(2)}) copy-start(bf16[24,48,3,3]{1,0,3,2:T(8,128)(2,1)} %param.10) | copy-start | bytes 62212
  6.2 10.6 %copy-start.3 = (bf16[48,24]{0,1:T(8,128)(2,1)S(1)}, bf16[48,24]{0,1:T(8,128)(2,1)}, u32[]{:S(2)}) copy-start(bf16[48,24]{0,1:T(8,128)(2,1)} %param.13) | copy-start | bytes 6916
  6.2 30.3 %all-to-all-start = ((bf16[128,3,8,128]{3,2,1,0:T(8,128)(2,1)}), bf16[128,3,8,128]{3,2,1,0:T(8,128)(2,1)S(1)}, u32[]{:S(2)}, u32[]{:S(2)}) async-start(bf16[128,3,8,128]{3,2,1,0:T(8,128)(2,1)} %bitcast.18), calls=%async_computation | async-start | bytes 1572864 | tf_op jit(solution)/shard_map/all_to_all | solution.py:552
  19.8 9.6 %copy-start.4 = (f32[24]{0:T(128)S(1)}, f32[24]{0:T(128)}, u32[]{:S(2)}) copy-start(f32[24]{0:T(128)} %cg.3) | copy-start | bytes 292
  19.8 9.6 %copy-start.5 = (f32[24]{0:T(128)S(1)}, f32[24]{0:T(128)}, u32[]{:S(2)}) copy-start(f32[24]{0:T(128)} %cb.3) | copy-start | bytes 292
  19.8 9.6 %copy-start.6 = (f32[48]{0:T(128)S(1)}, f32[48]{0:T(128)}, u32[]{:S(2)}) copy-start(f32[48]{0:T(128)} %mg.3) | copy-start | bytes 580
  19.9 9.6 %copy-start.7 = (f32[48]{0:T(128)S(1)}, f32[48]{0:T(128)}, u32[]{:S(2)}) copy-start(f32[48]{0:T(128)} %mb.3) | copy-start | bytes 580
  23.7 12.8 %collective-permute-start.3 = (bf16[384,128]{1,0:T(8,128)(2,1)S(1)}, bf16[384,128]{1,0:T(8,128)(2,1)S(1)}, u32[]{:S(2)}, u32[]{:S(2)}) collective-permute-start(bf16[384,128]{1,0:T(8,128)(2,1)S(1)} %get-tuple-element.51), channel_id=1, source_target_pairs={{1,0},{2,1},{3,2},{4,3},{5,4},{6,5},{7,6},{0,7},{9,8},{10,9},{11,1... | collective-permute-start | bytes 294920 | tf_op jit(solution)/shard_map/ppermute | solution.py:535
  29.5 7.1 %collective-permute-start.2 = (bf16[384,128]{1,0:T(8,128)(2,1)S(1)}, bf16[384,128]{1,0:T(8,128)(2,1)S(1)}, u32[]{:S(2)}, u32[]{:S(2)}) collective-permute-start(bf16[384,128]{1,0:T(8,128)(2,1)S(1)} %get-tuple-element.51), channel_id=1, source_target_pairs={{0,1},{1,2},{2,3},{3,4},{4,5},{5,6},{6,7},{7,0},{8,9},{9,10},{10,1... | collective-permute-start | bytes 294920 | tf_op jit(solution)/shard_map/ppermute | solution.py:535
  44.5 8.8 %collective-permute-start.4 = (bf16[8,12,8,128]{3,2,1,0:T(8,128)(2,1)S(1)}, bf16[8,12,8,128]{3,2,1,0:T(8,128)(2,1)S(1)}, u32[]{:S(2)}, u32[]{:S(2)}) collective-permute-start(bf16[8,12,8,128]{3,2,1,0:T(8,128)(2,1)S(1)} %get-tuple-element.64), channel_id=1, source_target_pairs={{0,8},{8,16},{16,24},{24,32},{32,40},{40,48},{48,56},{56,64},{64,7... | collective-permute-start | bytes 589832 | tf_op jit(solution)/shard_map/ppermute | solution.py:535
  47.5 5.8 %collective-permute-start.5 = (bf16[8,12,8,128]{3,2,1,0:T(8,128)(2,1)S(1)}, bf16[8,12,8,128]{3,2,1,0:T(8,128)(2,1)S(1)}, u32[]{:S(2)}, u32[]{:S(2)}) collective-permute-start(bf16[8,12,8,128]{3,2,1,0:T(8,128)(2,1)S(1)} %get-tuple-element.65), channel_id=1, source_target_pairs={{8,0},{16,8},{24,16},{32,24},{40,32},{48,40},{56,48},{64,56},{72,6... | collective-permute-start | bytes 589832 | tf_op jit(solution)/shard_map/ppermute | solution.py:535
  53.3 28.9 %all-to-all-start.1 = ((bf16[128,5,8,128]{3,2,1,0:T(8,128)(2,1)}), bf16[128,5,8,128]{3,2,1,0:T(8,128)(2,1)S(1)}, u32[]{:S(2)}, u32[]{:S(2)}) async-start(bf16[128,5,8,128]{3,2,1,0:T(8,128)(2,1)} %bitcast.17), calls=%async_computation.1 | async-start | bytes 2621440 | tf_op jit(solution)/shard_map/all_to_all | solution.py:621
  65.2 23.6 %collective-permute-start.7 = (f32[192,128]{1,0:T(8,128)S(1)}, f32[192,128]{1,0:T(8,128)S(1)}, u32[]{:S(2)}, u32[]{:S(2)}) collective-permute-start(f32[192,128]{1,0:T(8,128)S(1)} %get-tuple-element.73), channel_id=1, source_target_pairs={{1,0},{2,1},{3,2},{4,3},{5,4},{6,5},{7,6},{0,7},{9,8},{10,9},{11,1... | collective-permute-start | bytes 294920 | tf_op jit(solution)/shard_map/ppermute | solution.py:535
  70.9 17.9 %collective-permute-start.6 = (f32[192,128]{1,0:T(8,128)S(1)}, f32[192,128]{1,0:T(8,128)S(1)}, u32[]{:S(2)}, u32[]{:S(2)}) collective-permute-start(f32[192,128]{1,0:T(8,128)S(1)} %get-tuple-element.73), channel_id=1, source_target_pairs={{0,1},{1,2},{2,3},{3,4},{4,5},{5,6},{6,7},{7,0},{8,9},{9,10},{10,1... | collective-permute-start | bytes 294920 | tf_op jit(solution)/shard_map/ppermute | solution.py:535
  82.2 6.6 %copy-start = (bf16[128,5,8,128]{3,2,1,0:T(8,128)(2,1)}, bf16[128,5,8,128]{3,2,1,0:T(8,128)(2,1)S(1)}, u32[]{:S(2)}) copy-start(bf16[128,5,8,128]{3,2,1,0:T(8,128)(2,1)S(1)} %all-to-all-done.1) | copy-start | bytes 3932164
  83.0 14.4 %all-to-all-start.2 = ((f32[16,8,128]{2,1,0:T(8,128)}), f32[16,8,128]{2,1,0:T(8,128)S(1)}, u32[]{:S(2)}, u32[]{:S(2)}) async-start(f32[16,8,128]{2,1,0:T(8,128)} %total.1), calls=%async_computation.2 | async-start | bytes 131072 | tf_op jit(solution)/shard_map/all_to_all | solution.py:626

commit v3 on v2

--- a/solution.py
+++ b/solution.py
@@ -129,19 +129,9 @@
     send_rows(held, down, up, CH)
 
 
-def turn_out(value, eye, pieces, g, first_tile):
-    turned = dot(eye, value, NT)
-    for k in range(3):
-        part = turned[:, k * LANES : (k + 1) * LANES].reshape(ROWS, H, LANES)
-        pieces[:, g, first_tile + k] = part.astype(BF)
-
-
-def turn_in(pieces, g, first_tile, buffer):
-    parts = [
-        pieces[r, g, first_tile : first_tile + 3].astype(F32).reshape(3 * H, LANES)
-        for r in range(ROWS)
-    ]
-    lane = lanes_of(3 * H)
+def swap_blocks(parts):
+    lane = iota(parts[0].shape, 1)
+    parts = list(parts)
     for k in range(4):
         m = 1 << k
         high = (lane // (8 * m)) % 2 == 1
@@ -151,77 +141,102 @@
             a, b = parts[i], parts[i | m]
             parts[i] = jnp.where(high, pltpu.roll(b, 8 * m, 1), a)
             parts[i | m] = jnp.where(high, b, pltpu.roll(a, LANES - 8 * m, 1))
+    return parts
+
+
+def turn(tiles):
+    return tiles.reshape(LANES, LANES).T.reshape(ROWS, H, LANES)
+
+
+def swap_in(pieces, g, buffer):
+    parts = swap_blocks([pieces[r, g : g + 2].reshape(6 * H, LANES) for r in range(ROWS)])
     for i in range(ROWS):
-        buffer[:, i] = parts[i].reshape(3, H, LANES)
-    return buffer[...].reshape(CR, LANES)
+        value = parts[i].reshape(2, 3, H, LANES)
+        for n in range(2):
+            for k in range(3):
+                buffer[n, k * ROWS + i] = value[n, k]
+
+
+def swap_out(block, pieces, g):
+    parts = swap_blocks(
+        [
+            jnp.concatenate([block[g + n, k * ROWS + i] for n in range(2) for k in range(3)], axis=0)
+            for i in range(ROWS)
+        ]
+    )
+    for r in range(ROWS):
+        pieces[r, g : g + 2] = parts[r].reshape(2, 3, H, LANES)
 
 
 def mirror_kernel(d, pieces, turned, sems):
     far = Far(sems)
-    eye = identity(LANES)
     for g in range(GROUPS):
-        turn_out(d[g].astype(F32).reshape(CR, LANES).astype(BF), eye, turned, g, 0)
+        for k in range(3):
+            turned[:, g, k] = turn(d[g, k * ROWS : (k + 1) * ROWS])
         far.send(turned.at[:, g], pieces.at[:, g])
     far.finish()
 
 
-def weights_kernel(w, mix, a_out, b_far, mf_out, mb_far, a_far, mf_far, b_out, mb_out, sems):
-    far = Far(sems)
-
-    def spread(n, own, width):
-        col = iota((n, width), 1)
-        half = (width - own) // 2
-        rim = jnp.where(col < own + half, col - own, col - own - half) // 4
-        return jnp.where(jnp.where(col < own, col // 8, rim) == iota((n, width), 0), 1.0, 0.0).astype(BF)
-
-    def place(own, width):
-        col, h = iota((H, width), 1), iota((H, width), 0)
-        half = (width - own) // 2
-        rim = jnp.where(col < own + half, (col - own) % 4 - 4, (col - own - half) % 4 + 8)
-        return jnp.where(col < own, col % 8, rim) - h
-
-    sf, st = spread(CH, CR, 2 * CR), spread(MID, MR, 2 * MR)
-    pf, pt = place(CR, 2 * CR), place(MR, 2 * MR)
+def spread_channels(n, own, width):
+    col = iota((n, width), 1)
+    half = (width - own) // 2
+    rim = jnp.where(col < own + half, col - own, col - own - half) // 4
+    return jnp.where(jnp.where(col < own, col // 8, rim) == iota((n, width), 0), 1.0, 0.0).astype(BF)
+
+
+def row_distance(own, width):
+    col, h = iota((H, width), 1), iota((H, width), 0)
+    half = (width - own) // 2
+    rim = jnp.where(col < own + half, (col - own) % 4 - 4, (col - own - half) % 4 + 8)
+    return jnp.where(col < own, col % 8, rim) - h
+
+
+def weights_kernel(w, mix, a_out, mf_out, a_far, mf_far, mb_far, mb_out, sems):
+    far = Far(sems)
+    sf, st = spread_channels(CH, CR, 2 * CR), spread_channels(MID, MR, MR)
+    pf, pt = row_distance(CR, 2 * CR), row_distance(MR, MR)
+    masks = [jnp.where(pf == 4 * (a - 1), 1.0, 0.0)[None] for a in range(3)]
     for b in range(3):
-        total_a = jnp.zeros((MID, H, 2 * CR), F32)
-        total_b = jnp.zeros((CH, H, 2 * MR), F32)
+        total = jnp.zeros((MID, H, 2 * CR), F32)
         for a in range(3):
-            tap = w[3 * a + b]
-            mask = jnp.where(pf == 4 * (a - 1), 1.0, 0.0)
-            total_a += dot(tap, sf)[:, None, :] * mask[None]
-            mask = jnp.where(pt == -4 * (a - 1), 1.0, 0.0)
-            total_b += dot(tap, st, TN)[:, None, :] * mask[None]
-        a_out[b * MR : (b + 1) * MR] = total_a.reshape(MR, 2 * CR).astype(BF)
-        b_out[b * CR : (b + 1) * CR] = total_b.reshape(CR, 2 * MR).astype(BF)
+            total += dot(w[3 * a + b], sf)[:, None, :] * masks[a]
+        a_out[b * MR : (b + 1) * MR] = total.reshape(MR, 2 * CR).astype(BF)
+    far.send(a_out, a_far)
     mask = jnp.where(pf[:, :CR] == 0, 1.0, 0.0)
     mb_out[...] = (dot(mix[...], sf[:, :CR])[:, None, :] * mask[None]).reshape(MR, CR).astype(BF)
-    mask = jnp.where(pt[:, :MR] == 0, 1.0, 0.0)
-    mf_out[...] = (dot(mix[...], st[:, :MR], TN)[:, None, :] * mask[None]).reshape(CR, MR).astype(BF)
-    far.send(b_out, b_far)
     far.send(mb_out, mb_far)
-    far.send(a_out, a_far)
+    mask = jnp.where(pt == 0, 1.0, 0.0)
+    mf_out[...] = (dot(mix[...], st, TN)[:, None, :] * mask[None]).reshape(CR, MR).astype(BF)
     far.send(mf_out, mf_far)
     far.finish()
 
 
-def act_kernel(x, above, below, act, edge, act_far, held, sems):
-    far = Far(sems)
-    loads = [far.start(x.at[g], held.at[g]) for g in range(GROUPS)]
+def back_weights(w, out):
+    st, pt = spread_channels(MID, MR, 2 * MR), row_distance(MR, 2 * MR)
+    masks = [jnp.where(pt == -4 * (a - 1), 1.0, 0.0)[None] for a in range(3)]
+    for b in range(3):
+        total = jnp.zeros((CH, H, 2 * MR), F32)
+        for a in range(3):
+            total += dot(w[3 * a + b], st, TN)[:, None, :] * masks[a]
+        out[b * CR : (b + 1) * CR] = total.reshape(CR, 2 * MR).astype(BF)
+
+
+def act_kernel(x, above, below, act, edge, act_far, sems):
+    far = Far(sems)
     lane = lanes_of(CR)
     packed = jnp.zeros((CR, LANES), F32)
     for g in range(GROUPS):
-        loads[g].wait()
-        own = smooth(held[g].astype(F32).reshape(CR, LANES))
+        own = smooth(x[g].astype(F32).reshape(CR, LANES))
         high = smooth(above[g].astype(F32).reshape(CR // 2, LANES))
         low = smooth(below[g].astype(F32).reshape(CR // 2, LANES))
         rim = jnp.concatenate([high, low], axis=0)
         at = slice(g * LANES, (g + 1) * LANES)
         act[0:CR, at] = own.astype(BF)
         act[CR : 2 * CR, at] = rim.astype(BF)
+        far.send(act.at[:, at], act_far.at[:, at])
         packed = jnp.where(lane // 8 == g, pltpu.roll(own, (8 * g - 124) % LANES, 1), packed)
         packed = jnp.where(lane // 8 == 8 + g, pltpu.roll(rim, (8 * g - 60) % LANES, 1), packed)
     edge[...] = packed.astype(BF)
-    far.send(act, act_far)
     far.finish()
 
 
@@ -242,18 +257,15 @@
 
 
 def inside_kernel(
-    x_far, act, weights, mixer, cg, cb, mg, mb,
+    x, act, weights, mixer, cg, cb, mg, mb,
     slope_far, hidden_far, block_far, pieces_far, edge_inner_far, edge_x_far,
-    x, slope, hidden, block, pieces, edge_inner, edge_x, sems,
+    slope, hidden, block, pieces, edge_inner, edge_x, sems,
 ):
     far = Far(sems)
-    load = far.start(x_far, x)
-    eye = identity(LANES)
     lane, lane_c = lanes_of(MR), lanes_of(CR)
     gain, shift = splat(cg, MID), splat(cb, MID)
     gain_out, shift_out = splat(mg, CH), splat(mb, CH)
     packed, packed_x = jnp.zeros((MR, LANES), F32), jnp.zeros((CR, LANES), F32)
-    load.wait()
     for pair in range(GROUPS // 2):
         two = slice(pair * 2 * LANES, (pair + 1) * 2 * LANES)
         product = dot(weights[...], act[:, two])
@@ -270,6 +282,8 @@
             at = slice(g * LANES, (g + 1) * LANES)
             slope[:, at] = smooth_slope(pre) * gain
             hidden[:, at] = smooth(pre).astype(BF)
+        far.send(slope.at[:, two], slope_far.at[:, two])
+        far.send(hidden.at[:, two], hidden_far.at[:, two])
         mixed = dot(mixer[...], hidden[:, two])
         for half in range(2):
             g = 2 * pair + half
@@ -278,13 +292,12 @@
             packed_x = jnp.where(lane_c // 8 == g, pltpu.roll(own, (8 * g - 124) % LANES, 1), packed_x)
             value = (own + m * gain_out + shift_out).astype(BF)
             block[g] = value.astype(F32).reshape(CH, H, LANES).astype(BF)
-            turn_out(value, eye, pieces, g, 0)
-            far.send(block.at[g], block_far.at[g])
-            far.send(pieces.at[:, g], pieces_far.at[:, g, 2:5])
+        g = 2 * pair
+        far.send(block.at[g : g + 2], block_far.at[g : g + 2])
+        swap_out(block, pieces, g)
+        far.send(pieces.at[:, g : g + 2], pieces_far.at[:, g : g + 2, 2:5])
     edge_inner[...] = packed
     edge_x[...] = packed_x
-    far.send(slope, slope_far)
-    far.send(hidden, hidden_far)
     far.send(edge_inner, edge_inner_far)
     far.send(edge_x, edge_x_far)
     far.finish()
@@ -331,14 +344,16 @@
     edge_block[...] = value.astype(F32)
     far.send(edge_block, edge_block_far)
     hidden_edge = hidden_edge.astype(F32)
-    turned = dot(identity(LANES), value, NT)
+    parts = value.astype(F32).reshape(3, ROWS, H, LANES)
+    parts = swap_blocks([parts[:, i].reshape(3 * H, LANES) for i in range(ROWS)])
     for load in tails:
         load.wait()
-    low = iota((COLS, H, LANES), 1) < 4
-    for k in range(3):
-        part = pltpu.roll(turned[0 : COLS * H, k * LANES : (k + 1) * LANES].reshape(COLS, H, LANES), 4, 1)
-        ends[0, :, k] = jnp.where(low, part, ends[0, :, k].astype(F32)).astype(BF)
-        ends[1, :, k] = jnp.where(low, ends[1, :, k].astype(F32), part).astype(BF)
+    low = iota((3, H, LANES), 2) % 8 < 4
+    for g in range(GROUPS):
+        lower = pltpu.roll(parts[g], LANES - 4, 1).reshape(3, H, LANES)
+        upper = pltpu.roll(parts[g], 4, 1).reshape(3, H, LANES)
+        ends[0, g] = jnp.where(low, lower, ends[0, g].astype(F32)).astype(BF)
+        ends[1, g] = jnp.where(low, ends[1, g].astype(F32), upper).astype(BF)
     for i, r in enumerate((0, ROWS - 1)):
         far.send(ends.at[i], pieces_far.at[r, :, 2:5])
 
@@ -347,9 +362,10 @@
     packed = jnp.zeros((MR, LANES), F32)
     for pair in range(GROUPS // 2):
         two = slice(pair * 2 * LANES, (pair + 1) * 2 * LANES)
+        swap_in(arrived, 2 * pair, buffer)
         for half in range(2):
             g = 2 * pair + half
-            both = 0.5 * (d[g].astype(F32).reshape(CR, LANES) + turn_in(arrived, g, 0, buffer))
+            both = 0.5 * (d[g].astype(F32) + buffer[half].astype(F32)).reshape(CR, LANES)
             half_sum[g] = both.reshape(CH, H, LANES)
             gmi[:, g * LANES : (g + 1) * LANES] = (both * gain_out).astype(BF)
         into = dot(back[...], gmi[:, two])
@@ -442,13 +458,21 @@
     far.finish()
 
 
-def spread_kernel(grad_inner_far, above, below, weights_far, main, edge, rhs, grad_inner, weights, sems):
-    far = Far(sems)
-    loads = [far.start(grad_inner_far, grad_inner), far.start(weights_far, weights)]
+def spread_kernel(
+    grad_inner_far, above, below, w, half_far, x_far, block_far, edge_block_far,
+    edge, out_far, edge_value_far, edge_slope_far, block_out_far,
+    weights, rhs, grad_inner, half_sum, x, block, edge_block, out, edge_value, edge_slope, sems,
+):
+    far = Far(sems)
+    first = far.start(grad_inner_far, grad_inner)
+    loads = [far.start(half_far, half_sum), far.start(x_far, x)]
+    last = [far.start(block_far, block), far.start(edge_block_far, edge_block)]
+    back_weights(w, weights)
+    first.wait()
+    lane = lanes_of(CR)
+    packed, packed_value, packed_slope = (jnp.zeros((CR, LANES), F32) for _ in range(3))
     for load in loads:
         load.wait()
-    lane = lanes_of(CR)
-    packed = jnp.zeros((CR, LANES), F32)
     for pair in range(GROUPS // 2):
         for half in range(2):
             g = 2 * pair + half
@@ -461,32 +485,51 @@
             g = 2 * pair + half
             p = product[:, half * LANES : (half + 1) * LANES]
             left, mid, right = p[0:CR], p[CR : 2 * CR], p[2 * CR : 3 * CR]
-            main[:, g * LANES : (g + 1) * LANES] = (
+            total = (
                 mid
                 + jnp.where(lane < 124, pltpu.roll(left, LANES - 4, 1), 0.0)
                 + jnp.where(lane >= 4, pltpu.roll(right, 4, 1), 0.0)
             )
-            out = jnp.where(lane >= 124, right, left)
-            packed = jnp.where(lane // 8 == g, pltpu.roll(out, (8 * g - 124) % LANES, 1), packed)
+            slope = smooth_slope(x[g].astype(F32).reshape(CR, LANES))
+            value = half_sum[g].reshape(CR, LANES) + total * slope
+            out[g] = value.reshape(CH, H, LANES).astype(BF)
+            far.send(out.at[g], out_far.at[g])
+            here = lane // 8 == g
+            turn_by = (8 * g - 124) % LANES
+            packed = jnp.where(here, pltpu.roll(jnp.where(lane >= 124, right, left), turn_by, 1), packed)
+            packed_value = jnp.where(here, pltpu.roll(value, turn_by, 1), packed_value)
+            packed_slope = jnp.where(here, pltpu.roll(slope, turn_by, 1), packed_slope)
     edge[...] = packed[0 : CR // 2] + pltpu.roll(packed[CR // 2 : CR], 64, 1)
-
-
-def input_kernel(x_far, half_far, main, from_left, from_right, out_far, x, half_sum, grad_input, sems):
-    far = Far(sems)
-    loads = [(far.start(x_far.at[g], x.at[g]), far.start(half_far.at[g], half_sum.at[g])) for g in range(GROUPS)]
+    edge_value[...] = packed_value
+    edge_slope[...] = packed_slope
+    far.send(edge_value, edge_value_far)
+    far.send(edge_slope, edge_slope_far)
+    for load in last:
+        load.wait()
+    for g in range(GROUPS):
+        moved = pltpu.roll(edge_block[...], (124 - 8 * g) % LANES, 1)
+        value = jnp.where(at_edge(lane), moved, block[g].astype(F32).reshape(CR, LANES))
+        block[g] = value.reshape(CH, H, LANES).astype(BF)
+        far.send(block.at[g], block_out_far.at[g])
+    far.finish()
+
+
+def input_kernel(value_far, edge_value_far, edge_slope_far, from_left, from_right, out_far, value, out, edge_value, edge_slope, sems):
+    far = Far(sems)
+    first = [far.start(edge_value_far, edge_value), far.start(edge_slope_far, edge_slope)]
+    loads = [far.start(value_far.at[g], value.at[g]) for g in range(GROUPS)]
     lane = lanes_of(CR)
     rim = merge_edges(from_left[...], from_right[...])
     rim = jnp.concatenate([rim, pltpu.roll(rim, 64, 1)], axis=0)
+    for load in first:
+        load.wait()
+    rim = edge_value[...] + rim * edge_slope[...]
     for g in range(GROUPS):
-        for load in loads[g]:
-            load.wait()
-        q = pltpu.roll(rim, (124 - 8 * g) % LANES, 1)
-        total = main[:, g * LANES : (g + 1) * LANES]
-        total = total + jnp.where(jnp.logical_or(lane < 4, lane >= 124), q, 0.0)
-        slope = smooth_slope(x[g].astype(F32).reshape(CR, LANES))
-        value = half_sum[g].reshape(CR, LANES) + total * slope
-        grad_input[g] = value.reshape(CH, H, LANES).astype(BF)
-        far.send(grad_input.at[g], out_far.at[g])
+        loads[g].wait()
+        moved = pltpu.roll(rim, (124 - 8 * g) % LANES, 1)
+        total = jnp.where(at_edge(lane), moved, value[g].astype(F32).reshape(CR, LANES))
+        out[g] = total.reshape(CH, H, LANES).astype(BF)
+        far.send(out.at[g], out_far.at[g])
     far.finish()
 
 
@@ -498,22 +541,19 @@
     out[...] = jnp.broadcast_to((total * (1.0 / (ROWS * H * COLS)))[None], (ROWS, H, LANES))
 
 
-def symmetric_kernel(block_far, edge_far, arrived_far, out_far, edge, block, arrived, out, buffer, sems):
+def symmetric_kernel(block_far, arrived_far, out_far, block, arrived, out, sems):
     far = Far(sems)
     loads = [
         (far.start(block_far.at[g], block.at[g]), far.start(arrived_far.at[:, g, 2:5], arrived.at[:, g]))
         for g in range(GROUPS)
     ]
-    far.start(edge_far, edge).wait()
-    lane = lanes_of(CR)
     for g in range(GROUPS):
         for load in loads[g]:
             load.wait()
-        own = jnp.where(
-            at_edge(lane), pltpu.roll(edge[...], (124 - 8 * g) % LANES, 1), block[g].astype(F32).reshape(CR, LANES)
-        )
-        value = 0.5 * (own + turn_in(arrived, g, 0, buffer))
-        out[g] = value.reshape(CH, H, LANES).astype(BF)
+        for k in range(3):
+            at = slice(k * ROWS, (k + 1) * ROWS)
+            value = 0.5 * (block[g, at].astype(F32) + turn(arrived[:, g, k]).astype(F32))
+            out[g, at] = value.astype(BF)
         far.send(out.at[g], out_far.at[g])
     far.finish()
 
@@ -553,18 +593,15 @@
     d_arrived = d_arrived.reshape(cut)
 
     taps = jnp.transpose(conv_weight, (2, 3, 0, 1)).reshape(9, MID, CH)
-    wf, wb, mf, mbk, wf_far, mf_far = call(
+    wf, mf, wf_far, mf_far, mbk = call(
         weights_kernel,
-        [((3 * MR, 2 * CR), BF), ((3 * CR, 2 * MR), BF), ((CR, MR), BF), ((MR, CR), BF)]
-        + [((3 * MR, 2 * CR), BF), ((CR, MR), BF)],
-        (taps, mix_weight.T), "weights", far_out=(1, 3, 4, 5),
-        scratch=[vmem((3 * CR, 2 * MR), BF), vmem((MR, CR), BF)], copies=4,
+        [((3 * MR, 2 * CR), BF), ((CR, MR), BF)] * 2 + [((MR, CR), BF)],
+        (taps, mix_weight.T), "weights", far_out=(2, 3, 4), scratch=[vmem((MR, CR), BF)], copies=3,
     )
     act, edge, act_far = call(
         act_kernel,
         [((2 * CR, POS), BF), ((CR, LANES), BF), ((2 * CR, POS), BF)],
-        (pair_map, above, below), "act", far=(0,), far_out=(2,),
-        scratch=[vmem(tile, BF)], copies=GROUPS + 1,
+        (pair_map, above, below), "act", far_out=(2,), copies=GROUPS,
     )
     from_left, from_right = both_ways(edge, edge, "col")
     five = (ROWS, COLS, 5, H, LANES)
@@ -572,12 +609,12 @@
         inside_kernel,
         [((MR, POS), F32), ((MR, POS), BF), (tile, BF), (five, BF), ((MR, LANES), F32), ((CR, LANES), F32)],
         (pair_map, act, wf, mf, conv_gain, conv_bias, mix_gain, mix_bias),
-        "inside", smem=(4, 5, 6, 7), far=(0,), far_out=(0, 1, 2, 3, 4, 5),
+        "inside", smem=(4, 5, 6, 7), far_out=(0, 1, 2, 3, 4, 5),
         scratch=[
-            vmem(tile, BF), vmem((MR, POS), F32), vmem((MR, POS), BF), vmem(tile, BF), vmem(cut, BF),
+            vmem((MR, POS), F32), vmem((MR, POS), BF), vmem(tile, BF), vmem(cut, BF),
             vmem((MR, LANES), F32), vmem((CR, LANES), F32),
         ],
-        copies=2 * GROUPS + 5,
+        copies=2 * GROUPS + 2,
     )
     grad_inner, g_down, g_up, half_sum, pieces, edge_block, gmi, shifted, edge_rows, hidden, rim = call(
         inner_kernel,
@@ -603,7 +640,7 @@
             vmem(tile, BF), vmem((MR, POS), F32), vmem((MR, POS), BF), vmem((MR, LANES), F32), vmem((CR, LANES), F32),
             vmem((2 * MR, 2 * CR), BF), vmem((CR, MR), BF), vmem((MR, CR), BF),
             vmem((GROUPS, MID, H, LANES), BF), vmem(tile, F32), vmem((2, COLS, 3, H, LANES), BF),
-            vmem((CR, LANES), F32), vmem((3, ROWS, H, LANES), F32),
+            vmem((CR, LANES), F32), vmem((2, CH, H, LANES), BF),
         ],
         copies=16,
     )
@@ -624,25 +661,28 @@
         total_kernel, [((ROWS, H, LANES), F32)], (arrived,), "total", flops=500_000_000
     )
     spread_sums = lax.all_to_all(sums, "row", 0, 0, tiled=True)
-    main, g_edge = call(
+    taps, _ = lax.optimization_barrier((taps, pieces))
+    g_edge, inputs, edge_value, edge_slope, block = call(
         spread_kernel,
-        [((CR, POS), F32), ((CR // 2, LANES), F32)],
-        (grad_inner, g_above, g_below, wb),
-        "spread", far=(0, 3), copies=2,
-        scratch=[vmem((2 * MR, 2 * LANES), BF), vmem((GROUPS, MID, H, LANES), BF), vmem((3 * CR, 2 * MR), BF)],
+        [((CR // 2, LANES), F32), (tile, BF), ((CR, LANES), F32), ((CR, LANES), F32), (tile, BF)],
+        (grad_inner, g_above, g_below, taps, half_sum, pair_map, block, edge_block),
+        "spread", far=(0, 4, 5, 6, 7), far_out=(1, 2, 3, 4), copies=2 * GROUPS + 7,
+        scratch=[
+            vmem((3 * CR, 2 * MR), BF), vmem((2 * MR, 2 * LANES), BF), vmem((GROUPS, MID, H, LANES), BF),
+            vmem(tile, F32), vmem(tile, BF), vmem(tile, BF), vmem((CR, LANES), F32), vmem(tile, BF),
+            vmem((CR, LANES), F32), vmem((CR, LANES), F32),
+        ],
     )
     g_left, g_right = both_ways(g_edge, g_edge, "col")
-    g_left, g_right, _ = lax.optimization_barrier((g_left, g_right, sums))
+    g_left, g_right, block, _ = lax.optimization_barrier((g_left, g_right, block, sums))
     (grad_input,) = call(
-        input_kernel, [(tile, BF)], (pair_map, half_sum, main, g_left, g_right), "grad_input",
-        far=(0, 1), far_out=(0,), scratch=[vmem(tile, BF), vmem(tile, F32), vmem(tile, BF)], copies=3 * GROUPS,
+        input_kernel, [(tile, BF)], (inputs, edge_value, edge_slope, g_left, g_right), "grad_input",
+        far=(0, 1, 2), far_out=(0,), copies=2 * GROUPS + 2,
+        scratch=[vmem(tile, BF), vmem(tile, BF), vmem((CR, LANES), F32), vmem((CR, LANES), F32)],
     )
     (symmetric,) = call(
-        symmetric_kernel, [(tile, BF)], (block, edge_block, arrived), "symmetric", far=(0, 1, 2), far_out=(0,),
-        scratch=[
-            vmem((CR, LANES), F32), vmem(tile, BF), vmem(cut, BF), vmem(tile, BF), vmem((3, ROWS, H, LANES), F32),
-        ],
-        copies=3 * GROUPS + 1,
+        symmetric_kernel, [(tile, BF)], (block, arrived), "symmetric", far=(0, 1), far_out=(0,),
+        scratch=[vmem(tile, BF), vmem(cut, BF), vmem(tile, BF)], copies=3 * GROUPS,
     )
     conv, mix = call(
         unpack_kernel, [((9, MID, CH), F32), ((MID, CH), F32)], (spread_sums,), "unpack", flops=100_000_000

time: 98.7 us -> 93.5 us (0.947)
  Pallas kernels: 43.7 us -> 40.5 us
  waiting for transfers between devices: 11.4 us -> 10 us
    pallas_call x12, Pallas kernels: 43.7 us -> 40.5 us  [call(): pl.pallas_call(kernel, name=name, out_shape=[pltpu.HBM(s, t) if i in far_...]
    all_to_all x1, waiting for transfers between devices: 11.3 us -> 8.82 us  [local(): lax.all_to_all(pieces.reshape(ROWS * COLS, 5, H, LANES), everyone, 0, 0,...]
  transfers between devices with their start and end apart: 11 -> 11, of which waited for: 1 -> 3; matrix products, arithmetic and copies ran while one was open for 0% -> 0% of each run, Pallas kernels for 34% -> 32%
where the time goes in v3:
time: 93.5 us; the launch traced here: 93 us
  starting transfers between devices  41.6 us (44%)
  Pallas kernels  40.5 us (43%)
  waiting for transfers between devices  10 us (11%)
    pallas_call x12, Pallas kernels, call(): pl.pallas_call(kernel, name=name, out_shape=[pltpu.HBM(s, t) if i in far_...  40.5 us
    ppermute x8, starting transfers between devices, both_ways(): return (lax.ppermute(first, axis, onward), lax.ppermute(second, axis, back))  16.9 us
    all_to_all x1, starting transfers between devices, local(): lax.all_to_all(d_pieces.reshape(ROWS * COLS, 3, H, LANES), everyone, 0, 0...  10.6 us
    all_to_all x1, waiting for transfers between devices, local(): lax.all_to_all(pieces.reshape(ROWS * COLS, 5, H, LANES), everyone, 0, 0,...  8.82 us
    all_to_all x1, starting transfers between devices, local(): lax.all_to_all(pieces.reshape(ROWS * COLS, 5, H, LANES), everyone, 0, 0,...  8.44 us
    all_to_all x1, starting transfers between devices, local(): spread_sums = lax.all_to_all(sums, 'row', 0, 0, tiled=True)  5.72 us
  transfers between devices with their start and end apart: 11, of which 3 were waited for; matrix products, arithmetic and copies ran while one was open for 0% of the time, Pallas kernels for 32%

profile of v3, /device:TPU:1, one launch (start us, length us, event | category | flops | bytes accessed | tf_op | source)
XLA Modules:
  0.0 93.0 jit_solution(12876609005060975029)
XLA Ops:
  0.6 0.0 copy-start.1
  0.6 2.2 %rows.1 = (bf16[8,24,8,128]{3,2,1,0:T(8,128)(2,1)}, bf16[8,24,8,128]{3,2,1,0:T(8,128)(2,1)S(1)}) custom-call(bf16[8,48,8,128]{3,2,1,0:T(8,128)(2,1)} %x_far.1), custom_call_target="tpu_custom_call" | custom-call | flops 4000000000 | bytes 1000000 | tf_op jit(solution)/shard_map/rows/pallas_call | solution.py:75
  2.9 2.8 %collective-permute-start = (bf16[8,24,8,128]{3,2,1,0:T(8,128)(2,1)}, bf16[8,24,8,128]{3,2,1,0:T(8,128)(2,1)S(1)}, u32[]{:S(2)}, u32[]{:S(2)}) collective-permute-start(bf16[8,24,8,128]{3,2,1,0:T(8,128)(2,1)} %get-tuple-element.45), channel_id=1, source_target_pairs={{0,8},{8,16},{16,24},{24,32},{32,40},{40,48},{48,56},{56,64},{64,7... | collective-permute-start | bytes 1179656 | tf_op jit(solution)/shard_map/ppermute | solution.py:575
  5.6 1.0 %turn_d.1 = bf16[16,8,3,8,128]{4,3,2,1,0:T(8,128)(2,1)} custom-call(bf16[8,48,8,128]{3,2,1,0:T(8,128)(2,1)S(1)} %copy-done.1), custom_call_target="tpu_custom_call" | custom-call | flops 4000000000 | bytes 1000000 | tf_op jit(solution)/shard_map/turn_d/pallas_call | solution.py:75
  6.7 0.0 copy-start.4
  6.7 10.6 %all-to-all-start = ((bf16[128,3,8,128]{3,2,1,0:T(8,128)(2,1)}), bf16[128,3,8,128]{3,2,1,0:T(8,128)(2,1)S(1)}, u32[]{:S(2)}, u32[]{:S(2)}) async-start(bf16[128,3,8,128]{3,2,1,0:T(8,128)(2,1)} %bitcast.19), calls=%async_computation | async-start | bytes 1572864 | tf_op jit(solution)/shard_map/all_to_all | solution.py:592
  17.3 2.0 %weights.1 = (bf16[576,768]{1,0:T(8,128)(2,1)S(1)}, bf16[384,192]{1,0:T(8,128)(2,1)S(1)}, bf16[576,768]{1,0:T(8,128)(2,1)}, bf16[384,192]{1,0:T(8,128)(2,1)}, bf16[192,384]{1,0:T(8,128)(2,1)}) custom-call(bf16[9,24,48]{2,1,0:T(8,128)(2,1)S(1)} %bitcast.15, bf16[24,48]{1,0:T(8,128)(2,1)S(1)} %bitcast.17), custom_call_target="tpu_custom_call" | custom-call | flops 4000000000 | bytes 1000000 | tf_op jit(solution)/shard_map/weights/pallas_call | solution.py:75
  19.3 2.5 %act.1 = (bf16[768,1024]{1,0:T(8,128)(2,1)S(1)}, bf16[384,128]{1,0:T(8,128)(2,1)S(1)}, bf16[768,1024]{1,0:T(8,128)(2,1)}) custom-call(bf16[8,48,8,128]{3,2,1,0:T(8,128)(2,1)S(1)} %copy-done.2, bf16[8,24,8,128]{3,2,1,0:T(8,128)(2,1)S(1)} %collective-permute-done.above, bf16[8,24,8,128]{3,2,1,0:T(8,128)(2,1)S(1)} %collective-permute-done.1.below), custom_call_target="tpu_custom_call" | custom-call | flops 4000000000 | bytes 1000000 | tf_op jit(solution)/shard_map/act/pallas_call | solution.py:75
  21.8 5.8 %collective-permute-start.3 = (bf16[384,128]{1,0:T(8,128)(2,1)S(1)}, bf16[384,128]{1,0:T(8,128)(2,1)S(1)}, u32[]{:S(2)}, u32[]{:S(2)}) collective-permute-start(bf16[384,128]{1,0:T(8,128)(2,1)S(1)} %get-tuple-element.54), channel_id=1, source_target_pairs={{1,0},{2,1},{3,2},{4,3},{5,4},{6,5},{7,6},{0,7},{9,8},{10,9},{11,1... | collective-permute-start | bytes 294920 | tf_op jit(solution)/shard_map/ppermute | solution.py:575
  27.6 6.9 %inside.1 = (f32[192,1024]{1,0:T(8,128)}, bf16[192,1024]{1,0:T(8,128)(2,1)}, bf16[8,48,8,128]{3,2,1,0:T(8,128)(2,1)}, bf16[16,8,5,8,128]{4,3,2,1,0:T(8,128)(2,1)...) custom-call(bf16[8,48,8,128]{3,2,1,0:T(8,128)(2,1)S(1)} %copy-done.2, bf16[768,1024]{1,0:T(8,128)(2,1)S(1)} %get-tuple-element.47.act, ...), custom_call_target="tpu_custom_call" | custom-call | flops 4000000000 | bytes 1000000 | tf_op jit(solution)/shard_map/inside/pallas_call | solution.py:75
  34.6 0.6 collective-permute-done.2.from_left
  35.2 7.5 %inner.1 = (bf16[8,24,8,128]{3,2,1,0:T(8,128)(2,1)}, bf16[8,12,8,128]{3,2,1,0:T(8,128)(2,1)S(1)}, bf16[8,12,8,128]{3,2,1,0:T(8,128)(2,1)S(1)}, f32[8,48,8,128]{3...) custom-call(bf16[8,48,8,128]{3,2,1,0:T(8,128)(2,1)} %d_far.1, ...), custom_call_target="tpu_custom_call", output_to_operand_aliasing={{4}: (11, {})} | custom-call | flops 4000000000 | bytes 1000000 | tf_op jit(solution)/shard_map/inner/pallas_call | solution.py:75
  42.7 2.6 %collective-permute-start.4 = (bf16[8,12,8,128]{3,2,1,0:T(8,128)(2,1)S(1)}, bf16[8,12,8,128]{3,2,1,0:T(8,128)(2,1)S(1)}, u32[]{:S(2)}, u32[]{:S(2)}) collective-permute-start(bf16[8,12,8,128]{3,2,1,0:T(8,128)(2,1)S(1)} %get-tuple-element.67), channel_id=1, source_target_pairs={{0,8},{8,16},{16,24},{24,32},{32,40},{40,48},{48,56},{56,64},{64,7... | collective-permute-start | bytes 589832 | tf_op jit(solution)/shard_map/ppermute | solution.py:575
  45.3 5.8 %sums.1 = bf16[16,8,5,8,128]{4,3,2,1,0:T(8,128)(2,1)} custom-call(bf16[768,1024]{1,0:T(8,128)(2,1)} %get-tuple-element.60.act_far, bf16[384,1024]{1,0:T(8,128)(2,1)S(1)} %get-tuple-element.61.gmi, bf16[576,1024]{1,0:T(8,128)(2,1)S(1)} %get-tuple-element.62.shifted, bf16[576,128]{1,0:T(8,128)(2,1)S(1)} %get-tuple-element.63.edge_rows, ...), custom_call_target="tpu_custom_call", output_to_operand_aliasing={{}: (6, {})} | custom-call | flops 4000000000 | bytes 1000000 | tf_op jit(solution)/shard_map/sums/pallas_call | solution.py:75
  51.1 8.4 %all-to-all-start.1 = ((bf16[128,5,8,128]{3,2,1,0:T(8,128)(2,1)}), bf16[128,5,8,128]{3,2,1,0:T(8,128)(2,1)S(1)}, u32[]{:S(2)}, u32[]{:S(2)}) async-start(bf16[128,5,8,128]{3,2,1,0:T(8,128)(2,1)} %bitcast.18), calls=%async_computation.1 | async-start | bytes 2621440 | tf_op jit(solution)/shard_map/all_to_all | solution.py:658
  59.6 5.7 %spread.1 = (f32[192,128]{1,0:T(8,128)S(1)}, bf16[8,48,8,128]{3,2,1,0:T(8,128)(2,1)}, f32[384,128]{1,0:T(8,128)}, f32[384,128]{1,0:T(8,128)}, bf16[8,48,8,128]{3,2,1,0:T(8,128)(2,1)}) custom-call(bf16[8,24,8,128]{3,2,1,0:T(8,128)(2,1)} %get-tuple-element.59.grad_inner_far, bf16[8,12,8,128]{3,2,1,0:T(8,128)(2,1)S(1)} %collective-permute-done.4.above, ...), custom_call_target="tpu_custom_call" | custom-call | flops 4000000000 | bytes 1000000 | tf_op jit(solution)/shard_map/spread/pallas_call | solution.py:75
  65.3 5.8 %collective-permute-start.7 = (f32[192,128]{1,0:T(8,128)S(1)}, f32[192,128]{1,0:T(8,128)S(1)}, u32[]{:S(2)}, u32[]{:S(2)}) collective-permute-start(f32[192,128]{1,0:T(8,128)S(1)} %get-tuple-element.76), channel_id=1, source_target_pairs={{1,0},{2,1},{3,2},{4,3},{5,4},{6,5},{7,6},{0,7},{9,8},{10,9},{11,1... | collective-permute-start | bytes 294920 | tf_op jit(solution)/shard_map/ppermute | solution.py:575
  71.1 8.8 %all-to-all-done.1 = bf16[128,5,8,128]{3,2,1,0:T(8,128)(2,1)S(1)} async-done(((bf16[128,5,8,128]{3,2,1,0:T(8,128)(2,1)}), bf16[128,5,8,128]{3,2,1,0:T(8,128)(2,1)S(1)}, u32[]{:S(2)}, u32[]{:S(2)}) %all-to-all-start.1) | async-done | bytes 1310752 | tf_op jit(solution)/shard_map/all_to_all | solution.py:658
  79.9 0.8 total.1
  80.7 5.7 %all-to-all-start.2 = ((f32[16,8,128]{2,1,0:T(8,128)}), f32[16,8,128]{2,1,0:T(8,128)S(1)}, u32[]{:S(2)}, u32[]{:S(2)}) async-start(f32[16,8,128]{2,1,0:T(8,128)} %total.1), calls=%async_computation.2 | async-start | bytes 131072 | tf_op jit(solution)/shard_map/all_to_all | solution.py:663
  86.5 2.6 %symmetric.1 = bf16[8,48,8,128]{3,2,1,0:T(8,128)(2,1)} custom-call(bf16[8,48,8,128]{3,2,1,0:T(8,128)(2,1)} %get-tuple-element.78.block_far, bf16[16,8,5,8,128]{4,3,2,1,0:T(8,128)(2,1)} %bitcast.13), custom_call_target="tpu_custom_call" | custom-call | flops 4000000000 | bytes 1000000 | tf_op jit(solution)/shard_map/symmetric/pallas_call | solution.py:75
  89.1 2.6 %grad_input.1 = bf16[8,48,8,128]{3,2,1,0:T(8,128)(2,1)} custom-call(bf16[8,48,8,128]{3,2,1,0:T(8,128)(2,1)} %get-tuple-element.79.value_far, f32[384,128]{1,0:T(8,128)} %get-tuple-element.80.edge_value_far, f32[384,128]{1,0:T(8,128)} %get-tuple-element.81.edge_slope_far, f32[192,128]{1,0:T(8,128)S(1)} %collective-permute-done.6.from_left, ...), custom_call_target="tpu_custom_call" | custom-call | flops 4000000000 | bytes 1000000 | tf_op jit(solution)/shard_map/grad_input/pallas_call | solution.py:75
  91.7 0.6 all-to-all-done.2.tiles
  92.3 0.7 unpack.1
  (28 shorter events, 0.1 us)
Async XLA Ops:
  0.6 5.0 %copy-start.1 = (bf16[8,48,8,128]{3,2,1,0:T(8,128)(2,1)S(1)}, bf16[8,48,8,128]{3,2,1,0:T(8,128)(2,1)}, u32[]{:S(2)}) copy-start(bf16[8,48,8,128]{3,2,1,0:T(8,128)(2,1)} %d_far.1) | copy-start | bytes 2359300
  2.9 16.4 %collective-permute-start = (bf16[8,24,8,128]{3,2,1,0:T(8,128)(2,1)}, bf16[8,24,8,128]{3,2,1,0:T(8,128)(2,1)S(1)}, u32[]{:S(2)}, u32[]{:S(2)}) collective-permute-start(bf16[8,24,8,128]{3,2,1,0:T(8,128)(2,1)} %get-tuple-element.45), channel_id=1, source_target_pairs={{0,8},{8,16},{16,24},{24,32},{32,40},{40,48},{48,56},{56,64},{64,7... | collective-permute-start | bytes 1179656 | tf_op jit(solution)/shard_map/ppermute | solution.py:575
  5.6 13.7 %collective-permute-start.1 = (bf16[8,24,8,128]{3,2,1,0:T(8,128)(2,1)S(1)}, bf16[8,24,8,128]{3,2,1,0:T(8,128)(2,1)S(1)}, u32[]{:S(2)}, u32[]{:S(2)}) collective-permute-start(bf16[8,24,8,128]{3,2,1,0:T(8,128)(2,1)S(1)} %get-tuple-element.46), channel_id=1, source_target_pairs={{8,0},{16,8},{24,16},{32,24},{40,32},{48,40},{56,48},{64,56},{72,6... | collective-permute-start | bytes 1179656 | tf_op jit(solution)/shard_map/ppermute | solution.py:575
  6.7 10.6 %copy-start.3 = (bf16[24,48,3,3]{1,0,3,2:T(8,128)(2,1)S(1)}, bf16[24,48,3,3]{1,0,3,2:T(8,128)(2,1)}, u32[]{:S(2)}) copy-start(bf16[24,48,3,3]{1,0,3,2:T(8,128)(2,1)} %param.10) | copy-start | bytes 62212
  6.7 10.6 %copy-start.4 = (bf16[48,24]{0,1:T(8,128)(2,1)S(1)}, bf16[48,24]{0,1:T(8,128)(2,1)}, u32[]{:S(2)}) copy-start(bf16[48,24]{0,1:T(8,128)(2,1)} %param.13) | copy-start | bytes 6916
  6.7 28.5 %all-to-all-start = ((bf16[128,3,8,128]{3,2,1,0:T(8,128)(2,1)}), bf16[128,3,8,128]{3,2,1,0:T(8,128)(2,1)S(1)}, u32[]{:S(2)}, u32[]{:S(2)}) async-start(bf16[128,3,8,128]{3,2,1,0:T(8,128)(2,1)} %bitcast.19), calls=%async_computation | async-start | bytes 1572864 | tf_op jit(solution)/shard_map/all_to_all | solution.py:592
  17.3 2.1 %copy-start.2 = (bf16[8,48,8,128]{3,2,1,0:T(8,128)(2,1)S(1)}, bf16[8,48,8,128]{3,2,1,0:T(8,128)(2,1)}, u32[]{:S(2)}) copy-start(bf16[8,48,8,128]{3,2,1,0:T(8,128)(2,1)} %x_far.1) | copy-start | bytes 2359300
  19.3 8.3 %copy-start.5 = (f32[24]{0:T(128)S(1)}, f32[24]{0:T(128)}, u32[]{:S(2)}) copy-start(f32[24]{0:T(128)} %cg.3) | copy-start | bytes 292
  19.3 8.3 %copy-start.6 = (f32[24]{0:T(128)S(1)}, f32[24]{0:T(128)}, u32[]{:S(2)}) copy-start(f32[24]{0:T(128)} %cb.3) | copy-start | bytes 292
  19.3 8.3 %copy-start.7 = (f32[48]{0:T(128)S(1)}, f32[48]{0:T(128)}, u32[]{:S(2)}) copy-start(f32[48]{0:T(128)} %mg.3) | copy-start | bytes 580
  19.3 8.3 %copy-start.8 = (f32[48]{0:T(128)S(1)}, f32[48]{0:T(128)}, u32[]{:S(2)}) copy-start(f32[48]{0:T(128)} %mb.3) | copy-start | bytes 580
  21.8 12.7 %collective-permute-start.3 = (bf16[384,128]{1,0:T(8,128)(2,1)S(1)}, bf16[384,128]{1,0:T(8,128)(2,1)S(1)}, u32[]{:S(2)}, u32[]{:S(2)}) collective-permute-start(bf16[384,128]{1,0:T(8,128)(2,1)S(1)} %get-tuple-element.54), channel_id=1, source_target_pairs={{1,0},{2,1},{3,2},{4,3},{5,4},{6,5},{7,6},{0,7},{9,8},{10,9},{11,1... | collective-permute-start | bytes 294920 | tf_op jit(solution)/shard_map/ppermute | solution.py:575
  27.6 7.6 %collective-permute-start.2 = (bf16[384,128]{1,0:T(8,128)(2,1)S(1)}, bf16[384,128]{1,0:T(8,128)(2,1)S(1)}, u32[]{:S(2)}, u32[]{:S(2)}) collective-permute-start(bf16[384,128]{1,0:T(8,128)(2,1)S(1)} %get-tuple-element.54), channel_id=1, source_target_pairs={{0,1},{1,2},{2,3},{3,4},{4,5},{5,6},{6,7},{7,0},{8,9},{9,10},{10,1... | collective-permute-start | bytes 294920 | tf_op jit(solution)/shard_map/ppermute | solution.py:575
  42.7 8.4 %collective-permute-start.4 = (bf16[8,12,8,128]{3,2,1,0:T(8,128)(2,1)S(1)}, bf16[8,12,8,128]{3,2,1,0:T(8,128)(2,1)S(1)}, u32[]{:S(2)}, u32[]{:S(2)}) collective-permute-start(bf16[8,12,8,128]{3,2,1,0:T(8,128)(2,1)S(1)} %get-tuple-element.67), channel_id=1, source_target_pairs={{0,8},{8,16},{16,24},{24,32},{32,40},{40,48},{48,56},{56,64},{64,7... | collective-permute-start | bytes 589832 | tf_op jit(solution)/shard_map/ppermute | solution.py:575
  45.3 5.8 %collective-permute-start.5 = (bf16[8,12,8,128]{3,2,1,0:T(8,128)(2,1)S(1)}, bf16[8,12,8,128]{3,2,1,0:T(8,128)(2,1)S(1)}, u32[]{:S(2)}, u32[]{:S(2)}) collective-permute-start(bf16[8,12,8,128]{3,2,1,0:T(8,128)(2,1)S(1)} %get-tuple-element.68), channel_id=1, source_target_pairs={{8,0},{16,8},{24,16},{32,24},{40,32},{48,40},{56,48},{64,56},{72,6... | collective-permute-start | bytes 589832 | tf_op jit(solution)/shard_map/ppermute | solution.py:575
  51.1 28.8 %all-to-all-start.1 = ((bf16[128,5,8,128]{3,2,1,0:T(8,128)(2,1)}), bf16[128,5,8,128]{3,2,1,0:T(8,128)(2,1)S(1)}, u32[]{:S(2)}, u32[]{:S(2)}) async-start(bf16[128,5,8,128]{3,2,1,0:T(8,128)(2,1)} %bitcast.18), calls=%async_computation.1 | async-start | bytes 2621440 | tf_op jit(solution)/shard_map/all_to_all | solution.py:658
  65.3 21.1 %collective-permute-start.7 = (f32[192,128]{1,0:T(8,128)S(1)}, f32[192,128]{1,0:T(8,128)S(1)}, u32[]{:S(2)}, u32[]{:S(2)}) collective-permute-start(f32[192,128]{1,0:T(8,128)S(1)} %get-tuple-element.76), channel_id=1, source_target_pairs={{1,0},{2,1},{3,2},{4,3},{5,4},{6,5},{7,6},{0,7},{9,8},{10,9},{11,1... | collective-permute-start | bytes 294920 | tf_op jit(solution)/shard_map/ppermute | solution.py:575
  71.1 15.4 %collective-permute-start.6 = (f32[192,128]{1,0:T(8,128)S(1)}, f32[192,128]{1,0:T(8,128)S(1)}, u32[]{:S(2)}, u32[]{:S(2)}) collective-permute-start(f32[192,128]{1,0:T(8,128)S(1)} %get-tuple-element.76), channel_id=1, source_target_pairs={{0,1},{1,2},{2,3},{3,4},{4,5},{5,6},{6,7},{7,0},{8,9},{9,10},{10,1... | collective-permute-start | bytes 294920 | tf_op jit(solution)/shard_map/ppermute | solution.py:575
  79.9 6.6 %copy-start = (bf16[128,5,8,128]{3,2,1,0:T(8,128)(2,1)}, bf16[128,5,8,128]{3,2,1,0:T(8,128)(2,1)S(1)}, u32[]{:S(2)}) copy-start(bf16[128,5,8,128]{3,2,1,0:T(8,128)(2,1)S(1)} %all-to-all-done.1) | copy-start | bytes 3932164
  80.7 11.5 %all-to-all-start.2 = ((f32[16,8,128]{2,1,0:T(8,128)}), f32[16,8,128]{2,1,0:T(8,128)S(1)}, u32[]{:S(2)}, u32[]{:S(2)}) async-start(f32[16,8,128]{2,1,0:T(8,128)} %total.1), calls=%async_computation.2 | async-start | bytes 131072 | tf_op jit(solution)/shard_map/all_to_all | solution.py:663

commit v4 on v3

--- a/solution.py
+++ b/solution.py
@@ -121,14 +121,6 @@
         up[g] = jnp.where(after < GROUPS, first, 0.0).astype(BF)
 
 
-def rows_kernel(x, down, up, held, sems):
-    far = Far(sems)
-    loads = [far.start(x.at[g], held.at[g]) for g in range(GROUPS)]
-    for load in loads:
-        load.wait()
-    send_rows(held, down, up, CH)
-
-
 def swap_blocks(parts):
     lane = iota(parts[0].shape, 1)
     parts = list(parts)
@@ -168,9 +160,15 @@
         pieces[r, g : g + 2] = parts[r].reshape(2, 3, H, LANES)
 
 
-def mirror_kernel(d, pieces, turned, sems):
-    far = Far(sems)
+def first_kernel(x_far, d_far, down, up, pieces, x, d, turned, sems):
+    far = Far(sems)
+    loads = [far.start(x_far.at[g], x.at[g]) for g in range(GROUPS)]
+    later = [far.start(d_far.at[g], d.at[g]) for g in range(GROUPS)]
+    for load in loads:
+        load.wait()
+    send_rows(x, down, up, CH)
     for g in range(GROUPS):
+        later[g].wait()
         for k in range(3):
             turned[:, g, k] = turn(d[g, k * ROWS : (k + 1) * ROWS])
         far.send(turned.at[:, g], pieces.at[:, g])
@@ -320,18 +318,28 @@
     d, slope, hidden, edge_inner, edge_x, weights, mixer, back, grad_inner, half_sum, ends, edge_block, buffer, sems,
 ):
     far = Far(sems)
+    loads = [far.start(d_far.at[2 * p : 2 * p + 2], d.at[2 * p : 2 * p + 2]) for p in range(GROUPS // 2)]
     first = [far.start(weights_far.at[0:MR], weights.at[0:MR])]
     first.append(far.start(weights_far.at[2 * MR : 3 * MR], weights.at[MR : 2 * MR]))
     first += [far.start(edge_inner_far, edge_inner), far.start(edge_x_far, edge_x), far.start(mixer_far, mixer)]
-    later = [far.start(d_far, d), far.start(slope_far, slope), far.start(back_far, back), far.start(hidden_far, hidden)]
     tails = [
         far.start(pieces_in.at[r, :, 2:5], ends.at[i]) for i, r in enumerate((0, ROWS - 1))
     ]
+    later = [far.start(back_far, back), far.start(slope_far, slope), far.start(hidden_far, hidden)]
     lane, lane_c = lanes_of(MR), lanes_of(CR)
     gain, shift = splat(cg, MID), splat(cb, MID)
     gain_out, shift_out = splat(mg, CH), splat(mb, CH)
     rim = merge_edges(from_left[...].astype(F32), from_right[...].astype(F32)).astype(BF)
     rim_out[...] = rim
+    for pair in range(GROUPS // 2):
+        loads[pair].wait()
+        swap_in(arrived, 2 * pair, buffer)
+        for half in range(2):
+            g = 2 * pair + half
+            both = 0.5 * (d[g].astype(F32) + buffer[half].astype(F32)).reshape(CR, LANES)
+            half_sum[g] = both.reshape(CH, H, LANES)
+            gmi[:, g * LANES : (g + 1) * LANES] = (both * gain_out).astype(BF)
+        far.send(half_sum.at[2 * pair : 2 * pair + 2], half_sum_far.at[2 * pair : 2 * pair + 2])
     for load in first:
         load.wait()
     outer = dot(weights[:, 0:CR], rim) + pltpu.roll(dot(weights[:, CR : 2 * CR], rim), 64, 1)
@@ -362,12 +370,6 @@
     packed = jnp.zeros((MR, LANES), F32)
     for pair in range(GROUPS // 2):
         two = slice(pair * 2 * LANES, (pair + 1) * 2 * LANES)
-        swap_in(arrived, 2 * pair, buffer)
-        for half in range(2):
-            g = 2 * pair + half
-            both = 0.5 * (d[g].astype(F32) + buffer[half].astype(F32)).reshape(CR, LANES)
-            half_sum[g] = both.reshape(CH, H, LANES)
-            gmi[:, g * LANES : (g + 1) * LANES] = (both * gain_out).astype(BF)
         into = dot(back[...], gmi[:, two])
         for half in range(2):
             g = 2 * pair + half
@@ -382,8 +384,7 @@
             packed = jnp.where(lane // 8 == g, pltpu.roll(value, (8 * g - 124) % LANES, 1), packed)
             here = jnp.where(at_edge(lane), pltpu.roll(hidden_edge, turn, 1), hidden[:, at].astype(F32))
             hidden_out[:, at] = here.astype(BF)
-    far.send(grad_inner, grad_inner_far)
-    far.send(half_sum, half_sum_far)
+        far.send(grad_inner.at[2 * pair : 2 * pair + 2], grad_inner_far.at[2 * pair : 2 * pair + 2])
     send_rows(grad_inner, down, up, MID)
     packed = packed + pltpu.roll(packed, 64, 1)
     edge_rows[0:MR] = jnp.where(lane % 8 >= 4, packed, 0.0).astype(BF)
@@ -397,6 +398,8 @@
 ):
     far = Far(sems)
     loads = [far.start(act_far.at[k * CR : (k + 1) * CR], act.at[k * CR : (k + 1) * CR]) for k in range(2)]
+    sums_out[ROWS - 1] = jnp.zeros((COLS, 2, H, LANES), BF)
+    far.send(sums_out.at[ROWS - 1], pieces_far.at[ROWS - 1, :, 0:2])
     lane_c = lanes_of(CR)
     rim_value = rim[...].astype(F32)
     rim_own = jnp.where(lane_c < 64, rim_value, 0.0).astype(BF)
@@ -453,8 +456,7 @@
             rows = slice(k * H, (k + 1) * H)
             sums_out[r, :, 0] = jnp.broadcast_to(high[rows][None], (COLS, H, LANES)).astype(BF)
             sums_out[r, :, 1] = jnp.broadcast_to(low[rows][None], (COLS, H, LANES)).astype(BF)
-    sums_out[ROWS - 1] = jnp.zeros((COLS, 2, H, LANES), BF)
-    far.send(sums_out, pieces_far.at[:, :, 0:2])
+        far.send(sums_out.at[3 * p : 3 * p + 3], pieces_far.at[3 * p : 3 * p + 3, :, 0:2])
     far.finish()
 
 
@@ -580,15 +582,11 @@
     cut = (ROWS, COLS, 3, H, LANES)
     everyone = ("row", "col")
     vmem = pltpu.VMEM
-    down, up = call(
-        rows_kernel, [((GROUPS, CH // 2, H, LANES), BF)] * 2, (pair_map,), "rows",
-        far=(0,), scratch=[vmem(tile, BF)], copies=GROUPS,
+    down, up, d_pieces = call(
+        first_kernel, [((GROUPS, CH // 2, H, LANES), BF)] * 2 + [(cut, BF)], (pair_map, cotangent), "first",
+        far=(0, 1), far_out=(2,), scratch=[vmem(tile, BF), vmem(tile, BF), vmem(cut, BF)], copies=3 * GROUPS,
     )
     above, below = both_ways(down, up, "row")
-    (d_pieces,) = call(
-        mirror_kernel, [(cut, BF)], (cotangent,), "turn_d",
-        far_out=(0,), scratch=[vmem(cut, BF)], copies=GROUPS,
-    )
     d_arrived = lax.all_to_all(d_pieces.reshape(ROWS * COLS, 3, H, LANES), everyone, 0, 0, tiled=True)
     d_arrived = d_arrived.reshape(cut)
 
@@ -642,7 +640,7 @@
             vmem((GROUPS, MID, H, LANES), BF), vmem(tile, F32), vmem((2, COLS, 3, H, LANES), BF),
             vmem((CR, LANES), F32), vmem((2, CH, H, LANES), BF),
         ],
-        copies=16,
+        copies=25,
     )
     g_above, g_below = both_ways(g_down, g_up, "row")
     (pieces,) = call(
@@ -652,7 +650,7 @@
             vmem((2 * CR, POS), BF), vmem((ROWS, COLS, 2, H, LANES), BF),
             vmem((3 * MR, 2 * CR), F32), vmem((MR, CR), F32),
         ],
-        copies=3,
+        copies=8,
     )
     pieces, g_above, g_below = lax.optimization_barrier((pieces, g_above, g_below))
     arrived = lax.all_to_all(pieces.reshape(ROWS * COLS, 5, H, LANES), everyone, 0, 0, tiled=True)

time: 93.5 us -> 92.2 us (0.986)
  Pallas kernels: 40.5 us -> 39.1 us
    pallas_call x12 -> x11, Pallas kernels: 40.5 us -> 39.1 us  [call(): pl.pallas_call(kernel, name=name, out_shape=[pltpu.HBM(s, t) if i in far_...]
  transfers between devices with their start and end apart: 11 -> 11, of which waited for: 3 -> 3; matrix products, arithmetic and copies ran while one was open for 0% -> 0% of each run, Pallas kernels for 32% -> 31%
where the time goes in v4:
time: 92.2 us; the launch traced here: 91.8 us
  starting transfers between devices  41.8 us (45%)
  Pallas kernels  39.1 us (42%)
  waiting for transfers between devices  9.98 us (11%)
    pallas_call x11, Pallas kernels, call(): pl.pallas_call(kernel, name=name, out_shape=[pltpu.HBM(s, t) if i in far_...  39.1 us
    ppermute x8, starting transfers between devices, both_ways(): return (lax.ppermute(first, axis, onward), lax.ppermute(second, axis, back))  16.9 us
    all_to_all x1, starting transfers between devices, local(): lax.all_to_all(d_pieces.reshape(ROWS * COLS, 3, H, LANES), everyone, 0, 0...  10.6 us
    all_to_all x1, waiting for transfers between devices, local(): lax.all_to_all(pieces.reshape(ROWS * COLS, 5, H, LANES), everyone, 0, 0,...  8.83 us
    all_to_all x1, starting transfers between devices, local(): lax.all_to_all(pieces.reshape(ROWS * COLS, 5, H, LANES), everyone, 0, 0,...  8.59 us
    all_to_all x1, starting transfers between devices, local(): spread_sums = lax.all_to_all(sums, 'row', 0, 0, tiled=True)  5.72 us
  transfers between devices with their start and end apart: 11, of which 3 were waited for; matrix products, arithmetic and copies ran while one was open for 0% of the time, Pallas kernels for 31%

profile of v4, /device:TPU:1, one launch (start us, length us, event | category | flops | bytes accessed | tf_op | source)
XLA Modules:
  0.0 91.8 jit_solution(10245887436244516583)
XLA Ops:
  0.6 3.0 %first.1 = (bf16[8,24,8,128]{3,2,1,0:T(8,128)(2,1)S(1)}, bf16[8,24,8,128]{3,2,1,0:T(8,128)(2,1)S(1)}, bf16[16,8,3,8,128]{4,3,2,1,0:T(8,128)(2,1)}) custom-call(bf16[8,48,8,128]{3,2,1,0:T(8,128)(2,1)} %x_far.3, bf16[8,48,8,128]{3,2,1,0:T(8,128)(2,1)} %d_far.3), custom_call_target="tpu_custom_call" | custom-call | flops 4000000000 | bytes 1000000 | tf_op jit(solution)/shard_map/first/pallas_call | solution.py:75
  3.7 0.0 copy-start.2
  3.7 2.8 %collective-permute-start = (bf16[8,24,8,128]{3,2,1,0:T(8,128)(2,1)S(1)}, bf16[8,24,8,128]{3,2,1,0:T(8,128)(2,1)S(1)}, u32[]{:S(2)}, u32[]{:S(2)}) collective-permute-start(bf16[8,24,8,128]{3,2,1,0:T(8,128)(2,1)S(1)} %get-tuple-element.47), channel_id=1, source_target_pairs={{0,8},{8,16},{16,24},{24,32},{32,40},{40,48},{48,56},{56,64},{64,7... | collective-permute-start | bytes 1179656 | tf_op jit(solution)/shard_map/ppermute | solution.py:577
  6.4 10.6 %all-to-all-start = ((bf16[128,3,8,128]{3,2,1,0:T(8,128)(2,1)}), bf16[128,3,8,128]{3,2,1,0:T(8,128)(2,1)S(1)}, u32[]{:S(2)}, u32[]{:S(2)}) async-start(bf16[128,3,8,128]{3,2,1,0:T(8,128)(2,1)} %bitcast.19), calls=%async_computation | async-start | bytes 1572864 | tf_op jit(solution)/shard_map/all_to_all | solution.py:590
  17.0 2.0 %weights.1 = (bf16[576,768]{1,0:T(8,128)(2,1)S(1)}, bf16[384,192]{1,0:T(8,128)(2,1)S(1)}, bf16[576,768]{1,0:T(8,128)(2,1)}, bf16[384,192]{1,0:T(8,128)(2,1)}, bf16[192,384]{1,0:T(8,128)(2,1)}) custom-call(bf16[9,24,48]{2,1,0:T(8,128)(2,1)S(1)} %bitcast.15, bf16[24,48]{1,0:T(8,128)(2,1)S(1)} %bitcast.17), custom_call_target="tpu_custom_call" | custom-call | flops 4000000000 | bytes 1000000 | tf_op jit(solution)/shard_map/weights/pallas_call | solution.py:75
  19.0 0.0 copy-start.4
  19.0 0.0 copy-start.5
  19.1 2.5 %act.1 = (bf16[768,1024]{1,0:T(8,128)(2,1)S(1)}, bf16[384,128]{1,0:T(8,128)(2,1)S(1)}, bf16[768,1024]{1,0:T(8,128)(2,1)}) custom-call(bf16[8,48,8,128]{3,2,1,0:T(8,128)(2,1)S(1)} %copy-done.1, bf16[8,24,8,128]{3,2,1,0:T(8,128)(2,1)S(1)} %collective-permute-done.above, bf16[8,24,8,128]{3,2,1,0:T(8,128)(2,1)S(1)} %collective-permute-done.1.below), custom_call_target="tpu_custom_call" | custom-call | flops 4000000000 | bytes 1000000 | tf_op jit(solution)/shard_map/act/pallas_call | solution.py:75
  21.6 5.8 %collective-permute-start.3 = (bf16[384,128]{1,0:T(8,128)(2,1)S(1)}, bf16[384,128]{1,0:T(8,128)(2,1)S(1)}, u32[]{:S(2)}, u32[]{:S(2)}) collective-permute-start(bf16[384,128]{1,0:T(8,128)(2,1)S(1)} %get-tuple-element.56), channel_id=1, source_target_pairs={{1,0},{2,1},{3,2},{4,3},{5,4},{6,5},{7,6},{0,7},{9,8},{10,9},{11,1... | collective-permute-start | bytes 294920 | tf_op jit(solution)/shard_map/ppermute | solution.py:577
  27.4 6.9 %inside.1 = (f32[192,1024]{1,0:T(8,128)}, bf16[192,1024]{1,0:T(8,128)(2,1)}, bf16[8,48,8,128]{3,2,1,0:T(8,128)(2,1)}, bf16[16,8,5,8,128]{4,3,2,1,0:T(8,128)(2,1)...) custom-call(bf16[8,48,8,128]{3,2,1,0:T(8,128)(2,1)S(1)} %copy-done.1, bf16[768,1024]{1,0:T(8,128)(2,1)S(1)} %get-tuple-element.49.act, ...), custom_call_target="tpu_custom_call" | custom-call | flops 4000000000 | bytes 1000000 | tf_op jit(solution)/shard_map/inside/pallas_call | solution.py:75
  34.4 0.6 collective-permute-done.2.from_left
  34.9 6.5 %inner.1 = (bf16[8,24,8,128]{3,2,1,0:T(8,128)(2,1)}, bf16[8,12,8,128]{3,2,1,0:T(8,128)(2,1)S(1)}, bf16[8,12,8,128]{3,2,1,0:T(8,128)(2,1)S(1)}, f32[8,48,8,128]{3...) custom-call(bf16[8,48,8,128]{3,2,1,0:T(8,128)(2,1)} %d_far.3, ...), custom_call_target="tpu_custom_call", output_to_operand_aliasing={{4}: (11, {})} | custom-call | flops 4000000000 | bytes 1000000 | tf_op jit(solution)/shard_map/inner/pallas_call | solution.py:75
  41.4 2.6 %collective-permute-start.4 = (bf16[8,12,8,128]{3,2,1,0:T(8,128)(2,1)S(1)}, bf16[8,12,8,128]{3,2,1,0:T(8,128)(2,1)S(1)}, u32[]{:S(2)}, u32[]{:S(2)}) collective-permute-start(bf16[8,12,8,128]{3,2,1,0:T(8,128)(2,1)S(1)} %get-tuple-element.69), channel_id=1, source_target_pairs={{0,8},{8,16},{16,24},{24,32},{32,40},{40,48},{48,56},{56,64},{64,7... | collective-permute-start | bytes 589832 | tf_op jit(solution)/shard_map/ppermute | solution.py:577
  44.0 5.7 %sums.1 = bf16[16,8,5,8,128]{4,3,2,1,0:T(8,128)(2,1)} custom-call(bf16[768,1024]{1,0:T(8,128)(2,1)} %get-tuple-element.62.act_far, bf16[384,1024]{1,0:T(8,128)(2,1)S(1)} %get-tuple-element.63.gmi, bf16[576,1024]{1,0:T(8,128)(2,1)S(1)} %get-tuple-element.64.shifted, bf16[576,128]{1,0:T(8,128)(2,1)S(1)} %get-tuple-element.65.edge_rows, ...), custom_call_target="tpu_custom_call", output_to_operand_aliasing={{}: (6, {})} | custom-call | flops 4000000000 | bytes 1000000 | tf_op jit(solution)/shard_map/sums/pallas_call | solution.py:75
  49.7 8.6 %all-to-all-start.1 = ((bf16[128,5,8,128]{3,2,1,0:T(8,128)(2,1)}), bf16[128,5,8,128]{3,2,1,0:T(8,128)(2,1)S(1)}, u32[]{:S(2)}, u32[]{:S(2)}) async-start(bf16[128,5,8,128]{3,2,1,0:T(8,128)(2,1)} %bitcast.18), calls=%async_computation.1 | async-start | bytes 2621440 | tf_op jit(solution)/shard_map/all_to_all | solution.py:656
  58.3 5.7 %spread.1 = (f32[192,128]{1,0:T(8,128)S(1)}, bf16[8,48,8,128]{3,2,1,0:T(8,128)(2,1)}, f32[384,128]{1,0:T(8,128)}, f32[384,128]{1,0:T(8,128)}, bf16[8,48,8,128]{3,2,1,0:T(8,128)(2,1)}) custom-call(bf16[8,24,8,128]{3,2,1,0:T(8,128)(2,1)} %get-tuple-element.61.grad_inner_far, bf16[8,12,8,128]{3,2,1,0:T(8,128)(2,1)S(1)} %collective-permute-done.4.above, ...), custom_call_target="tpu_custom_call" | custom-call | flops 4000000000 | bytes 1000000 | tf_op jit(solution)/shard_map/spread/pallas_call | solution.py:75
  64.0 5.8 %collective-permute-start.7 = (f32[192,128]{1,0:T(8,128)S(1)}, f32[192,128]{1,0:T(8,128)S(1)}, u32[]{:S(2)}, u32[]{:S(2)}) collective-permute-start(f32[192,128]{1,0:T(8,128)S(1)} %get-tuple-element.78), channel_id=1, source_target_pairs={{1,0},{2,1},{3,2},{4,3},{5,4},{6,5},{7,6},{0,7},{9,8},{10,9},{11,1... | collective-permute-start | bytes 294920 | tf_op jit(solution)/shard_map/ppermute | solution.py:577
  69.8 8.8 %all-to-all-done.1 = bf16[128,5,8,128]{3,2,1,0:T(8,128)(2,1)S(1)} async-done(((bf16[128,5,8,128]{3,2,1,0:T(8,128)(2,1)}), bf16[128,5,8,128]{3,2,1,0:T(8,128)(2,1)S(1)}, u32[]{:S(2)}, u32[]{:S(2)}) %all-to-all-start.1) | async-done | bytes 1310752 | tf_op jit(solution)/shard_map/all_to_all | solution.py:656
  78.6 0.8 total.1
  79.5 5.7 %all-to-all-start.2 = ((f32[16,8,128]{2,1,0:T(8,128)}), f32[16,8,128]{2,1,0:T(8,128)S(1)}, u32[]{:S(2)}, u32[]{:S(2)}) async-start(f32[16,8,128]{2,1,0:T(8,128)} %total.1), calls=%async_computation.2 | async-start | bytes 131072 | tf_op jit(solution)/shard_map/all_to_all | solution.py:661
  85.2 2.6 %symmetric.1 = bf16[8,48,8,128]{3,2,1,0:T(8,128)(2,1)} custom-call(bf16[8,48,8,128]{3,2,1,0:T(8,128)(2,1)} %get-tuple-element.80.block_far, bf16[16,8,5,8,128]{4,3,2,1,0:T(8,128)(2,1)} %bitcast.13), custom_call_target="tpu_custom_call" | custom-call | flops 4000000000 | bytes 1000000 | tf_op jit(solution)/shard_map/symmetric/pallas_call | solution.py:75
  87.8 2.6 %grad_input.1 = bf16[8,48,8,128]{3,2,1,0:T(8,128)(2,1)} custom-call(bf16[8,48,8,128]{3,2,1,0:T(8,128)(2,1)} %get-tuple-element.81.value_far, f32[384,128]{1,0:T(8,128)} %get-tuple-element.82.edge_value_far, f32[384,128]{1,0:T(8,128)} %get-tuple-element.83.edge_slope_far, f32[192,128]{1,0:T(8,128)S(1)} %collective-permute-done.6.from_left, ...), custom_call_target="tpu_custom_call" | custom-call | flops 4000000000 | bytes 1000000 | tf_op jit(solution)/shard_map/grad_input/pallas_call | solution.py:75
  90.5 0.6 all-to-all-done.2.tiles
  91.0 0.7 unpack.1
  (25 shorter events, 0.1 us)
Async XLA Ops:
  3.7 13.3 %copy-start.2 = (bf16[24,48,3,3]{1,0,3,2:T(8,128)(2,1)S(1)}, bf16[24,48,3,3]{1,0,3,2:T(8,128)(2,1)}, u32[]{:S(2)}) copy-start(bf16[24,48,3,3]{1,0,3,2:T(8,128)(2,1)} %param.10) | copy-start | bytes 62212
  3.7 13.3 %copy-start.3 = (bf16[48,24]{0,1:T(8,128)(2,1)S(1)}, bf16[48,24]{0,1:T(8,128)(2,1)}, u32[]{:S(2)}) copy-start(bf16[48,24]{0,1:T(8,128)(2,1)} %param.13) | copy-start | bytes 6916
  3.7 15.4 %collective-permute-start = (bf16[8,24,8,128]{3,2,1,0:T(8,128)(2,1)S(1)}, bf16[8,24,8,128]{3,2,1,0:T(8,128)(2,1)S(1)}, u32[]{:S(2)}, u32[]{:S(2)}) collective-permute-start(bf16[8,24,8,128]{3,2,1,0:T(8,128)(2,1)S(1)} %get-tuple-element.47), channel_id=1, source_target_pairs={{0,8},{8,16},{16,24},{24,32},{32,40},{40,48},{48,56},{56,64},{64,7... | collective-permute-start | bytes 1179656 | tf_op jit(solution)/shard_map/ppermute | solution.py:577
  6.4 12.6 %collective-permute-start.1 = (bf16[8,24,8,128]{3,2,1,0:T(8,128)(2,1)S(1)}, bf16[8,24,8,128]{3,2,1,0:T(8,128)(2,1)S(1)}, u32[]{:S(2)}, u32[]{:S(2)}) collective-permute-start(bf16[8,24,8,128]{3,2,1,0:T(8,128)(2,1)S(1)} %get-tuple-element.48), channel_id=1, source_target_pairs={{8,0},{16,8},{24,16},{32,24},{40,32},{48,40},{56,48},{64,56},{72,6... | collective-permute-start | bytes 1179656 | tf_op jit(solution)/shard_map/ppermute | solution.py:577
  6.4 28.5 %all-to-all-start = ((bf16[128,3,8,128]{3,2,1,0:T(8,128)(2,1)}), bf16[128,3,8,128]{3,2,1,0:T(8,128)(2,1)S(1)}, u32[]{:S(2)}, u32[]{:S(2)}) async-start(bf16[128,3,8,128]{3,2,1,0:T(8,128)(2,1)} %bitcast.19), calls=%async_computation | async-start | bytes 1572864 | tf_op jit(solution)/shard_map/all_to_all | solution.py:590
  17.0 2.1 %copy-start.1 = (bf16[8,48,8,128]{3,2,1,0:T(8,128)(2,1)S(1)}, bf16[8,48,8,128]{3,2,1,0:T(8,128)(2,1)}, u32[]{:S(2)}) copy-start(bf16[8,48,8,128]{3,2,1,0:T(8,128)(2,1)} %x_far.3) | copy-start | bytes 2359300
  19.0 8.3 %copy-start.4 = (f32[24]{0:T(128)S(1)}, f32[24]{0:T(128)}, u32[]{:S(2)}) copy-start(f32[24]{0:T(128)} %cg.3) | copy-start | bytes 292
  19.0 8.3 %copy-start.5 = (f32[24]{0:T(128)S(1)}, f32[24]{0:T(128)}, u32[]{:S(2)}) copy-start(f32[24]{0:T(128)} %cb.3) | copy-start | bytes 292
  19.0 8.3 %copy-start.6 = (f32[48]{0:T(128)S(1)}, f32[48]{0:T(128)}, u32[]{:S(2)}) copy-start(f32[48]{0:T(128)} %mg.3) | copy-start | bytes 580
  19.1 8.3 %copy-start.7 = (f32[48]{0:T(128)S(1)}, f32[48]{0:T(128)}, u32[]{:S(2)}) copy-start(f32[48]{0:T(128)} %mb.3) | copy-start | bytes 580
  21.6 12.8 %collective-permute-start.3 = (bf16[384,128]{1,0:T(8,128)(2,1)S(1)}, bf16[384,128]{1,0:T(8,128)(2,1)S(1)}, u32[]{:S(2)}, u32[]{:S(2)}) collective-permute-start(bf16[384,128]{1,0:T(8,128)(2,1)S(1)} %get-tuple-element.56), channel_id=1, source_target_pairs={{1,0},{2,1},{3,2},{4,3},{5,4},{6,5},{7,6},{0,7},{9,8},{10,9},{11,1... | collective-permute-start | bytes 294920 | tf_op jit(solution)/shard_map/ppermute | solution.py:577
  27.4 7.6 %collective-permute-start.2 = (bf16[384,128]{1,0:T(8,128)(2,1)S(1)}, bf16[384,128]{1,0:T(8,128)(2,1)S(1)}, u32[]{:S(2)}, u32[]{:S(2)}) collective-permute-start(bf16[384,128]{1,0:T(8,128)(2,1)S(1)} %get-tuple-element.56), channel_id=1, source_target_pairs={{0,1},{1,2},{2,3},{3,4},{4,5},{5,6},{6,7},{7,0},{8,9},{9,10},{10,1... | collective-permute-start | bytes 294920 | tf_op jit(solution)/shard_map/ppermute | solution.py:577
  41.4 8.3 %collective-permute-start.4 = (bf16[8,12,8,128]{3,2,1,0:T(8,128)(2,1)S(1)}, bf16[8,12,8,128]{3,2,1,0:T(8,128)(2,1)S(1)}, u32[]{:S(2)}, u32[]{:S(2)}) collective-permute-start(bf16[8,12,8,128]{3,2,1,0:T(8,128)(2,1)S(1)} %get-tuple-element.69), channel_id=1, source_target_pairs={{0,8},{8,16},{16,24},{24,32},{32,40},{40,48},{48,56},{56,64},{64,7... | collective-permute-start | bytes 589832 | tf_op jit(solution)/shard_map/ppermute | solution.py:577
  44.0 5.7 %collective-permute-start.5 = (bf16[8,12,8,128]{3,2,1,0:T(8,128)(2,1)S(1)}, bf16[8,12,8,128]{3,2,1,0:T(8,128)(2,1)S(1)}, u32[]{:S(2)}, u32[]{:S(2)}) collective-permute-start(bf16[8,12,8,128]{3,2,1,0:T(8,128)(2,1)S(1)} %get-tuple-element.70), channel_id=1, source_target_pairs={{8,0},{16,8},{24,16},{32,24},{40,32},{48,40},{56,48},{64,56},{72,6... | collective-permute-start | bytes 589832 | tf_op jit(solution)/shard_map/ppermute | solution.py:577
  49.7 28.9 %all-to-all-start.1 = ((bf16[128,5,8,128]{3,2,1,0:T(8,128)(2,1)}), bf16[128,5,8,128]{3,2,1,0:T(8,128)(2,1)S(1)}, u32[]{:S(2)}, u32[]{:S(2)}) async-start(bf16[128,5,8,128]{3,2,1,0:T(8,128)(2,1)} %bitcast.18), calls=%async_computation.1 | async-start | bytes 2621440 | tf_op jit(solution)/shard_map/all_to_all | solution.py:656
  64.0 21.2 %collective-permute-start.7 = (f32[192,128]{1,0:T(8,128)S(1)}, f32[192,128]{1,0:T(8,128)S(1)}, u32[]{:S(2)}, u32[]{:S(2)}) collective-permute-start(f32[192,128]{1,0:T(8,128)S(1)} %get-tuple-element.78), channel_id=1, source_target_pairs={{1,0},{2,1},{3,2},{4,3},{5,4},{6,5},{7,6},{0,7},{9,8},{10,9},{11,1... | collective-permute-start | bytes 294920 | tf_op jit(solution)/shard_map/ppermute | solution.py:577
  69.8 15.4 %collective-permute-start.6 = (f32[192,128]{1,0:T(8,128)S(1)}, f32[192,128]{1,0:T(8,128)S(1)}, u32[]{:S(2)}, u32[]{:S(2)}) collective-permute-start(f32[192,128]{1,0:T(8,128)S(1)} %get-tuple-element.78), channel_id=1, source_target_pairs={{0,1},{1,2},{2,3},{3,4},{4,5},{5,6},{6,7},{7,0},{8,9},{9,10},{10,1... | collective-permute-start | bytes 294920 | tf_op jit(solution)/shard_map/ppermute | solution.py:577
  78.6 6.6 %copy-start = (bf16[128,5,8,128]{3,2,1,0:T(8,128)(2,1)}, bf16[128,5,8,128]{3,2,1,0:T(8,128)(2,1)S(1)}, u32[]{:S(2)}) copy-start(bf16[128,5,8,128]{3,2,1,0:T(8,128)(2,1)S(1)} %all-to-all-done.1) | copy-start | bytes 3932164
  79.5 11.5 %all-to-all-start.2 = ((f32[16,8,128]{2,1,0:T(8,128)}), f32[16,8,128]{2,1,0:T(8,128)S(1)}, u32[]{:S(2)}, u32[]{:S(2)}) async-start(f32[16,8,128]{2,1,0:T(8,128)} %total.1), calls=%async_computation.2 | async-start | bytes 131072 | tf_op jit(solution)/shard_map/all_to_all | solution.py:661

commit v5 on v4

--- a/solution.py
+++ b/solution.py
@@ -219,8 +219,10 @@
         out[b * CR : (b + 1) * CR] = total.reshape(CR, 2 * MR).astype(BF)
 
 
-def act_kernel(x, above, below, act, edge, act_far, sems):
-    far = Far(sems)
+def act_kernel(x, above, below, act, edge, wide_far, wide, rows, sems):
+    far = Far(sems)
+    for p in range(4):
+        wide[64 * p + CH : 64 * p + 64, :] = jnp.zeros((64 - CH, 4 * POS), BF)
     lane = lanes_of(CR)
     packed = jnp.zeros((CR, LANES), F32)
     for g in range(GROUPS):
@@ -231,10 +233,16 @@
         at = slice(g * LANES, (g + 1) * LANES)
         act[0:CR, at] = own.astype(BF)
         act[CR : 2 * CR, at] = rim.astype(BF)
-        far.send(act.at[:, at], act_far.at[:, at])
+        rows[0:CR] = own
+        rows[CR : 2 * CR] = rim
+        for m in range(4):
+            to = slice((m * GROUPS + g) * LANES, (m * GROUPS + g + 1) * LANES)
+            for p, (start, step) in enumerate(((CR, 4), (0, 8), (4, 8), (CR + CR // 2, 4))):
+                wide[64 * p : 64 * p + CH, to] = rows[pl.ds(start + m, CH, stride=step), :].astype(BF)
         packed = jnp.where(lane // 8 == g, pltpu.roll(own, (8 * g - 124) % LANES, 1), packed)
         packed = jnp.where(lane // 8 == 8 + g, pltpu.roll(rim, (8 * g - 60) % LANES, 1), packed)
     edge[...] = packed.astype(BF)
+    far.send(wide, wide_far)
     far.finish()
 
 
@@ -314,8 +322,8 @@
 def inner_kernel(
     d_far, arrived, slope_far, hidden_far, edge_inner_far, edge_x_far, from_left, from_right,
     weights_far, mixer_far, back_far, pieces_in, cg, cb, mg, mb,
-    grad_inner_far, down, up, half_sum_far, pieces_far, edge_block_far, gmi, shifted, edge_rows, hidden_out, rim_out,
-    d, slope, hidden, edge_inner, edge_x, weights, mixer, back, grad_inner, half_sum, ends, edge_block, buffer, sems,
+    grad_inner_far, down, up, half_sum_far, pieces_far, edge_block_far, gmi, taps_out, hidden_out, rim_wide,
+    d, slope, hidden, edge_inner, edge_x, weights, mixer, back, grad_inner, half_sum, ends, edge_block, buffer, rows, sems,
 ):
     far = Far(sems)
     loads = [far.start(d_far.at[2 * p : 2 * p + 2], d.at[2 * p : 2 * p + 2]) for p in range(GROUPS // 2)]
@@ -329,8 +337,18 @@
     lane, lane_c = lanes_of(MR), lanes_of(CR)
     gain, shift = splat(cg, MID), splat(cb, MID)
     gain_out, shift_out = splat(mg, CH), splat(mb, CH)
-    rim = merge_edges(from_left[...].astype(F32), from_right[...].astype(F32)).astype(BF)
-    rim_out[...] = rim
+    rim = merge_edges(from_left[...].astype(F32), from_right[...].astype(F32))
+    rows[...] = rim
+    for m in range(4):
+        to = slice(m * LANES, (m + 1) * LANES)
+        for p, (start, step) in enumerate(((0, 4), (0, 8), (4, 8), (CR // 2, 4))):
+            part = rows[pl.ds(start + m, CH, stride=step), :]
+            if step == 4:
+                part = pltpu.roll(part, 64, 1)
+            rim_wide[64 * p : 64 * p + CH, to] = part.astype(BF)
+    for p in range(4):
+        rim_wide[64 * p + CH : 64 * p + 64, :] = jnp.zeros((64 - CH, 4 * LANES), BF)
+    rim = rim.astype(BF)
     for pair in range(GROUPS // 2):
         loads[pair].wait()
         swap_in(arrived, 2 * pair, buffer)
@@ -378,84 +396,69 @@
             here = jnp.where(at_edge(lane), pltpu.roll(slope_edge, turn, 1), slope[:, at])
             value = into[:, half * LANES : (half + 1) * LANES] * here
             grad_inner[g] = value.reshape(MID, H, LANES).astype(BF)
-            shifted[0:MR, at] = jnp.where(lane < 124, pltpu.roll(value, LANES - 4, 1), 0.0).astype(BF)
-            shifted[MR : 2 * MR, at] = value.astype(BF)
-            shifted[2 * MR : 3 * MR, at] = jnp.where(lane >= 4, pltpu.roll(value, 4, 1), 0.0).astype(BF)
+            rows[0:MR] = value
+            for r in range(H):
+                part = jnp.concatenate([rows[pl.ds(r, MID, stride=8), :], jnp.zeros((H, LANES), F32)], axis=0)
+                lane_t = lanes_of(MID + H)
+                three = (
+                    jnp.where(lane_t < 124, pltpu.roll(part, LANES - 4, 1), 0.0),
+                    part,
+                    jnp.where(lane_t >= 4, pltpu.roll(part, 4, 1), 0.0),
+                )
+                to = slice((r % 4 * GROUPS + g) * LANES, (r % 4 * GROUPS + g + 1) * LANES)
+                for b in range(3):
+                    top = 32 * (3 * (r // 4) + b)
+                    taps_out[top : top + 32, to] = three[b].astype(BF)
             packed = jnp.where(lane // 8 == g, pltpu.roll(value, (8 * g - 124) % LANES, 1), packed)
             here = jnp.where(at_edge(lane), pltpu.roll(hidden_edge, turn, 1), hidden[:, at].astype(F32))
             hidden_out[:, at] = here.astype(BF)
         far.send(grad_inner.at[2 * pair : 2 * pair + 2], grad_inner_far.at[2 * pair : 2 * pair + 2])
     send_rows(grad_inner, down, up, MID)
-    packed = packed + pltpu.roll(packed, 64, 1)
-    edge_rows[0:MR] = jnp.where(lane % 8 >= 4, packed, 0.0).astype(BF)
-    edge_rows[MR : 2 * MR] = jnp.zeros((MR, LANES), BF)
-    edge_rows[2 * MR : 3 * MR] = jnp.where(lane % 8 < 4, packed, 0.0).astype(BF)
-    far.finish()
-
-
-def sums_kernel(
-    act_far, gmi, shifted, edge_rows, hidden, rim, pieces_in, pieces_far, act, sums_out, wide, mixwide, sems
-):
-    far = Far(sems)
-    loads = [far.start(act_far.at[k * CR : (k + 1) * CR], act.at[k * CR : (k + 1) * CR]) for k in range(2)]
+    rows[0:MR] = packed
+    for r in range(H):
+        part = jnp.concatenate([rows[pl.ds(r, MID, stride=8), :], jnp.zeros((H, LANES), F32)], axis=0)
+        lane_t = lanes_of(MID + H)
+        low = jnp.where(lane_t % 8 < 4, part, 0.0)
+        three = (part - low, jnp.zeros_like(part), low)
+        to = slice(4 * POS + r % 4 * LANES, 4 * POS + (r % 4 + 1) * LANES)
+        for b in range(3):
+            top = 32 * (3 * (r // 4) + b)
+            taps_out[top : top + 32, to] = three[b].astype(BF)
+    far.finish()
+
+
+def sums_kernel(wide_far, gmi, taps, hidden, rim_wide, pieces_in, pieces_far, wide, sums_out, sems):
+    far = Far(sems)
+    load = far.start(wide_far, wide)
     sums_out[ROWS - 1] = jnp.zeros((COLS, 2, H, LANES), BF)
     far.send(sums_out.at[ROWS - 1], pieces_far.at[ROWS - 1, :, 0:2])
-    lane_c = lanes_of(CR)
-    rim_value = rim[...].astype(F32)
-    rim_own = jnp.where(lane_c < 64, rim_value, 0.0).astype(BF)
-    rim_rest = jnp.where(lane_c >= 64, rim_value, 0.0).astype(BF)
-    mixwide[...] = dot(hidden[...], gmi[...], NT)
-    for k in range(2):
-        rows = slice(k * CR, (k + 1) * CR)
-        loads[k].wait()
-        wide[:, rows] = dot(shifted[...], act[rows], NT) + dot(edge_rows[...], (rim_own, rim_rest)[k], NT)
-
+    mixwide = dot(hidden[...], gmi[...], NT)
     h, col = iota((H, CR), 0), iota((H, CR), 1)
     same = jnp.where(col % 8 == h, 1.0, 0.0)[None]
-    other = jnp.where(col % 8 == (h + 4) % 8, 1.0, 0.0)[None]
-    low_half = col < CR // 2
-    across = jnp.where(jnp.where(low_half, col, col - CR // 2) % 4 == jnp.where(low_half, h, h - 4), 1.0, 0.0)[None]
+    mixed = jnp.sum(mixwide.reshape(MID, H, CR) * same, axis=1)
     col, lane_s = iota((CR, LANES), 0), iota((CR, LANES), 1)
-
-    def gather(keep, channel, side):
-        return jnp.where(jnp.logical_and(keep, channel + 64 * side == lane_s), 1.0, 0.0).astype(BF)
-
-    blocks = []
-    sums = []
+    mixed = exact_dot(mixed, jnp.where(col // 8 + 64 == lane_s, 1.0, 0.0).astype(BF))
+    total = dot(taps[:, 4 * POS :], rim_wide[...], NT)
+    load.wait()
+    total += dot(taps[:, 0 : 4 * POS], wide[...], NT)
+    lane = lanes_of(MID)
+    blocks, thirds = [], []
     for b in range(3):
-        block = wide[b * MR : (b + 1) * MR]
-        own = block[:, 0:CR].reshape(MID, H, CR)
-        rest = block[:, CR : 2 * CR].reshape(MID, H, CR)
-        sums.append([jnp.sum(own * same, axis=1), jnp.sum(own * other, axis=1), jnp.sum(rest * across, axis=1)])
-    mixed = jnp.sum(mixwide[...].reshape(MID, H, CR) * same, axis=1)
-    always = col >= 0
-    own_low = col % 8 < 4
-    rest_low = col < CR // 2
-    rest_channel = jnp.where(rest_low, col, col - CR // 2) // 4
-    for index in range(10):
-        side = index % 2
-        if index == 9:
-            value = exact_dot(mixed, gather(always, col // 8, side))
-        else:
-            a, b = index // 3, index % 3
-            if a == 1:
-                value = exact_dot(sums[b][0], gather(always, col // 8, side))
-            else:
-                low = a == 0
-                keep_own = own_low if low else jnp.logical_not(own_low)
-                keep_rest = rest_low if low else jnp.logical_not(rest_low)
-                value = exact_dot(sums[b][1], gather(keep_own, col // 8, side))
-                value += exact_dot(sums[b][2], gather(keep_rest, rest_channel, side))
-        blocks.append(value)
+        near, next_one = total[32 * b : 32 * b + MID], total[32 * (3 + b) : 32 * (3 + b) + MID]
+        moved = pltpu.roll(next_one[:, 0:LANES], 64, 1)
+        ahead = pltpu.roll(next_one[:, LANES : 2 * LANES], 64, 1)
+        blocks.append(near[:, 0:LANES] + jnp.where(lane < 64, moved, ahead))
+        thirds.append(jnp.where(lane < 64, near[:, LANES : 2 * LANES] + ahead, 0.0))
+    blocks.append(thirds[0] + pltpu.roll(thirds[1], 64, 1))
+    blocks.append(thirds[2] + mixed)
     for p in range(5):
-        value = blocks[2 * p] + blocks[2 * p + 1]
-        high = value.astype(BF).astype(F32)
-        low = value - high
+        high = blocks[p].astype(BF).astype(F32)
+        low = blocks[p] - high
         for k in range(3):
             r = 3 * p + k
-            rows = slice(k * H, (k + 1) * H)
-            sums_out[r, :, 0] = jnp.broadcast_to(high[rows][None], (COLS, H, LANES)).astype(BF)
-            sums_out[r, :, 1] = jnp.broadcast_to(low[rows][None], (COLS, H, LANES)).astype(BF)
+            at = slice(k * H, (k + 1) * H)
+            sums_out[r, :, 0] = jnp.broadcast_to(high[at][None], (COLS, H, LANES)).astype(BF)
+            sums_out[r, :, 1] = jnp.broadcast_to(low[at][None], (COLS, H, LANES)).astype(BF)
         far.send(sums_out.at[3 * p : 3 * p + 3], pieces_far.at[3 * p : 3 * p + 3, :, 0:2])
     far.finish()
 
@@ -516,10 +519,25 @@
     far.finish()
 
 
-def input_kernel(value_far, edge_value_far, edge_slope_far, from_left, from_right, out_far, value, out, edge_value, edge_slope, sems):
+def total_kernel(arrived, out):
+    total = jnp.zeros((H, LANES), F32)
+    for g in range(COLS):
+        part = arrived[:, g, 0:2].astype(F32)
+        total += jnp.sum(part[:, 0] + part[:, 1], axis=0)
+    out[...] = jnp.broadcast_to((total * (1.0 / (ROWS * H * COLS)))[None], (ROWS, H, LANES))
+
+
+def last_kernel(
+    block_far, arrived_far, value_far, edge_value_far, edge_slope_far, from_left, from_right, out_far, grad_far,
+    block, arrived, out, value, grad, edge_value, edge_slope, sems,
+):
     far = Far(sems)
     first = [far.start(edge_value_far, edge_value), far.start(edge_slope_far, edge_slope)]
     loads = [far.start(value_far.at[g], value.at[g]) for g in range(GROUPS)]
+    later = [
+        (far.start(block_far.at[g], block.at[g]), far.start(arrived_far.at[:, g, 2:5], arrived.at[:, g]))
+        for g in range(GROUPS)
+    ]
     lane = lanes_of(CR)
     rim = merge_edges(from_left[...], from_right[...])
     rim = jnp.concatenate([rim, pltpu.roll(rim, 64, 1)], axis=0)
@@ -530,44 +548,28 @@
         loads[g].wait()
         moved = pltpu.roll(rim, (124 - 8 * g) % LANES, 1)
         total = jnp.where(at_edge(lane), moved, value[g].astype(F32).reshape(CR, LANES))
-        out[g] = total.reshape(CH, H, LANES).astype(BF)
-        far.send(out.at[g], out_far.at[g])
-    far.finish()
-
-
-def total_kernel(arrived, out):
-    total = jnp.zeros((H, LANES), F32)
-    for g in range(COLS):
-        part = arrived[:, g, 0:2].astype(F32)
-        total += jnp.sum(part[:, 0] + part[:, 1], axis=0)
-    out[...] = jnp.broadcast_to((total * (1.0 / (ROWS * H * COLS)))[None], (ROWS, H, LANES))
-
-
-def symmetric_kernel(block_far, arrived_far, out_far, block, arrived, out, sems):
-    far = Far(sems)
-    loads = [
-        (far.start(block_far.at[g], block.at[g]), far.start(arrived_far.at[:, g, 2:5], arrived.at[:, g]))
-        for g in range(GROUPS)
-    ]
+        grad[g] = total.reshape(CH, H, LANES).astype(BF)
+        far.send(grad.at[g], grad_far.at[g])
     for g in range(GROUPS):
-        for load in loads[g]:
+        for load in later[g]:
             load.wait()
         for k in range(3):
             at = slice(k * ROWS, (k + 1) * ROWS)
-            value = 0.5 * (block[g, at].astype(F32) + turn(arrived[:, g, k]).astype(F32))
-            out[g, at] = value.astype(BF)
+            both = 0.5 * (block[g, at].astype(F32) + turn(arrived[:, g, k]).astype(F32))
+            out[g, at] = both.astype(BF)
         far.send(out.at[g], out_far.at[g])
     far.finish()
 
 
 def unpack_kernel(tiles, conv, mix):
-    for p in range(5):
+    order = ((0, 3), (1, 4), (2, 5), (6, 7), (8, None))
+    for p, (left, right) in enumerate(order):
         value = tiles[3 * p : 3 * p + 3].reshape(3 * H, LANES)
-        conv[2 * p] = value[:, 0:CH]
-        if p < 4:
-            conv[2 * p + 1] = value[:, 64 : 64 + CH]
+        conv[left] = value[:, 0:CH]
+        if right is None:
+            mix[...] = value[:, 64 : 64 + CH]
         else:
-            mix[...] = value[:, 64 : 64 + CH]
+            conv[right] = value[:, 64 : 64 + CH]
 
 
 def both_ways(first, second, axis):
@@ -596,10 +598,11 @@
         [((3 * MR, 2 * CR), BF), ((CR, MR), BF)] * 2 + [((MR, CR), BF)],
         (taps, mix_weight.T), "weights", far_out=(2, 3, 4), scratch=[vmem((MR, CR), BF)], copies=3,
     )
-    act, edge, act_far = call(
+    act, edge, wide = call(
         act_kernel,
-        [((2 * CR, POS), BF), ((CR, LANES), BF), ((2 * CR, POS), BF)],
-        (pair_map, above, below), "act", far_out=(2,), copies=GROUPS,
+        [((2 * CR, POS), BF), ((CR, LANES), BF), ((256, 4 * POS), BF)],
+        (pair_map, above, below), "act", far_out=(2,), copies=1,
+        scratch=[vmem((256, 4 * POS), BF), vmem((2 * CR, LANES), F32)],
     )
     from_left, from_right = both_ways(edge, edge, "col")
     five = (ROWS, COLS, 5, H, LANES)
@@ -614,7 +617,7 @@
         ],
         copies=2 * GROUPS + 2,
     )
-    grad_inner, g_down, g_up, half_sum, pieces, edge_block, gmi, shifted, edge_rows, hidden, rim = call(
+    grad_inner, g_down, g_up, half_sum, pieces, edge_block, gmi, tap_rows, hidden, rim_wide = call(
         inner_kernel,
         [
             ((GROUPS, MID, H, LANES), BF),
@@ -624,10 +627,9 @@
             (five, BF),
             ((CR, LANES), F32),
             ((CR, POS), BF),
-            ((3 * MR, POS), BF),
-            ((3 * MR, LANES), BF),
+            ((192, 4 * POS + 4 * LANES), BF),
             ((MR, POS), BF),
-            ((CR, LANES), BF),
+            ((256, 4 * LANES), BF),
         ],
         (
             cotangent, d_arrived, slope, hidden, edge_inner, edge_x, from_left, from_right,
@@ -638,19 +640,15 @@
             vmem(tile, BF), vmem((MR, POS), F32), vmem((MR, POS), BF), vmem((MR, LANES), F32), vmem((CR, LANES), F32),
             vmem((2 * MR, 2 * CR), BF), vmem((CR, MR), BF), vmem((MR, CR), BF),
             vmem((GROUPS, MID, H, LANES), BF), vmem(tile, F32), vmem((2, COLS, 3, H, LANES), BF),
-            vmem((CR, LANES), F32), vmem((2, CH, H, LANES), BF),
+            vmem((CR, LANES), F32), vmem((2, CH, H, LANES), BF), vmem((CR, LANES), F32),
         ],
         copies=25,
     )
     g_above, g_below = both_ways(g_down, g_up, "row")
     (pieces,) = call(
-        sums_kernel, [(five, BF)], (act_far, gmi, shifted, edge_rows, hidden, rim, pieces), "sums",
-        far=(0, 6), far_out=(0,), alias={6: 0},
-        scratch=[
-            vmem((2 * CR, POS), BF), vmem((ROWS, COLS, 2, H, LANES), BF),
-            vmem((3 * MR, 2 * CR), F32), vmem((MR, CR), F32),
-        ],
-        copies=8,
+        sums_kernel, [(five, BF)], (wide, gmi, tap_rows, hidden, rim_wide, pieces), "sums",
+        far=(0, 5), far_out=(0,), alias={5: 0},
+        scratch=[vmem((256, 4 * POS), BF), vmem((ROWS, COLS, 2, H, LANES), BF)], copies=7,
     )
     pieces, g_above, g_below = lax.optimization_barrier((pieces, g_above, g_below))
     arrived = lax.all_to_all(pieces.reshape(ROWS * COLS, 5, H, LANES), everyone, 0, 0, tiled=True)
@@ -673,14 +671,13 @@
     )
     g_left, g_right = both_ways(g_edge, g_edge, "col")
     g_left, g_right, block, _ = lax.optimization_barrier((g_left, g_right, block, sums))
-    (grad_input,) = call(
-        input_kernel, [(tile, BF)], (inputs, edge_value, edge_slope, g_left, g_right), "grad_input",
-        far=(0, 1, 2), far_out=(0,), copies=2 * GROUPS + 2,
-        scratch=[vmem(tile, BF), vmem(tile, BF), vmem((CR, LANES), F32), vmem((CR, LANES), F32)],
-    )
-    (symmetric,) = call(
-        symmetric_kernel, [(tile, BF)], (block, arrived), "symmetric", far=(0, 1), far_out=(0,),
-        scratch=[vmem(tile, BF), vmem(cut, BF), vmem(tile, BF)], copies=3 * GROUPS,
+    symmetric, grad_input = call(
+        last_kernel, [(tile, BF)] * 2, (block, arrived, inputs, edge_value, edge_slope, g_left, g_right), "last",
+        far=(0, 1, 2, 3, 4), far_out=(0, 1), copies=5 * GROUPS + 2,
+        scratch=[
+            vmem(tile, BF), vmem(cut, BF), vmem(tile, BF), vmem(tile, BF), vmem(tile, BF),
+            vmem((CR, LANES), F32), vmem((CR, LANES), F32),
+        ],
     )
     conv, mix = call(
         unpack_kernel, [((9, MID, CH), F32), ((MID, CH), F32)], (spread_sums,), "unpack", flops=100_000_000

time: 92.2 us -> 93.6 us (1.015)
  waiting for transfers between devices: 9.98 us -> 12.2 us
  Pallas kernels: 39.1 us -> 37.5 us
    all_to_all x1, waiting for transfers between devices: 0.57 us -> 2.15 us  [local(): spread_sums = lax.all_to_all(sums, 'row', 0, 0, tiled=True)]
    pallas_call x11 -> x10, Pallas kernels: 39.1 us -> 37.5 us  [call(): pl.pallas_call(kernel, name=name, out_shape=[pltpu.HBM(s, t) if i in far_...]
  transfers between devices with their start and end apart: 11 -> 11, of which waited for: 3 -> 4; matrix products, arithmetic and copies ran while one was open for 0% -> 0% of each run, Pallas kernels for 31% -> 29%
where the time goes in v5:
time: 93.6 us; the launch traced here: 93.2 us
  starting transfers between devices  42.6 us (46%)
  Pallas kernels  37.5 us (40%)
  waiting for transfers between devices  12.2 us (13%)
    pallas_call x10, Pallas kernels, call(): pl.pallas_call(kernel, name=name, out_shape=[pltpu.HBM(s, t) if i in far_...  37.5 us
    ppermute x8, starting transfers between devices, both_ways(): return (lax.ppermute(first, axis, onward), lax.ppermute(second, axis, back))  17.3 us
    all_to_all x1, starting transfers between devices, local(): lax.all_to_all(d_pieces.reshape(ROWS * COLS, 3, H, LANES), everyone, 0, 0...  10.6 us
    all_to_all x1, starting transfers between devices, local(): lax.all_to_all(pieces.reshape(ROWS * COLS, 5, H, LANES), everyone, 0, 0,...  9 us
    all_to_all x1, waiting for transfers between devices, local(): lax.all_to_all(pieces.reshape(ROWS * COLS, 5, H, LANES), everyone, 0, 0,...  8.76 us
    all_to_all x1, starting transfers between devices, local(): spread_sums = lax.all_to_all(sums, 'row', 0, 0, tiled=True)  5.72 us
    all_to_all x1, waiting for transfers between devices, local(): spread_sums = lax.all_to_all(sums, 'row', 0, 0, tiled=True)  2.15 us
  transfers between devices with their start and end apart: 11, of which 4 were waited for; matrix products, arithmetic and copies ran while one was open for 0% of the time, Pallas kernels for 29%

profile of v5, /device:TPU:1, one launch (start us, length us, event | category | flops | bytes accessed | tf_op | source)
XLA Modules:
  0.0 93.2 jit_solution(4596897547677889928)
XLA Ops:
  0.6 3.0 %first.1 = (bf16[8,24,8,128]{3,2,1,0:T(8,128)(2,1)S(1)}, bf16[8,24,8,128]{3,2,1,0:T(8,128)(2,1)S(1)}, bf16[16,8,3,8,128]{4,3,2,1,0:T(8,128)(2,1)}) custom-call(bf16[8,48,8,128]{3,2,1,0:T(8,128)(2,1)} %x_far.3, bf16[8,48,8,128]{3,2,1,0:T(8,128)(2,1)} %d_far.3), custom_call_target="tpu_custom_call" | custom-call | flops 4000000000 | bytes 1000000 | tf_op jit(solution)/shard_map/first/pallas_call | solution.py:75
  3.7 0.0 copy-start.2
  3.7 2.8 %collective-permute-start = (bf16[8,24,8,128]{3,2,1,0:T(8,128)(2,1)S(1)}, bf16[8,24,8,128]{3,2,1,0:T(8,128)(2,1)S(1)}, u32[]{:S(2)}, u32[]{:S(2)}) collective-permute-start(bf16[8,24,8,128]{3,2,1,0:T(8,128)(2,1)S(1)} %get-tuple-element.48), channel_id=1, source_target_pairs={{0,8},{8,16},{16,24},{24,32},{32,40},{40,48},{48,56},{56,64},{64,7... | collective-permute-start | bytes 1179656 | tf_op jit(solution)/shard_map/ppermute | solution.py:579
  6.4 10.6 %all-to-all-start = ((bf16[128,3,8,128]{3,2,1,0:T(8,128)(2,1)}), bf16[128,3,8,128]{3,2,1,0:T(8,128)(2,1)S(1)}, u32[]{:S(2)}, u32[]{:S(2)}) async-start(bf16[128,3,8,128]{3,2,1,0:T(8,128)(2,1)} %bitcast.19), calls=%async_computation | async-start | bytes 1572864 | tf_op jit(solution)/shard_map/all_to_all | solution.py:592
  17.0 2.0 %weights.1 = (bf16[576,768]{1,0:T(8,128)(2,1)S(1)}, bf16[384,192]{1,0:T(8,128)(2,1)S(1)}, bf16[576,768]{1,0:T(8,128)(2,1)}, bf16[384,192]{1,0:T(8,128)(2,1)}, bf16[192,384]{1,0:T(8,128)(2,1)}) custom-call(bf16[9,24,48]{2,1,0:T(8,128)(2,1)S(1)} %bitcast.15, bf16[24,48]{1,0:T(8,128)(2,1)S(1)} %bitcast.17), custom_call_target="tpu_custom_call" | custom-call | flops 4000000000 | bytes 1000000 | tf_op jit(solution)/shard_map/weights/pallas_call | solution.py:75
  19.0 0.0 copy-start.4
  19.1 0.0 copy-start.7
  19.1 3.6 %act.1 = (bf16[768,1024]{1,0:T(8,128)(2,1)S(1)}, bf16[384,128]{1,0:T(8,128)(2,1)S(1)}, bf16[256,4096]{1,0:T(8,128)(2,1)}) custom-call(bf16[8,48,8,128]{3,2,1,0:T(8,128)(2,1)S(1)} %copy-done.1, bf16[8,24,8,128]{3,2,1,0:T(8,128)(2,1)S(1)} %collective-permute-done.above, bf16[8,24,8,128]{3,2,1,0:T(8,128)(2,1)S(1)} %collective-permute-done.1.below), custom_call_target="tpu_custom_call" | custom-call | flops 4000000000 | bytes 1000000 | tf_op jit(solution)/shard_map/act/pallas_call | solution.py:75
  22.7 5.8 %collective-permute-start.3 = (bf16[384,128]{1,0:T(8,128)(2,1)S(1)}, bf16[384,128]{1,0:T(8,128)(2,1)S(1)}, u32[]{:S(2)}, u32[]{:S(2)}) collective-permute-start(bf16[384,128]{1,0:T(8,128)(2,1)S(1)} %get-tuple-element.57), channel_id=1, source_target_pairs={{1,0},{2,1},{3,2},{4,3},{5,4},{6,5},{7,6},{0,7},{9,8},{10,9},{11,1... | collective-permute-start | bytes 294920 | tf_op jit(solution)/shard_map/ppermute | solution.py:579
  28.5 7.0 %inside.1 = (f32[192,1024]{1,0:T(8,128)}, bf16[192,1024]{1,0:T(8,128)(2,1)}, bf16[8,48,8,128]{3,2,1,0:T(8,128)(2,1)}, bf16[16,8,5,8,128]{4,3,2,1,0:T(8,128)(2,1)...) custom-call(bf16[8,48,8,128]{3,2,1,0:T(8,128)(2,1)S(1)} %copy-done.1, bf16[768,1024]{1,0:T(8,128)(2,1)S(1)} %get-tuple-element.50.act, ...), custom_call_target="tpu_custom_call" | custom-call | flops 4000000000 | bytes 1000000 | tf_op jit(solution)/shard_map/inside/pallas_call | solution.py:75
  35.5 0.1 collective-permute-done.2.from_left
  35.6 6.8 %inner.1 = (bf16[8,24,8,128]{3,2,1,0:T(8,128)(2,1)}, bf16[8,12,8,128]{3,2,1,0:T(8,128)(2,1)S(1)}, bf16[8,12,8,128]{3,2,1,0:T(8,128)(2,1)S(1)}, f32[8,48,8,128]{3...) custom-call(bf16[8,48,8,128]{3,2,1,0:T(8,128)(2,1)} %d_far.3, ...), custom_call_target="tpu_custom_call", output_to_operand_aliasing={{4}: (11, {})} | custom-call | flops 4000000000 | bytes 1000000 | tf_op jit(solution)/shard_map/inner/pallas_call | solution.py:75
  42.4 3.0 %collective-permute-start.4 = (bf16[8,12,8,128]{3,2,1,0:T(8,128)(2,1)S(1)}, bf16[8,12,8,128]{3,2,1,0:T(8,128)(2,1)S(1)}, u32[]{:S(2)}, u32[]{:S(2)}) collective-permute-start(bf16[8,12,8,128]{3,2,1,0:T(8,128)(2,1)S(1)} %get-tuple-element.69), channel_id=1, source_target_pairs={{0,8},{8,16},{16,24},{24,32},{32,40},{40,48},{48,56},{56,64},{64,7... | collective-permute-start | bytes 589832 | tf_op jit(solution)/shard_map/ppermute | solution.py:579
  45.3 4.2 %sums.1 = bf16[16,8,5,8,128]{4,3,2,1,0:T(8,128)(2,1)} custom-call(bf16[256,4096]{1,0:T(8,128)(2,1)} %get-tuple-element.63.wide_far, bf16[384,1024]{1,0:T(8,128)(2,1)S(1)} %get-tuple-element.64.gmi, bf16[192,4608]{1,0:T(8,128)(2,1)S(1)} %get-tuple-element.65.taps, bf16[192,1024]{1,0:T(8,128)(2,1)S(1)} %get-tuple-element.66.hidden, ...), custom_call_target="tpu_custom_call", output_to_operand_aliasing={{}: (5, {})} | custom-call | flops 4000000000 | bytes 1000000 | tf_op jit(solution)/shard_map/sums/pallas_call | solution.py:75
  49.6 1.2 %collective-permute-done.5.below = bf16[8,12,8,128]{3,2,1,0:T(8,128)(2,1)S(1)} collective-permute-done((bf16[8,12,8,128]{3,2,1,0:T(8,128)(2,1)S(1)}, bf16[8,12,8,128]{3,2,1,0:T(8,128)(2,1)S(1)}, u32[]{:S(2)}, u32[]{:S(2)}) %collective-permute-start.5) | collective-permute-done | bytes 196640 | tf_op jit(solution)/shard_map/ppermute | solution.py:579
  50.7 9.0 %all-to-all-start.1 = ((bf16[128,5,8,128]{3,2,1,0:T(8,128)(2,1)}), bf16[128,5,8,128]{3,2,1,0:T(8,128)(2,1)S(1)}, u32[]{:S(2)}, u32[]{:S(2)}) async-start(bf16[128,5,8,128]{3,2,1,0:T(8,128)(2,1)} %bitcast.18), calls=%async_computation.1 | async-start | bytes 2621440 | tf_op jit(solution)/shard_map/all_to_all | solution.py:654
  59.7 5.8 %spread.1 = (f32[192,128]{1,0:T(8,128)S(1)}, bf16[8,48,8,128]{3,2,1,0:T(8,128)(2,1)}, f32[384,128]{1,0:T(8,128)}, f32[384,128]{1,0:T(8,128)}, bf16[8,48,8,128]{3,2,1,0:T(8,128)(2,1)}) custom-call(bf16[8,24,8,128]{3,2,1,0:T(8,128)(2,1)} %get-tuple-element.62.grad_inner_far, bf16[8,12,8,128]{3,2,1,0:T(8,128)(2,1)S(1)} %collective-permute-done.4.above, ...), custom_call_target="tpu_custom_call" | custom-call | flops 4000000000 | bytes 1000000 | tf_op jit(solution)/shard_map/spread/pallas_call | solution.py:75
  65.5 5.8 %collective-permute-start.7 = (f32[192,128]{1,0:T(8,128)S(1)}, f32[192,128]{1,0:T(8,128)S(1)}, u32[]{:S(2)}, u32[]{:S(2)}) collective-permute-start(f32[192,128]{1,0:T(8,128)S(1)} %get-tuple-element.78), channel_id=1, source_target_pairs={{1,0},{2,1},{3,2},{4,3},{5,4},{6,5},{7,6},{0,7},{9,8},{10,9},{11,1... | collective-permute-start | bytes 294920 | tf_op jit(solution)/shard_map/ppermute | solution.py:579
  71.3 8.8 %all-to-all-done.1 = bf16[128,5,8,128]{3,2,1,0:T(8,128)(2,1)S(1)} async-done(((bf16[128,5,8,128]{3,2,1,0:T(8,128)(2,1)}), bf16[128,5,8,128]{3,2,1,0:T(8,128)(2,1)S(1)}, u32[]{:S(2)}, u32[]{:S(2)}) %all-to-all-start.1) | async-done | bytes 1310752 | tf_op jit(solution)/shard_map/all_to_all | solution.py:654
  80.1 0.8 total.1
  80.9 5.7 %all-to-all-start.2 = ((f32[16,8,128]{2,1,0:T(8,128)}), f32[16,8,128]{2,1,0:T(8,128)S(1)}, u32[]{:S(2)}, u32[]{:S(2)}) async-start(f32[16,8,128]{2,1,0:T(8,128)} %total.1), calls=%async_computation.2 | async-start | bytes 131072 | tf_op jit(solution)/shard_map/all_to_all | solution.py:659
  86.6 3.6 %last.1 = (bf16[8,48,8,128]{3,2,1,0:T(8,128)(2,1)}, bf16[8,48,8,128]{3,2,1,0:T(8,128)(2,1)}) custom-call(bf16[8,48,8,128]{3,2,1,0:T(8,128)(2,1)} %get-tuple-element.80.block_far, bf16[16,8,5,8,128]{4,3,2,1,0:T(8,128)(2,1)} %bitcast.13, bf16[8,48,8,128]{3,2,1,0:T(8,128)(2,1)} %get-tuple-element.81.value_far, f32[384,128]{1,0:T(8,128)} %get-tuple-element.82.edge_value_far, ...), custom_call_target="tpu_custom_call" | custom-call | flops 4000000000 | bytes 1000000 | tf_op jit(solution)/shard_map/last/pallas_call | solution.py:75
  90.3 2.2 %all-to-all-done.2.tiles = f32[16,8,128]{2,1,0:T(8,128)S(1)} async-done(((f32[16,8,128]{2,1,0:T(8,128)}), f32[16,8,128]{2,1,0:T(8,128)S(1)}, u32[]{:S(2)}, u32[]{:S(2)}) %all-to-all-start.2) | async-done | bytes 65568 | tf_op jit(solution)/shard_map/all_to_all | solution.py:659
  92.4 0.7 unpack.1
  (24 shorter events, 0.1 us)
Async XLA Ops:
  3.7 13.3 %copy-start.2 = (bf16[24,48,3,3]{1,0,3,2:T(8,128)(2,1)S(1)}, bf16[24,48,3,3]{1,0,3,2:T(8,128)(2,1)}, u32[]{:S(2)}) copy-start(bf16[24,48,3,3]{1,0,3,2:T(8,128)(2,1)} %param.10) | copy-start | bytes 62212
  3.7 13.3 %copy-start.3 = (bf16[48,24]{0,1:T(8,128)(2,1)S(1)}, bf16[48,24]{0,1:T(8,128)(2,1)}, u32[]{:S(2)}) copy-start(bf16[48,24]{0,1:T(8,128)(2,1)} %param.13) | copy-start | bytes 6916
  3.7 15.4 %collective-permute-start = (bf16[8,24,8,128]{3,2,1,0:T(8,128)(2,1)S(1)}, bf16[8,24,8,128]{3,2,1,0:T(8,128)(2,1)S(1)}, u32[]{:S(2)}, u32[]{:S(2)}) collective-permute-start(bf16[8,24,8,128]{3,2,1,0:T(8,128)(2,1)S(1)} %get-tuple-element.48), channel_id=1, source_target_pairs={{0,8},{8,16},{16,24},{24,32},{32,40},{40,48},{48,56},{56,64},{64,7... | collective-permute-start | bytes 1179656 | tf_op jit(solution)/shard_map/ppermute | solution.py:579
  6.4 12.7 %collective-permute-start.1 = (bf16[8,24,8,128]{3,2,1,0:T(8,128)(2,1)S(1)}, bf16[8,24,8,128]{3,2,1,0:T(8,128)(2,1)S(1)}, u32[]{:S(2)}, u32[]{:S(2)}) collective-permute-start(bf16[8,24,8,128]{3,2,1,0:T(8,128)(2,1)S(1)} %get-tuple-element.49), channel_id=1, source_target_pairs={{8,0},{16,8},{24,16},{32,24},{40,32},{48,40},{56,48},{64,56},{72,6... | collective-permute-start | bytes 1179656 | tf_op jit(solution)/shard_map/ppermute | solution.py:579
  6.4 29.1 %all-to-all-start = ((bf16[128,3,8,128]{3,2,1,0:T(8,128)(2,1)}), bf16[128,3,8,128]{3,2,1,0:T(8,128)(2,1)S(1)}, u32[]{:S(2)}, u32[]{:S(2)}) async-start(bf16[128,3,8,128]{3,2,1,0:T(8,128)(2,1)} %bitcast.19), calls=%async_computation | async-start | bytes 1572864 | tf_op jit(solution)/shard_map/all_to_all | solution.py:592
  17.0 2.1 %copy-start.1 = (bf16[8,48,8,128]{3,2,1,0:T(8,128)(2,1)S(1)}, bf16[8,48,8,128]{3,2,1,0:T(8,128)(2,1)}, u32[]{:S(2)}) copy-start(bf16[8,48,8,128]{3,2,1,0:T(8,128)(2,1)} %x_far.3) | copy-start | bytes 2359300
  19.0 9.5 %copy-start.4 = (f32[24]{0:T(128)S(1)}, f32[24]{0:T(128)}, u32[]{:S(2)}) copy-start(f32[24]{0:T(128)} %cg.3) | copy-start | bytes 292
  19.0 9.5 %copy-start.5 = (f32[24]{0:T(128)S(1)}, f32[24]{0:T(128)}, u32[]{:S(2)}) copy-start(f32[24]{0:T(128)} %cb.3) | copy-start | bytes 292
  19.0 9.5 %copy-start.6 = (f32[48]{0:T(128)S(1)}, f32[48]{0:T(128)}, u32[]{:S(2)}) copy-start(f32[48]{0:T(128)} %mg.3) | copy-start | bytes 580
  19.1 9.5 %copy-start.7 = (f32[48]{0:T(128)S(1)}, f32[48]{0:T(128)}, u32[]{:S(2)}) copy-start(f32[48]{0:T(128)} %mb.3) | copy-start | bytes 580
  22.7 12.8 %collective-permute-start.3 = (bf16[384,128]{1,0:T(8,128)(2,1)S(1)}, bf16[384,128]{1,0:T(8,128)(2,1)S(1)}, u32[]{:S(2)}, u32[]{:S(2)}) collective-permute-start(bf16[384,128]{1,0:T(8,128)(2,1)S(1)} %get-tuple-element.57), channel_id=1, source_target_pairs={{1,0},{2,1},{3,2},{4,3},{5,4},{6,5},{7,6},{0,7},{9,8},{10,9},{11,1... | collective-permute-start | bytes 294920 | tf_op jit(solution)/shard_map/ppermute | solution.py:579
  28.5 7.1 %collective-permute-start.2 = (bf16[384,128]{1,0:T(8,128)(2,1)S(1)}, bf16[384,128]{1,0:T(8,128)(2,1)S(1)}, u32[]{:S(2)}, u32[]{:S(2)}) collective-permute-start(bf16[384,128]{1,0:T(8,128)(2,1)S(1)} %get-tuple-element.57), channel_id=1, source_target_pairs={{0,1},{1,2},{2,3},{3,4},{4,5},{5,6},{6,7},{7,0},{8,9},{9,10},{10,1... | collective-permute-start | bytes 294920 | tf_op jit(solution)/shard_map/ppermute | solution.py:579
  42.4 7.2 %collective-permute-start.4 = (bf16[8,12,8,128]{3,2,1,0:T(8,128)(2,1)S(1)}, bf16[8,12,8,128]{3,2,1,0:T(8,128)(2,1)S(1)}, u32[]{:S(2)}, u32[]{:S(2)}) collective-permute-start(bf16[8,12,8,128]{3,2,1,0:T(8,128)(2,1)S(1)} %get-tuple-element.69), channel_id=1, source_target_pairs={{0,8},{8,16},{16,24},{24,32},{32,40},{40,48},{48,56},{56,64},{64,7... | collective-permute-start | bytes 589832 | tf_op jit(solution)/shard_map/ppermute | solution.py:579
  45.3 5.4 %collective-permute-start.5 = (bf16[8,12,8,128]{3,2,1,0:T(8,128)(2,1)S(1)}, bf16[8,12,8,128]{3,2,1,0:T(8,128)(2,1)S(1)}, u32[]{:S(2)}, u32[]{:S(2)}) collective-permute-start(bf16[8,12,8,128]{3,2,1,0:T(8,128)(2,1)S(1)} %get-tuple-element.70), channel_id=1, source_target_pairs={{8,0},{16,8},{24,16},{32,24},{40,32},{48,40},{56,48},{64,56},{72,6... | collective-permute-start | bytes 589832 | tf_op jit(solution)/shard_map/ppermute | solution.py:579
  50.7 29.3 %all-to-all-start.1 = ((bf16[128,5,8,128]{3,2,1,0:T(8,128)(2,1)}), bf16[128,5,8,128]{3,2,1,0:T(8,128)(2,1)S(1)}, u32[]{:S(2)}, u32[]{:S(2)}) async-start(bf16[128,5,8,128]{3,2,1,0:T(8,128)(2,1)} %bitcast.18), calls=%async_computation.1 | async-start | bytes 2621440 | tf_op jit(solution)/shard_map/all_to_all | solution.py:654
  65.5 21.1 %collective-permute-start.7 = (f32[192,128]{1,0:T(8,128)S(1)}, f32[192,128]{1,0:T(8,128)S(1)}, u32[]{:S(2)}, u32[]{:S(2)}) collective-permute-start(f32[192,128]{1,0:T(8,128)S(1)} %get-tuple-element.78), channel_id=1, source_target_pairs={{1,0},{2,1},{3,2},{4,3},{5,4},{6,5},{7,6},{0,7},{9,8},{10,9},{11,1... | collective-permute-start | bytes 294920 | tf_op jit(solution)/shard_map/ppermute | solution.py:579
  71.3 15.3 %collective-permute-start.6 = (f32[192,128]{1,0:T(8,128)S(1)}, f32[192,128]{1,0:T(8,128)S(1)}, u32[]{:S(2)}, u32[]{:S(2)}) collective-permute-start(f32[192,128]{1,0:T(8,128)S(1)} %get-tuple-element.78), channel_id=1, source_target_pairs={{0,1},{1,2},{2,3},{3,4},{4,5},{5,6},{6,7},{7,0},{8,9},{9,10},{10,1... | collective-permute-start | bytes 294920 | tf_op jit(solution)/shard_map/ppermute | solution.py:579
  80.1 6.6 %copy-start = (bf16[128,5,8,128]{3,2,1,0:T(8,128)(2,1)}, bf16[128,5,8,128]{3,2,1,0:T(8,128)(2,1)S(1)}, u32[]{:S(2)}) copy-start(bf16[128,5,8,128]{3,2,1,0:T(8,128)(2,1)S(1)} %all-to-all-done.1) | copy-start | bytes 3932164
  80.9 11.5 %all-to-all-start.2 = ((f32[16,8,128]{2,1,0:T(8,128)}), f32[16,8,128]{2,1,0:T(8,128)S(1)}, u32[]{:S(2)}, u32[]{:S(2)}) async-start(f32[16,8,128]{2,1,0:T(8,128)} %total.1), calls=%async_computation.2 | async-start | bytes 131072 | tf_op jit(solution)/shard_map/all_to_all | solution.py:659

commit v6 on v5

--- a/solution.py
+++ b/solution.py
@@ -28,6 +28,13 @@
     s = v * v
     t = jnp.tanh(TANH_SCALE * (v + CUBIC * (v * s)))
     return 0.5 * (1.0 + t) + (0.5 * v) * (1.0 - t * t) * (TANH_SCALE * (1.0 + (3.0 * CUBIC) * s))
+
+
+def smooth_both(v):
+    s = v * v
+    t = jnp.tanh(TANH_SCALE * (v + CUBIC * (v * s)))
+    upper, half = 0.5 * (1.0 + t), 0.5 * v
+    return half * (1.0 + t), upper + half * (1.0 - t * t) * (TANH_SCALE * (1.0 + (3.0 * CUBIC) * s))
 
 
 def dot(a, b, dims=NN):
@@ -162,16 +169,16 @@
 
 def first_kernel(x_far, d_far, down, up, pieces, x, d, turned, sems):
     far = Far(sems)
-    loads = [far.start(x_far.at[g], x.at[g]) for g in range(GROUPS)]
-    later = [far.start(d_far.at[g], d.at[g]) for g in range(GROUPS)]
-    for load in loads:
-        load.wait()
-    send_rows(x, down, up, CH)
+    loads = [far.start(d_far.at[g], d.at[g]) for g in range(GROUPS)]
+    later = [far.start(x_far.at[g], x.at[g]) for g in range(GROUPS)]
     for g in range(GROUPS):
-        later[g].wait()
+        loads[g].wait()
         for k in range(3):
             turned[:, g, k] = turn(d[g, k * ROWS : (k + 1) * ROWS])
         far.send(turned.at[:, g], pieces.at[:, g])
+    for load in later:
+        load.wait()
+    send_rows(x, down, up, CH)
     far.finish()
 
 
@@ -194,11 +201,16 @@
     sf, st = spread_channels(CH, CR, 2 * CR), spread_channels(MID, MR, MR)
     pf, pt = row_distance(CR, 2 * CR), row_distance(MR, MR)
     masks = [jnp.where(pf == 4 * (a - 1), 1.0, 0.0)[None] for a in range(3)]
+    col = iota((CH, CR), 1)
+    above = jnp.where(col < CR // 2, sf[:, CR:].astype(F32), 0.0).astype(BF)
+    below = jnp.where(col < CR // 2, 0.0, sf[:, CR:].astype(F32)).astype(BF)
     for b in range(3):
-        total = jnp.zeros((MID, H, 2 * CR), F32)
+        total = jnp.zeros((MID, H, CR), F32)
         for a in range(3):
-            total += dot(w[3 * a + b], sf)[:, None, :] * masks[a]
-        a_out[b * MR : (b + 1) * MR] = total.reshape(MR, 2 * CR).astype(BF)
+            total += dot(w[3 * a + b], sf[:, :CR])[:, None, :] * masks[a][:, :, :CR]
+        rest = (dot(w[b], above) + dot(w[6 + b], below))[:, None, :] * (masks[0] + masks[2])[:, :, CR:]
+        a_out[b * MR : (b + 1) * MR, 0:CR] = total.reshape(MR, CR).astype(BF)
+        a_out[b * MR : (b + 1) * MR, CR : 2 * CR] = rest.reshape(MR, CR).astype(BF)
     far.send(a_out, a_far)
     mask = jnp.where(pf[:, :CR] == 0, 1.0, 0.0)
     mb_out[...] = (dot(mix[...], sf[:, :CR])[:, None, :] * mask[None]).reshape(MR, CR).astype(BF)
@@ -239,10 +251,10 @@
             to = slice((m * GROUPS + g) * LANES, (m * GROUPS + g + 1) * LANES)
             for p, (start, step) in enumerate(((CR, 4), (0, 8), (4, 8), (CR + CR // 2, 4))):
                 wide[64 * p : 64 * p + CH, to] = rows[pl.ds(start + m, CH, stride=step), :].astype(BF)
+            far.send(wide.at[:, to], wide_far.at[:, to])
         packed = jnp.where(lane // 8 == g, pltpu.roll(own, (8 * g - 124) % LANES, 1), packed)
         packed = jnp.where(lane // 8 == 8 + g, pltpu.roll(rim, (8 * g - 60) % LANES, 1), packed)
     edge[...] = packed.astype(BF)
-    far.send(wide, wide_far)
     far.finish()
 
 
@@ -286,8 +298,9 @@
             packed = jnp.where(lane // 8 == g, pltpu.roll(inner, (8 * g - 124) % LANES, 1), packed)
             pre = inner * gain + shift
             at = slice(g * LANES, (g + 1) * LANES)
-            slope[:, at] = smooth_slope(pre) * gain
-            hidden[:, at] = smooth(pre).astype(BF)
+            smoothed, steep = smooth_both(pre)
+            slope[:, at] = steep * gain
+            hidden[:, at] = smoothed.astype(BF)
         far.send(slope.at[:, two], slope_far.at[:, two])
         far.send(hidden.at[:, two], hidden_far.at[:, two])
         mixed = dot(mixer[...], hidden[:, two])
@@ -321,8 +334,8 @@
 
 def inner_kernel(
     d_far, arrived, slope_far, hidden_far, edge_inner_far, edge_x_far, from_left, from_right,
-    weights_far, mixer_far, back_far, pieces_in, cg, cb, mg, mb,
-    grad_inner_far, down, up, half_sum_far, pieces_far, edge_block_far, gmi, taps_out, hidden_out, rim_wide,
+    weights_far, mixer_far, back_far, pieces_in, cg, cb, mg, mb, wide_far,
+    grad_inner_far, down, up, half_sum_far, pieces_far, edge_block_far, gmi, taps_out, hidden_out, rim_wide, wide,
     d, slope, hidden, edge_inner, edge_x, weights, mixer, back, grad_inner, half_sum, ends, edge_block, buffer, rows, sems,
 ):
     far = Far(sems)
@@ -334,6 +347,7 @@
         far.start(pieces_in.at[r, :, 2:5], ends.at[i]) for i, r in enumerate((0, ROWS - 1))
     ]
     later = [far.start(back_far, back), far.start(slope_far, slope), far.start(hidden_far, hidden)]
+    far.send(wide_far, wide)
     lane, lane_c = lanes_of(MR), lanes_of(CR)
     gain, shift = splat(cg, MID), splat(cb, MID)
     gain_out, shift_out = splat(mg, CH), splat(mb, CH)
@@ -363,8 +377,9 @@
     outer = dot(weights[:, 0:CR], rim) + pltpu.roll(dot(weights[:, CR : 2 * CR], rim), 64, 1)
     outer = jnp.where(lane % 8 < 4, outer[MR : 2 * MR], outer[0:MR])
     pre = (edge_inner[...] + outer) * gain + shift
-    slope_edge = smooth_slope(pre) * gain
-    hidden_edge = smooth(pre).astype(BF)
+    hidden_edge, slope_edge = smooth_both(pre)
+    slope_edge = slope_edge * gain
+    hidden_edge = hidden_edge.astype(BF)
     mixed = dot(mixer[...], hidden_edge)
     value = (edge_x[...] + mixed * gain_out + shift_out).astype(BF)
     edge_block[...] = value.astype(F32)
@@ -427,11 +442,21 @@
     far.finish()
 
 
-def sums_kernel(wide_far, gmi, taps, hidden, rim_wide, pieces_in, pieces_far, wide, sums_out, sems):
+def holder(t, yh, zh, xh):
+    xl, yl, core, zl = t // 8, t // 4 % 2, t // 2 % 2, t % 2
+    return (4 * xl + 2 * yh + yl) * 2 + core, 4 * zh + 2 * zl + xh
+
+
+def holders(t):
+    return [holder(t, *at) for at in near_groups()]
+
+
+def near_groups():
+    return [(yh, zh, xh) for yh in range(2) for zh in range(2) for xh in range(2)]
+
+
+def sums_kernel(wide, gmi, taps, hidden, rim_wide, pieces_in, pieces_far, sums_out, sems):
     far = Far(sems)
-    load = far.start(wide_far, wide)
-    sums_out[ROWS - 1] = jnp.zeros((COLS, 2, H, LANES), BF)
-    far.send(sums_out.at[ROWS - 1], pieces_far.at[ROWS - 1, :, 0:2])
     mixwide = dot(hidden[...], gmi[...], NT)
     h, col = iota((H, CR), 0), iota((H, CR), 1)
     same = jnp.where(col % 8 == h, 1.0, 0.0)[None]
@@ -439,7 +464,6 @@
     col, lane_s = iota((CR, LANES), 0), iota((CR, LANES), 1)
     mixed = exact_dot(mixed, jnp.where(col // 8 + 64 == lane_s, 1.0, 0.0).astype(BF))
     total = dot(taps[:, 4 * POS :], rim_wide[...], NT)
-    load.wait()
     total += dot(taps[:, 0 : 4 * POS], wide[...], NT)
     lane = lanes_of(MID)
     blocks, thirds = [], []
@@ -451,15 +475,16 @@
         thirds.append(jnp.where(lane < 64, near[:, LANES : 2 * LANES] + ahead, 0.0))
     blocks.append(thirds[0] + pltpu.roll(thirds[1], 64, 1))
     blocks.append(thirds[2] + mixed)
-    for p in range(5):
-        high = blocks[p].astype(BF).astype(F32)
-        low = blocks[p] - high
-        for k in range(3):
-            r = 3 * p + k
-            at = slice(k * H, (k + 1) * H)
-            sums_out[r, :, 0] = jnp.broadcast_to(high[at][None], (COLS, H, LANES)).astype(BF)
-            sums_out[r, :, 1] = jnp.broadcast_to(low[at][None], (COLS, H, LANES)).astype(BF)
-        far.send(sums_out.at[3 * p : 3 * p + 3], pieces_far.at[3 * p : 3 * p + 3, :, 0:2])
+    blocks.append(jnp.zeros((MID, LANES), F32))
+    for t in range(ROWS):
+        part = blocks[t // 3][t % 3 * H : (t % 3 + 1) * H]
+        high = part.astype(BF).astype(F32)
+        both = jnp.concatenate([high[None], (part - high)[None]], axis=0).astype(BF)
+        for r, c in holders(t):
+            sums_out[r, c] = both
+        if t % 2:
+            for r in sorted({r for r, _ in holders(t)}):
+                far.send(sums_out.at[r], pieces_far.at[r, :, 0:2])
     far.finish()
 
 
@@ -601,7 +626,7 @@
     act, edge, wide = call(
         act_kernel,
         [((2 * CR, POS), BF), ((CR, LANES), BF), ((256, 4 * POS), BF)],
-        (pair_map, above, below), "act", far_out=(2,), copies=1,
+        (pair_map, above, below), "act", far_out=(2,), copies=4 * GROUPS,
         scratch=[vmem((256, 4 * POS), BF), vmem((2 * CR, LANES), F32)],
     )
     from_left, from_right = both_ways(edge, edge, "col")
@@ -617,7 +642,7 @@
         ],
         copies=2 * GROUPS + 2,
     )
-    grad_inner, g_down, g_up, half_sum, pieces, edge_block, gmi, tap_rows, hidden, rim_wide = call(
+    grad_inner, g_down, g_up, half_sum, pieces, edge_block, gmi, tap_rows, hidden, rim_wide, wide = call(
         inner_kernel,
         [
             ((GROUPS, MID, H, LANES), BF),
@@ -630,25 +655,25 @@
             ((192, 4 * POS + 4 * LANES), BF),
             ((MR, POS), BF),
             ((256, 4 * LANES), BF),
+            ((256, 4 * POS), BF),
         ],
         (
             cotangent, d_arrived, slope, hidden, edge_inner, edge_x, from_left, from_right,
-            wf_far, mf_far, mbk, pieces, conv_gain, conv_bias, mix_gain, mix_bias,
+            wf_far, mf_far, mbk, pieces, conv_gain, conv_bias, mix_gain, mix_bias, wide,
         ),
-        "inner", smem=(12, 13, 14, 15), far=(0, 2, 3, 4, 5, 8, 9, 10, 11), far_out=(0, 3, 4, 5), alias={11: 4},
+        "inner", smem=(12, 13, 14, 15), far=(0, 2, 3, 4, 5, 8, 9, 10, 11, 16), far_out=(0, 3, 4, 5), alias={11: 4},
         scratch=[
             vmem(tile, BF), vmem((MR, POS), F32), vmem((MR, POS), BF), vmem((MR, LANES), F32), vmem((CR, LANES), F32),
             vmem((2 * MR, 2 * CR), BF), vmem((CR, MR), BF), vmem((MR, CR), BF),
             vmem((GROUPS, MID, H, LANES), BF), vmem(tile, F32), vmem((2, COLS, 3, H, LANES), BF),
             vmem((CR, LANES), F32), vmem((2, CH, H, LANES), BF), vmem((CR, LANES), F32),
         ],
-        copies=25,
+        copies=26,
     )
     g_above, g_below = both_ways(g_down, g_up, "row")
     (pieces,) = call(
         sums_kernel, [(five, BF)], (wide, gmi, tap_rows, hidden, rim_wide, pieces), "sums",
-        far=(0, 5), far_out=(0,), alias={5: 0},
-        scratch=[vmem((256, 4 * POS), BF), vmem((ROWS, COLS, 2, H, LANES), BF)], copies=7,
+        far=(5,), far_out=(0,), alias={5: 0}, scratch=[vmem((ROWS, COLS, 2, H, LANES), BF)], copies=ROWS,
     )
     pieces, g_above, g_below = lax.optimization_barrier((pieces, g_above, g_below))
     arrived = lax.all_to_all(pieces.reshape(ROWS * COLS, 5, H, LANES), everyone, 0, 0, tiled=True)
@@ -656,7 +681,8 @@
     (sums,) = call(
         total_kernel, [((ROWS, H, LANES), F32)], (arrived,), "total", flops=500_000_000
     )
-    spread_sums = lax.all_to_all(sums, "row", 0, 0, tiled=True)
+    groups = [[r * COLS + c for r, c in (holder(t, *at) for t in range(ROWS))] for at in near_groups()]
+    spread_sums = lax.all_to_all(sums, everyone, 0, 0, axis_index_groups=groups, tiled=True)
     taps, _ = lax.optimization_barrier((taps, pieces))
     g_edge, inputs, edge_value, edge_slope, block = call(
         spread_kernel,

time: 93.6 us -> 91.9 us (0.982)
  Pallas kernels: 37.5 us -> 35.1 us
  waiting for transfers between devices: 12.2 us -> 13.6 us
    pallas_call x10, Pallas kernels: 37.5 us -> 35.1 us  [call(): pl.pallas_call(kernel, name=name, out_shape=[pltpu.HBM(s, t) if i in far_...]
    ppermute x8, waiting for transfers between devices: 1.26 us -> 3.06 us  [both_ways(): return (lax.ppermute(first, axis, onward), lax.ppermute(second, axis, back))]
  transfers between devices with their start and end apart: 11 -> 11, of which waited for: 4 -> 5; matrix products, arithmetic and copies ran while one was open for 0% -> 0% of each run, Pallas kernels for 29% -> 27%
where the time goes in v6:
time: 91.9 us; the launch traced here: 91.5 us
  starting transfers between devices  41.9 us (46%)
  Pallas kernels  35.1 us (38%)
  waiting for transfers between devices  13.6 us (15%)
    pallas_call x10, Pallas kernels, call(): pl.pallas_call(kernel, name=name, out_shape=[pltpu.HBM(s, t) if i in far_...  35.1 us
    ppermute x8, starting transfers between devices, both_ways(): return (lax.ppermute(first, axis, onward), lax.ppermute(second, axis, back))  17.3 us
    all_to_all x1, starting transfers between devices, local(): lax.all_to_all(d_pieces.reshape(ROWS * COLS, 3, H, LANES), everyone, 0, 0...  10.6 us
    all_to_all x1, starting transfers between devices, local(): lax.all_to_all(pieces.reshape(ROWS * COLS, 5, H, LANES), everyone, 0, 0,...  9 us
    all_to_all x1, waiting for transfers between devices, local(): lax.all_to_all(pieces.reshape(ROWS * COLS, 5, H, LANES), everyone, 0, 0,...  8.76 us
    all_to_all x1, starting transfers between devices, local(): lax.all_to_all(sums, everyone, 0, 0, axis_index_groups=groups, tiled=True)  5.11 us
    ppermute x8, waiting for transfers between devices, both_ways(): return (lax.ppermute(first, axis, onward), lax.ppermute(second, axis, back))  3.06 us
  transfers between devices with their start and end apart: 11, of which 5 were waited for; matrix products, arithmetic and copies ran while one was open for 0% of the time, Pallas kernels for 27%

profile of v6, /device:TPU:1, one launch (start us, length us, event | category | flops | bytes accessed | tf_op | source)
XLA Modules:
  0.0 91.5 jit_solution(12879483126954429540)
XLA Ops:
  0.6 2.5 %first.1 = (bf16[8,24,8,128]{3,2,1,0:T(8,128)(2,1)S(1)}, bf16[8,24,8,128]{3,2,1,0:T(8,128)(2,1)S(1)}, bf16[16,8,3,8,128]{4,3,2,1,0:T(8,128)(2,1)}) custom-call(bf16[8,48,8,128]{3,2,1,0:T(8,128)(2,1)} %x_far.3, bf16[8,48,8,128]{3,2,1,0:T(8,128)(2,1)} %d_far.3), custom_call_target="tpu_custom_call" | custom-call | flops 4000000000 | bytes 1000000 | tf_op jit(solution)/shard_map/first/pallas_call | solution.py:82
  3.1 0.0 copy-start.2
  3.1 2.8 %collective-permute-start = (bf16[8,24,8,128]{3,2,1,0:T(8,128)(2,1)S(1)}, bf16[8,24,8,128]{3,2,1,0:T(8,128)(2,1)S(1)}, u32[]{:S(2)}, u32[]{:S(2)}) collective-permute-start(bf16[8,24,8,128]{3,2,1,0:T(8,128)(2,1)S(1)} %get-tuple-element.49), channel_id=1, source_target_pairs={{0,8},{8,16},{16,24},{24,32},{32,40},{40,48},{48,56},{56,64},{64,7... | collective-permute-start | bytes 1179656 | tf_op jit(solution)/shard_map/ppermute | solution.py:604
  5.9 10.6 %all-to-all-start = ((bf16[128,3,8,128]{3,2,1,0:T(8,128)(2,1)}), bf16[128,3,8,128]{3,2,1,0:T(8,128)(2,1)S(1)}, u32[]{:S(2)}, u32[]{:S(2)}) async-start(bf16[128,3,8,128]{3,2,1,0:T(8,128)(2,1)} %bitcast.19), calls=%async_computation | async-start | bytes 1572864 | tf_op jit(solution)/shard_map/all_to_all | solution.py:617
  16.5 1.7 %weights.1 = (bf16[576,768]{1,0:T(8,128)(2,1)S(1)}, bf16[384,192]{1,0:T(8,128)(2,1)S(1)}, bf16[576,768]{1,0:T(8,128)(2,1)}, bf16[384,192]{1,0:T(8,128)(2,1)}, bf16[192,384]{1,0:T(8,128)(2,1)}) custom-call(bf16[9,24,48]{2,1,0:T(8,128)(2,1)S(1)} %bitcast.15, bf16[24,48]{1,0:T(8,128)(2,1)S(1)} %bitcast.17), custom_call_target="tpu_custom_call" | custom-call | flops 4000000000 | bytes 1000000 | tf_op jit(solution)/shard_map/weights/pallas_call | solution.py:82
  18.2 0.0 copy-start.4
  18.2 3.8 %act.1 = (bf16[768,1024]{1,0:T(8,128)(2,1)S(1)}, bf16[384,128]{1,0:T(8,128)(2,1)S(1)}, bf16[256,4096]{1,0:T(8,128)(2,1)}) custom-call(bf16[8,48,8,128]{3,2,1,0:T(8,128)(2,1)S(1)} %copy-done.1, bf16[8,24,8,128]{3,2,1,0:T(8,128)(2,1)S(1)} %collective-permute-done.above, bf16[8,24,8,128]{3,2,1,0:T(8,128)(2,1)S(1)} %collective-permute-done.1.below), custom_call_target="tpu_custom_call" | custom-call | flops 4000000000 | bytes 1000000 | tf_op jit(solution)/shard_map/act/pallas_call | solution.py:82
  22.1 5.8 %collective-permute-start.3 = (bf16[384,128]{1,0:T(8,128)(2,1)S(1)}, bf16[384,128]{1,0:T(8,128)(2,1)S(1)}, u32[]{:S(2)}, u32[]{:S(2)}) collective-permute-start(bf16[384,128]{1,0:T(8,128)(2,1)S(1)} %get-tuple-element.58), channel_id=1, source_target_pairs={{1,0},{2,1},{3,2},{4,3},{5,4},{6,5},{7,6},{0,7},{9,8},{10,9},{11,1... | collective-permute-start | bytes 294920 | tf_op jit(solution)/shard_map/ppermute | solution.py:604
  27.8 7.0 %inside.1 = (f32[192,1024]{1,0:T(8,128)}, bf16[192,1024]{1,0:T(8,128)(2,1)}, bf16[8,48,8,128]{3,2,1,0:T(8,128)(2,1)}, bf16[16,8,5,8,128]{4,3,2,1,0:T(8,128)(2,1)...) custom-call(bf16[8,48,8,128]{3,2,1,0:T(8,128)(2,1)S(1)} %copy-done.1, bf16[768,1024]{1,0:T(8,128)(2,1)S(1)} %get-tuple-element.51.act, ...), custom_call_target="tpu_custom_call" | custom-call | flops 4000000000 | bytes 1000000 | tf_op jit(solution)/shard_map/inside/pallas_call | solution.py:82
  34.8 0.1 collective-permute-done.2.from_left
  34.9 6.8 %inner.1 = (bf16[8,24,8,128]{3,2,1,0:T(8,128)(2,1)}, bf16[8,12,8,128]{3,2,1,0:T(8,128)(2,1)S(1)}, bf16[8,12,8,128]{3,2,1,0:T(8,128)(2,1)S(1)}, f32[8,48,8,128]{3...) custom-call(bf16[8,48,8,128]{3,2,1,0:T(8,128)(2,1)} %d_far.3, ...), custom_call_target="tpu_custom_call", output_to_operand_aliasing={{4}: (11, {})} | custom-call | flops 4000000000 | bytes 1000000 | tf_op jit(solution)/shard_map/inner/pallas_call | solution.py:82
  41.7 3.0 %collective-permute-start.4 = (bf16[8,12,8,128]{3,2,1,0:T(8,128)(2,1)S(1)}, bf16[8,12,8,128]{3,2,1,0:T(8,128)(2,1)S(1)}, u32[]{:S(2)}, u32[]{:S(2)}) collective-permute-start(bf16[8,12,8,128]{3,2,1,0:T(8,128)(2,1)S(1)} %get-tuple-element.71), channel_id=1, source_target_pairs={{0,8},{8,16},{16,24},{24,32},{32,40},{40,48},{48,56},{56,64},{64,7... | collective-permute-start | bytes 589832 | tf_op jit(solution)/shard_map/ppermute | solution.py:604
  44.7 2.4 %sums.1 = bf16[16,8,5,8,128]{4,3,2,1,0:T(8,128)(2,1)} custom-call(bf16[256,4096]{1,0:T(8,128)(2,1)S(1)} %get-tuple-element.65.wide, bf16[384,1024]{1,0:T(8,128)(2,1)S(1)} %get-tuple-element.66.gmi, bf16[192,4608]{1,0:T(8,128)(2,1)S(1)} %get-tuple-element.67.taps, bf16[192,1024]{1,0:T(8,128)(2,1)S(1)} %get-tuple-element.68.hidden, ...), custom_call_target="tpu_custom_call", output_to_operand_aliasing={{}: (5, {})} | custom-call | flops 4000000000 | bytes 1000000 | tf_op jit(solution)/shard_map/sums/pallas_call | solution.py:82
  47.1 0.2 collective-permute-done.4.above
  47.3 2.8 %collective-permute-done.5.below = bf16[8,12,8,128]{3,2,1,0:T(8,128)(2,1)S(1)} collective-permute-done((bf16[8,12,8,128]{3,2,1,0:T(8,128)(2,1)S(1)}, bf16[8,12,8,128]{3,2,1,0:T(8,128)(2,1)S(1)}, u32[]{:S(2)}, u32[]{:S(2)}) %collective-permute-start.5) | collective-permute-done | bytes 196640 | tf_op jit(solution)/shard_map/ppermute | solution.py:604
  50.1 9.0 %all-to-all-start.1 = ((bf16[128,5,8,128]{3,2,1,0:T(8,128)(2,1)}), bf16[128,5,8,128]{3,2,1,0:T(8,128)(2,1)S(1)}, u32[]{:S(2)}, u32[]{:S(2)}) async-start(bf16[128,5,8,128]{3,2,1,0:T(8,128)(2,1)} %bitcast.18), calls=%async_computation.1 | async-start | bytes 2621440 | tf_op jit(solution)/shard_map/all_to_all | solution.py:679
  59.1 5.8 %spread.1 = (f32[192,128]{1,0:T(8,128)S(1)}, bf16[8,48,8,128]{3,2,1,0:T(8,128)(2,1)}, f32[384,128]{1,0:T(8,128)}, f32[384,128]{1,0:T(8,128)}, bf16[8,48,8,128]{3,2,1,0:T(8,128)(2,1)}) custom-call(bf16[8,24,8,128]{3,2,1,0:T(8,128)(2,1)} %get-tuple-element.64.grad_inner_far, bf16[8,12,8,128]{3,2,1,0:T(8,128)(2,1)S(1)} %collective-permute-done.4.above, ...), custom_call_target="tpu_custom_call" | custom-call | flops 4000000000 | bytes 1000000 | tf_op jit(solution)/shard_map/spread/pallas_call | solution.py:82
  64.9 5.8 %collective-permute-start.7 = (f32[192,128]{1,0:T(8,128)S(1)}, f32[192,128]{1,0:T(8,128)S(1)}, u32[]{:S(2)}, u32[]{:S(2)}) collective-permute-start(f32[192,128]{1,0:T(8,128)S(1)} %get-tuple-element.80), channel_id=1, source_target_pairs={{1,0},{2,1},{3,2},{4,3},{5,4},{6,5},{7,6},{0,7},{9,8},{10,9},{11,1... | collective-permute-start | bytes 294920 | tf_op jit(solution)/shard_map/ppermute | solution.py:604
  70.6 8.8 %all-to-all-done.1 = bf16[128,5,8,128]{3,2,1,0:T(8,128)(2,1)S(1)} async-done(((bf16[128,5,8,128]{3,2,1,0:T(8,128)(2,1)}), bf16[128,5,8,128]{3,2,1,0:T(8,128)(2,1)S(1)}, u32[]{:S(2)}, u32[]{:S(2)}) %all-to-all-start.1) | async-done | bytes 1310752 | tf_op jit(solution)/shard_map/all_to_all | solution.py:679
  79.4 0.8 total.1
  80.2 5.1 %all-to-all-start.2 = ((f32[16,8,128]{2,1,0:T(8,128)}), f32[16,8,128]{2,1,0:T(8,128)S(1)}, u32[]{:S(2)}, u32[]{:S(2)}) async-start(f32[16,8,128]{2,1,0:T(8,128)} %total.1), calls=%async_computation.2 | async-start | bytes 131072 | tf_op jit(solution)/shard_map/all_to_all | solution.py:685
  85.4 3.6 %last.1 = (bf16[8,48,8,128]{3,2,1,0:T(8,128)(2,1)}, bf16[8,48,8,128]{3,2,1,0:T(8,128)(2,1)}) custom-call(bf16[8,48,8,128]{3,2,1,0:T(8,128)(2,1)} %get-tuple-element.82.block_far, bf16[16,8,5,8,128]{4,3,2,1,0:T(8,128)(2,1)} %bitcast.13, bf16[8,48,8,128]{3,2,1,0:T(8,128)(2,1)} %get-tuple-element.83.value_far, f32[384,128]{1,0:T(8,128)} %get-tuple-element.84.edge_value_far, ...), custom_call_target="tpu_custom_call" | custom-call | flops 4000000000 | bytes 1000000 | tf_op jit(solution)/shard_map/last/pallas_call | solution.py:82
  89.0 1.8 %all-to-all-done.2.tiles = f32[16,8,128]{2,1,0:T(8,128)S(1)} async-done(((f32[16,8,128]{2,1,0:T(8,128)}), f32[16,8,128]{2,1,0:T(8,128)S(1)}, u32[]{:S(2)}, u32[]{:S(2)}) %all-to-all-start.2) | async-done | bytes 65568 | tf_op jit(solution)/shard_map/all_to_all | solution.py:685
  90.8 0.7 unpack.1
  (24 shorter events, 0.1 us)
Async XLA Ops:
  3.1 13.3 %copy-start.2 = (bf16[24,48,3,3]{1,0,3,2:T(8,128)(2,1)S(1)}, bf16[24,48,3,3]{1,0,3,2:T(8,128)(2,1)}, u32[]{:S(2)}) copy-start(bf16[24,48,3,3]{1,0,3,2:T(8,128)(2,1)} %param.10) | copy-start | bytes 62212
  3.1 13.3 %copy-start.3 = (bf16[48,24]{0,1:T(8,128)(2,1)S(1)}, bf16[48,24]{0,1:T(8,128)(2,1)}, u32[]{:S(2)}) copy-start(bf16[48,24]{0,1:T(8,128)(2,1)} %param.13) | copy-start | bytes 6916
  3.1 15.1 %collective-permute-start = (bf16[8,24,8,128]{3,2,1,0:T(8,128)(2,1)S(1)}, bf16[8,24,8,128]{3,2,1,0:T(8,128)(2,1)S(1)}, u32[]{:S(2)}, u32[]{:S(2)}) collective-permute-start(bf16[8,24,8,128]{3,2,1,0:T(8,128)(2,1)S(1)} %get-tuple-element.49), channel_id=1, source_target_pairs={{0,8},{8,16},{16,24},{24,32},{32,40},{40,48},{48,56},{56,64},{64,7... | collective-permute-start | bytes 1179656 | tf_op jit(solution)/shard_map/ppermute | solution.py:604
  5.9 12.3 %collective-permute-start.1 = (bf16[8,24,8,128]{3,2,1,0:T(8,128)(2,1)S(1)}, bf16[8,24,8,128]{3,2,1,0:T(8,128)(2,1)S(1)}, u32[]{:S(2)}, u32[]{:S(2)}) collective-permute-start(bf16[8,24,8,128]{3,2,1,0:T(8,128)(2,1)S(1)} %get-tuple-element.50), channel_id=1, source_target_pairs={{8,0},{16,8},{24,16},{32,24},{40,32},{48,40},{56,48},{64,56},{72,6... | collective-permute-start | bytes 1179656 | tf_op jit(solution)/shard_map/ppermute | solution.py:604
  5.9 29.0 %all-to-all-start = ((bf16[128,3,8,128]{3,2,1,0:T(8,128)(2,1)}), bf16[128,3,8,128]{3,2,1,0:T(8,128)(2,1)S(1)}, u32[]{:S(2)}, u32[]{:S(2)}) async-start(bf16[128,3,8,128]{3,2,1,0:T(8,128)(2,1)} %bitcast.19), calls=%async_computation | async-start | bytes 1572864 | tf_op jit(solution)/shard_map/all_to_all | solution.py:617
  16.5 1.8 %copy-start.1 = (bf16[8,48,8,128]{3,2,1,0:T(8,128)(2,1)S(1)}, bf16[8,48,8,128]{3,2,1,0:T(8,128)(2,1)}, u32[]{:S(2)}) copy-start(bf16[8,48,8,128]{3,2,1,0:T(8,128)(2,1)} %x_far.3) | copy-start | bytes 2359300
  18.2 9.7 %copy-start.4 = (f32[24]{0:T(128)S(1)}, f32[24]{0:T(128)}, u32[]{:S(2)}) copy-start(f32[24]{0:T(128)} %cg.3) | copy-start | bytes 292
  18.2 9.7 %copy-start.5 = (f32[24]{0:T(128)S(1)}, f32[24]{0:T(128)}, u32[]{:S(2)}) copy-start(f32[24]{0:T(128)} %cb.3) | copy-start | bytes 292
  18.2 9.6 %copy-start.6 = (f32[48]{0:T(128)S(1)}, f32[48]{0:T(128)}, u32[]{:S(2)}) copy-start(f32[48]{0:T(128)} %mg.3) | copy-start | bytes 580
  18.2 9.6 %copy-start.7 = (f32[48]{0:T(128)S(1)}, f32[48]{0:T(128)}, u32[]{:S(2)}) copy-start(f32[48]{0:T(128)} %mb.3) | copy-start | bytes 580
  22.1 12.8 %collective-permute-start.3 = (bf16[384,128]{1,0:T(8,128)(2,1)S(1)}, bf16[384,128]{1,0:T(8,128)(2,1)S(1)}, u32[]{:S(2)}, u32[]{:S(2)}) collective-permute-start(bf16[384,128]{1,0:T(8,128)(2,1)S(1)} %get-tuple-element.58), channel_id=1, source_target_pairs={{1,0},{2,1},{3,2},{4,3},{5,4},{6,5},{7,6},{0,7},{9,8},{10,9},{11,1... | collective-permute-start | bytes 294920 | tf_op jit(solution)/shard_map/ppermute | solution.py:604
  27.8 7.1 %collective-permute-start.2 = (bf16[384,128]{1,0:T(8,128)(2,1)S(1)}, bf16[384,128]{1,0:T(8,128)(2,1)S(1)}, u32[]{:S(2)}, u32[]{:S(2)}) collective-permute-start(bf16[384,128]{1,0:T(8,128)(2,1)S(1)} %get-tuple-element.58), channel_id=1, source_target_pairs={{0,1},{1,2},{2,3},{3,4},{4,5},{5,6},{6,7},{7,0},{8,9},{9,10},{10,1... | collective-permute-start | bytes 294920 | tf_op jit(solution)/shard_map/ppermute | solution.py:604
  41.7 5.6 %collective-permute-start.4 = (bf16[8,12,8,128]{3,2,1,0:T(8,128)(2,1)S(1)}, bf16[8,12,8,128]{3,2,1,0:T(8,128)(2,1)S(1)}, u32[]{:S(2)}, u32[]{:S(2)}) collective-permute-start(bf16[8,12,8,128]{3,2,1,0:T(8,128)(2,1)S(1)} %get-tuple-element.71), channel_id=1, source_target_pairs={{0,8},{8,16},{16,24},{24,32},{32,40},{40,48},{48,56},{56,64},{64,7... | collective-permute-start | bytes 589832 | tf_op jit(solution)/shard_map/ppermute | solution.py:604
  44.7 5.4 %collective-permute-start.5 = (bf16[8,12,8,128]{3,2,1,0:T(8,128)(2,1)S(1)}, bf16[8,12,8,128]{3,2,1,0:T(8,128)(2,1)S(1)}, u32[]{:S(2)}, u32[]{:S(2)}) collective-permute-start(bf16[8,12,8,128]{3,2,1,0:T(8,128)(2,1)S(1)} %get-tuple-element.72), channel_id=1, source_target_pairs={{8,0},{16,8},{24,16},{32,24},{40,32},{48,40},{56,48},{64,56},{72,6... | collective-permute-start | bytes 589832 | tf_op jit(solution)/shard_map/ppermute | solution.py:604
  50.1 29.3 %all-to-all-start.1 = ((bf16[128,5,8,128]{3,2,1,0:T(8,128)(2,1)}), bf16[128,5,8,128]{3,2,1,0:T(8,128)(2,1)S(1)}, u32[]{:S(2)}, u32[]{:S(2)}) async-start(bf16[128,5,8,128]{3,2,1,0:T(8,128)(2,1)} %bitcast.18), calls=%async_computation.1 | async-start | bytes 2621440 | tf_op jit(solution)/shard_map/all_to_all | solution.py:679
  64.9 20.5 %collective-permute-start.7 = (f32[192,128]{1,0:T(8,128)S(1)}, f32[192,128]{1,0:T(8,128)S(1)}, u32[]{:S(2)}, u32[]{:S(2)}) collective-permute-start(f32[192,128]{1,0:T(8,128)S(1)} %get-tuple-element.80), channel_id=1, source_target_pairs={{1,0},{2,1},{3,2},{4,3},{5,4},{6,5},{7,6},{0,7},{9,8},{10,9},{11,1... | collective-permute-start | bytes 294920 | tf_op jit(solution)/shard_map/ppermute | solution.py:604
  70.6 14.7 %collective-permute-start.6 = (f32[192,128]{1,0:T(8,128)S(1)}, f32[192,128]{1,0:T(8,128)S(1)}, u32[]{:S(2)}, u32[]{:S(2)}) collective-permute-start(f32[192,128]{1,0:T(8,128)S(1)} %get-tuple-element.80), channel_id=1, source_target_pairs={{0,1},{1,2},{2,3},{3,4},{4,5},{5,6},{6,7},{7,0},{8,9},{9,10},{10,1... | collective-permute-start | bytes 294920 | tf_op jit(solution)/shard_map/ppermute | solution.py:604
  79.4 6.0 %copy-start = (bf16[128,5,8,128]{3,2,1,0:T(8,128)(2,1)}, bf16[128,5,8,128]{3,2,1,0:T(8,128)(2,1)S(1)}, u32[]{:S(2)}) copy-start(bf16[128,5,8,128]{3,2,1,0:T(8,128)(2,1)S(1)} %all-to-all-done.1) | copy-start | bytes 3932164
  80.2 10.6 %all-to-all-start.2 = ((f32[16,8,128]{2,1,0:T(8,128)}), f32[16,8,128]{2,1,0:T(8,128)S(1)}, u32[]{:S(2)}, u32[]{:S(2)}) async-start(f32[16,8,128]{2,1,0:T(8,128)} %total.1), calls=%async_computation.2 | async-start | bytes 131072 | tf_op jit(solution)/shard_map/all_to_all | solution.py:685

commit v7 on v6

--- a/solution.py
+++ b/solution.py
@@ -597,9 +597,9 @@
             conv[right] = value[:, 64 : 64 + CH]
 
 
-def both_ways(first, second, axis):
+def both_ways(first, second, axis, around):
     count = lax.axis_size(axis)
-    onward = [(i, (i + 1) % count) for i in range(count)]
+    onward = [(i, (i + 1) % count) for i in range(count if around else count - 1)]
     back = [(t, s) for s, t in onward]
     return lax.ppermute(first, axis, onward), lax.ppermute(second, axis, back)
 
@@ -613,7 +613,7 @@
         first_kernel, [((GROUPS, CH // 2, H, LANES), BF)] * 2 + [(cut, BF)], (pair_map, cotangent), "first",
         far=(0, 1), far_out=(2,), scratch=[vmem(tile, BF), vmem(tile, BF), vmem(cut, BF)], copies=3 * GROUPS,
     )
-    above, below = both_ways(down, up, "row")
+    above, below = both_ways(down, up, "row", True)
     d_arrived = lax.all_to_all(d_pieces.reshape(ROWS * COLS, 3, H, LANES), everyone, 0, 0, tiled=True)
     d_arrived = d_arrived.reshape(cut)
 
@@ -629,7 +629,7 @@
         (pair_map, above, below), "act", far_out=(2,), copies=4 * GROUPS,
         scratch=[vmem((256, 4 * POS), BF), vmem((2 * CR, LANES), F32)],
     )
-    from_left, from_right = both_ways(edge, edge, "col")
+    from_left, from_right = both_ways(edge, edge, "col", False)
     five = (ROWS, COLS, 5, H, LANES)
     slope, hidden, block, pieces, edge_inner, edge_x = call(
         inside_kernel,
@@ -670,7 +670,7 @@
         ],
         copies=26,
     )
-    g_above, g_below = both_ways(g_down, g_up, "row")
+    g_above, g_below = both_ways(g_down, g_up, "row", True)
     (pieces,) = call(
         sums_kernel, [(five, BF)], (wide, gmi, tap_rows, hidden, rim_wide, pieces), "sums",
         far=(5,), far_out=(0,), alias={5: 0}, scratch=[vmem((ROWS, COLS, 2, H, LANES), BF)], copies=ROWS,
@@ -695,7 +695,7 @@
             vmem((CR, LANES), F32), vmem((CR, LANES), F32),
         ],
     )
-    g_left, g_right = both_ways(g_edge, g_edge, "col")
+    g_left, g_right = both_ways(g_edge, g_edge, "col", False)
     g_left, g_right, block, _ = lax.optimization_barrier((g_left, g_right, block, sums))
     symmetric, grad_input = call(
         last_kernel, [(tile, BF)] * 2, (block, arrived, inputs, edge_value, edge_slope, g_left, g_right), "last",

time: 91.9 us -> 94.8 us (1.032)
  starting transfers between devices: 41.9 us -> 45.8 us
  waiting for transfers between devices: 13.6 us -> 12.5 us
    all_to_all x1, starting transfers between devices: 9 us -> 11.3 us  [local(): lax.all_to_all(pieces.reshape(ROWS * COLS, 5, H, LANES), everyone, 0, 0,...]
    ppermute x8, starting transfers between devices: 17.3 us -> 18.8 us  [both_ways(): return (lax.ppermute(first, axis, onward), lax.ppermute(second, axis, back))]
    all_to_all x1, waiting for transfers between devices: 8.76 us -> 7.72 us  [local(): lax.all_to_all(pieces.reshape(ROWS * COLS, 5, H, LANES), everyone, 0, 0,...]
  transfers between devices with their start and end apart: 11 -> 11, of which waited for: 5 -> 4; matrix products, arithmetic and copies ran while one was open for 0% -> 0% of each run, Pallas kernels for 27% -> 27%
where the time goes in v7:
time: 94.8 us; the launch traced here: 94.3 us
  starting transfers between devices  45.8 us (48%)
  Pallas kernels  35.1 us (37%)
  waiting for transfers between devices  12.5 us (13%)
    pallas_call x10, Pallas kernels, call(): pl.pallas_call(kernel, name=name, out_shape=[pltpu.HBM(s, t) if i in far_...  35.1 us
    ppermute x8, starting transfers between devices, both_ways(): return (lax.ppermute(first, axis, onward), lax.ppermute(second, axis, back))  18.8 us
    all_to_all x1, starting transfers between devices, local(): lax.all_to_all(pieces.reshape(ROWS * COLS, 5, H, LANES), everyone, 0, 0,...  11.3 us
    all_to_all x1, starting transfers between devices, local(): lax.all_to_all(d_pieces.reshape(ROWS * COLS, 3, H, LANES), everyone, 0, 0...  10.6 us
    all_to_all x1, waiting for transfers between devices, local(): lax.all_to_all(pieces.reshape(ROWS * COLS, 5, H, LANES), everyone, 0, 0,...  7.72 us
    all_to_all x1, starting transfers between devices, local(): lax.all_to_all(sums, everyone, 0, 0, axis_index_groups=groups, tiled=True)  5.11 us
    ppermute x8, waiting for transfers between devices, both_ways(): return (lax.ppermute(first, axis, onward), lax.ppermute(second, axis, back))  2.99 us
  transfers between devices with their start and end apart: 11, of which 4 were waited for; matrix products, arithmetic and copies ran while one was open for 0% of the time, Pallas kernels for 27%

profile of v7, /device:TPU:1, one launch (start us, length us, event | category | flops | bytes accessed | tf_op | source)
XLA Modules:
  0.0 94.3 jit_solution(7377410908309233469)
XLA Ops:
  0.6 2.5 %first.1 = (bf16[8,24,8,128]{3,2,1,0:T(8,128)(2,1)S(1)}, bf16[8,24,8,128]{3,2,1,0:T(8,128)(2,1)S(1)}, bf16[16,8,3,8,128]{4,3,2,1,0:T(8,128)(2,1)}) custom-call(bf16[8,48,8,128]{3,2,1,0:T(8,128)(2,1)} %x_far.3, bf16[8,48,8,128]{3,2,1,0:T(8,128)(2,1)} %d_far.3), custom_call_target="tpu_custom_call" | custom-call | flops 4000000000 | bytes 1000000 | tf_op jit(solution)/shard_map/first/pallas_call | solution.py:82
  3.1 0.0 copy-start.2
  3.1 2.8 %collective-permute-start = (bf16[8,24,8,128]{3,2,1,0:T(8,128)(2,1)S(1)}, bf16[8,24,8,128]{3,2,1,0:T(8,128)(2,1)S(1)}, u32[]{:S(2)}, u32[]{:S(2)}) collective-permute-start(bf16[8,24,8,128]{3,2,1,0:T(8,128)(2,1)S(1)} %get-tuple-element.49), channel_id=1, source_target_pairs={{0,8},{8,16},{16,24},{24,32},{32,40},{40,48},{48,56},{56,64},{64,7... | collective-permute-start | bytes 1179656 | tf_op jit(solution)/shard_map/ppermute | solution.py:604
  5.9 10.6 %all-to-all-start = ((bf16[128,3,8,128]{3,2,1,0:T(8,128)(2,1)}), bf16[128,3,8,128]{3,2,1,0:T(8,128)(2,1)S(1)}, u32[]{:S(2)}, u32[]{:S(2)}) async-start(bf16[128,3,8,128]{3,2,1,0:T(8,128)(2,1)} %bitcast.19), calls=%async_computation | async-start | bytes 1572864 | tf_op jit(solution)/shard_map/all_to_all | solution.py:617
  16.5 1.7 %weights.1 = (bf16[576,768]{1,0:T(8,128)(2,1)S(1)}, bf16[384,192]{1,0:T(8,128)(2,1)S(1)}, bf16[576,768]{1,0:T(8,128)(2,1)}, bf16[384,192]{1,0:T(8,128)(2,1)}, bf16[192,384]{1,0:T(8,128)(2,1)}) custom-call(bf16[9,24,48]{2,1,0:T(8,128)(2,1)S(1)} %bitcast.15, bf16[24,48]{1,0:T(8,128)(2,1)S(1)} %bitcast.17), custom_call_target="tpu_custom_call" | custom-call | flops 4000000000 | bytes 1000000 | tf_op jit(solution)/shard_map/weights/pallas_call | solution.py:82
  18.2 3.8 %act.1 = (bf16[768,1024]{1,0:T(8,128)(2,1)S(1)}, bf16[384,128]{1,0:T(8,128)(2,1)S(1)}, bf16[256,4096]{1,0:T(8,128)(2,1)}) custom-call(bf16[8,48,8,128]{3,2,1,0:T(8,128)(2,1)S(1)} %copy-done.1, bf16[8,24,8,128]{3,2,1,0:T(8,128)(2,1)S(1)} %collective-permute-done.above, bf16[8,24,8,128]{3,2,1,0:T(8,128)(2,1)S(1)} %collective-permute-done.1.below), custom_call_target="tpu_custom_call" | custom-call | flops 4000000000 | bytes 1000000 | tf_op jit(solution)/shard_map/act/pallas_call | solution.py:82
  22.1 1.3 %collective-permute-start.3 = (bf16[384,128]{1,0:T(8,128)(2,1)S(1)}, bf16[384,128]{1,0:T(8,128)(2,1)S(1)}, u32[]{:S(2)}, u32[]{:S(2)}) collective-permute-start(bf16[384,128]{1,0:T(8,128)(2,1)S(1)} %get-tuple-element.58), channel_id=1, source_target_pairs={{1,0},{2,1},{3,2},{4,3},{5,4},{6,5},{7,6},{9,8},{10,9},{11,10},{12... | collective-permute-start | bytes 294920 | tf_op jit(solution)/shard_map/ppermute | solution.py:604
  23.4 5.7 %collective-permute-start.2 = (bf16[384,128]{1,0:T(8,128)(2,1)S(1)}, bf16[384,128]{1,0:T(8,128)(2,1)S(1)}, u32[]{:S(2)}, u32[]{:S(2)}) collective-permute-start(bf16[384,128]{1,0:T(8,128)(2,1)S(1)} %get-tuple-element.58), channel_id=1, source_target_pairs={{0,1},{1,2},{2,3},{3,4},{4,5},{5,6},{6,7},{8,9},{9,10},{10,11},{11... | collective-permute-start | bytes 294920 | tf_op jit(solution)/shard_map/ppermute | solution.py:604
  29.1 7.0 %inside.1 = (f32[192,1024]{1,0:T(8,128)}, bf16[192,1024]{1,0:T(8,128)(2,1)}, bf16[8,48,8,128]{3,2,1,0:T(8,128)(2,1)}, bf16[16,8,5,8,128]{4,3,2,1,0:T(8,128)(2,1)...) custom-call(bf16[8,48,8,128]{3,2,1,0:T(8,128)(2,1)S(1)} %copy-done.1, bf16[768,1024]{1,0:T(8,128)(2,1)S(1)} %get-tuple-element.51.act, ...), custom_call_target="tpu_custom_call" | custom-call | flops 4000000000 | bytes 1000000 | tf_op jit(solution)/shard_map/inside/pallas_call | solution.py:82
  36.1 6.8 %inner.1 = (bf16[8,24,8,128]{3,2,1,0:T(8,128)(2,1)}, bf16[8,12,8,128]{3,2,1,0:T(8,128)(2,1)S(1)}, bf16[8,12,8,128]{3,2,1,0:T(8,128)(2,1)S(1)}, f32[8,48,8,128]{3...) custom-call(bf16[8,48,8,128]{3,2,1,0:T(8,128)(2,1)} %d_far.3, ...), custom_call_target="tpu_custom_call", output_to_operand_aliasing={{4}: (11, {})} | custom-call | flops 4000000000 | bytes 1000000 | tf_op jit(solution)/shard_map/inner/pallas_call | solution.py:82
  42.9 2.3 %collective-permute-start.4 = (bf16[8,12,8,128]{3,2,1,0:T(8,128)(2,1)S(1)}, bf16[8,12,8,128]{3,2,1,0:T(8,128)(2,1)S(1)}, u32[]{:S(2)}, u32[]{:S(2)}) collective-permute-start(bf16[8,12,8,128]{3,2,1,0:T(8,128)(2,1)S(1)} %get-tuple-element.71), channel_id=1, source_target_pairs={{0,8},{8,16},{16,24},{24,32},{32,40},{40,48},{48,56},{56,64},{64,7... | collective-permute-start | bytes 589832 | tf_op jit(solution)/shard_map/ppermute | solution.py:604
  45.1 2.4 %sums.1 = bf16[16,8,5,8,128]{4,3,2,1,0:T(8,128)(2,1)} custom-call(bf16[256,4096]{1,0:T(8,128)(2,1)S(1)} %get-tuple-element.65.wide, bf16[384,1024]{1,0:T(8,128)(2,1)S(1)} %get-tuple-element.66.gmi, bf16[192,4608]{1,0:T(8,128)(2,1)S(1)} %get-tuple-element.67.taps, bf16[192,1024]{1,0:T(8,128)(2,1)S(1)} %get-tuple-element.68.hidden, ...), custom_call_target="tpu_custom_call", output_to_operand_aliasing={{}: (5, {})} | custom-call | flops 4000000000 | bytes 1000000 | tf_op jit(solution)/shard_map/sums/pallas_call | solution.py:82
  47.6 0.2 collective-permute-done.4.above
  47.8 2.8 %collective-permute-done.5.below = bf16[8,12,8,128]{3,2,1,0:T(8,128)(2,1)S(1)} collective-permute-done((bf16[8,12,8,128]{3,2,1,0:T(8,128)(2,1)S(1)}, bf16[8,12,8,128]{3,2,1,0:T(8,128)(2,1)S(1)}, u32[]{:S(2)}, u32[]{:S(2)}) %collective-permute-start.5) | collective-permute-done | bytes 196640 | tf_op jit(solution)/shard_map/ppermute | solution.py:604
  50.5 11.3 %all-to-all-start.1 = ((bf16[128,5,8,128]{3,2,1,0:T(8,128)(2,1)}), bf16[128,5,8,128]{3,2,1,0:T(8,128)(2,1)S(1)}, u32[]{:S(2)}, u32[]{:S(2)}) async-start(bf16[128,5,8,128]{3,2,1,0:T(8,128)(2,1)} %bitcast.18), calls=%async_computation.1 | async-start | bytes 2621440 | tf_op jit(solution)/shard_map/all_to_all | solution.py:679
  61.9 5.8 %spread.1 = (f32[192,128]{1,0:T(8,128)S(1)}, bf16[8,48,8,128]{3,2,1,0:T(8,128)(2,1)}, f32[384,128]{1,0:T(8,128)}, f32[384,128]{1,0:T(8,128)}, bf16[8,48,8,128]{3,2,1,0:T(8,128)(2,1)}) custom-call(bf16[8,24,8,128]{3,2,1,0:T(8,128)(2,1)} %get-tuple-element.64.grad_inner_far, bf16[8,12,8,128]{3,2,1,0:T(8,128)(2,1)S(1)} %collective-permute-done.4.above, ...), custom_call_target="tpu_custom_call" | custom-call | flops 4000000000 | bytes 1000000 | tf_op jit(solution)/shard_map/spread/pallas_call | solution.py:82
  67.7 1.3 %collective-permute-start.7 = (f32[192,128]{1,0:T(8,128)S(1)}, f32[192,128]{1,0:T(8,128)S(1)}, u32[]{:S(2)}, u32[]{:S(2)}) collective-permute-start(f32[192,128]{1,0:T(8,128)S(1)} %get-tuple-element.80), channel_id=1, source_target_pairs={{1,0},{2,1},{3,2},{4,3},{5,4},{6,5},{7,6},{9,8},{10,9},{11,10},{12... | collective-permute-start | bytes 294920 | tf_op jit(solution)/shard_map/ppermute | solution.py:604
  69.0 5.5 %collective-permute-start.6 = (f32[192,128]{1,0:T(8,128)S(1)}, f32[192,128]{1,0:T(8,128)S(1)}, u32[]{:S(2)}, u32[]{:S(2)}) collective-permute-start(f32[192,128]{1,0:T(8,128)S(1)} %get-tuple-element.80), channel_id=1, source_target_pairs={{0,1},{1,2},{2,3},{3,4},{4,5},{5,6},{6,7},{8,9},{9,10},{10,11},{11... | collective-permute-start | bytes 294920 | tf_op jit(solution)/shard_map/ppermute | solution.py:604
  74.5 7.7 %all-to-all-done.1 = bf16[128,5,8,128]{3,2,1,0:T(8,128)(2,1)S(1)} async-done(((bf16[128,5,8,128]{3,2,1,0:T(8,128)(2,1)}), bf16[128,5,8,128]{3,2,1,0:T(8,128)(2,1)S(1)}, u32[]{:S(2)}, u32[]{:S(2)}) %all-to-all-start.1) | async-done | bytes 1310752 | tf_op jit(solution)/shard_map/all_to_all | solution.py:679
  82.2 0.8 total.1
  83.0 5.1 %all-to-all-start.2 = ((f32[16,8,128]{2,1,0:T(8,128)}), f32[16,8,128]{2,1,0:T(8,128)S(1)}, u32[]{:S(2)}, u32[]{:S(2)}) async-start(f32[16,8,128]{2,1,0:T(8,128)} %total.1), calls=%async_computation.2 | async-start | bytes 131072 | tf_op jit(solution)/shard_map/all_to_all | solution.py:685
  88.2 3.6 %last.1 = (bf16[8,48,8,128]{3,2,1,0:T(8,128)(2,1)}, bf16[8,48,8,128]{3,2,1,0:T(8,128)(2,1)}) custom-call(bf16[8,48,8,128]{3,2,1,0:T(8,128)(2,1)} %get-tuple-element.82.block_far, bf16[16,8,5,8,128]{4,3,2,1,0:T(8,128)(2,1)} %bitcast.13, bf16[8,48,8,128]{3,2,1,0:T(8,128)(2,1)} %get-tuple-element.83.value_far, f32[384,128]{1,0:T(8,128)} %get-tuple-element.84.edge_value_far, ...), custom_call_target="tpu_custom_call" | custom-call | flops 4000000000 | bytes 1000000 | tf_op jit(solution)/shard_map/last/pallas_call | solution.py:82
  91.8 1.8 %all-to-all-done.2.tiles = f32[16,8,128]{2,1,0:T(8,128)S(1)} async-done(((f32[16,8,128]{2,1,0:T(8,128)}), f32[16,8,128]{2,1,0:T(8,128)S(1)}, u32[]{:S(2)}, u32[]{:S(2)}) %all-to-all-start.2) | async-done | bytes 65568 | tf_op jit(solution)/shard_map/all_to_all | solution.py:685
  93.6 0.7 unpack.1
  (24 shorter events, 0.1 us)
Async XLA Ops:
  3.1 13.3 %copy-start.2 = (bf16[24,48,3,3]{1,0,3,2:T(8,128)(2,1)S(1)}, bf16[24,48,3,3]{1,0,3,2:T(8,128)(2,1)}, u32[]{:S(2)}) copy-start(bf16[24,48,3,3]{1,0,3,2:T(8,128)(2,1)} %param.10) | copy-start | bytes 62212
  3.1 13.3 %copy-start.3 = (bf16[48,24]{0,1:T(8,128)(2,1)S(1)}, bf16[48,24]{0,1:T(8,128)(2,1)}, u32[]{:S(2)}) copy-start(bf16[48,24]{0,1:T(8,128)(2,1)} %param.13) | copy-start | bytes 6916
  3.1 15.1 %collective-permute-start = (bf16[8,24,8,128]{3,2,1,0:T(8,128)(2,1)S(1)}, bf16[8,24,8,128]{3,2,1,0:T(8,128)(2,1)S(1)}, u32[]{:S(2)}, u32[]{:S(2)}) collective-permute-start(bf16[8,24,8,128]{3,2,1,0:T(8,128)(2,1)S(1)} %get-tuple-element.49), channel_id=1, source_target_pairs={{0,8},{8,16},{16,24},{24,32},{32,40},{40,48},{48,56},{56,64},{64,7... | collective-permute-start | bytes 1179656 | tf_op jit(solution)/shard_map/ppermute | solution.py:604
  5.9 12.3 %collective-permute-start.1 = (bf16[8,24,8,128]{3,2,1,0:T(8,128)(2,1)S(1)}, bf16[8,24,8,128]{3,2,1,0:T(8,128)(2,1)S(1)}, u32[]{:S(2)}, u32[]{:S(2)}) collective-permute-start(bf16[8,24,8,128]{3,2,1,0:T(8,128)(2,1)S(1)} %get-tuple-element.50), channel_id=1, source_target_pairs={{8,0},{16,8},{24,16},{32,24},{40,32},{48,40},{56,48},{64,56},{72,6... | collective-permute-start | bytes 1179656 | tf_op jit(solution)/shard_map/ppermute | solution.py:604
  5.9 30.2 %all-to-all-start = ((bf16[128,3,8,128]{3,2,1,0:T(8,128)(2,1)}), bf16[128,3,8,128]{3,2,1,0:T(8,128)(2,1)S(1)}, u32[]{:S(2)}, u32[]{:S(2)}) async-start(bf16[128,3,8,128]{3,2,1,0:T(8,128)(2,1)} %bitcast.19), calls=%async_computation | async-start | bytes 1572864 | tf_op jit(solution)/shard_map/all_to_all | solution.py:617
  16.5 1.8 %copy-start.1 = (bf16[8,48,8,128]{3,2,1,0:T(8,128)(2,1)S(1)}, bf16[8,48,8,128]{3,2,1,0:T(8,128)(2,1)}, u32[]{:S(2)}) copy-start(bf16[8,48,8,128]{3,2,1,0:T(8,128)(2,1)} %x_far.3) | copy-start | bytes 2359300
  18.2 10.9 %copy-start.4 = (f32[24]{0:T(128)S(1)}, f32[24]{0:T(128)}, u32[]{:S(2)}) copy-start(f32[24]{0:T(128)} %cg.3) | copy-start | bytes 292
  18.2 10.9 %copy-start.5 = (f32[24]{0:T(128)S(1)}, f32[24]{0:T(128)}, u32[]{:S(2)}) copy-start(f32[24]{0:T(128)} %cb.3) | copy-start | bytes 292
  18.2 10.9 %copy-start.6 = (f32[48]{0:T(128)S(1)}, f32[48]{0:T(128)}, u32[]{:S(2)}) copy-start(f32[48]{0:T(128)} %mg.3) | copy-start | bytes 580
  18.2 10.9 %copy-start.7 = (f32[48]{0:T(128)S(1)}, f32[48]{0:T(128)}, u32[]{:S(2)}) copy-start(f32[48]{0:T(128)} %mb.3) | copy-start | bytes 580
  22.1 14.0 %collective-permute-start.3 = (bf16[384,128]{1,0:T(8,128)(2,1)S(1)}, bf16[384,128]{1,0:T(8,128)(2,1)S(1)}, u32[]{:S(2)}, u32[]{:S(2)}) collective-permute-start(bf16[384,128]{1,0:T(8,128)(2,1)S(1)} %get-tuple-element.58), channel_id=1, source_target_pairs={{1,0},{2,1},{3,2},{4,3},{5,4},{6,5},{7,6},{9,8},{10,9},{11,10},{12... | collective-permute-start | bytes 294920 | tf_op jit(solution)/shard_map/ppermute | solution.py:604
  23.4 12.7 %collective-permute-start.2 = (bf16[384,128]{1,0:T(8,128)(2,1)S(1)}, bf16[384,128]{1,0:T(8,128)(2,1)S(1)}, u32[]{:S(2)}, u32[]{:S(2)}) collective-permute-start(bf16[384,128]{1,0:T(8,128)(2,1)S(1)} %get-tuple-element.58), channel_id=1, source_target_pairs={{0,1},{1,2},{2,3},{3,4},{4,5},{5,6},{6,7},{8,9},{9,10},{10,11},{11... | collective-permute-start | bytes 294920 | tf_op jit(solution)/shard_map/ppermute | solution.py:604
  42.9 4.9 %collective-permute-start.4 = (bf16[8,12,8,128]{3,2,1,0:T(8,128)(2,1)S(1)}, bf16[8,12,8,128]{3,2,1,0:T(8,128)(2,1)S(1)}, u32[]{:S(2)}, u32[]{:S(2)}) collective-permute-start(bf16[8,12,8,128]{3,2,1,0:T(8,128)(2,1)S(1)} %get-tuple-element.71), channel_id=1, source_target_pairs={{0,8},{8,16},{16,24},{24,32},{32,40},{40,48},{48,56},{56,64},{64,7... | collective-permute-start | bytes 589832 | tf_op jit(solution)/shard_map/ppermute | solution.py:604
  45.1 5.4 %collective-permute-start.5 = (bf16[8,12,8,128]{3,2,1,0:T(8,128)(2,1)S(1)}, bf16[8,12,8,128]{3,2,1,0:T(8,128)(2,1)S(1)}, u32[]{:S(2)}, u32[]{:S(2)}) collective-permute-start(bf16[8,12,8,128]{3,2,1,0:T(8,128)(2,1)S(1)} %get-tuple-element.72), channel_id=1, source_target_pairs={{8,0},{16,8},{24,16},{32,24},{40,32},{48,40},{56,48},{64,56},{72,6... | collective-permute-start | bytes 589832 | tf_op jit(solution)/shard_map/ppermute | solution.py:604
  50.5 31.7 %all-to-all-start.1 = ((bf16[128,5,8,128]{3,2,1,0:T(8,128)(2,1)}), bf16[128,5,8,128]{3,2,1,0:T(8,128)(2,1)S(1)}, u32[]{:S(2)}, u32[]{:S(2)}) async-start(bf16[128,5,8,128]{3,2,1,0:T(8,128)(2,1)} %bitcast.18), calls=%async_computation.1 | async-start | bytes 2621440 | tf_op jit(solution)/shard_map/all_to_all | solution.py:679
  67.7 20.5 %collective-permute-start.7 = (f32[192,128]{1,0:T(8,128)S(1)}, f32[192,128]{1,0:T(8,128)S(1)}, u32[]{:S(2)}, u32[]{:S(2)}) collective-permute-start(f32[192,128]{1,0:T(8,128)S(1)} %get-tuple-element.80), channel_id=1, source_target_pairs={{1,0},{2,1},{3,2},{4,3},{5,4},{6,5},{7,6},{9,8},{10,9},{11,10},{12... | collective-permute-start | bytes 294920 | tf_op jit(solution)/shard_map/ppermute | solution.py:604
  69.0 19.2 %collective-permute-start.6 = (f32[192,128]{1,0:T(8,128)S(1)}, f32[192,128]{1,0:T(8,128)S(1)}, u32[]{:S(2)}, u32[]{:S(2)}) collective-permute-start(f32[192,128]{1,0:T(8,128)S(1)} %get-tuple-element.80), channel_id=1, source_target_pairs={{0,1},{1,2},{2,3},{3,4},{4,5},{5,6},{6,7},{8,9},{9,10},{10,11},{11... | collective-permute-start | bytes 294920 | tf_op jit(solution)/shard_map/ppermute | solution.py:604
  82.2 6.0 %copy-start = (bf16[128,5,8,128]{3,2,1,0:T(8,128)(2,1)}, bf16[128,5,8,128]{3,2,1,0:T(8,128)(2,1)S(1)}, u32[]{:S(2)}) copy-start(bf16[128,5,8,128]{3,2,1,0:T(8,128)(2,1)S(1)} %all-to-all-done.1) | copy-start | bytes 3932164
  83.0 10.6 %all-to-all-start.2 = ((f32[16,8,128]{2,1,0:T(8,128)}), f32[16,8,128]{2,1,0:T(8,128)S(1)}, u32[]{:S(2)}, u32[]{:S(2)}) async-start(f32[16,8,128]{2,1,0:T(8,128)} %total.1), calls=%async_computation.2 | async-start | bytes 131072 | tf_op jit(solution)/shard_map/all_to_all | solution.py:685

commit v8 on v6

--- a/solution.py
+++ b/solution.py
@@ -258,15 +258,17 @@
     far.finish()
 
 
-def merge_edges(from_left, from_right):
-    lane = lanes_of(from_left.shape[0])
+def merge_edges(first, second):
+    lane = lanes_of(first.shape[0])
     col = lax.axis_index("col")
+    even = col % 2 == 0
+    right, left = jnp.where(even, first, second), jnp.where(even, second, first)
     has_left = jnp.where(col > 0, 1.0, 0.0)
     has_right = jnp.where(col < COLS - 1, 1.0, 0.0)
     return jnp.where(
         lane % 8 < 4,
-        pltpu.roll(from_right, LANES - 4, 1) * has_right,
-        pltpu.roll(from_left, 4, 1) * has_left,
+        pltpu.roll(right, LANES - 4, 1) * has_right,
+        pltpu.roll(left, 4, 1) * has_left,
     )
 
 
@@ -333,7 +335,7 @@
 
 
 def inner_kernel(
-    d_far, arrived, slope_far, hidden_far, edge_inner_far, edge_x_far, from_left, from_right,
+    d_far, arrived, slope_far, hidden_far, edge_inner_far, edge_x_far, edges_a, edges_b,
     weights_far, mixer_far, back_far, pieces_in, cg, cb, mg, mb, wide_far,
     grad_inner_far, down, up, half_sum_far, pieces_far, edge_block_far, gmi, taps_out, hidden_out, rim_wide, wide,
     d, slope, hidden, edge_inner, edge_x, weights, mixer, back, grad_inner, half_sum, ends, edge_block, buffer, rows, sems,
@@ -351,7 +353,7 @@
     lane, lane_c = lanes_of(MR), lanes_of(CR)
     gain, shift = splat(cg, MID), splat(cb, MID)
     gain_out, shift_out = splat(mg, CH), splat(mb, CH)
-    rim = merge_edges(from_left[...].astype(F32), from_right[...].astype(F32))
+    rim = merge_edges(edges_a[...].astype(F32), edges_b[...].astype(F32))
     rows[...] = rim
     for m in range(4):
         to = slice(m * LANES, (m + 1) * LANES)
@@ -553,7 +555,7 @@
 
 
 def last_kernel(
-    block_far, arrived_far, value_far, edge_value_far, edge_slope_far, from_left, from_right, out_far, grad_far,
+    block_far, arrived_far, value_far, edge_value_far, edge_slope_far, edges_a, edges_b, out_far, grad_far,
     block, arrived, out, value, grad, edge_value, edge_slope, sems,
 ):
     far = Far(sems)
@@ -564,7 +566,7 @@
         for g in range(GROUPS)
     ]
     lane = lanes_of(CR)
-    rim = merge_edges(from_left[...], from_right[...])
+    rim = merge_edges(edges_a[...], edges_b[...])
     rim = jnp.concatenate([rim, pltpu.roll(rim, 64, 1)], axis=0)
     for load in first:
         load.wait()
@@ -604,6 +606,13 @@
     return lax.ppermute(first, axis, onward), lax.ppermute(second, axis, back)
 
 
+def swap_cols(edge):
+    count = lax.axis_size("col")
+    first = [(i, i ^ 1) for i in range(count)]
+    second = [(i, min(max(((i + 1) ^ 1) - 1, 0), count - 1)) for i in range(count)]
+    return lax.ppermute(edge, "col", first), lax.ppermute(edge, "col", second)
+
+
 def local(pair_map, cotangent, conv_weight, conv_gain, conv_bias, mix_weight, mix_gain, mix_bias):
     tile = (GROUPS, CH, H, LANES)
     cut = (ROWS, COLS, 3, H, LANES)
@@ -629,7 +638,7 @@
         (pair_map, above, below), "act", far_out=(2,), copies=4 * GROUPS,
         scratch=[vmem((256, 4 * POS), BF), vmem((2 * CR, LANES), F32)],
     )
-    from_left, from_right = both_ways(edge, edge, "col")
+    edges_a, edges_b = swap_cols(edge)
     five = (ROWS, COLS, 5, H, LANES)
     slope, hidden, block, pieces, edge_inner, edge_x = call(
         inside_kernel,
@@ -658,7 +667,7 @@
             ((256, 4 * POS), BF),
         ],
         (
-            cotangent, d_arrived, slope, hidden, edge_inner, edge_x, from_left, from_right,
+            cotangent, d_arrived, slope, hidden, edge_inner, edge_x, edges_a, edges_b,
             wf_far, mf_far, mbk, pieces, conv_gain, conv_bias, mix_gain, mix_bias, wide,
         ),
         "inner", smem=(12, 13, 14, 15), far=(0, 2, 3, 4, 5, 8, 9, 10, 11, 16), far_out=(0, 3, 4, 5), alias={11: 4},
@@ -695,7 +704,7 @@
             vmem((CR, LANES), F32), vmem((CR, LANES), F32),
         ],
     )
-    g_left, g_right = both_ways(g_edge, g_edge, "col")
+    g_left, g_right = swap_cols(g_edge)
     g_left, g_right, block, _ = lax.optimization_barrier((g_left, g_right, block, sums))
     symmetric, grad_input = call(
         last_kernel, [(tile, BF)] * 2, (block, arrived, inputs, edge_value, edge_slope, g_left, g_right), "last",

time: 91.9 us -> 92.5 us (level)
  starting transfers between devices: 41.9 us -> 43 us
    ppermute x0 -> x4, starting transfers between devices: none -> 12.5 us  [swap_cols(): return (lax.ppermute(edge, 'col', first), lax.ppermute(edge, 'col', second))]
    ppermute x8 -> x4, starting transfers between devices: 17.3 us -> 4.88 us  [both_ways(): return (lax.ppermute(first, axis, onward), lax.ppermute(second, axis, back))]
    ppermute x8 -> x4, waiting for transfers between devices: 3.06 us -> 2.98 us  [both_ways(): return (lax.ppermute(first, axis, onward), lax.ppermute(second, axis, back))]
  transfers between devices with their start and end apart: 11 -> 11, of which waited for: 5 -> 4; matrix products, arithmetic and copies ran while one was open for 0% -> 0% of each run, Pallas kernels for 27% -> 27%
where the time goes in v8:
time: 92.5 us; the launch traced here: 92.1 us
  starting transfers between devices  43 us (46%)
  Pallas kernels  35.1 us (38%)
  waiting for transfers between devices  13.1 us (14%)
    pallas_call x10, Pallas kernels, call(): pl.pallas_call(kernel, name=name, out_shape=[pltpu.HBM(s, t) if i in far_...  35.1 us
    ppermute x4, starting transfers between devices, swap_cols(): return (lax.ppermute(edge, 'col', first), lax.ppermute(edge, 'col', second))  12.5 us
    all_to_all x1, starting transfers between devices, local(): lax.all_to_all(d_pieces.reshape(ROWS * COLS, 3, H, LANES), everyone, 0, 0...  10.6 us
    all_to_all x1, starting transfers between devices, local(): lax.all_to_all(pieces.reshape(ROWS * COLS, 5, H, LANES), everyone, 0, 0,...  9.34 us
    all_to_all x1, waiting for transfers between devices, local(): lax.all_to_all(pieces.reshape(ROWS * COLS, 5, H, LANES), everyone, 0, 0,...  8.33 us
    all_to_all x1, starting transfers between devices, local(): lax.all_to_all(sums, everyone, 0, 0, axis_index_groups=groups, tiled=True)  5.68 us
    ppermute x4, starting transfers between devices, both_ways(): return (lax.ppermute(first, axis, onward), lax.ppermute(second, axis, back))  4.88 us
    ppermute x4, waiting for transfers between devices, both_ways(): return (lax.ppermute(first, axis, onward), lax.ppermute(second, axis, back))  2.98 us
  transfers between devices with their start and end apart: 11, of which 4 were waited for; matrix products, arithmetic and copies ran while one was open for 0% of the time, Pallas kernels for 27%

profile of v8, /device:TPU:1, one launch (start us, length us, event | category | flops | bytes accessed | tf_op | source)
XLA Modules:
  0.0 92.1 jit_solution(4726836263933978579)
XLA Ops:
  0.6 2.5 %first.1 = (bf16[8,24,8,128]{3,2,1,0:T(8,128)(2,1)S(1)}, bf16[8,24,8,128]{3,2,1,0:T(8,128)(2,1)S(1)}, bf16[16,8,3,8,128]{4,3,2,1,0:T(8,128)(2,1)}) custom-call(bf16[8,48,8,128]{3,2,1,0:T(8,128)(2,1)} %x_far.3, bf16[8,48,8,128]{3,2,1,0:T(8,128)(2,1)} %d_far.3), custom_call_target="tpu_custom_call" | custom-call | flops 4000000000 | bytes 1000000 | tf_op jit(solution)/shard_map/first/pallas_call | solution.py:82
  3.1 0.0 copy-start.3
  3.1 2.8 %collective-permute-start = (bf16[8,24,8,128]{3,2,1,0:T(8,128)(2,1)S(1)}, bf16[8,24,8,128]{3,2,1,0:T(8,128)(2,1)S(1)}, u32[]{:S(2)}, u32[]{:S(2)}) collective-permute-start(bf16[8,24,8,128]{3,2,1,0:T(8,128)(2,1)S(1)} %get-tuple-element.49), channel_id=1, source_target_pairs={{0,8},{8,16},{16,24},{24,32},{32,40},{40,48},{48,56},{56,64},{64,7... | collective-permute-start | bytes 1179656 | tf_op jit(solution)/shard_map/ppermute | solution.py:606
  5.9 10.6 %all-to-all-start = ((bf16[128,3,8,128]{3,2,1,0:T(8,128)(2,1)}), bf16[128,3,8,128]{3,2,1,0:T(8,128)(2,1)S(1)}, u32[]{:S(2)}, u32[]{:S(2)}) async-start(bf16[128,3,8,128]{3,2,1,0:T(8,128)(2,1)} %bitcast.19), calls=%async_computation | async-start | bytes 1572864 | tf_op jit(solution)/shard_map/all_to_all | solution.py:626
  16.5 1.7 %weights.1 = (bf16[576,768]{1,0:T(8,128)(2,1)S(1)}, bf16[384,192]{1,0:T(8,128)(2,1)S(1)}, bf16[576,768]{1,0:T(8,128)(2,1)}, bf16[384,192]{1,0:T(8,128)(2,1)}, bf16[192,384]{1,0:T(8,128)(2,1)}) custom-call(bf16[9,24,48]{2,1,0:T(8,128)(2,1)S(1)} %bitcast.15, bf16[24,48]{1,0:T(8,128)(2,1)S(1)} %bitcast.17), custom_call_target="tpu_custom_call" | custom-call | flops 4000000000 | bytes 1000000 | tf_op jit(solution)/shard_map/weights/pallas_call | solution.py:82
  18.2 3.8 %act.1 = (bf16[768,1024]{1,0:T(8,128)(2,1)S(1)}, bf16[384,128]{1,0:T(8,128)(2,1)S(1)}, bf16[256,4096]{1,0:T(8,128)(2,1)}) custom-call(bf16[8,48,8,128]{3,2,1,0:T(8,128)(2,1)S(1)} %copy-done.1, bf16[8,24,8,128]{3,2,1,0:T(8,128)(2,1)S(1)} %collective-permute-done.above, bf16[8,24,8,128]{3,2,1,0:T(8,128)(2,1)S(1)} %collective-permute-done.1.below), custom_call_target="tpu_custom_call" | custom-call | flops 4000000000 | bytes 1000000 | tf_op jit(solution)/shard_map/act/pallas_call | solution.py:82
  22.1 0.7 collective-permute-start.3
  22.7 5.7 %collective-permute-start.2 = (bf16[384,128]{1,0:T(8,128)(2,1)S(1)}, bf16[384,128]{1,0:T(8,128)(2,1)S(1)}, u32[]{:S(2)}, u32[]{:S(2)}) collective-permute-start(bf16[384,128]{1,0:T(8,128)(2,1)S(1)} %get-tuple-element.58), channel_id=1, source_target_pairs={{0,1},{1,0},{2,3},{3,2},{4,5},{5,4},{6,7},{7,6},{8,9},{9,8},{10,11... | collective-permute-start | bytes 294920 | tf_op jit(solution)/shard_map/ppermute | solution.py:613
  28.4 7.0 %inside.1 = (f32[192,1024]{1,0:T(8,128)}, bf16[192,1024]{1,0:T(8,128)(2,1)}, bf16[8,48,8,128]{3,2,1,0:T(8,128)(2,1)}, bf16[16,8,5,8,128]{4,3,2,1,0:T(8,128)(2,1)...) custom-call(bf16[8,48,8,128]{3,2,1,0:T(8,128)(2,1)S(1)} %copy-done.1, bf16[768,1024]{1,0:T(8,128)(2,1)S(1)} %get-tuple-element.51.act, ...), custom_call_target="tpu_custom_call" | custom-call | flops 4000000000 | bytes 1000000 | tf_op jit(solution)/shard_map/inside/pallas_call | solution.py:82
  35.4 6.8 %inner.1 = (bf16[8,24,8,128]{3,2,1,0:T(8,128)(2,1)}, bf16[8,12,8,128]{3,2,1,0:T(8,128)(2,1)S(1)}, bf16[8,12,8,128]{3,2,1,0:T(8,128)(2,1)S(1)}, f32[8,48,8,128]{3...) custom-call(bf16[8,48,8,128]{3,2,1,0:T(8,128)(2,1)} %d_far.3, ...), custom_call_target="tpu_custom_call", output_to_operand_aliasing={{4}: (11, {})} | custom-call | flops 4000000000 | bytes 1000000 | tf_op jit(solution)/shard_map/inner/pallas_call | solution.py:82
  42.2 2.1 %collective-permute-start.4 = (bf16[8,12,8,128]{3,2,1,0:T(8,128)(2,1)S(1)}, bf16[8,12,8,128]{3,2,1,0:T(8,128)(2,1)S(1)}, u32[]{:S(2)}, u32[]{:S(2)}) collective-permute-start(bf16[8,12,8,128]{3,2,1,0:T(8,128)(2,1)S(1)} %get-tuple-element.71), channel_id=1, source_target_pairs={{0,8},{8,16},{16,24},{24,32},{32,40},{40,48},{48,56},{56,64},{64,7... | collective-permute-start | bytes 589832 | tf_op jit(solution)/shard_map/ppermute | solution.py:606
  44.4 2.4 %sums.1 = bf16[16,8,5,8,128]{4,3,2,1,0:T(8,128)(2,1)} custom-call(bf16[256,4096]{1,0:T(8,128)(2,1)S(1)} %get-tuple-element.65.wide, bf16[384,1024]{1,0:T(8,128)(2,1)S(1)} %get-tuple-element.66.gmi, bf16[192,4608]{1,0:T(8,128)(2,1)S(1)} %get-tuple-element.67.taps, bf16[192,1024]{1,0:T(8,128)(2,1)S(1)} %get-tuple-element.68.hidden, ...), custom_call_target="tpu_custom_call", output_to_operand_aliasing={{}: (5, {})} | custom-call | flops 4000000000 | bytes 1000000 | tf_op jit(solution)/shard_map/sums/pallas_call | solution.py:82
  46.8 0.2 collective-permute-done.4.above
  47.0 2.8 %collective-permute-done.5.below = bf16[8,12,8,128]{3,2,1,0:T(8,128)(2,1)S(1)} collective-permute-done((bf16[8,12,8,128]{3,2,1,0:T(8,128)(2,1)S(1)}, bf16[8,12,8,128]{3,2,1,0:T(8,128)(2,1)S(1)}, u32[]{:S(2)}, u32[]{:S(2)}) %collective-permute-start.5) | collective-permute-done | bytes 196640 | tf_op jit(solution)/shard_map/ppermute | solution.py:606
  49.8 9.3 %all-to-all-start.1 = ((bf16[128,5,8,128]{3,2,1,0:T(8,128)(2,1)}), bf16[128,5,8,128]{3,2,1,0:T(8,128)(2,1)S(1)}, u32[]{:S(2)}, u32[]{:S(2)}) async-start(bf16[128,5,8,128]{3,2,1,0:T(8,128)(2,1)} %bitcast.18), calls=%async_computation.1 | async-start | bytes 2621440 | tf_op jit(solution)/shard_map/all_to_all | solution.py:688
  59.1 5.8 %spread.1 = (f32[192,128]{1,0:T(8,128)S(1)}, bf16[8,48,8,128]{3,2,1,0:T(8,128)(2,1)}, f32[384,128]{1,0:T(8,128)}, f32[384,128]{1,0:T(8,128)}, bf16[8,48,8,128]{3,2,1,0:T(8,128)(2,1)}) custom-call(bf16[8,24,8,128]{3,2,1,0:T(8,128)(2,1)} %get-tuple-element.64.grad_inner_far, bf16[8,12,8,128]{3,2,1,0:T(8,128)(2,1)S(1)} %collective-permute-done.4.above, ...), custom_call_target="tpu_custom_call" | custom-call | flops 4000000000 | bytes 1000000 | tf_op jit(solution)/shard_map/spread/pallas_call | solution.py:82
  64.9 0.7 collective-permute-start.7
  65.6 5.5 %collective-permute-start.6 = (f32[192,128]{1,0:T(8,128)S(1)}, f32[192,128]{1,0:T(8,128)S(1)}, u32[]{:S(2)}, u32[]{:S(2)}) collective-permute-start(f32[192,128]{1,0:T(8,128)S(1)} %get-tuple-element.80), channel_id=1, source_target_pairs={{0,1},{1,0},{2,3},{3,2},{4,5},{5,4},{6,7},{7,6},{8,9},{9,8},{10,11... | collective-permute-start | bytes 294920 | tf_op jit(solution)/shard_map/ppermute | solution.py:613
  71.1 8.3 %all-to-all-done.1 = bf16[128,5,8,128]{3,2,1,0:T(8,128)(2,1)S(1)} async-done(((bf16[128,5,8,128]{3,2,1,0:T(8,128)(2,1)}), bf16[128,5,8,128]{3,2,1,0:T(8,128)(2,1)S(1)}, u32[]{:S(2)}, u32[]{:S(2)}) %all-to-all-start.1) | async-done | bytes 1310752 | tf_op jit(solution)/shard_map/all_to_all | solution.py:688
  79.4 0.8 total.1
  80.3 5.7 %all-to-all-start.2 = ((f32[16,8,128]{2,1,0:T(8,128)}), f32[16,8,128]{2,1,0:T(8,128)S(1)}, u32[]{:S(2)}, u32[]{:S(2)}) async-start(f32[16,8,128]{2,1,0:T(8,128)} %total.1), calls=%async_computation.2 | async-start | bytes 131072 | tf_op jit(solution)/shard_map/all_to_all | solution.py:694
  86.0 3.6 %last.1 = (bf16[8,48,8,128]{3,2,1,0:T(8,128)(2,1)}, bf16[8,48,8,128]{3,2,1,0:T(8,128)(2,1)}) custom-call(bf16[8,48,8,128]{3,2,1,0:T(8,128)(2,1)} %get-tuple-element.82.block_far, bf16[16,8,5,8,128]{4,3,2,1,0:T(8,128)(2,1)} %bitcast.13, bf16[8,48,8,128]{3,2,1,0:T(8,128)(2,1)} %get-tuple-element.83.value_far, f32[384,128]{1,0:T(8,128)} %get-tuple-element.84.edge_value_far, ...), custom_call_target="tpu_custom_call" | custom-call | flops 4000000000 | bytes 1000000 | tf_op jit(solution)/shard_map/last/pallas_call | solution.py:82
  89.6 1.8 %all-to-all-done.2.tiles = f32[16,8,128]{2,1,0:T(8,128)S(1)} async-done(((f32[16,8,128]{2,1,0:T(8,128)}), f32[16,8,128]{2,1,0:T(8,128)S(1)}, u32[]{:S(2)}, u32[]{:S(2)}) %all-to-all-start.2) | async-done | bytes 65568 | tf_op jit(solution)/shard_map/all_to_all | solution.py:694
  91.4 0.7 unpack.1
  (24 shorter events, 0.1 us)
Async XLA Ops:
  3.1 13.3 %copy-start.2 = (bf16[24,48,3,3]{1,0,3,2:T(8,128)(2,1)S(1)}, bf16[24,48,3,3]{1,0,3,2:T(8,128)(2,1)}, u32[]{:S(2)}) copy-start(bf16[24,48,3,3]{1,0,3,2:T(8,128)(2,1)} %param.10) | copy-start | bytes 62212
  3.1 13.3 %copy-start.3 = (bf16[48,24]{0,1:T(8,128)(2,1)S(1)}, bf16[48,24]{0,1:T(8,128)(2,1)}, u32[]{:S(2)}) copy-start(bf16[48,24]{0,1:T(8,128)(2,1)} %param.13) | copy-start | bytes 6916
  3.1 15.1 %collective-permute-start = (bf16[8,24,8,128]{3,2,1,0:T(8,128)(2,1)S(1)}, bf16[8,24,8,128]{3,2,1,0:T(8,128)(2,1)S(1)}, u32[]{:S(2)}, u32[]{:S(2)}) collective-permute-start(bf16[8,24,8,128]{3,2,1,0:T(8,128)(2,1)S(1)} %get-tuple-element.49), channel_id=1, source_target_pairs={{0,8},{8,16},{16,24},{24,32},{32,40},{40,48},{48,56},{56,64},{64,7... | collective-permute-start | bytes 1179656 | tf_op jit(solution)/shard_map/ppermute | solution.py:606
  5.9 12.3 %collective-permute-start.1 = (bf16[8,24,8,128]{3,2,1,0:T(8,128)(2,1)S(1)}, bf16[8,24,8,128]{3,2,1,0:T(8,128)(2,1)S(1)}, u32[]{:S(2)}, u32[]{:S(2)}) collective-permute-start(bf16[8,24,8,128]{3,2,1,0:T(8,128)(2,1)S(1)} %get-tuple-element.50), channel_id=1, source_target_pairs={{8,0},{16,8},{24,16},{32,24},{40,32},{48,40},{56,48},{64,56},{72,6... | collective-permute-start | bytes 1179656 | tf_op jit(solution)/shard_map/ppermute | solution.py:606
  5.9 29.6 %all-to-all-start = ((bf16[128,3,8,128]{3,2,1,0:T(8,128)(2,1)}), bf16[128,3,8,128]{3,2,1,0:T(8,128)(2,1)S(1)}, u32[]{:S(2)}, u32[]{:S(2)}) async-start(bf16[128,3,8,128]{3,2,1,0:T(8,128)(2,1)} %bitcast.19), calls=%async_computation | async-start | bytes 1572864 | tf_op jit(solution)/shard_map/all_to_all | solution.py:626
  16.5 1.8 %copy-start.1 = (bf16[8,48,8,128]{3,2,1,0:T(8,128)(2,1)S(1)}, bf16[8,48,8,128]{3,2,1,0:T(8,128)(2,1)}, u32[]{:S(2)}) copy-start(bf16[8,48,8,128]{3,2,1,0:T(8,128)(2,1)} %x_far.3) | copy-start | bytes 2359300
  18.2 10.3 %copy-start.4 = (f32[24]{0:T(128)S(1)}, f32[24]{0:T(128)}, u32[]{:S(2)}) copy-start(f32[24]{0:T(128)} %cg.3) | copy-start | bytes 292
  18.2 10.3 %copy-start.5 = (f32[24]{0:T(128)S(1)}, f32[24]{0:T(128)}, u32[]{:S(2)}) copy-start(f32[24]{0:T(128)} %cb.3) | copy-start | bytes 292
  18.2 10.3 %copy-start.6 = (f32[48]{0:T(128)S(1)}, f32[48]{0:T(128)}, u32[]{:S(2)}) copy-start(f32[48]{0:T(128)} %mg.3) | copy-start | bytes 580
  18.2 10.2 %copy-start.7 = (f32[48]{0:T(128)S(1)}, f32[48]{0:T(128)}, u32[]{:S(2)}) copy-start(f32[48]{0:T(128)} %mb.3) | copy-start | bytes 580
  22.1 13.4 %collective-permute-start.3 = (bf16[384,128]{1,0:T(8,128)(2,1)S(1)}, bf16[384,128]{1,0:T(8,128)(2,1)S(1)}, u32[]{:S(2)}, u32[]{:S(2)}) collective-permute-start(bf16[384,128]{1,0:T(8,128)(2,1)S(1)} %get-tuple-element.58), channel_id=1, source_target_pairs={{0,0},{1,2},{2,1},{3,4},{4,3},{5,6},{6,5},{7,7},{8,8},{9,10},{10,9... | collective-permute-start | bytes 294920 | tf_op jit(solution)/shard_map/ppermute | solution.py:613
  22.7 12.7 %collective-permute-start.2 = (bf16[384,128]{1,0:T(8,128)(2,1)S(1)}, bf16[384,128]{1,0:T(8,128)(2,1)S(1)}, u32[]{:S(2)}, u32[]{:S(2)}) collective-permute-start(bf16[384,128]{1,0:T(8,128)(2,1)S(1)} %get-tuple-element.58), channel_id=1, source_target_pairs={{0,1},{1,0},{2,3},{3,2},{4,5},{5,4},{6,7},{7,6},{8,9},{9,8},{10,11... | collective-permute-start | bytes 294920 | tf_op jit(solution)/shard_map/ppermute | solution.py:613
  42.2 4.7 %collective-permute-start.4 = (bf16[8,12,8,128]{3,2,1,0:T(8,128)(2,1)S(1)}, bf16[8,12,8,128]{3,2,1,0:T(8,128)(2,1)S(1)}, u32[]{:S(2)}, u32[]{:S(2)}) collective-permute-start(bf16[8,12,8,128]{3,2,1,0:T(8,128)(2,1)S(1)} %get-tuple-element.71), channel_id=1, source_target_pairs={{0,8},{8,16},{16,24},{24,32},{32,40},{40,48},{48,56},{56,64},{64,7... | collective-permute-start | bytes 589832 | tf_op jit(solution)/shard_map/ppermute | solution.py:606
  44.4 5.4 %collective-permute-start.5 = (bf16[8,12,8,128]{3,2,1,0:T(8,128)(2,1)S(1)}, bf16[8,12,8,128]{3,2,1,0:T(8,128)(2,1)S(1)}, u32[]{:S(2)}, u32[]{:S(2)}) collective-permute-start(bf16[8,12,8,128]{3,2,1,0:T(8,128)(2,1)S(1)} %get-tuple-element.72), channel_id=1, source_target_pairs={{8,0},{16,8},{24,16},{32,24},{40,32},{48,40},{56,48},{64,56},{72,6... | collective-permute-start | bytes 589832 | tf_op jit(solution)/shard_map/ppermute | solution.py:606
  49.8 29.7 %all-to-all-start.1 = ((bf16[128,5,8,128]{3,2,1,0:T(8,128)(2,1)}), bf16[128,5,8,128]{3,2,1,0:T(8,128)(2,1)S(1)}, u32[]{:S(2)}, u32[]{:S(2)}) async-start(bf16[128,5,8,128]{3,2,1,0:T(8,128)(2,1)} %bitcast.18), calls=%async_computation.1 | async-start | bytes 2621440 | tf_op jit(solution)/shard_map/all_to_all | solution.py:688
  64.9 21.0 %collective-permute-start.7 = (f32[192,128]{1,0:T(8,128)S(1)}, f32[192,128]{1,0:T(8,128)S(1)}, u32[]{:S(2)}, u32[]{:S(2)}) collective-permute-start(f32[192,128]{1,0:T(8,128)S(1)} %get-tuple-element.80), channel_id=1, source_target_pairs={{0,0},{1,2},{2,1},{3,4},{4,3},{5,6},{6,5},{7,7},{8,8},{9,10},{10,9... | collective-permute-start | bytes 294920 | tf_op jit(solution)/shard_map/ppermute | solution.py:613
  65.6 20.4 %collective-permute-start.6 = (f32[192,128]{1,0:T(8,128)S(1)}, f32[192,128]{1,0:T(8,128)S(1)}, u32[]{:S(2)}, u32[]{:S(2)}) collective-permute-start(f32[192,128]{1,0:T(8,128)S(1)} %get-tuple-element.80), channel_id=1, source_target_pairs={{0,1},{1,0},{2,3},{3,2},{4,5},{5,4},{6,7},{7,6},{8,9},{9,8},{10,11... | collective-permute-start | bytes 294920 | tf_op jit(solution)/shard_map/ppermute | solution.py:613
  79.4 6.5 %copy-start = (bf16[128,5,8,128]{3,2,1,0:T(8,128)(2,1)}, bf16[128,5,8,128]{3,2,1,0:T(8,128)(2,1)S(1)}, u32[]{:S(2)}) copy-start(bf16[128,5,8,128]{3,2,1,0:T(8,128)(2,1)S(1)} %all-to-all-done.1) | copy-start | bytes 3932164
  80.3 11.1 %all-to-all-start.2 = ((f32[16,8,128]{2,1,0:T(8,128)}), f32[16,8,128]{2,1,0:T(8,128)S(1)}, u32[]{:S(2)}, u32[]{:S(2)}) async-start(f32[16,8,128]{2,1,0:T(8,128)} %total.1), calls=%async_computation.2 | async-start | bytes 131072 | tf_op jit(solution)/shard_map/all_to_all | solution.py:694

commit v9 on v6

--- a/solution.py
+++ b/solution.py
@@ -333,24 +333,20 @@
 
 
 def inner_kernel(
-    d_far, arrived, slope_far, hidden_far, edge_inner_far, edge_x_far, from_left, from_right,
-    weights_far, mixer_far, back_far, pieces_in, cg, cb, mg, mb, wide_far,
-    grad_inner_far, down, up, half_sum_far, pieces_far, edge_block_far, gmi, taps_out, hidden_out, rim_wide, wide,
-    d, slope, hidden, edge_inner, edge_x, weights, mixer, back, grad_inner, half_sum, ends, edge_block, buffer, rows, sems,
+    d_far, arrived, slope_far, edge_inner_far, from_left, from_right, weights_far, back_far, cg, cb, mg, wide_far,
+    grad_inner_far, down, up, half_sum_far, gmi, taps_out, rim_wide, wide, hidden_edge,
+    d, slope, edge_inner, weights, back, grad_inner, half_sum, buffer, rows, sems,
 ):
     far = Far(sems)
     loads = [far.start(d_far.at[2 * p : 2 * p + 2], d.at[2 * p : 2 * p + 2]) for p in range(GROUPS // 2)]
     first = [far.start(weights_far.at[0:MR], weights.at[0:MR])]
     first.append(far.start(weights_far.at[2 * MR : 3 * MR], weights.at[MR : 2 * MR]))
-    first += [far.start(edge_inner_far, edge_inner), far.start(edge_x_far, edge_x), far.start(mixer_far, mixer)]
-    tails = [
-        far.start(pieces_in.at[r, :, 2:5], ends.at[i]) for i, r in enumerate((0, ROWS - 1))
-    ]
-    later = [far.start(back_far, back), far.start(slope_far, slope), far.start(hidden_far, hidden)]
+    first.append(far.start(edge_inner_far, edge_inner))
+    later = [far.start(back_far, back), far.start(slope_far, slope)]
     far.send(wide_far, wide)
     lane, lane_c = lanes_of(MR), lanes_of(CR)
     gain, shift = splat(cg, MID), splat(cb, MID)
-    gain_out, shift_out = splat(mg, CH), splat(mb, CH)
+    gain_out = splat(mg, CH)
     rim = merge_edges(from_left[...].astype(F32), from_right[...].astype(F32))
     rows[...] = rim
     for m in range(4):
@@ -377,26 +373,8 @@
     outer = dot(weights[:, 0:CR], rim) + pltpu.roll(dot(weights[:, CR : 2 * CR], rim), 64, 1)
     outer = jnp.where(lane % 8 < 4, outer[MR : 2 * MR], outer[0:MR])
     pre = (edge_inner[...] + outer) * gain + shift
-    hidden_edge, slope_edge = smooth_both(pre)
+    hidden_edge[...], slope_edge = smooth_both(pre)
     slope_edge = slope_edge * gain
-    hidden_edge = hidden_edge.astype(BF)
-    mixed = dot(mixer[...], hidden_edge)
-    value = (edge_x[...] + mixed * gain_out + shift_out).astype(BF)
-    edge_block[...] = value.astype(F32)
-    far.send(edge_block, edge_block_far)
-    hidden_edge = hidden_edge.astype(F32)
-    parts = value.astype(F32).reshape(3, ROWS, H, LANES)
-    parts = swap_blocks([parts[:, i].reshape(3 * H, LANES) for i in range(ROWS)])
-    for load in tails:
-        load.wait()
-    low = iota((3, H, LANES), 2) % 8 < 4
-    for g in range(GROUPS):
-        lower = pltpu.roll(parts[g], LANES - 4, 1).reshape(3, H, LANES)
-        upper = pltpu.roll(parts[g], 4, 1).reshape(3, H, LANES)
-        ends[0, g] = jnp.where(low, lower, ends[0, g].astype(F32)).astype(BF)
-        ends[1, g] = jnp.where(low, ends[1, g].astype(F32), upper).astype(BF)
-    for i, r in enumerate((0, ROWS - 1)):
-        far.send(ends.at[i], pieces_far.at[r, :, 2:5])
 
     for load in later:
         load.wait()
@@ -425,8 +403,6 @@
                     top = 32 * (3 * (r // 4) + b)
                     taps_out[top : top + 32, to] = three[b].astype(BF)
             packed = jnp.where(lane // 8 == g, pltpu.roll(value, (8 * g - 124) % LANES, 1), packed)
-            here = jnp.where(at_edge(lane), pltpu.roll(hidden_edge, turn, 1), hidden[:, at].astype(F32))
-            hidden_out[:, at] = here.astype(BF)
         far.send(grad_inner.at[2 * pair : 2 * pair + 2], grad_inner_far.at[2 * pair : 2 * pair + 2])
     send_rows(grad_inner, down, up, MID)
     rows[0:MR] = packed
@@ -455,16 +431,49 @@
     return [(yh, zh, xh) for yh in range(2) for zh in range(2) for xh in range(2)]
 
 
-def sums_kernel(wide, gmi, taps, hidden, rim_wide, pieces_in, pieces_far, sums_out, sems):
+def sums_kernel(
+    wide, gmi, taps, rim_wide, hidden_edge, hidden_far, edge_x_far, mixer_far, mg, mb, pieces_in,
+    pieces_far, edge_block_far,
+    hidden, edge_x, mixer, ends, edge_block, sums_out, sems,
+):
     far = Far(sems)
+    loads = [far.start(mixer_far, mixer), far.start(edge_x_far, edge_x)]
+    tails = [
+        far.start(pieces_in.at[r, :, 2:5], ends.at[i]) for i, r in enumerate((0, ROWS - 1))
+    ]
+    late = far.start(hidden_far, hidden)
+    total = dot(taps[:, 4 * POS :], rim_wide[...], NT)
+    total += dot(taps[:, 0 : 4 * POS], wide[...], NT)
+    for load in loads:
+        load.wait()
+    value = edge_x[...] + dot(mixer[...], hidden_edge[...].astype(BF)) * splat(mg, CH) + splat(mb, CH)
+    value = value.astype(BF).astype(F32)
+    edge_block[...] = value
+    far.send(edge_block, edge_block_far)
+    parts = value.reshape(3, ROWS, H, LANES)
+    parts = swap_blocks([parts[:, i].reshape(3 * H, LANES) for i in range(ROWS)])
+    for load in tails:
+        load.wait()
+    low = iota((3, H, LANES), 2) % 8 < 4
+    for g in range(GROUPS):
+        lower = pltpu.roll(parts[g], LANES - 4, 1).reshape(3, H, LANES)
+        upper = pltpu.roll(parts[g], 4, 1).reshape(3, H, LANES)
+        ends[0, g] = jnp.where(low, lower, ends[0, g].astype(F32)).astype(BF)
+        ends[1, g] = jnp.where(low, ends[1, g].astype(F32), upper).astype(BF)
+    for i, r in enumerate((0, ROWS - 1)):
+        far.send(ends.at[i], pieces_far.at[r, :, 2:5])
+    late.wait()
+    lane = lanes_of(MR)
+    for g in range(GROUPS):
+        at = slice(g * LANES, (g + 1) * LANES)
+        moved = pltpu.roll(hidden_edge[...], (124 - 8 * g) % LANES, 1)
+        hidden[:, at] = jnp.where(at_edge(lane), moved, hidden[:, at].astype(F32)).astype(BF)
     mixwide = dot(hidden[...], gmi[...], NT)
     h, col = iota((H, CR), 0), iota((H, CR), 1)
     same = jnp.where(col % 8 == h, 1.0, 0.0)[None]
     mixed = jnp.sum(mixwide.reshape(MID, H, CR) * same, axis=1)
     col, lane_s = iota((CR, LANES), 0), iota((CR, LANES), 1)
     mixed = exact_dot(mixed, jnp.where(col // 8 + 64 == lane_s, 1.0, 0.0).astype(BF))
-    total = dot(taps[:, 4 * POS :], rim_wide[...], NT)
-    total += dot(taps[:, 0 : 4 * POS], wide[...], NT)
     lane = lanes_of(MID)
     blocks, thirds = [], []
     for b in range(3):
@@ -629,7 +638,6 @@
         (pair_map, above, below), "act", far_out=(2,), copies=4 * GROUPS,
         scratch=[vmem((256, 4 * POS), BF), vmem((2 * CR, LANES), F32)],
     )
-    from_left, from_right = both_ways(edge, edge, "col")
     five = (ROWS, COLS, 5, H, LANES)
     slope, hidden, block, pieces, edge_inner, edge_x = call(
         inside_kernel,
@@ -642,38 +650,44 @@
         ],
         copies=2 * GROUPS + 2,
     )
-    grad_inner, g_down, g_up, half_sum, pieces, edge_block, gmi, tap_rows, hidden, rim_wide, wide = call(
+    edge, edge_inner = lax.optimization_barrier((edge, edge_inner))
+    from_left, from_right = both_ways(edge, edge, "col")
+    grad_inner, g_down, g_up, half_sum, gmi, tap_rows, rim_wide, wide, hidden_edge = call(
         inner_kernel,
         [
             ((GROUPS, MID, H, LANES), BF),
             ((GROUPS, MID // 2, H, LANES), BF),
             ((GROUPS, MID // 2, H, LANES), BF),
             (tile, F32),
-            (five, BF),
-            ((CR, LANES), F32),
             ((CR, POS), BF),
             ((192, 4 * POS + 4 * LANES), BF),
-            ((MR, POS), BF),
             ((256, 4 * LANES), BF),
             ((256, 4 * POS), BF),
+            ((MR, LANES), F32),
         ],
         (
-            cotangent, d_arrived, slope, hidden, edge_inner, edge_x, from_left, from_right,
-            wf_far, mf_far, mbk, pieces, conv_gain, conv_bias, mix_gain, mix_bias, wide,
+            cotangent, d_arrived, slope, edge_inner, from_left, from_right, wf_far, mbk,
+            conv_gain, conv_bias, mix_gain, wide,
         ),
-        "inner", smem=(12, 13, 14, 15), far=(0, 2, 3, 4, 5, 8, 9, 10, 11, 16), far_out=(0, 3, 4, 5), alias={11: 4},
+        "inner", smem=(8, 9, 10), far=(0, 2, 3, 6, 7, 11), far_out=(0, 3),
         scratch=[
-            vmem(tile, BF), vmem((MR, POS), F32), vmem((MR, POS), BF), vmem((MR, LANES), F32), vmem((CR, LANES), F32),
-            vmem((2 * MR, 2 * CR), BF), vmem((CR, MR), BF), vmem((MR, CR), BF),
-            vmem((GROUPS, MID, H, LANES), BF), vmem(tile, F32), vmem((2, COLS, 3, H, LANES), BF),
-            vmem((CR, LANES), F32), vmem((2, CH, H, LANES), BF), vmem((CR, LANES), F32),
+            vmem(tile, BF), vmem((MR, POS), F32), vmem((MR, LANES), F32),
+            vmem((2 * MR, 2 * CR), BF), vmem((MR, CR), BF),
+            vmem((GROUPS, MID, H, LANES), BF), vmem(tile, F32),
+            vmem((2, CH, H, LANES), BF), vmem((CR, LANES), F32),
         ],
-        copies=26,
+        copies=18,
     )
     g_above, g_below = both_ways(g_down, g_up, "row")
-    (pieces,) = call(
-        sums_kernel, [(five, BF)], (wide, gmi, tap_rows, hidden, rim_wide, pieces), "sums",
-        far=(5,), far_out=(0,), alias={5: 0}, scratch=[vmem((ROWS, COLS, 2, H, LANES), BF)], copies=ROWS,
+    pieces, edge_block = call(
+        sums_kernel, [(five, BF), ((CR, LANES), F32)],
+        (wide, gmi, tap_rows, rim_wide, hidden_edge, hidden, edge_x, mf_far, mix_gain, mix_bias, pieces), "sums",
+        smem=(8, 9), far=(5, 6, 7, 10), far_out=(0, 1), alias={10: 0},
+        scratch=[
+            vmem((MR, POS), BF), vmem((CR, LANES), F32), vmem((CR, MR), BF), vmem((2, COLS, 3, H, LANES), BF),
+            vmem((CR, LANES), F32), vmem((ROWS, COLS, 2, H, LANES), BF),
+        ],
+        copies=ROWS + 8,
     )
     pieces, g_above, g_below = lax.optimization_barrier((pieces, g_above, g_below))
     arrived = lax.all_to_all(pieces.reshape(ROWS * COLS, 5, H, LANES), everyone, 0, 0, tiled=True)

time: 91.9 us -> 94.8 us (1.032)
  waiting for transfers between devices: 13.6 us -> 18 us
  starting transfers between devices: 41.9 us -> 38.9 us
  Pallas kernels: 35.1 us -> 36.6 us
    ppermute x8, waiting for transfers between devices: 3.06 us -> 7.44 us  [both_ways(): return (lax.ppermute(first, axis, onward), lax.ppermute(second, axis, back))]
    all_to_all x1, starting transfers between devices: 9 us -> 5.83 us  [local(): lax.all_to_all(pieces.reshape(ROWS * COLS, 5, H, LANES), everyone, 0, 0,...]
    pallas_call x10, Pallas kernels: 35.1 us -> 36.6 us  [call(): pl.pallas_call(kernel, name=name, out_shape=[pltpu.HBM(s, t) if i in far_...]
  transfers between devices with their start and end apart: 11 -> 11, of which waited for: 5 -> 5; matrix products, arithmetic and copies ran while one was open for 0% -> 0% of each run, Pallas kernels for 27% -> 29%
where the time goes in v9:
time: 94.8 us; the launch traced here: 94.5 us
  starting transfers between devices  38.9 us (41%)
  Pallas kernels  36.6 us (39%)
  waiting for transfers between devices  18 us (19%)
    pallas_call x10, Pallas kernels, call(): pl.pallas_call(kernel, name=name, out_shape=[pltpu.HBM(s, t) if i in far_...  36.6 us
    ppermute x8, starting transfers between devices, both_ways(): return (lax.ppermute(first, axis, onward), lax.ppermute(second, axis, back))  17.4 us
    all_to_all x1, starting transfers between devices, local(): lax.all_to_all(d_pieces.reshape(ROWS * COLS, 3, H, LANES), everyone, 0, 0...  10.6 us
    all_to_all x1, waiting for transfers between devices, local(): lax.all_to_all(pieces.reshape(ROWS * COLS, 5, H, LANES), everyone, 0, 0,...  8.78 us
    ppermute x8, waiting for transfers between devices, both_ways(): return (lax.ppermute(first, axis, onward), lax.ppermute(second, axis, back))  7.44 us
    all_to_all x1, starting transfers between devices, local(): lax.all_to_all(pieces.reshape(ROWS * COLS, 5, H, LANES), everyone, 0, 0,...  5.83 us
    all_to_all x1, starting transfers between devices, local(): lax.all_to_all(sums, everyone, 0, 0, axis_index_groups=groups, tiled=True)  5.11 us
  transfers between devices with their start and end apart: 11, of which 5 were waited for; matrix products, arithmetic and copies ran while one was open for 0% of the time, Pallas kernels for 29%

profile of v9, /device:TPU:1, one launch (start us, length us, event | category | flops | bytes accessed | tf_op | source)
XLA Modules:
  0.0 94.5 jit_solution(13286684363944611262)
XLA Ops:
  0.6 2.5 %first.1 = (bf16[8,24,8,128]{3,2,1,0:T(8,128)(2,1)S(1)}, bf16[8,24,8,128]{3,2,1,0:T(8,128)(2,1)S(1)}, bf16[16,8,3,8,128]{4,3,2,1,0:T(8,128)(2,1)}) custom-call(bf16[8,48,8,128]{3,2,1,0:T(8,128)(2,1)} %x_far.3, bf16[8,48,8,128]{3,2,1,0:T(8,128)(2,1)} %d_far.3), custom_call_target="tpu_custom_call" | custom-call | flops 4000000000 | bytes 1000000 | tf_op jit(solution)/shard_map/first/pallas_call | solution.py:82
  3.1 0.0 copy-start.2
  3.1 2.8 %collective-permute-start = (bf16[8,24,8,128]{3,2,1,0:T(8,128)(2,1)S(1)}, bf16[8,24,8,128]{3,2,1,0:T(8,128)(2,1)S(1)}, u32[]{:S(2)}, u32[]{:S(2)}) collective-permute-start(bf16[8,24,8,128]{3,2,1,0:T(8,128)(2,1)S(1)} %get-tuple-element.51), channel_id=1, source_target_pairs={{0,8},{8,16},{16,24},{24,32},{32,40},{40,48},{48,56},{56,64},{64,7... | collective-permute-start | bytes 1179656 | tf_op jit(solution)/shard_map/ppermute | solution.py:613
  5.9 10.6 %all-to-all-start = ((bf16[128,3,8,128]{3,2,1,0:T(8,128)(2,1)}), bf16[128,3,8,128]{3,2,1,0:T(8,128)(2,1)S(1)}, u32[]{:S(2)}, u32[]{:S(2)}) async-start(bf16[128,3,8,128]{3,2,1,0:T(8,128)(2,1)} %bitcast.19), calls=%async_computation | async-start | bytes 1572864 | tf_op jit(solution)/shard_map/all_to_all | solution.py:626
  16.5 1.7 %weights.1 = (bf16[576,768]{1,0:T(8,128)(2,1)S(1)}, bf16[384,192]{1,0:T(8,128)(2,1)S(1)}, bf16[576,768]{1,0:T(8,128)(2,1)}, bf16[384,192]{1,0:T(8,128)(2,1)}, bf16[192,384]{1,0:T(8,128)(2,1)}) custom-call(bf16[9,24,48]{2,1,0:T(8,128)(2,1)S(1)} %bitcast.15, bf16[24,48]{1,0:T(8,128)(2,1)S(1)} %bitcast.17), custom_call_target="tpu_custom_call" | custom-call | flops 4000000000 | bytes 1000000 | tf_op jit(solution)/shard_map/weights/pallas_call | solution.py:82
  18.2 0.0 copy-start.5
  18.2 3.8 %act.1 = (bf16[768,1024]{1,0:T(8,128)(2,1)S(1)}, bf16[384,128]{1,0:T(8,128)(2,1)S(1)}, bf16[256,4096]{1,0:T(8,128)(2,1)}) custom-call(bf16[8,48,8,128]{3,2,1,0:T(8,128)(2,1)S(1)} %copy-done.1, bf16[8,24,8,128]{3,2,1,0:T(8,128)(2,1)S(1)} %collective-permute-done.above, bf16[8,24,8,128]{3,2,1,0:T(8,128)(2,1)S(1)} %collective-permute-done.1.below), custom_call_target="tpu_custom_call" | custom-call | flops 4000000000 | bytes 1000000 | tf_op jit(solution)/shard_map/act/pallas_call | solution.py:82
  22.1 6.9 %inside.1 = (f32[192,1024]{1,0:T(8,128)}, bf16[192,1024]{1,0:T(8,128)(2,1)}, bf16[8,48,8,128]{3,2,1,0:T(8,128)(2,1)}, bf16[16,8,5,8,128]{4,3,2,1,0:T(8,128)(2,1)...) custom-call(bf16[8,48,8,128]{3,2,1,0:T(8,128)(2,1)S(1)} %copy-done.1, bf16[768,1024]{1,0:T(8,128)(2,1)S(1)} %get-tuple-element.53.act, ...), custom_call_target="tpu_custom_call" | custom-call | flops 4000000000 | bytes 1000000 | tf_op jit(solution)/shard_map/inside/pallas_call | solution.py:82
  29.0 5.8 %collective-permute-start.3 = (bf16[384,128]{1,0:T(8,128)(2,1)S(1)}, bf16[384,128]{1,0:T(8,128)(2,1)S(1)}, u32[]{:S(2)}, u32[]{:S(2)}) collective-permute-start(bf16[384,128]{1,0:T(8,128)(2,1)S(1)} %get-tuple-element.60), channel_id=1, source_target_pairs={{1,0},{2,1},{3,2},{4,3},{5,4},{6,5},{7,6},{0,7},{9,8},{10,9},{11,1... | collective-permute-start | bytes 294920 | tf_op jit(solution)/shard_map/ppermute | solution.py:613
  34.8 1.8 %collective-permute-done.3.from_right = bf16[384,128]{1,0:T(8,128)(2,1)S(1)} collective-permute-done((bf16[384,128]{1,0:T(8,128)(2,1)S(1)}, bf16[384,128]{1,0:T(8,128)(2,1)S(1)}, u32[]{:S(2)}, u32[]{:S(2)}) %collective-permute-start.3) | collective-permute-done | bytes 98336 | tf_op jit(solution)/shard_map/ppermute | solution.py:613
  36.6 5.3 %collective-permute-done.2.from_left = bf16[384,128]{1,0:T(8,128)(2,1)S(1)} collective-permute-done((bf16[384,128]{1,0:T(8,128)(2,1)S(1)}, bf16[384,128]{1,0:T(8,128)(2,1)S(1)}, u32[]{:S(2)}, u32[]{:S(2)}) %collective-permute-start.2) | collective-permute-done | bytes 98336 | tf_op jit(solution)/shard_map/ppermute | solution.py:613
  41.8 5.8 %inner.1 = (bf16[8,24,8,128]{3,2,1,0:T(8,128)(2,1)}, bf16[8,12,8,128]{3,2,1,0:T(8,128)(2,1)S(1)}, bf16[8,12,8,128]{3,2,1,0:T(8,128)(2,1)S(1)}, f32[8,48,8,128]{3...) custom-call(bf16[8,48,8,128]{3,2,1,0:T(8,128)(2,1)} %d_far.3, ...), custom_call_target="tpu_custom_call" | custom-call | flops 4000000000 | bytes 1000000 | tf_op jit(solution)/shard_map/inner/pallas_call | solution.py:82
  47.6 3.0 %collective-permute-start.4 = (bf16[8,12,8,128]{3,2,1,0:T(8,128)(2,1)S(1)}, bf16[8,12,8,128]{3,2,1,0:T(8,128)(2,1)S(1)}, u32[]{:S(2)}, u32[]{:S(2)}) collective-permute-start(bf16[8,12,8,128]{3,2,1,0:T(8,128)(2,1)S(1)} %get-tuple-element.75), channel_id=1, source_target_pairs={{0,8},{8,16},{16,24},{24,32},{32,40},{40,48},{48,56},{56,64},{64,7... | collective-permute-start | bytes 589832 | tf_op jit(solution)/shard_map/ppermute | solution.py:613
  50.6 5.0 %sums.1 = (bf16[16,8,5,8,128]{4,3,2,1,0:T(8,128)(2,1)}, f32[384,128]{1,0:T(8,128)}) custom-call(bf16[256,4096]{1,0:T(8,128)(2,1)S(1)} %get-tuple-element.65.wide, bf16[384,1024]{1,0:T(8,128)(2,1)S(1)} %get-tuple-element.66.gmi, bf16[192,4608]{1,0:T(8,128)(2,1)S(1)} %get-tuple-element.67.taps, ...), custom_call_target="tpu_custom_call", output_to_operand_aliasing={{0}: (10, {})} | custom-call | flops 4000000000 | bytes 1000000 | tf_op jit(solution)/shard_map/sums/pallas_call | solution.py:82
  55.7 0.3 collective-permute-done.5.below
  56.0 5.8 %all-to-all-start.1 = ((bf16[128,5,8,128]{3,2,1,0:T(8,128)(2,1)}), bf16[128,5,8,128]{3,2,1,0:T(8,128)(2,1)S(1)}, u32[]{:S(2)}, u32[]{:S(2)}) async-start(bf16[128,5,8,128]{3,2,1,0:T(8,128)(2,1)} %bitcast.18), calls=%async_computation.1 | async-start | bytes 2621440 | tf_op jit(solution)/shard_map/all_to_all | solution.py:693
  61.9 5.8 %spread.1 = (f32[192,128]{1,0:T(8,128)S(1)}, bf16[8,48,8,128]{3,2,1,0:T(8,128)(2,1)}, f32[384,128]{1,0:T(8,128)}, f32[384,128]{1,0:T(8,128)}, bf16[8,48,8,128]{3,2,1,0:T(8,128)(2,1)}) custom-call(bf16[8,24,8,128]{3,2,1,0:T(8,128)(2,1)} %get-tuple-element.64.grad_inner_far, bf16[8,12,8,128]{3,2,1,0:T(8,128)(2,1)S(1)} %collective-permute-done.4.above, ...), custom_call_target="tpu_custom_call" | custom-call | flops 4000000000 | bytes 1000000 | tf_op jit(solution)/shard_map/spread/pallas_call | solution.py:82
  67.6 5.9 %collective-permute-start.7 = (f32[192,128]{1,0:T(8,128)S(1)}, f32[192,128]{1,0:T(8,128)S(1)}, u32[]{:S(2)}, u32[]{:S(2)}) collective-permute-start(f32[192,128]{1,0:T(8,128)S(1)} %get-tuple-element.84), channel_id=1, source_target_pairs={{1,0},{2,1},{3,2},{4,3},{5,4},{6,5},{7,6},{0,7},{9,8},{10,9},{11,1... | collective-permute-start | bytes 294920 | tf_op jit(solution)/shard_map/ppermute | solution.py:613
  73.5 8.8 %all-to-all-done.1 = bf16[128,5,8,128]{3,2,1,0:T(8,128)(2,1)S(1)} async-done(((bf16[128,5,8,128]{3,2,1,0:T(8,128)(2,1)}), bf16[128,5,8,128]{3,2,1,0:T(8,128)(2,1)S(1)}, u32[]{:S(2)}, u32[]{:S(2)}) %all-to-all-start.1) | async-done | bytes 1310752 | tf_op jit(solution)/shard_map/all_to_all | solution.py:693
  82.3 0.8 total.1
  83.2 5.1 %all-to-all-start.2 = ((f32[16,8,128]{2,1,0:T(8,128)}), f32[16,8,128]{2,1,0:T(8,128)S(1)}, u32[]{:S(2)}, u32[]{:S(2)}) async-start(f32[16,8,128]{2,1,0:T(8,128)} %total.1), calls=%async_computation.2 | async-start | bytes 131072 | tf_op jit(solution)/shard_map/all_to_all | solution.py:699
  88.3 3.6 %last.1 = (bf16[8,48,8,128]{3,2,1,0:T(8,128)(2,1)}, bf16[8,48,8,128]{3,2,1,0:T(8,128)(2,1)}) custom-call(bf16[8,48,8,128]{3,2,1,0:T(8,128)(2,1)} %get-tuple-element.86.block_far, bf16[16,8,5,8,128]{4,3,2,1,0:T(8,128)(2,1)} %bitcast.13, bf16[8,48,8,128]{3,2,1,0:T(8,128)(2,1)} %get-tuple-element.87.value_far, f32[384,128]{1,0:T(8,128)} %get-tuple-element.88.edge_value_far, ...), custom_call_target="tpu_custom_call" | custom-call | flops 4000000000 | bytes 1000000 | tf_op jit(solution)/shard_map/last/pallas_call | solution.py:82
  91.9 1.8 %all-to-all-done.2.tiles = f32[16,8,128]{2,1,0:T(8,128)S(1)} async-done(((f32[16,8,128]{2,1,0:T(8,128)}), f32[16,8,128]{2,1,0:T(8,128)S(1)}, u32[]{:S(2)}, u32[]{:S(2)}) %all-to-all-start.2) | async-done | bytes 65568 | tf_op jit(solution)/shard_map/all_to_all | solution.py:699
  93.7 0.7 unpack.1
  (24 shorter events, 0.1 us)
Async XLA Ops:
  3.1 13.3 %copy-start.2 = (bf16[24,48,3,3]{1,0,3,2:T(8,128)(2,1)S(1)}, bf16[24,48,3,3]{1,0,3,2:T(8,128)(2,1)}, u32[]{:S(2)}) copy-start(bf16[24,48,3,3]{1,0,3,2:T(8,128)(2,1)} %param.10) | copy-start | bytes 62212
  3.1 13.3 %copy-start.3 = (bf16[48,24]{0,1:T(8,128)(2,1)S(1)}, bf16[48,24]{0,1:T(8,128)(2,1)}, u32[]{:S(2)}) copy-start(bf16[48,24]{0,1:T(8,128)(2,1)} %param.13) | copy-start | bytes 6916
  3.1 15.1 %collective-permute-start = (bf16[8,24,8,128]{3,2,1,0:T(8,128)(2,1)S(1)}, bf16[8,24,8,128]{3,2,1,0:T(8,128)(2,1)S(1)}, u32[]{:S(2)}, u32[]{:S(2)}) collective-permute-start(bf16[8,24,8,128]{3,2,1,0:T(8,128)(2,1)S(1)} %get-tuple-element.51), channel_id=1, source_target_pairs={{0,8},{8,16},{16,24},{24,32},{32,40},{40,48},{48,56},{56,64},{64,7... | collective-permute-start | bytes 1179656 | tf_op jit(solution)/shard_map/ppermute | solution.py:613
  5.9 12.3 %collective-permute-start.1 = (bf16[8,24,8,128]{3,2,1,0:T(8,128)(2,1)S(1)}, bf16[8,24,8,128]{3,2,1,0:T(8,128)(2,1)S(1)}, u32[]{:S(2)}, u32[]{:S(2)}) collective-permute-start(bf16[8,24,8,128]{3,2,1,0:T(8,128)(2,1)S(1)} %get-tuple-element.52), channel_id=1, source_target_pairs={{8,0},{16,8},{24,16},{32,24},{40,32},{48,40},{56,48},{64,56},{72,6... | collective-permute-start | bytes 1179656 | tf_op jit(solution)/shard_map/ppermute | solution.py:613
  5.9 36.0 %all-to-all-start = ((bf16[128,3,8,128]{3,2,1,0:T(8,128)(2,1)}), bf16[128,3,8,128]{3,2,1,0:T(8,128)(2,1)S(1)}, u32[]{:S(2)}, u32[]{:S(2)}) async-start(bf16[128,3,8,128]{3,2,1,0:T(8,128)(2,1)} %bitcast.19), calls=%async_computation | async-start | bytes 1572864 | tf_op jit(solution)/shard_map/all_to_all | solution.py:626
  16.5 1.8 %copy-start.1 = (bf16[8,48,8,128]{3,2,1,0:T(8,128)(2,1)S(1)}, bf16[8,48,8,128]{3,2,1,0:T(8,128)(2,1)}, u32[]{:S(2)}) copy-start(bf16[8,48,8,128]{3,2,1,0:T(8,128)(2,1)} %x_far.3) | copy-start | bytes 2359300
  18.1 3.9 %copy-start.4 = (f32[24]{0:T(128)S(1)}, f32[24]{0:T(128)}, u32[]{:S(2)}) copy-start(f32[24]{0:T(128)} %cg.3) | copy-start | bytes 292
  18.2 3.9 %copy-start.5 = (f32[24]{0:T(128)S(1)}, f32[24]{0:T(128)}, u32[]{:S(2)}) copy-start(f32[24]{0:T(128)} %cb.3) | copy-start | bytes 292
  18.2 3.9 %copy-start.6 = (f32[48]{0:T(128)S(1)}, f32[48]{0:T(128)}, u32[]{:S(2)}) copy-start(f32[48]{0:T(128)} %mg.5) | copy-start | bytes 580
  18.2 3.9 %copy-start.7 = (f32[48]{0:T(128)S(1)}, f32[48]{0:T(128)}, u32[]{:S(2)}) copy-start(f32[48]{0:T(128)} %mb.3) | copy-start | bytes 580
  29.0 7.6 %collective-permute-start.3 = (bf16[384,128]{1,0:T(8,128)(2,1)S(1)}, bf16[384,128]{1,0:T(8,128)(2,1)S(1)}, u32[]{:S(2)}, u32[]{:S(2)}) collective-permute-start(bf16[384,128]{1,0:T(8,128)(2,1)S(1)} %get-tuple-element.60), channel_id=1, source_target_pairs={{1,0},{2,1},{3,2},{4,3},{5,4},{6,5},{7,6},{0,7},{9,8},{10,9},{11,1... | collective-permute-start | bytes 294920 | tf_op jit(solution)/shard_map/ppermute | solution.py:613
  34.8 7.1 %collective-permute-start.2 = (bf16[384,128]{1,0:T(8,128)(2,1)S(1)}, bf16[384,128]{1,0:T(8,128)(2,1)S(1)}, u32[]{:S(2)}, u32[]{:S(2)}) collective-permute-start(bf16[384,128]{1,0:T(8,128)(2,1)S(1)} %get-tuple-element.60), channel_id=1, source_target_pairs={{0,1},{1,2},{2,3},{3,4},{4,5},{5,6},{6,7},{7,0},{8,9},{9,10},{10,1... | collective-permute-start | bytes 294920 | tf_op jit(solution)/shard_map/ppermute | solution.py:613
  47.6 8.0 %collective-permute-start.4 = (bf16[8,12,8,128]{3,2,1,0:T(8,128)(2,1)S(1)}, bf16[8,12,8,128]{3,2,1,0:T(8,128)(2,1)S(1)}, u32[]{:S(2)}, u32[]{:S(2)}) collective-permute-start(bf16[8,12,8,128]{3,2,1,0:T(8,128)(2,1)S(1)} %get-tuple-element.75), channel_id=1, source_target_pairs={{0,8},{8,16},{16,24},{24,32},{32,40},{40,48},{48,56},{56,64},{64,7... | collective-permute-start | bytes 589832 | tf_op jit(solution)/shard_map/ppermute | solution.py:613
  50.6 5.4 %collective-permute-start.5 = (bf16[8,12,8,128]{3,2,1,0:T(8,128)(2,1)S(1)}, bf16[8,12,8,128]{3,2,1,0:T(8,128)(2,1)S(1)}, u32[]{:S(2)}, u32[]{:S(2)}) collective-permute-start(bf16[8,12,8,128]{3,2,1,0:T(8,128)(2,1)S(1)} %get-tuple-element.76), channel_id=1, source_target_pairs={{8,0},{16,8},{24,16},{32,24},{40,32},{48,40},{56,48},{64,56},{72,6... | collective-permute-start | bytes 589832 | tf_op jit(solution)/shard_map/ppermute | solution.py:613
  56.0 26.3 %all-to-all-start.1 = ((bf16[128,5,8,128]{3,2,1,0:T(8,128)(2,1)}), bf16[128,5,8,128]{3,2,1,0:T(8,128)(2,1)S(1)}, u32[]{:S(2)}, u32[]{:S(2)}) async-start(bf16[128,5,8,128]{3,2,1,0:T(8,128)(2,1)} %bitcast.18), calls=%async_computation.1 | async-start | bytes 2621440 | tf_op jit(solution)/shard_map/all_to_all | solution.py:693
  67.6 20.6 %collective-permute-start.7 = (f32[192,128]{1,0:T(8,128)S(1)}, f32[192,128]{1,0:T(8,128)S(1)}, u32[]{:S(2)}, u32[]{:S(2)}) collective-permute-start(f32[192,128]{1,0:T(8,128)S(1)} %get-tuple-element.84), channel_id=1, source_target_pairs={{1,0},{2,1},{3,2},{4,3},{5,4},{6,5},{7,6},{0,7},{9,8},{10,9},{11,1... | collective-permute-start | bytes 294920 | tf_op jit(solution)/shard_map/ppermute | solution.py:613
  73.5 14.7 %collective-permute-start.6 = (f32[192,128]{1,0:T(8,128)S(1)}, f32[192,128]{1,0:T(8,128)S(1)}, u32[]{:S(2)}, u32[]{:S(2)}) collective-permute-start(f32[192,128]{1,0:T(8,128)S(1)} %get-tuple-element.84), channel_id=1, source_target_pairs={{0,1},{1,2},{2,3},{3,4},{4,5},{5,6},{6,7},{7,0},{8,9},{9,10},{10,1... | collective-permute-start | bytes 294920 | tf_op jit(solution)/shard_map/ppermute | solution.py:613
  82.3 6.0 %copy-start = (bf16[128,5,8,128]{3,2,1,0:T(8,128)(2,1)}, bf16[128,5,8,128]{3,2,1,0:T(8,128)(2,1)S(1)}, u32[]{:S(2)}) copy-start(bf16[128,5,8,128]{3,2,1,0:T(8,128)(2,1)S(1)} %all-to-all-done.1) | copy-start | bytes 3932164
  83.2 10.6 %all-to-all-start.2 = ((f32[16,8,128]{2,1,0:T(8,128)}), f32[16,8,128]{2,1,0:T(8,128)S(1)}, u32[]{:S(2)}, u32[]{:S(2)}) async-start(f32[16,8,128]{2,1,0:T(8,128)} %total.1), calls=%async_computation.2 | async-start | bytes 131072 | tf_op jit(solution)/shard_map/all_to_all | solution.py:699

commit v10 on v8

--- a/solution.py
+++ b/solution.py
@@ -261,8 +261,8 @@
 def merge_edges(first, second):
     lane = lanes_of(first.shape[0])
     col = lax.axis_index("col")
-    even = col % 2 == 0
-    right, left = jnp.where(even, first, second), jnp.where(even, second, first)
+    odd = col % 2 == 1
+    right, left = jnp.where(odd, first, second), jnp.where(odd, second, first)
     has_left = jnp.where(col > 0, 1.0, 0.0)
     has_right = jnp.where(col < COLS - 1, 1.0, 0.0)
     return jnp.where(
@@ -610,7 +610,7 @@
     count = lax.axis_size("col")
     first = [(i, i ^ 1) for i in range(count)]
     second = [(i, min(max(((i + 1) ^ 1) - 1, 0), count - 1)) for i in range(count)]
-    return lax.ppermute(edge, "col", first), lax.ppermute(edge, "col", second)
+    return lax.ppermute(edge, "col", second), lax.ppermute(edge, "col", first)
 
 
 def local(pair_map, cotangent, conv_weight, conv_gain, conv_bias, mix_weight, mix_gain, mix_bias):

time: 92.5 us -> 92.8 us (level)
  waiting for transfers between devices: 13.1 us -> 15.7 us
  starting transfers between devices: 43 us -> 40.7 us
    ppermute x4, starting transfers between devices: 12.5 us -> 7.43 us  [swap_cols(): return (lax.ppermute(edge, 'col', second), lax.ppermute(edge, 'col', first))]
    all_to_all x1, starting transfers between devices: 9.34 us -> 13.1 us  [local(): lax.all_to_all(pieces.reshape(ROWS * COLS, 5, H, LANES), everyone, 0, 0,...]
    all_to_all x1, waiting for transfers between devices: 8.33 us -> 10.9 us  [local(): lax.all_to_all(pieces.reshape(ROWS * COLS, 5, H, LANES), everyone, 0, 0,...]
where the time goes in v10:
time: 92.8 us; the launch traced here: 92.4 us
  starting transfers between devices  40.7 us (44%)
  Pallas kernels  35.1 us (38%)
  waiting for transfers between devices  15.7 us (17%)
    pallas_call x10, Pallas kernels, call(): pl.pallas_call(kernel, name=name, out_shape=[pltpu.HBM(s, t) if i in far_...  35.1 us
    all_to_all x1, starting transfers between devices, local(): lax.all_to_all(pieces.reshape(ROWS * COLS, 5, H, LANES), everyone, 0, 0,...  13.1 us
    all_to_all x1, waiting for transfers between devices, local(): lax.all_to_all(pieces.reshape(ROWS * COLS, 5, H, LANES), everyone, 0, 0,...  10.9 us
    all_to_all x1, starting transfers between devices, local(): lax.all_to_all(d_pieces.reshape(ROWS * COLS, 3, H, LANES), everyone, 0, 0...  10.6 us
    ppermute x4, starting transfers between devices, swap_cols(): return (lax.ppermute(edge, 'col', second), lax.ppermute(edge, 'col', first))  7.43 us
    all_to_all x1, starting transfers between devices, local(): lax.all_to_all(sums, everyone, 0, 0, axis_index_groups=groups, tiled=True)  5.11 us
    ppermute x4, starting transfers between devices, both_ways(): return (lax.ppermute(first, axis, onward), lax.ppermute(second, axis, back))  4.54 us
    ppermute x4, waiting for transfers between devices, both_ways(): return (lax.ppermute(first, axis, onward), lax.ppermute(second, axis, back))  2.98 us
  transfers between devices with their start and end apart: 11, of which 4 were waited for; matrix products, arithmetic and copies ran while one was open for 0% of the time, Pallas kernels for 27%

profile of v10, /device:TPU:1, one launch (start us, length us, event | category | flops | bytes accessed | tf_op | source)
XLA Modules:
  0.0 92.4 jit_solution(18134302562413211733)
XLA Ops:
  0.6 2.5 %first.1 = (bf16[8,24,8,128]{3,2,1,0:T(8,128)(2,1)S(1)}, bf16[8,24,8,128]{3,2,1,0:T(8,128)(2,1)S(1)}, bf16[16,8,3,8,128]{4,3,2,1,0:T(8,128)(2,1)}) custom-call(bf16[8,48,8,128]{3,2,1,0:T(8,128)(2,1)} %x_far.3, bf16[8,48,8,128]{3,2,1,0:T(8,128)(2,1)} %d_far.3), custom_call_target="tpu_custom_call" | custom-call | flops 4000000000 | bytes 1000000 | tf_op jit(solution)/shard_map/first/pallas_call | solution.py:82
  3.1 0.0 copy-start.2
  3.1 2.8 %collective-permute-start = (bf16[8,24,8,128]{3,2,1,0:T(8,128)(2,1)S(1)}, bf16[8,24,8,128]{3,2,1,0:T(8,128)(2,1)S(1)}, u32[]{:S(2)}, u32[]{:S(2)}) collective-permute-start(bf16[8,24,8,128]{3,2,1,0:T(8,128)(2,1)S(1)} %get-tuple-element.49), channel_id=1, source_target_pairs={{0,8},{8,16},{16,24},{24,32},{32,40},{40,48},{48,56},{56,64},{64,7... | collective-permute-start | bytes 1179656 | tf_op jit(solution)/shard_map/ppermute | solution.py:606
  5.9 10.6 %all-to-all-start = ((bf16[128,3,8,128]{3,2,1,0:T(8,128)(2,1)}), bf16[128,3,8,128]{3,2,1,0:T(8,128)(2,1)S(1)}, u32[]{:S(2)}, u32[]{:S(2)}) async-start(bf16[128,3,8,128]{3,2,1,0:T(8,128)(2,1)} %bitcast.19), calls=%async_computation | async-start | bytes 1572864 | tf_op jit(solution)/shard_map/all_to_all | solution.py:626
  16.5 1.7 %weights.1 = (bf16[576,768]{1,0:T(8,128)(2,1)S(1)}, bf16[384,192]{1,0:T(8,128)(2,1)S(1)}, bf16[576,768]{1,0:T(8,128)(2,1)}, bf16[384,192]{1,0:T(8,128)(2,1)}, bf16[192,384]{1,0:T(8,128)(2,1)}) custom-call(bf16[9,24,48]{2,1,0:T(8,128)(2,1)S(1)} %bitcast.15, bf16[24,48]{1,0:T(8,128)(2,1)S(1)} %bitcast.17), custom_call_target="tpu_custom_call" | custom-call | flops 4000000000 | bytes 1000000 | tf_op jit(solution)/shard_map/weights/pallas_call | solution.py:82
  18.2 3.8 %act.1 = (bf16[768,1024]{1,0:T(8,128)(2,1)S(1)}, bf16[384,128]{1,0:T(8,128)(2,1)S(1)}, bf16[256,4096]{1,0:T(8,128)(2,1)}) custom-call(bf16[8,48,8,128]{3,2,1,0:T(8,128)(2,1)S(1)} %copy-done.1, bf16[8,24,8,128]{3,2,1,0:T(8,128)(2,1)S(1)} %collective-permute-done.above, bf16[8,24,8,128]{3,2,1,0:T(8,128)(2,1)S(1)} %collective-permute-done.1.below), custom_call_target="tpu_custom_call" | custom-call | flops 4000000000 | bytes 1000000 | tf_op jit(solution)/shard_map/act/pallas_call | solution.py:82
  22.1 3.0 %collective-permute-start.3 = (bf16[384,128]{1,0:T(8,128)(2,1)S(1)}, bf16[384,128]{1,0:T(8,128)(2,1)S(1)}, u32[]{:S(2)}, u32[]{:S(2)}) collective-permute-start(bf16[384,128]{1,0:T(8,128)(2,1)S(1)} %get-tuple-element.58), channel_id=1, source_target_pairs={{0,1},{1,0},{2,3},{3,2},{4,5},{5,4},{6,7},{7,6},{8,9},{9,8},{10,11... | collective-permute-start | bytes 294920 | tf_op jit(solution)/shard_map/ppermute | solution.py:613
  25.0 0.8 collective-permute-start.2
  25.9 7.0 %inside.1 = (f32[192,1024]{1,0:T(8,128)}, bf16[192,1024]{1,0:T(8,128)(2,1)}, bf16[8,48,8,128]{3,2,1,0:T(8,128)(2,1)}, bf16[16,8,5,8,128]{4,3,2,1,0:T(8,128)(2,1)...) custom-call(bf16[8,48,8,128]{3,2,1,0:T(8,128)(2,1)S(1)} %copy-done.1, bf16[768,1024]{1,0:T(8,128)(2,1)S(1)} %get-tuple-element.51.act, ...), custom_call_target="tpu_custom_call" | custom-call | flops 4000000000 | bytes 1000000 | tf_op jit(solution)/shard_map/inside/pallas_call | solution.py:82
  32.9 6.8 %inner.1 = (bf16[8,24,8,128]{3,2,1,0:T(8,128)(2,1)}, bf16[8,12,8,128]{3,2,1,0:T(8,128)(2,1)S(1)}, bf16[8,12,8,128]{3,2,1,0:T(8,128)(2,1)S(1)}, f32[8,48,8,128]{3...) custom-call(bf16[8,48,8,128]{3,2,1,0:T(8,128)(2,1)} %d_far.3, ...), custom_call_target="tpu_custom_call", output_to_operand_aliasing={{4}: (11, {})} | custom-call | flops 4000000000 | bytes 1000000 | tf_op jit(solution)/shard_map/inner/pallas_call | solution.py:82
  39.7 1.8 %collective-permute-start.4 = (bf16[8,12,8,128]{3,2,1,0:T(8,128)(2,1)S(1)}, bf16[8,12,8,128]{3,2,1,0:T(8,128)(2,1)S(1)}, u32[]{:S(2)}, u32[]{:S(2)}) collective-permute-start(bf16[8,12,8,128]{3,2,1,0:T(8,128)(2,1)S(1)} %get-tuple-element.71), channel_id=1, source_target_pairs={{0,8},{8,16},{16,24},{24,32},{32,40},{40,48},{48,56},{56,64},{64,7... | collective-permute-start | bytes 589832 | tf_op jit(solution)/shard_map/ppermute | solution.py:606
  41.5 2.4 %sums.1 = bf16[16,8,5,8,128]{4,3,2,1,0:T(8,128)(2,1)} custom-call(bf16[256,4096]{1,0:T(8,128)(2,1)S(1)} %get-tuple-element.65.wide, bf16[384,1024]{1,0:T(8,128)(2,1)S(1)} %get-tuple-element.66.gmi, bf16[192,4608]{1,0:T(8,128)(2,1)S(1)} %get-tuple-element.67.taps, bf16[192,1024]{1,0:T(8,128)(2,1)S(1)} %get-tuple-element.68.hidden, ...), custom_call_target="tpu_custom_call", output_to_operand_aliasing={{}: (5, {})} | custom-call | flops 4000000000 | bytes 1000000 | tf_op jit(solution)/shard_map/sums/pallas_call | solution.py:82
  43.9 0.2 collective-permute-done.4.above
  44.1 2.8 %collective-permute-done.5.below = bf16[8,12,8,128]{3,2,1,0:T(8,128)(2,1)S(1)} collective-permute-done((bf16[8,12,8,128]{3,2,1,0:T(8,128)(2,1)S(1)}, bf16[8,12,8,128]{3,2,1,0:T(8,128)(2,1)S(1)}, u32[]{:S(2)}, u32[]{:S(2)}) %collective-permute-start.5) | collective-permute-done | bytes 196640 | tf_op jit(solution)/shard_map/ppermute | solution.py:606
  46.9 13.1 %all-to-all-start.1 = ((bf16[128,5,8,128]{3,2,1,0:T(8,128)(2,1)}), bf16[128,5,8,128]{3,2,1,0:T(8,128)(2,1)S(1)}, u32[]{:S(2)}, u32[]{:S(2)}) async-start(bf16[128,5,8,128]{3,2,1,0:T(8,128)(2,1)} %bitcast.18), calls=%async_computation.1 | async-start | bytes 2621440 | tf_op jit(solution)/shard_map/all_to_all | solution.py:688
  60.0 5.8 %spread.1 = (f32[192,128]{1,0:T(8,128)S(1)}, bf16[8,48,8,128]{3,2,1,0:T(8,128)(2,1)}, f32[384,128]{1,0:T(8,128)}, f32[384,128]{1,0:T(8,128)}, bf16[8,48,8,128]{3,2,1,0:T(8,128)(2,1)}) custom-call(bf16[8,24,8,128]{3,2,1,0:T(8,128)(2,1)} %get-tuple-element.64.grad_inner_far, bf16[8,12,8,128]{3,2,1,0:T(8,128)(2,1)S(1)} %collective-permute-done.4.above, ...), custom_call_target="tpu_custom_call" | custom-call | flops 4000000000 | bytes 1000000 | tf_op jit(solution)/shard_map/spread/pallas_call | solution.py:82
  65.8 3.0 %collective-permute-start.7 = (f32[192,128]{1,0:T(8,128)S(1)}, f32[192,128]{1,0:T(8,128)S(1)}, u32[]{:S(2)}, u32[]{:S(2)}) collective-permute-start(f32[192,128]{1,0:T(8,128)S(1)} %get-tuple-element.80), channel_id=1, source_target_pairs={{0,1},{1,0},{2,3},{3,2},{4,5},{5,4},{6,7},{7,6},{8,9},{9,8},{10,11... | collective-permute-start | bytes 294920 | tf_op jit(solution)/shard_map/ppermute | solution.py:613
  68.8 0.7 collective-permute-start.6
  69.4 10.9 %all-to-all-done.1 = bf16[128,5,8,128]{3,2,1,0:T(8,128)(2,1)S(1)} async-done(((bf16[128,5,8,128]{3,2,1,0:T(8,128)(2,1)}), bf16[128,5,8,128]{3,2,1,0:T(8,128)(2,1)S(1)}, u32[]{:S(2)}, u32[]{:S(2)}) %all-to-all-start.1) | async-done | bytes 1310752 | tf_op jit(solution)/shard_map/all_to_all | solution.py:688
  80.3 0.8 total.1
  81.1 5.1 %all-to-all-start.2 = ((f32[16,8,128]{2,1,0:T(8,128)}), f32[16,8,128]{2,1,0:T(8,128)S(1)}, u32[]{:S(2)}, u32[]{:S(2)}) async-start(f32[16,8,128]{2,1,0:T(8,128)} %total.1), calls=%async_computation.2 | async-start | bytes 131072 | tf_op jit(solution)/shard_map/all_to_all | solution.py:694
  86.3 3.6 %last.1 = (bf16[8,48,8,128]{3,2,1,0:T(8,128)(2,1)}, bf16[8,48,8,128]{3,2,1,0:T(8,128)(2,1)}) custom-call(bf16[8,48,8,128]{3,2,1,0:T(8,128)(2,1)} %get-tuple-element.82.block_far, bf16[16,8,5,8,128]{4,3,2,1,0:T(8,128)(2,1)} %bitcast.13, bf16[8,48,8,128]{3,2,1,0:T(8,128)(2,1)} %get-tuple-element.83.value_far, f32[384,128]{1,0:T(8,128)} %get-tuple-element.84.edge_value_far, ...), custom_call_target="tpu_custom_call" | custom-call | flops 4000000000 | bytes 1000000 | tf_op jit(solution)/shard_map/last/pallas_call | solution.py:82
  89.9 1.8 %all-to-all-done.2.tiles = f32[16,8,128]{2,1,0:T(8,128)S(1)} async-done(((f32[16,8,128]{2,1,0:T(8,128)}), f32[16,8,128]{2,1,0:T(8,128)S(1)}, u32[]{:S(2)}, u32[]{:S(2)}) %all-to-all-start.2) | async-done | bytes 65568 | tf_op jit(solution)/shard_map/all_to_all | solution.py:694
  91.7 0.7 unpack.1
  (24 shorter events, 0.1 us)
Async XLA Ops:
  3.1 13.3 %copy-start.2 = (bf16[24,48,3,3]{1,0,3,2:T(8,128)(2,1)S(1)}, bf16[24,48,3,3]{1,0,3,2:T(8,128)(2,1)}, u32[]{:S(2)}) copy-start(bf16[24,48,3,3]{1,0,3,2:T(8,128)(2,1)} %param.10) | copy-start | bytes 62212
  3.1 13.3 %copy-start.3 = (bf16[48,24]{0,1:T(8,128)(2,1)S(1)}, bf16[48,24]{0,1:T(8,128)(2,1)}, u32[]{:S(2)}) copy-start(bf16[48,24]{0,1:T(8,128)(2,1)} %param.13) | copy-start | bytes 6916
  3.1 15.1 %collective-permute-start = (bf16[8,24,8,128]{3,2,1,0:T(8,128)(2,1)S(1)}, bf16[8,24,8,128]{3,2,1,0:T(8,128)(2,1)S(1)}, u32[]{:S(2)}, u32[]{:S(2)}) collective-permute-start(bf16[8,24,8,128]{3,2,1,0:T(8,128)(2,1)S(1)} %get-tuple-element.49), channel_id=1, source_target_pairs={{0,8},{8,16},{16,24},{24,32},{32,40},{40,48},{48,56},{56,64},{64,7... | collective-permute-start | bytes 1179656 | tf_op jit(solution)/shard_map/ppermute | solution.py:606
  5.9 12.3 %collective-permute-start.1 = (bf16[8,24,8,128]{3,2,1,0:T(8,128)(2,1)S(1)}, bf16[8,24,8,128]{3,2,1,0:T(8,128)(2,1)S(1)}, u32[]{:S(2)}, u32[]{:S(2)}) collective-permute-start(bf16[8,24,8,128]{3,2,1,0:T(8,128)(2,1)S(1)} %get-tuple-element.50), channel_id=1, source_target_pairs={{8,0},{16,8},{24,16},{32,24},{40,32},{48,40},{56,48},{64,56},{72,6... | collective-permute-start | bytes 1179656 | tf_op jit(solution)/shard_map/ppermute | solution.py:606
  5.9 27.0 %all-to-all-start = ((bf16[128,3,8,128]{3,2,1,0:T(8,128)(2,1)}), bf16[128,3,8,128]{3,2,1,0:T(8,128)(2,1)S(1)}, u32[]{:S(2)}, u32[]{:S(2)}) async-start(bf16[128,3,8,128]{3,2,1,0:T(8,128)(2,1)} %bitcast.19), calls=%async_computation | async-start | bytes 1572864 | tf_op jit(solution)/shard_map/all_to_all | solution.py:626
  16.5 1.8 %copy-start.1 = (bf16[8,48,8,128]{3,2,1,0:T(8,128)(2,1)S(1)}, bf16[8,48,8,128]{3,2,1,0:T(8,128)(2,1)}, u32[]{:S(2)}) copy-start(bf16[8,48,8,128]{3,2,1,0:T(8,128)(2,1)} %x_far.3) | copy-start | bytes 2359300
  18.2 7.7 %copy-start.4 = (f32[24]{0:T(128)S(1)}, f32[24]{0:T(128)}, u32[]{:S(2)}) copy-start(f32[24]{0:T(128)} %cg.3) | copy-start | bytes 292
  18.2 7.7 %copy-start.5 = (f32[24]{0:T(128)S(1)}, f32[24]{0:T(128)}, u32[]{:S(2)}) copy-start(f32[24]{0:T(128)} %cb.3) | copy-start | bytes 292
  18.2 7.7 %copy-start.6 = (f32[48]{0:T(128)S(1)}, f32[48]{0:T(128)}, u32[]{:S(2)}) copy-start(f32[48]{0:T(128)} %mg.3) | copy-start | bytes 580
  18.2 7.7 %copy-start.7 = (f32[48]{0:T(128)S(1)}, f32[48]{0:T(128)}, u32[]{:S(2)}) copy-start(f32[48]{0:T(128)} %mb.3) | copy-start | bytes 580
  22.1 10.8 %collective-permute-start.3 = (bf16[384,128]{1,0:T(8,128)(2,1)S(1)}, bf16[384,128]{1,0:T(8,128)(2,1)S(1)}, u32[]{:S(2)}, u32[]{:S(2)}) collective-permute-start(bf16[384,128]{1,0:T(8,128)(2,1)S(1)} %get-tuple-element.58), channel_id=1, source_target_pairs={{0,1},{1,0},{2,3},{3,2},{4,5},{5,4},{6,7},{7,6},{8,9},{9,8},{10,11... | collective-permute-start | bytes 294920 | tf_op jit(solution)/shard_map/ppermute | solution.py:613
  25.0 7.9 %collective-permute-start.2 = (bf16[384,128]{1,0:T(8,128)(2,1)S(1)}, bf16[384,128]{1,0:T(8,128)(2,1)S(1)}, u32[]{:S(2)}, u32[]{:S(2)}) collective-permute-start(bf16[384,128]{1,0:T(8,128)(2,1)S(1)} %get-tuple-element.58), channel_id=1, source_target_pairs={{0,0},{1,2},{2,1},{3,4},{4,3},{5,6},{6,5},{7,7},{8,8},{9,10},{10,9... | collective-permute-start | bytes 294920 | tf_op jit(solution)/shard_map/ppermute | solution.py:613
  39.7 4.4 %collective-permute-start.4 = (bf16[8,12,8,128]{3,2,1,0:T(8,128)(2,1)S(1)}, bf16[8,12,8,128]{3,2,1,0:T(8,128)(2,1)S(1)}, u32[]{:S(2)}, u32[]{:S(2)}) collective-permute-start(bf16[8,12,8,128]{3,2,1,0:T(8,128)(2,1)S(1)} %get-tuple-element.71), channel_id=1, source_target_pairs={{0,8},{8,16},{16,24},{24,32},{32,40},{40,48},{48,56},{56,64},{64,7... | collective-permute-start | bytes 589832 | tf_op jit(solution)/shard_map/ppermute | solution.py:606
  41.5 5.4 %collective-permute-start.5 = (bf16[8,12,8,128]{3,2,1,0:T(8,128)(2,1)S(1)}, bf16[8,12,8,128]{3,2,1,0:T(8,128)(2,1)S(1)}, u32[]{:S(2)}, u32[]{:S(2)}) collective-permute-start(bf16[8,12,8,128]{3,2,1,0:T(8,128)(2,1)S(1)} %get-tuple-element.72), channel_id=1, source_target_pairs={{8,0},{16,8},{24,16},{32,24},{40,32},{48,40},{56,48},{64,56},{72,6... | collective-permute-start | bytes 589832 | tf_op jit(solution)/shard_map/ppermute | solution.py:606
  46.9 33.4 %all-to-all-start.1 = ((bf16[128,5,8,128]{3,2,1,0:T(8,128)(2,1)}), bf16[128,5,8,128]{3,2,1,0:T(8,128)(2,1)S(1)}, u32[]{:S(2)}, u32[]{:S(2)}) async-start(bf16[128,5,8,128]{3,2,1,0:T(8,128)(2,1)} %bitcast.18), calls=%async_computation.1 | async-start | bytes 2621440 | tf_op jit(solution)/shard_map/all_to_all | solution.py:688
  65.8 20.5 %collective-permute-start.7 = (f32[192,128]{1,0:T(8,128)S(1)}, f32[192,128]{1,0:T(8,128)S(1)}, u32[]{:S(2)}, u32[]{:S(2)}) collective-permute-start(f32[192,128]{1,0:T(8,128)S(1)} %get-tuple-element.80), channel_id=1, source_target_pairs={{0,1},{1,0},{2,3},{3,2},{4,5},{5,4},{6,7},{7,6},{8,9},{9,8},{10,11... | collective-permute-start | bytes 294920 | tf_op jit(solution)/shard_map/ppermute | solution.py:613
  68.8 17.5 %collective-permute-start.6 = (f32[192,128]{1,0:T(8,128)S(1)}, f32[192,128]{1,0:T(8,128)S(1)}, u32[]{:S(2)}, u32[]{:S(2)}) collective-permute-start(f32[192,128]{1,0:T(8,128)S(1)} %get-tuple-element.80), channel_id=1, source_target_pairs={{0,0},{1,2},{2,1},{3,4},{4,3},{5,6},{6,5},{7,7},{8,8},{9,10},{10,9... | collective-permute-start | bytes 294920 | tf_op jit(solution)/shard_map/ppermute | solution.py:613
  80.3 6.0 %copy-start = (bf16[128,5,8,128]{3,2,1,0:T(8,128)(2,1)}, bf16[128,5,8,128]{3,2,1,0:T(8,128)(2,1)S(1)}, u32[]{:S(2)}) copy-start(bf16[128,5,8,128]{3,2,1,0:T(8,128)(2,1)S(1)} %all-to-all-done.1) | copy-start | bytes 3932164
  81.1 10.6 %all-to-all-start.2 = ((f32[16,8,128]{2,1,0:T(8,128)}), f32[16,8,128]{2,1,0:T(8,128)S(1)}, u32[]{:S(2)}, u32[]{:S(2)}) async-start(f32[16,8,128]{2,1,0:T(8,128)} %total.1), calls=%async_computation.2 | async-start | bytes 131072 | tf_op jit(solution)/shard_map/all_to_all | solution.py:694

commit v11 on v6

--- a/solution.py
+++ b/solution.py
@@ -604,6 +604,15 @@
     return lax.ppermute(first, axis, onward), lax.ppermute(second, axis, back)
 
 
+def around_cols(edge):
+    onward = []
+    for r in range(ROWS):
+        onward += [(r * COLS + c, r * COLS + c + 1) for c in range(COLS - 1)]
+        onward.append((r * COLS + COLS - 1, (r ^ (ROWS // 2)) * COLS))
+    back = [(t, s) for s, t in onward]
+    return lax.ppermute(edge, ("row", "col"), onward), lax.ppermute(edge, ("row", "col"), back)
+
+
 def local(pair_map, cotangent, conv_weight, conv_gain, conv_bias, mix_weight, mix_gain, mix_bias):
     tile = (GROUPS, CH, H, LANES)
     cut = (ROWS, COLS, 3, H, LANES)
@@ -629,7 +638,7 @@
         (pair_map, above, below), "act", far_out=(2,), copies=4 * GROUPS,
         scratch=[vmem((256, 4 * POS), BF), vmem((2 * CR, LANES), F32)],
     )
-    from_left, from_right = both_ways(edge, edge, "col")
+    from_left, from_right = around_cols(edge)
     five = (ROWS, COLS, 5, H, LANES)
     slope, hidden, block, pieces, edge_inner, edge_x = call(
         inside_kernel,
@@ -695,7 +704,7 @@
             vmem((CR, LANES), F32), vmem((CR, LANES), F32),
         ],
     )
-    g_left, g_right = both_ways(g_edge, g_edge, "col")
+    g_left, g_right = around_cols(g_edge)
     g_left, g_right, block, _ = lax.optimization_barrier((g_left, g_right, block, sums))
     symmetric, grad_input = call(
         last_kernel, [(tile, BF)] * 2, (block, arrived, inputs, edge_value, edge_slope, g_left, g_right), "last",

time: 91.9 us -> 91.7 us (level)
    ppermute x8 -> x4, starting transfers between devices: 17.3 us -> 5.5 us  [both_ways(): return (lax.ppermute(first, axis, onward), lax.ppermute(second, axis, back))]
    ppermute x0 -> x4, starting transfers between devices: none -> 11 us  [the longest x2 11 us: around_cols(): lax.ppermute(edge, ('row', 'col'), back)]
    ppermute x8 -> x4, waiting for transfers between devices: 3.06 us -> 2.98 us  [both_ways(): return (lax.ppermute(first, axis, onward), lax.ppermute(second, axis, back))]
  transfers between devices with their start and end apart: 11 -> 11, of which waited for: 5 -> 4; matrix products, arithmetic and copies ran while one was open for 0% -> 0% of each run, Pallas kernels for 27% -> 28%
where the time goes in v11:
time: 91.7 us; the launch traced here: 91.2 us
  starting transfers between devices  41.5 us (45%)
  Pallas kernels  35.1 us (38%)
  waiting for transfers between devices  13.8 us (15%)
    pallas_call x10, Pallas kernels, call(): pl.pallas_call(kernel, name=name, out_shape=[pltpu.HBM(s, t) if i in far_...  35.1 us
    ppermute x2, starting transfers between devices, around_cols(): lax.ppermute(edge, ('row', 'col'), back)  11 us
    all_to_all x1, starting transfers between devices, local(): lax.all_to_all(d_pieces.reshape(ROWS * COLS, 3, H, LANES), everyone, 0, 0...  10.6 us
    all_to_all x1, starting transfers between devices, local(): lax.all_to_all(pieces.reshape(ROWS * COLS, 5, H, LANES), everyone, 0, 0,...  9.28 us
    all_to_all x1, waiting for transfers between devices, local(): lax.all_to_all(pieces.reshape(ROWS * COLS, 5, H, LANES), everyone, 0, 0,...  9.03 us
    ppermute x4, starting transfers between devices, both_ways(): return (lax.ppermute(first, axis, onward), lax.ppermute(second, axis, back))  5.5 us
    all_to_all x1, starting transfers between devices, local(): lax.all_to_all(sums, everyone, 0, 0, axis_index_groups=groups, tiled=True)  5.17 us
    ppermute x4, waiting for transfers between devices, both_ways(): return (lax.ppermute(first, axis, onward), lax.ppermute(second, axis, back))  2.98 us
  transfers between devices with their start and end apart: 11, of which 4 were waited for; matrix products, arithmetic and copies ran while one was open for 0% of the time, Pallas kernels for 28%

profile of v11, /device:TPU:1, one launch (start us, length us, event | category | flops | bytes accessed | tf_op | source)
XLA Modules:
  0.0 91.2 jit_solution(15139422441672937547)
XLA Ops:
  0.6 2.5 %first.1 = (bf16[8,24,8,128]{3,2,1,0:T(8,128)(2,1)S(1)}, bf16[8,24,8,128]{3,2,1,0:T(8,128)(2,1)S(1)}, bf16[16,8,3,8,128]{4,3,2,1,0:T(8,128)(2,1)}) custom-call(bf16[8,48,8,128]{3,2,1,0:T(8,128)(2,1)} %x_far.3, bf16[8,48,8,128]{3,2,1,0:T(8,128)(2,1)} %d_far.3), custom_call_target="tpu_custom_call" | custom-call | flops 4000000000 | bytes 1000000 | tf_op jit(solution)/shard_map/first/pallas_call | solution.py:82
  3.1 0.0 copy-start.2
  3.1 0.0 copy-start.3
  3.1 2.8 %collective-permute-start = (bf16[8,24,8,128]{3,2,1,0:T(8,128)(2,1)S(1)}, bf16[8,24,8,128]{3,2,1,0:T(8,128)(2,1)S(1)}, u32[]{:S(2)}, u32[]{:S(2)}) collective-permute-start(bf16[8,24,8,128]{3,2,1,0:T(8,128)(2,1)S(1)} %get-tuple-element.49), channel_id=1, source_target_pairs={{0,8},{8,16},{16,24},{24,32},{32,40},{40,48},{48,56},{56,64},{64,7... | collective-permute-start | bytes 1179656 | tf_op jit(solution)/shard_map/ppermute | solution.py:604
  5.9 10.6 %all-to-all-start = ((bf16[128,3,8,128]{3,2,1,0:T(8,128)(2,1)}), bf16[128,3,8,128]{3,2,1,0:T(8,128)(2,1)S(1)}, u32[]{:S(2)}, u32[]{:S(2)}) async-start(bf16[128,3,8,128]{3,2,1,0:T(8,128)(2,1)} %bitcast.19), calls=%async_computation | async-start | bytes 1572864 | tf_op jit(solution)/shard_map/all_to_all | solution.py:626
  16.5 0.0 copy-start.1
  16.5 1.7 %weights.1 = (bf16[576,768]{1,0:T(8,128)(2,1)S(1)}, bf16[384,192]{1,0:T(8,128)(2,1)S(1)}, bf16[576,768]{1,0:T(8,128)(2,1)}, bf16[384,192]{1,0:T(8,128)(2,1)}, bf16[192,384]{1,0:T(8,128)(2,1)}) custom-call(bf16[9,24,48]{2,1,0:T(8,128)(2,1)S(1)} %bitcast.15, bf16[24,48]{1,0:T(8,128)(2,1)S(1)} %bitcast.17), custom_call_target="tpu_custom_call" | custom-call | flops 4000000000 | bytes 1000000 | tf_op jit(solution)/shard_map/weights/pallas_call | solution.py:82
  18.2 3.8 %act.1 = (bf16[768,1024]{1,0:T(8,128)(2,1)S(1)}, bf16[384,128]{1,0:T(8,128)(2,1)S(1)}, bf16[256,4096]{1,0:T(8,128)(2,1)}) custom-call(bf16[8,48,8,128]{3,2,1,0:T(8,128)(2,1)S(1)} %copy-done.1, bf16[8,24,8,128]{3,2,1,0:T(8,128)(2,1)S(1)} %collective-permute-done.above, bf16[8,24,8,128]{3,2,1,0:T(8,128)(2,1)S(1)} %collective-permute-done.1.below), custom_call_target="tpu_custom_call" | custom-call | flops 4000000000 | bytes 1000000 | tf_op jit(solution)/shard_map/act/pallas_call | solution.py:82
  22.1 5.5 %collective-permute-start.3 = (bf16[384,128]{1,0:T(8,128)(2,1)S(1)}, bf16[384,128]{1,0:T(8,128)(2,1)S(1)}, u32[]{:S(2)}, u32[]{:S(2)}) collective-permute-start(bf16[384,128]{1,0:T(8,128)(2,1)S(1)} %get-tuple-element.58), channel_id=1, source_target_pairs={{1,0},{2,1},{3,2},{4,3},{5,4},{6,5},{7,6},{64,7},{9,8},{10,9},{11,... | collective-permute-start | bytes 294920 | tf_op jit(solution)/shard_map/ppermute | solution.py:613
  27.6 7.0 %inside.1 = (f32[192,1024]{1,0:T(8,128)}, bf16[192,1024]{1,0:T(8,128)(2,1)}, bf16[8,48,8,128]{3,2,1,0:T(8,128)(2,1)}, bf16[16,8,5,8,128]{4,3,2,1,0:T(8,128)(2,1)...) custom-call(bf16[8,48,8,128]{3,2,1,0:T(8,128)(2,1)S(1)} %copy-done.1, bf16[768,1024]{1,0:T(8,128)(2,1)S(1)} %get-tuple-element.51.act, ...), custom_call_target="tpu_custom_call" | custom-call | flops 4000000000 | bytes 1000000 | tf_op jit(solution)/shard_map/inside/pallas_call | solution.py:82
  34.6 6.8 %inner.1 = (bf16[8,24,8,128]{3,2,1,0:T(8,128)(2,1)}, bf16[8,12,8,128]{3,2,1,0:T(8,128)(2,1)S(1)}, bf16[8,12,8,128]{3,2,1,0:T(8,128)(2,1)S(1)}, f32[8,48,8,128]{3...) custom-call(bf16[8,48,8,128]{3,2,1,0:T(8,128)(2,1)} %d_far.3, ...), custom_call_target="tpu_custom_call", output_to_operand_aliasing={{4}: (11, {})} | custom-call | flops 4000000000 | bytes 1000000 | tf_op jit(solution)/shard_map/inner/pallas_call | solution.py:82
  41.4 2.7 %collective-permute-start.4 = (bf16[8,12,8,128]{3,2,1,0:T(8,128)(2,1)S(1)}, bf16[8,12,8,128]{3,2,1,0:T(8,128)(2,1)S(1)}, u32[]{:S(2)}, u32[]{:S(2)}) collective-permute-start(bf16[8,12,8,128]{3,2,1,0:T(8,128)(2,1)S(1)} %get-tuple-element.71), channel_id=1, source_target_pairs={{0,8},{8,16},{16,24},{24,32},{32,40},{40,48},{48,56},{56,64},{64,7... | collective-permute-start | bytes 589832 | tf_op jit(solution)/shard_map/ppermute | solution.py:604
  44.1 2.4 %sums.1 = bf16[16,8,5,8,128]{4,3,2,1,0:T(8,128)(2,1)} custom-call(bf16[256,4096]{1,0:T(8,128)(2,1)S(1)} %get-tuple-element.65.wide, bf16[384,1024]{1,0:T(8,128)(2,1)S(1)} %get-tuple-element.66.gmi, bf16[192,4608]{1,0:T(8,128)(2,1)S(1)} %get-tuple-element.67.taps, bf16[192,1024]{1,0:T(8,128)(2,1)S(1)} %get-tuple-element.68.hidden, ...), custom_call_target="tpu_custom_call", output_to_operand_aliasing={{}: (5, {})} | custom-call | flops 4000000000 | bytes 1000000 | tf_op jit(solution)/shard_map/sums/pallas_call | solution.py:82
  46.5 0.2 collective-permute-done.4.above
  46.7 2.8 %collective-permute-done.5.below = bf16[8,12,8,128]{3,2,1,0:T(8,128)(2,1)S(1)} collective-permute-done((bf16[8,12,8,128]{3,2,1,0:T(8,128)(2,1)S(1)}, bf16[8,12,8,128]{3,2,1,0:T(8,128)(2,1)S(1)}, u32[]{:S(2)}, u32[]{:S(2)}) %collective-permute-start.5) | collective-permute-done | bytes 196640 | tf_op jit(solution)/shard_map/ppermute | solution.py:604
  49.5 9.3 %all-to-all-start.1 = ((bf16[128,5,8,128]{3,2,1,0:T(8,128)(2,1)}), bf16[128,5,8,128]{3,2,1,0:T(8,128)(2,1)S(1)}, u32[]{:S(2)}, u32[]{:S(2)}) async-start(bf16[128,5,8,128]{3,2,1,0:T(8,128)(2,1)} %bitcast.18), calls=%async_computation.1 | async-start | bytes 2621440 | tf_op jit(solution)/shard_map/all_to_all | solution.py:688
  58.8 5.8 %spread.1 = (f32[192,128]{1,0:T(8,128)S(1)}, bf16[8,48,8,128]{3,2,1,0:T(8,128)(2,1)}, f32[384,128]{1,0:T(8,128)}, f32[384,128]{1,0:T(8,128)}, bf16[8,48,8,128]{3,2,1,0:T(8,128)(2,1)}) custom-call(bf16[8,24,8,128]{3,2,1,0:T(8,128)(2,1)} %get-tuple-element.64.grad_inner_far, bf16[8,12,8,128]{3,2,1,0:T(8,128)(2,1)S(1)} %collective-permute-done.4.above, ...), custom_call_target="tpu_custom_call" | custom-call | flops 4000000000 | bytes 1000000 | tf_op jit(solution)/shard_map/spread/pallas_call | solution.py:82
  64.6 5.5 %collective-permute-start.7 = (f32[192,128]{1,0:T(8,128)S(1)}, f32[192,128]{1,0:T(8,128)S(1)}, u32[]{:S(2)}, u32[]{:S(2)}) collective-permute-start(f32[192,128]{1,0:T(8,128)S(1)} %get-tuple-element.80), channel_id=1, source_target_pairs={{1,0},{2,1},{3,2},{4,3},{5,4},{6,5},{7,6},{64,7},{9,8},{10,9},{11,... | collective-permute-start | bytes 294920 | tf_op jit(solution)/shard_map/ppermute | solution.py:613
  70.1 9.0 %all-to-all-done.1 = bf16[128,5,8,128]{3,2,1,0:T(8,128)(2,1)S(1)} async-done(((bf16[128,5,8,128]{3,2,1,0:T(8,128)(2,1)}), bf16[128,5,8,128]{3,2,1,0:T(8,128)(2,1)S(1)}, u32[]{:S(2)}, u32[]{:S(2)}) %all-to-all-start.1) | async-done | bytes 1310752 | tf_op jit(solution)/shard_map/all_to_all | solution.py:688
  79.1 0.8 total.1
  79.9 5.2 %all-to-all-start.2 = ((f32[16,8,128]{2,1,0:T(8,128)}), f32[16,8,128]{2,1,0:T(8,128)S(1)}, u32[]{:S(2)}, u32[]{:S(2)}) async-start(f32[16,8,128]{2,1,0:T(8,128)} %total.1), calls=%async_computation.2 | async-start | bytes 131072 | tf_op jit(solution)/shard_map/all_to_all | solution.py:694
  85.1 3.6 %last.1 = (bf16[8,48,8,128]{3,2,1,0:T(8,128)(2,1)}, bf16[8,48,8,128]{3,2,1,0:T(8,128)(2,1)}) custom-call(bf16[8,48,8,128]{3,2,1,0:T(8,128)(2,1)} %get-tuple-element.82.block_far, bf16[16,8,5,8,128]{4,3,2,1,0:T(8,128)(2,1)} %bitcast.13, bf16[8,48,8,128]{3,2,1,0:T(8,128)(2,1)} %get-tuple-element.83.value_far, f32[384,128]{1,0:T(8,128)} %get-tuple-element.84.edge_value_far, ...), custom_call_target="tpu_custom_call" | custom-call | flops 4000000000 | bytes 1000000 | tf_op jit(solution)/shard_map/last/pallas_call | solution.py:82
  88.8 1.7 %all-to-all-done.2.tiles = f32[16,8,128]{2,1,0:T(8,128)S(1)} async-done(((f32[16,8,128]{2,1,0:T(8,128)}), f32[16,8,128]{2,1,0:T(8,128)S(1)}, u32[]{:S(2)}, u32[]{:S(2)}) %all-to-all-start.2) | async-done | bytes 65568 | tf_op jit(solution)/shard_map/all_to_all | solution.py:694
  90.5 0.7 unpack.1
  (24 shorter events, 0.1 us)
Async XLA Ops:
  3.1 13.3 %copy-start.2 = (bf16[24,48,3,3]{1,0,3,2:T(8,128)(2,1)S(1)}, bf16[24,48,3,3]{1,0,3,2:T(8,128)(2,1)}, u32[]{:S(2)}) copy-start(bf16[24,48,3,3]{1,0,3,2:T(8,128)(2,1)} %param.10) | copy-start | bytes 62212
  3.1 13.3 %copy-start.3 = (bf16[48,24]{0,1:T(8,128)(2,1)S(1)}, bf16[48,24]{0,1:T(8,128)(2,1)}, u32[]{:S(2)}) copy-start(bf16[48,24]{0,1:T(8,128)(2,1)} %param.13) | copy-start | bytes 6916
  3.1 15.1 %collective-permute-start = (bf16[8,24,8,128]{3,2,1,0:T(8,128)(2,1)S(1)}, bf16[8,24,8,128]{3,2,1,0:T(8,128)(2,1)S(1)}, u32[]{:S(2)}, u32[]{:S(2)}) collective-permute-start(bf16[8,24,8,128]{3,2,1,0:T(8,128)(2,1)S(1)} %get-tuple-element.49), channel_id=1, source_target_pairs={{0,8},{8,16},{16,24},{24,32},{32,40},{40,48},{48,56},{56,64},{64,7... | collective-permute-start | bytes 1179656 | tf_op jit(solution)/shard_map/ppermute | solution.py:604
  5.9 12.3 %collective-permute-start.1 = (bf16[8,24,8,128]{3,2,1,0:T(8,128)(2,1)S(1)}, bf16[8,24,8,128]{3,2,1,0:T(8,128)(2,1)S(1)}, u32[]{:S(2)}, u32[]{:S(2)}) collective-permute-start(bf16[8,24,8,128]{3,2,1,0:T(8,128)(2,1)S(1)} %get-tuple-element.50), channel_id=1, source_target_pairs={{8,0},{16,8},{24,16},{32,24},{40,32},{48,40},{56,48},{64,56},{72,6... | collective-permute-start | bytes 1179656 | tf_op jit(solution)/shard_map/ppermute | solution.py:604
  5.9 28.7 %all-to-all-start = ((bf16[128,3,8,128]{3,2,1,0:T(8,128)(2,1)}), bf16[128,3,8,128]{3,2,1,0:T(8,128)(2,1)S(1)}, u32[]{:S(2)}, u32[]{:S(2)}) async-start(bf16[128,3,8,128]{3,2,1,0:T(8,128)(2,1)} %bitcast.19), calls=%async_computation | async-start | bytes 1572864 | tf_op jit(solution)/shard_map/all_to_all | solution.py:626
  16.5 1.8 %copy-start.1 = (bf16[8,48,8,128]{3,2,1,0:T(8,128)(2,1)S(1)}, bf16[8,48,8,128]{3,2,1,0:T(8,128)(2,1)}, u32[]{:S(2)}) copy-start(bf16[8,48,8,128]{3,2,1,0:T(8,128)(2,1)} %x_far.3) | copy-start | bytes 2359300
  18.2 9.4 %copy-start.4 = (f32[24]{0:T(128)S(1)}, f32[24]{0:T(128)}, u32[]{:S(2)}) copy-start(f32[24]{0:T(128)} %cg.3) | copy-start | bytes 292
  18.2 9.4 %copy-start.5 = (f32[24]{0:T(128)S(1)}, f32[24]{0:T(128)}, u32[]{:S(2)}) copy-start(f32[24]{0:T(128)} %cb.3) | copy-start | bytes 292
  18.2 9.4 %copy-start.6 = (f32[48]{0:T(128)S(1)}, f32[48]{0:T(128)}, u32[]{:S(2)}) copy-start(f32[48]{0:T(128)} %mg.3) | copy-start | bytes 580
  18.2 9.4 %copy-start.7 = (f32[48]{0:T(128)S(1)}, f32[48]{0:T(128)}, u32[]{:S(2)}) copy-start(f32[48]{0:T(128)} %mb.3) | copy-start | bytes 580
  22.1 12.5 %collective-permute-start.3 = (bf16[384,128]{1,0:T(8,128)(2,1)S(1)}, bf16[384,128]{1,0:T(8,128)(2,1)S(1)}, u32[]{:S(2)}, u32[]{:S(2)}) collective-permute-start(bf16[384,128]{1,0:T(8,128)(2,1)S(1)} %get-tuple-element.58), channel_id=1, source_target_pairs={{1,0},{2,1},{3,2},{4,3},{5,4},{6,5},{7,6},{64,7},{9,8},{10,9},{11,... | collective-permute-start | bytes 294920 | tf_op jit(solution)/shard_map/ppermute | solution.py:613
  27.5 7.0 %collective-permute-start.2 = (bf16[384,128]{1,0:T(8,128)(2,1)S(1)}, bf16[384,128]{1,0:T(8,128)(2,1)S(1)}, u32[]{:S(2)}, u32[]{:S(2)}) collective-permute-start(bf16[384,128]{1,0:T(8,128)(2,1)S(1)} %get-tuple-element.58), channel_id=1, source_target_pairs={{0,1},{1,2},{2,3},{3,4},{4,5},{5,6},{6,7},{7,64},{8,9},{9,10},{10,... | collective-permute-start | bytes 294920 | tf_op jit(solution)/shard_map/ppermute | solution.py:613
  41.4 5.4 %collective-permute-start.4 = (bf16[8,12,8,128]{3,2,1,0:T(8,128)(2,1)S(1)}, bf16[8,12,8,128]{3,2,1,0:T(8,128)(2,1)S(1)}, u32[]{:S(2)}, u32[]{:S(2)}) collective-permute-start(bf16[8,12,8,128]{3,2,1,0:T(8,128)(2,1)S(1)} %get-tuple-element.71), channel_id=1, source_target_pairs={{0,8},{8,16},{16,24},{24,32},{32,40},{40,48},{48,56},{56,64},{64,7... | collective-permute-start | bytes 589832 | tf_op jit(solution)/shard_map/ppermute | solution.py:604
  44.1 5.4 %collective-permute-start.5 = (bf16[8,12,8,128]{3,2,1,0:T(8,128)(2,1)S(1)}, bf16[8,12,8,128]{3,2,1,0:T(8,128)(2,1)S(1)}, u32[]{:S(2)}, u32[]{:S(2)}) collective-permute-start(bf16[8,12,8,128]{3,2,1,0:T(8,128)(2,1)S(1)} %get-tuple-element.72), channel_id=1, source_target_pairs={{8,0},{16,8},{24,16},{32,24},{40,32},{48,40},{56,48},{64,56},{72,6... | collective-permute-start | bytes 589832 | tf_op jit(solution)/shard_map/ppermute | solution.py:604
  49.5 29.6 %all-to-all-start.1 = ((bf16[128,5,8,128]{3,2,1,0:T(8,128)(2,1)}), bf16[128,5,8,128]{3,2,1,0:T(8,128)(2,1)S(1)}, u32[]{:S(2)}, u32[]{:S(2)}) async-start(bf16[128,5,8,128]{3,2,1,0:T(8,128)(2,1)} %bitcast.18), calls=%async_computation.1 | async-start | bytes 2621440 | tf_op jit(solution)/shard_map/all_to_all | solution.py:688
  64.6 20.5 %collective-permute-start.7 = (f32[192,128]{1,0:T(8,128)S(1)}, f32[192,128]{1,0:T(8,128)S(1)}, u32[]{:S(2)}, u32[]{:S(2)}) collective-permute-start(f32[192,128]{1,0:T(8,128)S(1)} %get-tuple-element.80), channel_id=1, source_target_pairs={{1,0},{2,1},{3,2},{4,3},{5,4},{6,5},{7,6},{64,7},{9,8},{10,9},{11,... | collective-permute-start | bytes 294920 | tf_op jit(solution)/shard_map/ppermute | solution.py:613
  70.1 15.1 %collective-permute-start.6 = (f32[192,128]{1,0:T(8,128)S(1)}, f32[192,128]{1,0:T(8,128)S(1)}, u32[]{:S(2)}, u32[]{:S(2)}) collective-permute-start(f32[192,128]{1,0:T(8,128)S(1)} %get-tuple-element.80), channel_id=1, source_target_pairs={{0,1},{1,2},{2,3},{3,4},{4,5},{5,6},{6,7},{7,64},{8,9},{9,10},{10,... | collective-permute-start | bytes 294920 | tf_op jit(solution)/shard_map/ppermute | solution.py:613
  79.1 6.0 %copy-start = (bf16[128,5,8,128]{3,2,1,0:T(8,128)(2,1)}, bf16[128,5,8,128]{3,2,1,0:T(8,128)(2,1)S(1)}, u32[]{:S(2)}) copy-start(bf16[128,5,8,128]{3,2,1,0:T(8,128)(2,1)S(1)} %all-to-all-done.1) | copy-start | bytes 3932164
  79.9 10.6 %all-to-all-start.2 = ((f32[16,8,128]{2,1,0:T(8,128)}), f32[16,8,128]{2,1,0:T(8,128)S(1)}, u32[]{:S(2)}, u32[]{:S(2)}) async-start(f32[16,8,128]{2,1,0:T(8,128)} %total.1), calls=%async_computation.2 | async-start | bytes 131072 | tf_op jit(solution)/shard_map/all_to_all | solution.py:694
